TPU v7x, 32 devices: a whole 2x2x4 slice. The times are simulated.
32 devices in a mesh: pts: 2 (over core), geo: 16 (over z, y, x).
Axes of the slice: x: 2, y: 2, z: 4, core: 2. Of those that a mesh axis runs over, the one named last changes fastest.
Arguments:
- points: bfloat16 [16, 1024, 256], P('geo', 'pts'), may hold values from -6 to 6
- result_grad: bfloat16 [16, 1024, 256], P('geo', 'pts'), may hold values from -6 to 6
- lists_one: int32 [16, 8, 4], P('geo', 'pts'), may hold values from 0 to 7, all different within a row
- lists_two: int32 [16, 8, 4], P('geo', 'pts'), may hold values from 0 to 7, all different within a row
- rotation: int32 [16, 1024], P('geo', 'pts'), may hold values from 0 to 1023, each once within a row
- gain_one: bfloat16 [256], replicated, may hold values from 0.25 to 1.75
- qkv_one: bfloat16 [256, 768], replicated, may hold values from -0.375 to 0.375
- out_one: bfloat16 [256, 256], replicated, may hold values from -0.375 to 0.375
- gain_two: bfloat16 [256], replicated, may hold values from 0.25 to 1.75
- qkv_two: bfloat16 [256, 768], replicated, may hold values from -0.375 to 0.375
- out_two: bfloat16 [256, 256], replicated, may hold values from -0.375 to 0.375
Outputs:
- result: bfloat16 [16, 1024, 256], P('geo', 'pts')
- points_grad: bfloat16 [16, 1024, 256], P('geo', 'pts')
- gain_one_grad: float32 [256], replicated
- qkv_one_grad: float32 [256, 768], replicated
- out_one_grad: float32 [256, 256], replicated
- gain_two_grad: float32 [256], replicated
- qkv_two_grad: float32 [256, 768], replicated
- out_two_grad: float32 [256, 256], replicated
Inputs may be any that keep to these rules, and one draw needn't show every extreme that they name: `lists_one`: each ball lists 4 different balls of its geometry. `lists_two`: each ball lists 4 different balls of its geometry. `rotation`: each geometry's row is a permutation of its points.
All inputs are finite; a program needn't handle non-finite values.
Results may differ from a plain program's by a relative error of at most 0.012.
Values may be sent and summed in bfloat16 or wider, within the bound.
No kernel may reach another device: no remote copies, remote signals or barrier semaphores. Data moves between devices by JAX's collectives and lax.ppermute only.
A program may use at most 64 MiB of HBM per device.

v0:
```python
import jax
import jax.numpy as jnp
from jax import lax
from jax.sharding import PartitionSpec as P

HEADS = 4
BALL = 128
LISTED = 4


HIGH = lax.Precision.HIGHEST
EPSILON = 1e-06


def invert(order):
    return jnp.zeros_like(order).at[order].set(jnp.arange(order.shape[0], dtype=jnp.int32))


def ball_softmax(query_ball, keys):
    head_dim = query_ball.shape[-1]
    products = jnp.einsum("qhd,khd->hqk", query_ball, keys, preferred_element_type=jnp.float32)
    scores = products * head_dim ** (-0.5)
    topmost = jnp.max(scores, axis=-1, keepdims=True)
    exponent = jnp.exp(scores - topmost)
    return exponent / jnp.sum(exponent, axis=-1, keepdims=True)


def ball_forward(query_ball, keys, values):
    weights = ball_softmax(query_ball, keys).astype(jnp.bfloat16)
    mixed = jnp.einsum("hqk,khd->qhd", weights, values, preferred_element_type=jnp.float32)
    return mixed.astype(jnp.bfloat16)


def ball_backward(query_ball, keys, values, grad_ball):
    head_dim = query_ball.shape[-1]
    attention = ball_softmax(query_ball, keys)
    weights = attention.astype(jnp.bfloat16)
    weights_grad = jnp.einsum("qhd,khd->hqk", grad_ball, values, preferred_element_type=jnp.float32)
    weights_grad = lax.optimization_barrier(weights_grad.astype(jnp.bfloat16)).astype(jnp.float32)
    values_grad = jnp.einsum("hqk,qhd->khd", weights, grad_ball, preferred_element_type=jnp.float32)
    inner = jnp.sum(attention * weights_grad, axis=-1, keepdims=True)
    scores_grad = (attention * (weights_grad - inner) * head_dim ** (-0.5)).astype(jnp.bfloat16)
    query_grad = jnp.einsum("hqk,khd->qhd", scores_grad, keys, preferred_element_type=jnp.float32)
    keys_grad = jnp.einsum(
        "hqk,qhd->khd", scores_grad, query_ball, preferred_element_type=jnp.float32
    )
    return (query_grad, keys_grad, values_grad)


def attend_forward(queries, gathered, listed):
    rows_count, width = queries.shape
    head_dim = width // HEADS
    blocks = gathered.reshape(gathered.shape[0] // BALL, BALL, 2 * width)
    query_blocks = queries.reshape(rows_count // BALL, BALL, HEADS, head_dim)

    def one_ball(packed):
        query_ball, chosen_ids = packed
        chosen = jnp.take(blocks, chosen_ids, axis=0).reshape(LISTED * BALL, 2, HEADS, head_dim)
        return ball_forward(query_ball, chosen[:, 0], chosen[:, 1]).reshape(BALL, width)

    return lax.map(one_ball, (query_blocks, listed)).reshape(rows_count, width)


def attend_backward(queries, gathered, listed, mixed_grad):
    rows_count, width = queries.shape
    head_dim = width // HEADS
    total_balls = gathered.shape[0] // BALL
    blocks = gathered.reshape(total_balls, BALL, 2 * width)
    query_blocks = queries.reshape(rows_count // BALL, BALL, HEADS, head_dim)
    grad_blocks = mixed_grad.reshape(rows_count // BALL, BALL, HEADS, head_dim)

    def one_ball(buffer, packed):
        query_ball, grad_ball, chosen_ids = packed
        chosen = jnp.take(blocks, chosen_ids, axis=0).reshape(LISTED * BALL, 2, HEADS, head_dim)
        query_grad, keys_grad, values_grad = ball_backward(
            query_ball, chosen[:, 0], chosen[:, 1], grad_ball
        )
        stacked = jnp.stack([keys_grad, values_grad], axis=1).reshape(LISTED, BALL, 2 * width)
        buffer = buffer.at[chosen_ids].add(stacked)
        return (buffer, query_grad.reshape(BALL, width))

    empty = jnp.zeros((total_balls, BALL, 2 * width), jnp.float32)
    buffer, query_grads = lax.scan(one_ball, empty, (query_blocks, grad_blocks, listed))
    return (query_grads.reshape(rows_count, width), buffer.reshape(total_balls * BALL, 2 * width))


def layer_forward(rows, listed, gain, weight_in, weight_out):
    width = rows.shape[-1]
    inputs = rows.astype(jnp.float32)
    meansq = jnp.mean(inputs * inputs, axis=-1, keepdims=True)
    factor = lax.rsqrt(meansq + EPSILON)
    normed = (inputs * factor * gain.astype(jnp.float32)).astype(jnp.bfloat16)
    queries = jnp.dot(normed, weight_in[:, :width], preferred_element_type=jnp.float32).astype(
        jnp.bfloat16
    )
    keyvals = jnp.dot(normed, weight_in[:, width:], preferred_element_type=jnp.float32).astype(
        jnp.bfloat16
    )
    gathered = lax.all_gather(keyvals, "pts", axis=0, tiled=True)
    mixed = attend_forward(queries, gathered, listed)
    output = (inputs + jnp.dot(mixed, weight_out, preferred_element_type=jnp.float32)).astype(
        jnp.bfloat16
    )
    saved = (
        inputs,
        factor,
        normed,
        normed,
        queries,
        gathered,
        mixed,
        listed,
        gain,
        weight_in,
        weight_out,
    )
    return (output, saved)


def layer_backward(grad_out, saved):
    (
        inputs,
        factor,
        normed,
        all_normed,
        queries,
        gathered,
        mixed,
        listed,
        gain,
        weight_in,
        weight_out,
    ) = saved
    rows_count, width = grad_out.shape
    out_grad = jnp.einsum("nd,ne->de", mixed, grad_out, preferred_element_type=jnp.float32)
    mixed_grad = jnp.einsum(
        "ne,de->nd", grad_out, weight_out, preferred_element_type=jnp.float32
    ).astype(jnp.bfloat16)
    query_grad, partial_kv = attend_backward(queries, gathered, listed, mixed_grad)
    query_grad = query_grad.astype(jnp.bfloat16)
    query_weight_grad = jnp.einsum(
        "nd,ne->de", normed, query_grad, preferred_element_type=jnp.float32
    )
    normed_grad = jnp.einsum(
        "ne,de->nd", query_grad, weight_in[:, :width], preferred_element_type=jnp.float32
    )
    kv_weight = weight_in[:, width:].astype(jnp.float32)
    kv_grad = lax.psum_scatter(
        partial_kv.astype(jnp.bfloat16), "pts", scatter_dimension=0, tiled=True
    ).astype(jnp.float32)
    kv_weight_grad = jnp.einsum("nd,nc->dc", normed.astype(jnp.float32), kv_grad, precision=HIGH)
    normed_grad = normed_grad + jnp.einsum("nc,dc->nd", kv_grad, kv_weight, precision=HIGH)
    normed_grad = lax.optimization_barrier(normed_grad.astype(jnp.bfloat16)).astype(jnp.float32)
    scaled = normed_grad * gain.astype(jnp.float32)
    gain_grad = jnp.sum(normed_grad * (inputs * factor), axis=0)
    inner = jnp.mean(scaled * inputs, axis=-1, keepdims=True)
    inputs_grad = factor * scaled - inputs * (factor * factor * factor) * inner
    rows_grad = (grad_out.astype(jnp.float32) + inputs_grad).astype(jnp.bfloat16)
    weight_in_grad = jnp.concatenate([query_weight_grad, kv_weight_grad], axis=1)
    return (rows_grad, (gain_grad, weight_in_grad, out_grad))


def local(
    points,
    result_grad,
    lists_one,
    lists_two,
    rotation,
    gain_one,
    qkv_one,
    out_one,
    gain_two,
    qkv_two,
    out_two,
):
    rows_count, width = (points.shape[1], points.shape[2])
    hidden, first_saved = layer_forward(points[0], lists_one[0], gain_one, qkv_one, out_one)
    geometry_rows = lax.all_gather(hidden, "pts", axis=0, tiled=True)
    moved = jnp.take(geometry_rows, rotation[0], axis=0)
    result, second_saved = layer_forward(moved, lists_two[0], gain_two, qkv_two, out_two)
    moved_grad, grads_two = layer_backward(result_grad[0], second_saved)
    order = lax.all_gather(rotation[0], "pts", axis=0, tiled=True)
    all_grads = lax.all_gather(moved_grad, "pts", axis=0, tiled=True)
    inverse = invert(order)
    start = lax.axis_index("pts") * rows_count
    mine = lax.dynamic_slice_in_dim(inverse, start, rows_count, 0)
    hidden_grad = jnp.take(all_grads, mine, axis=0)
    points_grad, grads_one = layer_backward(hidden_grad, first_saved)
    pieces = list(grads_one) + list(grads_two)
    flat = jnp.concatenate([item.reshape(-1) for item in pieces])
    summed = lax.psum(flat, ("pts", "geo"))
    outputs = []
    offset = 0
    for item in pieces:
        length = item.size
        outputs.append(summed[offset : offset + length].reshape(item.shape))
        offset = offset + length
    return (
        result[None],
        points_grad[None],
        outputs[0],
        outputs[1],
        outputs[2],
        outputs[3],
        outputs[4],
        outputs[5],
    )


def solution(mesh):
    placed = (
        P("geo", "pts", None),
        P("geo", "pts", None),
        P("geo", "pts", None),
        P("geo", "pts", None),
        P("geo", "pts"),
        P(),
        P(),
        P(),
        P(),
        P(),
        P(),
    )
    return jax.shard_map(
        local,
        mesh=mesh,
        in_specs=placed,
        out_specs=(P("geo", "pts", None), P("geo", "pts", None), P(), P(), P(), P(), P(), P()),
        check_vma=False,
    )
```

profile of v0, /device:TPU:0, one launch (start us, length us, event | category | flops | bytes accessed | tf_op | source)
XLA Modules:
  0.0 457.2 jit_solution(15188328131203307751)
XLA Ops:
  14.4 9.3 %all-gather.4.cloned.1.call-done = bf16[1024,512]{1,0:T(8,128)(2,1)} async-done(((bf16[512,512]{1,0:T(8,128)(2,1)}), bf16[1024,512]{1,0:T(8,128)(2,1)}) %all-gather.4.cloned.1.call-update) | async-done | bytes 1048592 | tf_op jit(solution)/shard_map/all_gather | solution.py:99
  23.8 21.3 %while.44 = (s32[]{:T(128)}, bf16[4,128,256]{2,1,0:T(8,128)(2,1)S(1)}, s32[4,4]{1,0:T(4,128)}, bf16[8,128,512]{2,1,0:T(8,128)(2,1)}, bf16[4,128,4,64]{1,3,2,0:T(8,128)(2,1)S(1)}, /*index=5*/s32[]{:T(128)}) while((s32[]{:T(128)}, bf16[4,128,256]{2,1,0:T(8,128)(2,1)S(1)}, s32[4,4]{1,0:T(4,128)}, bf16[8,128,512]{2,1,0:T(8,128)(2,1)}, ...), condition=%wide.region_4.6_spmd, body=%wide.region_1.5_spmd.sunk | while | flops 102795800 | bytes 8593573 | solution.py:61
  54.1 8.0 %all-gather.6.cloned.1.call-done = bf16[1024,512]{1,0:T(8,128)(2,1)} async-done(((bf16[512,512]{1,0:T(8,128)(2,1)}), bf16[1024,512]{1,0:T(8,128)(2,1)}) %all-gather.6.cloned.1.call-update) | async-done | bytes 1048592 | tf_op jit(solution)/shard_map/all_gather | solution.py:99
  64.4 88.1 %while.46 = (s32[]{:T(128)}, f32[8,128,512]{2,1,0:T(8,128)}, bf16[4,128,256]{2,1,0:T(8,128)(2,1)}, s32[4,4]{1,0:T(4,128)}, bf16[4,128,4,64]{1,3,2,0:T(8,128)(2,1...) while((s32[]{:T(128)}, f32[8,128,512]{2,1,0:T(8,128)}, ...), condition=%wide.region_15.18_spmd, body=%wide.region_10.0_spmd.sunk | while | flops 174853664 | bytes 31285600 | solution.py:83
  70.9 3.9 fusion.250
  74.8 4.2 fusion.249
  83.0 3.4 scatter_fusion
  92.9 3.9 fusion.250
  96.8 4.2 fusion.249
  105.0 3.4 scatter_fusion
  114.9 3.9 fusion.250
  118.8 4.2 fusion.249
  127.0 3.4 scatter_fusion
  137.0 3.9 fusion.250
  140.8 4.2 fusion.249
  149.1 3.4 scatter_fusion
  157.3 4.5 scatter_custom_fusion.2
  175.3 82.6 %while.47 = (s32[]{:T(128)}, f32[8,128,512]{2,1,0:T(8,128)}, bf16[4,128,256]{2,1,0:T(8,128)(2,1)}, s32[4,4]{1,0:T(4,128)S(1)}, bf16[4,128,4,64]{1,3,2,0:T(8,128)...) while((s32[]{:T(128)}, f32[8,128,512]{2,1,0:T(8,128)}, ...), condition=%wide.region_24.27_spmd, body=%wide.region_19.26_spmd.sunk | while | flops 174853664 | bytes 31285600 | solution.py:83
  180.5 3.9 fusion.259
  184.4 4.2 fusion.258
  192.6 3.4 scatter_fusion.1
  201.2 3.9 fusion.259
  205.1 4.2 fusion.258
  213.3 3.4 scatter_fusion.1
  221.8 3.9 fusion.259
  225.7 4.2 fusion.258
  233.9 3.4 scatter_fusion.1
  242.5 3.9 fusion.259
  246.3 4.2 fusion.258
  254.6 3.4 scatter_fusion.1
  261.8 25.5 %while.45 = (s32[]{:T(128)}, bf16[4,128,256]{2,1,0:T(8,128)(2,1)}, s32[4,4]{1,0:T(4,128)}, bf16[8,128,512]{2,1,0:T(8,128)(2,1)S(1)}, bf16[4,128,4,64]{1,3,2,0:T(8,128)(2,1)}, /*index=5*/s32[]{:T(128)}) while((s32[]{:T(128)}, bf16[4,128,256]{2,1,0:T(8,128)(2,1)}, s32[4,4]{1,0:T(4,128)}, bf16[8,128,512]{2,1,0:T(8,128)(2,1)S(1)}, ...), condition=%wide.region_9.12_spmd, body=%wide.region_6.11_spmd.sunk | while | flops 102795800 | bytes 8593573 | solution.py:61
  309.9 133.4 %all-reduce.2.cloned.1.call-done = f32[524800]{0:T(1024)} async-done(((f32[524800]{0:T(1024)}), f32[524800]{0:T(1024)}) %all-reduce.2.cloned.1.call-update) | async-done | bytes 2099216 | tf_op jit(solution)/shard_map/psum | solution.py:191
  (442 shorter events, 194.3 us)
Async XLA Ops:
  7.2 38.0 %copy-start = (bf16[256,256]{1,0:T(8,128)(2,1)S(1)}, bf16[256,256]{1,0:T(8,128)(2,1)}, u32[]{:S(2)}) copy-start(bf16[256,256]{1,0:T(8,128)(2,1)} %param.30) | copy-start | bytes 393220
  7.2 16.6 %all-gather.4.cloned.1.call-start = ((), (), s32[]{:S(2)}) async-start(), calls=%async_computation.2 | async-start | bytes 1572864 | tf_op jit(solution)/shard_map/all_gather | solution.py:99
  7.9 6.4 %copy-start.33 = (f32[256]{0:T(256)}, f32[256]{0:T(256)S(1)}, u32[]{:S(2)}) copy-start(f32[256]{0:T(256)S(1)} %convert_element_type.154) | copy-start | bytes 3076
  7.9 6.4 %copy-start.31 = (s32[1,512]{1,0:T(1,128)S(1)}, s32[1,512]{1,0:T(1,128)}, u32[]{:S(2)}) copy-start(s32[1,512]{1,0:T(1,128)} %param.27) | copy-start | bytes 6148
  11.8 50.2 %all-gather.6.cloned.1.call-start = ((), (), s32[]{:S(2)}) async-start(), calls=%async_computation.3 | async-start | bytes 1572864 | tf_op jit(solution)/shard_map/all_gather | solution.py:99
  12.6 40.0 %copy-start.37 = (f32[256]{0:T(256)}, f32[256]{0:T(256)S(1)}, u32[]{:S(2)}) copy-start(f32[256]{0:T(256)S(1)} %convert_element_type.160) | copy-start | bytes 3076
  23.8 21.4 %copy-start.4 = (bf16[1,512,256]{2,1,0:T(8,128)(2,1)S(1)}, bf16[1,512,256]{2,1,0:T(8,128)(2,1)}, u32[]{:S(2)}) copy-start(bf16[1,512,256]{2,1,0:T(8,128)(2,1)} %param.23) | copy-start | bytes 786436
  45.1 4.8 %copy-start.12 = (bf16[4,128,4,64]{1,3,2,0:T(8,128)(2,1)}, bf16[4,128,4,64]{1,3,2,0:T(8,128)(2,1)S(1)}, u32[]{:S(2)}) copy-start(bf16[4,128,4,64]{1,3,2,0:T(8,128)(2,1)S(1)} %get-tuple-element.543) | copy-start | bytes 786436
  45.1 4.8 %copy-start.17 = (bf16[4,128,256]{2,1,0:T(8,128)(2,1)}, bf16[4,128,256]{2,1,0:T(8,128)(2,1)S(1)}, u32[]{:S(2)}) copy-start(bf16[4,128,256]{2,1,0:T(8,128)(2,1)S(1)} %get-tuple-element.140) | copy-start | bytes 786436
  45.1 5.4 %copy-start.28 = (bf16[256,768]{1,0:T(8,128)(2,1)S(1)}, bf16[256,768]{1,0:T(8,128)(2,1)}, u32[]{:S(2)}) copy-start(bf16[256,768]{1,0:T(8,128)(2,1)} %param.32) | copy-start | bytes 1179652
  47.7 4.0 copy-start.25
  49.7 14.7 %copy-start.5 = (bf16[512,256]{1,0:T(8,128)(2,1)}, bf16[512,256]{1,0:T(8,128)(2,1)S(1)}, u32[]{:S(2)}) copy-start(bf16[512,256]{1,0:T(8,128)(2,1)S(1)} %gather_fusion.4) | copy-start | bytes 786436
  51.7 113.5 %reduce-scatter.3.cloned.1.call-start = ((), (), s32[]{:S(2)}) async-start(), calls=%async_computation.4 | async-start | bytes 1572864 | tf_op jit(solution)/shard_map/reduce_scatter | solution.py:148
  74.8 4.3 copy-start.46
  96.8 4.2 copy-start.46
  118.8 4.2 copy-start.46
  140.8 4.3 copy-start.46
  152.5 12.7 %copy-start.29 = (bf16[256,768]{1,0:T(8,128)(2,1)S(1)}, bf16[256,768]{1,0:T(8,128)(2,1)}, u32[]{:S(2)}) copy-start(bf16[256,768]{1,0:T(8,128)(2,1)} %param.32) | copy-start | bytes 1179652
  152.5 14.1 %copy-start.21 = (bf16[4,128,256]{2,1,0:T(8,128)(2,1)S(1)}, bf16[4,128,256]{2,1,0:T(8,128)(2,1)}, u32[]{:S(2)}) copy-start(bf16[4,128,256]{2,1,0:T(8,128)(2,1)} %get-tuple-element.142) | copy-start | bytes 786436
  155.3 11.6 %copy-start.6 = (bf16[512,256]{1,0:T(8,128)(2,1)S(1)}, bf16[512,256]{1,0:T(8,128)(2,1)}, u32[]{:S(2)}) copy-start(bf16[512,256]{1,0:T(8,128)(2,1)} %copy-done.5) | copy-start | bytes 786436
  155.3 11.6 %copy-start.38 = (f32[256]{0:T(256)S(1)}, f32[256]{0:T(256)}, u32[]{:S(2)}) copy-start(f32[256]{0:T(256)} %copy-done.37) | copy-start | bytes 3076
  155.3 12.5 %copy-start.9 = (bf16[1,512,256]{2,1,0:T(8,128)(2,1)S(1)}, bf16[1,512,256]{2,1,0:T(8,128)(2,1)}, u32[]{:S(2)}) copy-start(bf16[1,512,256]{2,1,0:T(8,128)(2,1)} %param.24) | copy-start | bytes 786436
  155.3 12.5 %copy-start.36 = (f32[512]{0:T(512)S(1)}, f32[512]{0:T(512)}, u32[]{:S(2)}) copy-start(f32[512]{0:T(512)} %get-tuple-element.268) | copy-start | bytes 6148
  155.3 138.6 %reduce-scatter.5.cloned.1.call-start = ((), (), s32[]{:S(2)}) async-start(), calls=%async_computation.5 | async-start | bytes 1572864 | tf_op jit(solution)/shard_map/reduce_scatter | solution.py:148
  161.9 10.3 %copy-start.41 = (pred[512]{0:T(512)(128)(4,1)}, pred[512]{0:T(512)(128)(4,1)S(1)}, u32[]{:S(2)}) copy-start(pred[512]{0:T(512)(128)(4,1)S(1)} %get-tuple-element.254) | copy-start | bytes 1540
  184.4 4.2 copy-start.47
  205.1 4.2 copy-start.47
  225.7 4.2 copy-start.47
  246.3 4.2 copy-start.47
  260.8 182.5 %all-reduce.2.cloned.1.call-start = ((), (), s32[]{:S(2)}) async-start(), calls=%async_computation.6 | async-start | bytes 4202496 | tf_op jit(solution)/shard_map/psum | solution.py:191
  261.8 27.0 %copy-start.39 = (f32[256]{0:T(256)S(1)}, f32[256]{0:T(256)}, u32[]{:S(2)}) copy-start(f32[256]{0:T(256)} %copy-done.37) | copy-start | bytes 3076
  297.1 5.5 %copy-start.40 = (f32[256]{0:T(256)S(1)}, f32[256]{0:T(256)}, u32[]{:S(2)}) copy-start(f32[256]{0:T(256)} %get-tuple-element.194) | copy-start | bytes 3076
  (45 other events, 112.1 us)
Sparse Core Ops, SparseCore 0:
  12.0 11.7 all-gather.3
  51.8 10.1 all-gather.5
  155.4 9.6 reduce-scatter.2
  260.9 9.7 reduce-scatter.4
  308.0 135.2 all-reduce.1
where the time goes:
time: 461 us; the launch traced here: 457 us
  waiting for transfers between devices  154 us (33%)
  matrix products  135 us (29%)
  local copies, waits for them, and re-layouts  88.3 us (19%)
  other arithmetic  57.4 us (12%)
  between operations  14.4 us (3%)
  blocking collectives  6.41 us (1%)
    psum x1, waiting for transfers between devices, local(): summed = lax.psum(flat, ('pts', 'geo'))  133 us
    dot_general x8, matrix products, ball_backward(): jnp.einsum('hqk,qhd->khd', scores_grad, query_ball, preferred_element_typ...  33.8 us
    dot_general x8, matrix products, ball_backward(): jnp.einsum('hqk,khd->qhd', scores_grad, keys, preferred_element_type=jnp....  31.1 us
    scatter-add x8, other arithmetic, one_ball(): buffer = buffer.at[chosen_ids].add(stacked)  27.1 us
    sub x16, matrix products, ball_softmax(): exponent = jnp.exp(scores - topmost)  24 us
    all_gather x2, waiting for transfers between devices, layer_forward(): gathered = lax.all_gather(keyvals, 'pts', axis=0, tiled=True)  17.3 us
    gather x16, local copies, waits for them, and re-layouts, one_ball(): jnp.take(blocks, chosen_ids, axis=0)  14.2 us
    dynamic_update_slice x16, local copies, waits for them, and re-layouts, attend_backward(): lax.scan(one_ball, empty, (query_blocks, grad_blocks, listed))  12.6 us
  transfers between devices with their start and end apart: 5, of which 4 were waited for; matrix products, arithmetic and copies ran while one was open for 9% of the time, Pallas kernels for 0%

commit v1 on v0

v1 whole, which is shorter than its diff:
```python
import functools

import jax
import jax.numpy as jnp
from jax import lax
from jax.experimental import pallas as pl
from jax.experimental.pallas import tpu as pltpu
from jax.sharding import PartitionSpec as P

HEADS = 4
BALL = 128
LISTED = 4
EPSILON = 1e-06
BF = jnp.bfloat16
F32 = jnp.float32
SWAP = ((0, 1), (1, 0))
PIECES = 4

VMEM = pl.BlockSpec(memory_space=pltpu.VMEM)
SMEM = pl.BlockSpec(memory_space=pltpu.SMEM)
PARAMS = pltpu.CompilerParams(vmem_limit_bytes=40 * 1024 * 1024)


def dot(a, b, dims=((1,), (0,))):
    return lax.dot_general(a, b, (dims, ((), ())), preferred_element_type=F32)


def norm_factor(x):
    return lax.rsqrt(jnp.mean(x * x, axis=-1, keepdims=True) + EPSILON)


def own_columns(weight, core, half):
    width = weight.shape[0]
    return [weight[:, pl.ds(pl.multiple_of(i * width + core * half, half), half)] for i in range(3)]


def project(normed, columns):
    qkv = dot(normed, jnp.concatenate(columns, axis=1))
    half = columns[0].shape[1]
    scale = (2 * half // HEADS) ** (-0.5)
    return qkv[:, :half].astype(BF) * BF(scale), qkv[:, half:].astype(BF)


def stack_heads(rows):
    lane = lax.broadcasted_iota(jnp.int32, rows.shape, 1)
    first = lane < rows.shape[1] // 2
    zero = jnp.zeros_like(rows)
    return jnp.concatenate([jnp.where(first, rows, zero), jnp.where(first, zero, rows)], axis=0)


def unstack_heads(stacked):
    rows = stacked.shape[0] // 2
    lane = lax.broadcasted_iota(jnp.int32, (rows, stacked.shape[1]), 1)
    return jnp.where(lane < stacked.shape[1] // 2, stacked[:rows], stacked[rows:])


def listed_balls(ball, mine, other, core, offset, local_balls):
    base = offset + lax.rem(ball, local_balls) * LISTED
    is_mine = ball // local_balls == core
    return [jnp.where(is_mine, mine[base + j], other[base + j]) for j in range(LISTED)]


def rows_of(ball):
    return pl.ds(pl.multiple_of(ball * BALL, BALL), BALL)


def pick(ref, listed, first, half):
    return jnp.concatenate([ref[rows_of(i), first : first + half] for i in listed], axis=0)


def softmax_parts(stacked, keys):
    scores = dot(stacked, keys, ((1,), (1,)))
    exponent = jnp.exp(scores - jnp.max(scores, axis=-1, keepdims=True))
    return exponent, 1.0 / jnp.sum(exponent, axis=-1, keepdims=True)


def mix(exponent, inverse, values):
    return unstack_heads(dot(exponent.astype(BF), values) * inverse)


def ball_backward(stacked, keys, values, exponent, inverse, mixed, mixed_grad):
    grad = stack_heads(mixed_grad.astype(F32)) * inverse
    inner = jnp.sum(grad * jnp.concatenate([mixed, mixed], axis=0), axis=-1, keepdims=True)
    grad = grad.astype(BF)
    scores_grad = (exponent * (dot(grad, values, ((1,), (1,))) - inner)).astype(BF)
    scale = (stacked.shape[1] // 2) ** (-0.5)
    queries_grad = unstack_heads(dot(scores_grad, keys)) * scale
    keys_grad = dot(stacked, scores_grad, ((0,), (0,)))
    values_grad = dot(grad, exponent.astype(BF), ((0,), (0,)))
    return queries_grad.astype(BF), keys_grad, values_grad


def add_listed(ref, listed, part):
    for j, i in enumerate(listed):
        ref[i] += part[:, j * BALL : (j + 1) * BALL]


def qkv_grads(dq, dk_ref, dv_ref):
    balls = dk_ref.shape[0]
    parts = [dq]
    for ref in (dk_ref, dv_ref):
        parts.append(jnp.concatenate([ref[i].T for i in range(balls)], axis=0).astype(BF))
    return jnp.concatenate(parts, axis=1)


def store_pieces(ref, pieces, slot_bits):
    for p, piece in enumerate(pieces):
        ref[p ^ slot_bits] = piece.astype(BF)


def weight_pieces(normed, grads, mixed, grad_out):
    half = mixed.shape[1]
    weight = dot(normed, grads, ((0,), (0,)))
    out = dot(mixed, grad_out, ((0,), (0,)))
    pieces = [weight[:, i * half : (i + 1) * half] for i in range(3)]
    return pieces + [jnp.concatenate([out[:, :half], out[:, half:]], axis=0)]


def norm_backward(normed_grad, x, gain, grad_out):
    factor = norm_factor(x)
    scaled = normed_grad.astype(BF).astype(F32) * gain
    inner = jnp.mean(scaled * x, axis=-1, keepdims=True)
    return (grad_out.astype(F32) + factor * scaled - x * (factor * factor * factor) * inner).astype(BF)


def slot_bits():
    return lax.rem(lax.axis_index("geo"), PIECES)


def first_forward(mine, other, x_mine, x_other, gain, weight, mixed_ref, q_ref, kv_ref, normed_ref):
    core = lax.axis_index("pts")
    local, width = x_mine.shape
    half = width // 2
    columns = own_columns(weight, core, half)
    scaled_gain = gain[...].astype(F32)
    for place, ref in ((core, x_mine), (1 - core, x_other)):
        x = ref[...].astype(F32)
        normed = (x * norm_factor(x) * scaled_gain).astype(BF)
        rows = pl.ds(pl.multiple_of(place * local, local), local)
        normed_ref[rows, :] = normed
        q_ref[rows, :], kv_ref[rows, :] = project(normed, columns)

    def one_ball(ball, carry):
        listed = listed_balls(ball, mine, other, core, 0, local // BALL)
        stacked = stack_heads(q_ref[rows_of(ball), :])
        exponent, inverse = softmax_parts(stacked, pick(kv_ref, listed, 0, half))
        mixed = mix(exponent, inverse, pick(kv_ref, listed, half, half))
        mixed_ref[rows_of(ball), :] = mixed.astype(BF)
        return carry

    lax.fori_loop(0, 2 * local // BALL, one_ball, 0)


def second_layer(
    mine, other, rot_mine, rot_other, x_mine, x_other, mixed_mine, mixed_other, grad_mine, grad_other,
    out_one, gain, weight, out_two,
    moved_ref, mixed_ref, part_ref, pieces_ref,
    both_ref, hidden_ref, grad_ref, normed_ref, q_ref, kv_ref, mg_ref, dq_ref, dk_ref, dv_ref,
):
    core = lax.axis_index("pts")
    local, width = x_mine.shape
    half = width // 2
    total = 2 * local

    def lanes(place):
        return pl.ds(pl.multiple_of(place * half, half), half)

    def rows(place):
        return pl.ds(pl.multiple_of(place * local, local), local)

    both_ref[:, lanes(core)] = mixed_mine[...]
    both_ref[:, lanes(1 - core)] = mixed_other[...]
    for place, ref, grad in ((core, x_mine, grad_mine), (1 - core, x_other, grad_other)):
        out = dot(both_ref[rows(place), :], out_one[...])
        hidden_ref[rows(place), :] = (ref[...].astype(F32) + out).astype(BF)
        grad_ref[rows(place), :] = grad[...]
    hidden = hidden_ref[...]
    columns = own_columns(weight, core, half)
    scaled_gain = gain[...].astype(F32)
    lane = lax.broadcasted_iota(jnp.int32, (BALL, total), 1).astype(F32)
    for place, ref in ((core, rot_mine), (1 - core, rot_other)):
        for j in range(local // BALL):
            row = ref[j : j + 1, :].astype(F32)
            column = jnp.broadcast_to(row, (BALL, BALL)).T[:, :1]
            moved = dot((lane == column).astype(BF), hidden)
            at = pl.ds(pl.multiple_of(place * local + j * BALL, BALL), BALL)
            normed = (moved * norm_factor(moved) * scaled_gain).astype(BF)
            moved_ref[at, :] = moved.astype(BF)
            normed_ref[at, :] = normed
    q_ref[...], kv_ref[...] = project(normed_ref[...], columns)
    out_columns = out_two[pl.ds(pl.multiple_of(core * half, half), half), :]
    mg_ref[...] = dot(grad_ref[...], out_columns, ((1,), (1,))).astype(BF)
    dk_ref[...] = jnp.zeros_like(dk_ref)
    dv_ref[...] = jnp.zeros_like(dv_ref)

    def one_ball(ball, carry):
        listed = listed_balls(ball, mine, other, core, (local // BALL) * LISTED, local // BALL)
        at = rows_of(ball)
        stacked = stack_heads(q_ref[at, :])
        keys = pick(kv_ref, listed, 0, half)
        values = pick(kv_ref, listed, half, half)
        exponent, inverse = softmax_parts(stacked, keys)
        mixed = mix(exponent, inverse, values)
        mixed_ref[at, :] = mixed.astype(BF)
        dq, dk, dv = ball_backward(stacked, keys, values, exponent, inverse, mixed, mg_ref[at, :])
        dq_ref[at, :] = dq
        add_listed(dk_ref, listed, dk)
        add_listed(dv_ref, listed, dv)
        return carry

    lax.fori_loop(0, total // BALL, one_ball, 0)
    grads = qkv_grads(dq_ref[...], dk_ref, dv_ref)
    part_ref[...] = dot(grads, jnp.concatenate(columns, axis=1), ((1,), (1,))).astype(BF)
    store_pieces(pieces_ref, weight_pieces(normed_ref[...], grads, mixed_ref[...], grad_ref[...]), slot_bits())


def first_backward(
    mine, other, rot_mine, rot_other, part_mine, part_other, moved_ref, grad_mine, grad_other, gain_two,
    mixed_ref, normed_ref, q_ref, kv_ref, weight, out_one, pieces_two,
    keep_ref, send_ref, part_keep, part_send, hidden_grad_mine,
    rows_grad_ref, hg_ref, mg_ref, dq_ref, dk_ref, dv_ref, pieces_ref,
):
    core = lax.axis_index("pts")
    local, width = grad_mine.shape
    half = width // 2
    total = 2 * local

    def rows(place):
        return pl.ds(pl.multiple_of(place * local, local), local)

    gain = gain_two[...].astype(F32)
    for place, grad in ((core, grad_mine), (1 - core, grad_other)):
        normed_grad = part_mine[rows(place), :].astype(F32) + part_other[rows(place), :].astype(F32)
        x = moved_ref[rows(place), :].astype(F32)
        rows_grad_ref[rows(place), :] = norm_backward(normed_grad, x, gain, grad[...])

    place_of = jnp.where(core == 0, rot_mine[: local // BALL, :], rot_other[: local // BALL, :])
    place_of_high = jnp.where(core == 0, rot_other[: local // BALL, :], rot_mine[: local // BALL, :])
    row_of = [place_of[j : j + 1, :] for j in range(local // BALL)]
    row_of += [place_of_high[j : j + 1, :] for j in range(local // BALL)]
    order = jnp.concatenate(row_of, axis=1).astype(F32)
    rows_grad = rows_grad_ref[...]
    sub = lax.broadcasted_iota(jnp.int32, (BALL, total), 0).astype(F32)
    out_rows = out_one[pl.ds(pl.multiple_of(core * half, half), half), :]
    for j in range(total // BALL):
        chosen = (sub + float(j * BALL) == order).astype(BF)
        hg_ref[j * BALL : (j + 1) * BALL, :] = dot(chosen, rows_grad).astype(BF)
    hidden_grad = hg_ref[...]
    hidden_grad_mine[...] = hg_ref[rows(core), :]
    mg_ref[...] = dot(hidden_grad, out_rows, ((1,), (1,))).astype(BF)
    dk_ref[...] = jnp.zeros_like(dk_ref)
    dv_ref[...] = jnp.zeros_like(dv_ref)

    def one_ball(ball, carry):
        listed = listed_balls(ball, mine, other, core, 0, local // BALL)
        at = rows_of(ball)
        stacked = stack_heads(q_ref[at, :])
        keys = pick(kv_ref, listed, 0, half)
        values = pick(kv_ref, listed, half, half)
        exponent, inverse = softmax_parts(stacked, keys)
        mixed = mixed_ref[at, :].astype(F32)
        dq, dk, dv = ball_backward(stacked, keys, values, exponent, inverse, mixed, mg_ref[at, :])
        dq_ref[at, :] = dq
        add_listed(dk_ref, listed, dk)
        add_listed(dv_ref, listed, dv)
        return carry

    lax.fori_loop(0, total // BALL, one_ball, 0)
    grads = qkv_grads(dq_ref[...], dk_ref, dv_ref)
    columns = jnp.concatenate(own_columns(weight, core, half), axis=1)
    store_pieces(pieces_ref, weight_pieces(normed_ref[...], grads, mixed_ref[...], hidden_grad), slot_bits())
    for slot in range(PIECES // 2):
        keep_ref[slot, 0] = pieces_ref[slot]
        keep_ref[slot, 1] = pieces_two[slot]
        send_ref[slot, 0] = pieces_ref[slot + PIECES // 2]
        send_ref[slot, 1] = pieces_two[slot + PIECES // 2]
    part = dot(grads, columns, ((1,), (1,)))
    hg_ref[...] = part.astype(BF)
    part_keep[...] = hg_ref[rows(core), :]
    part_send[...] = hg_ref[rows(1 - core), :]


def finish_rows(
    part_mine, part_other, x_mine, gain, hidden_grad, moved, mixed_mine, mixed_other, out_two,
    points_grad, result, both_ref,
):
    core = lax.axis_index("pts")
    local, width = x_mine.shape
    half = width // 2
    normed_grad = part_mine[...].astype(F32) + part_other[...].astype(F32)
    points_grad[...] = norm_backward(
        normed_grad, x_mine[...].astype(F32), gain[...].astype(F32), hidden_grad[...]
    )
    rows = pl.ds(pl.multiple_of(core * local, local), local)
    both_ref[:, pl.ds(pl.multiple_of(core * half, half), half)] = mixed_mine[rows, :]
    both_ref[:, pl.ds(pl.multiple_of((1 - core) * half, half), half)] = mixed_other[...]
    out = dot(both_ref[...], out_two[...])
    result[...] = (moved[rows, :].astype(F32) + out).astype(BF)


def finish_weights(
    near_mine, far_mine, near_other, far_other, gain_one, gain_two, weight_one, weight_two,
    gain_one_grad, qkv_one_grad, out_one_grad, gain_two_grad, qkv_two_grad, out_two_grad,
    slots_ref,
):
    core = lax.axis_index("pts")
    half = near_mine.shape[-1]
    width = 2 * half
    mask = slot_bits()
    groups = ((core, near_mine, far_mine), (1 - core, near_other, far_other))
    for side, (_, near, far) in enumerate(groups):
        for slot in range(PIECES // 2):
            slots_ref[side, slot] = near[slot]
            slots_ref[side, slot + PIECES // 2] = far[slot]
    layers = (
        (gain_one, weight_one, gain_one_grad, qkv_one_grad, out_one_grad),
        (gain_two, weight_two, gain_two_grad, qkv_two_grad, out_two_grad),
    )
    for layer, (gain, weight, gain_grad, qkv_grad, out_grad) in enumerate(layers):
        folded = jnp.zeros((width, half), F32)
        for side, (place, _, _) in enumerate(groups):
            for p in range(3):
                piece = slots_ref[side, p ^ mask, layer].astype(F32)
                at = pl.ds(pl.multiple_of(p * width + place * half, half), half)
                qkv_grad[:, at] = piece
                folded = folded + piece * weight[:, at].astype(F32)
            piece = slots_ref[side, 3 ^ mask, layer].astype(F32)
            at = pl.ds(pl.multiple_of(place * half, half), half)
            out_grad[at, :half] = piece[:half]
            out_grad[at, half:] = piece[half:]
        gain_grad[...] = jnp.sum(folded.T, axis=0, keepdims=True) / gain[...].astype(F32)


def shape(dims, dtype=BF):
    return jax.ShapeDtypeStruct(dims, dtype)


def call(body, name, ins, outs, scratch=()):
    specs = [SMEM if kind == "s" else VMEM for kind, _ in ins]
    return pl.pallas_call(
        body,
        name=name,
        out_shape=outs,
        in_specs=specs,
        out_specs=[VMEM] * len(outs),
        scratch_shapes=[pltpu.VMEM(dims, dtype) for dims, dtype in scratch],
        compiler_params=PARAMS,
    )(*[array for _, array in ins])


def add(a, b):
    return (a.astype(F32) + b.astype(F32)).astype(BF)


def local(
    geo,
    points,
    result_grad,
    lists_one,
    lists_two,
    rotation,
    gain_one,
    qkv_one,
    out_one,
    gain_two,
    qkv_two,
    out_two,
):
    rows, width = points.shape[1:]
    half = width // 2
    total = 2 * rows
    balls = total // BALL

    def swap(array):
        return lax.ppermute(array, "pts", SWAP)

    def across(array, bit):
        return lax.ppermute(array, "geo", [(i, i ^ bit) for i in range(geo)])

    x = points[0]
    grad = result_grad[0]
    lists = jnp.concatenate([lists_one.reshape(-1), lists_two.reshape(-1)])
    rot = rotation.reshape(rows // BALL, BALL)
    x_other = swap(x)
    lists_other = swap(lists)
    grad_other = swap(grad)
    rot_other = swap(rot)
    gain_one = gain_one.reshape(1, width)
    gain_two = gain_two.reshape(1, width)

    mixed, q, kv, normed = call(
        first_forward,
        "first_forward",
        [("s", lists), ("s", lists_other)] + [("v", a) for a in (x, x_other, gain_one, qkv_one)],
        [shape((total, half)), shape((total, half)), shape((total, width)), shape((total, width))],
    )
    mixed_other = swap(mixed)
    blocks = ((balls, half, BALL), F32)
    moved, mixed_two, part_two, pieces_two = call(
        second_layer,
        "second_layer",
        [("s", lists), ("s", lists_other)]
        + [
            ("v", a)
            for a in (
                rot, rot_other, x, x_other, mixed, mixed_other, grad, grad_other, out_one, gain_two, qkv_two, out_two
            )
        ],
        [shape((total, width)), shape((total, half)), shape((total, width)), shape((PIECES, width, half))],
        [
            ((total, width), BF),
            ((total, width), BF),
            ((total, width), BF),
            ((total, width), BF),
            ((total, half), BF),
            ((total, width), BF),
            ((total, half), BF),
            ((total, half), BF),
            blocks,
            blocks,
        ],
    )
    part_two_other = swap(part_two)
    core = lax.axis_index("pts")
    mixed_two_other = swap(lax.dynamic_slice_in_dim(mixed_two, (1 - core) * rows, rows, 0))
    keep, send, part_keep, part_send, hidden_grad = call(
        first_backward,
        "first_backward",
        [("s", lists), ("s", lists_other)]
        + [
            ("v", a)
            for a in (
                rot, rot_other, part_two, part_two_other, moved, grad, grad_other, gain_two,
                mixed, normed, q, kv, qkv_one, out_one, pieces_two,
            )
        ],
        [shape((PIECES // 2, 2, width, half))] * 2 + [shape((rows, width))] * 3,
        [
            ((total, width), BF),
            ((total, width), BF),
            ((total, half), BF),
            ((total, half), BF),
            blocks,
            blocks,
            ((PIECES, width, half), BF),
        ],
    )
    part_other = swap(part_send)
    summed = add(keep, across(send, 2))
    summed = add(summed[:1], across(summed[1:], 1))
    bit = PIECES
    while bit < geo:
        summed = add(summed, across(summed, bit))
        bit *= 2
    near = jnp.concatenate([summed, across(summed, 1)], axis=0)
    far = across(near, 2)
    near_other = swap(near)
    far_other = swap(far)
    points_grad, result = call(
        finish_rows,
        "finish_rows",
        [
            ("v", a)
            for a in (part_keep, part_other, x, gain_one, hidden_grad, moved, mixed_two, mixed_two_other, out_two)
        ],
        [shape((rows, width))] * 2,
        [((rows, width), BF)],
    )
    vector, matrix, square = (shape(dims, F32) for dims in ((1, width), (width, 3 * width), (width, width)))
    grads = call(
        finish_weights,
        "finish_weights",
        [("v", a) for a in (near, far, near_other, far_other, gain_one, gain_two, qkv_one, qkv_two)],
        [vector, matrix, square] * 2,
        [((2, PIECES, 2, width, half), BF)],
    )
    return (
        result[None],
        points_grad[None],
        grads[0].reshape(width),
        grads[1],
        grads[2],
        grads[3].reshape(width),
        grads[4],
        grads[5],
    )


def solution(mesh):
    rows = P("geo", "pts", None)
    placed = (rows,) * 4 + (P("geo", "pts"),) + (P(),) * 6
    return jax.shard_map(
        functools.partial(local, mesh.shape["geo"]),
        mesh=mesh,
        in_specs=placed,
        out_specs=(rows, rows) + (P(),) * 6,
        check_vma=False,
    )
```

time: 461 us -> 79.3 us (0.17)
  matrix products: 135 us -> 0 us
  waiting for transfers between devices: 154 us -> 30.2 us
  local copies, waits for them, and re-layouts: 88.3 us -> 3.39 us
  other arithmetic: 57.4 us -> 0.29 us
  Pallas kernels: 0 us -> 29.3 us
  starting transfers between devices: 0.43 us -> 15.1 us
  between operations: 14.4 us -> 0.77 us
  blocking collectives: 6.41 us -> 0 us
    psum x1 -> x0, waiting for transfers between devices: 133 us -> none  [local(): summed = lax.psum(flat, ('pts', 'geo'))]
    dot_general x66 -> x0, matrix products: 111 us -> none  [the longest x8 33.8 us: ball_backward(): jnp.einsum('hqk,qhd->khd', scores_grad, query_ball, preferred_element_typ...]
    ppermute x0 -> x16, waiting for transfers between devices: none -> 30.2 us  [the longest x6 26 us: across(): return lax.ppermute(array, 'geo', [(i, i ^ bit) for i in range(geo)])]
    pallas_call x0 -> x5, Pallas kernels: none -> 29.3 us  [call(): pl.pallas_call(body, name=name, out_shape=outs, in_specs=specs, out_specs...]
    scatter-add x8 -> x0, other arithmetic: 27.1 us -> none  [one_ball(): buffer = buffer.at[chosen_ids].add(stacked)]
    sub x16 -> x0, matrix products: 24 us -> none  [ball_softmax(): exponent = jnp.exp(scores - topmost)]
    gather x18 -> x0, local copies, waits for them, and re-layouts: 18.1 us -> none  [the longest x16 14.2 us: one_ball(): jnp.take(blocks, chosen_ids, axis=0)]
    all_gather x2 -> x0, waiting for transfers between devices: 17.3 us -> none  [layer_forward(): gathered = lax.all_gather(keyvals, 'pts', axis=0, tiled=True)]
  transfers between devices with their start and end apart: 5 -> 16, of which waited for: 4 -> 10; matrix products, arithmetic and copies ran while one was open for 9% -> 1% of each run, Pallas kernels for 0% -> 9%
where the time goes in v1:
time: 79.3 us; the launch traced here: 79 us
  waiting for transfers between devices  30.2 us (38%)
  Pallas kernels  29.3 us (37%)
  starting transfers between devices  15.1 us (19%)
  local copies, waits for them, and re-layouts  3.39 us (4%)
    pallas_call x5, Pallas kernels, call(): pl.pallas_call(body, name=name, out_shape=outs, in_specs=specs, out_specs...  29.3 us
    ppermute x6, waiting for transfers between devices, across(): return lax.ppermute(array, 'geo', [(i, i ^ bit) for i in range(geo)])  26 us
    ppermute x6, starting transfers between devices, across(): return lax.ppermute(array, 'geo', [(i, i ^ bit) for i in range(geo)])  12.1 us
    ppermute x10, waiting for transfers between devices, swap(): return lax.ppermute(array, 'pts', SWAP)  4.22 us
    ppermute x10, starting transfers between devices, swap(): return lax.ppermute(array, 'pts', SWAP)  2.91 us
    unnamed x24, local copies, waits for them, and re-layouts  2.51 us
  transfers between devices with their start and end apart: 16, of which 10 were waited for; matrix products, arithmetic and copies ran while one was open for 1% of the time, Pallas kernels for 9%

profile of v1, /device:TPU:0, one launch (start us, length us, event | category | flops | bytes accessed | tf_op | source)
XLA Modules:
  0.0 79.0 jit_solution(13291627253976705035)
XLA Ops:
  0.6 0.5 collective-permute-start.2
  1.2 0.8 reshape.37
  2.2 0.5 collective-permute-start.4
  2.8 0.5 collective-permute-done.other
  3.2 1.0 %copy-done = bf16[256,768]{1,0:T(8,128)(2,1)S(1)} copy-done((bf16[256,768]{1,0:T(8,128)(2,1)S(1)}, bf16[256,768]{1,0:T(8,128)(2,1)}, u32[]{:S(2)}) %copy-start) | copy-done | bytes 393240
  4.2 0.9 %copy-done.2 = bf16[1,512,256]{2,1,0:T(8,128)(2,1)S(1)} copy-done((bf16[1,512,256]{2,1,0:T(8,128)(2,1)S(1)}, bf16[1,512,256]{2,1,0:T(8,128)(2,1)}, u32[]{:S(2)}) %copy-start.2) | copy-done | bytes 262168
  5.2 4.8 %first_forward.1 = (bf16[1024,128]{1,0:T(8,128)(2,1)S(1)}, bf16[1024,128]{1,0:T(8,128)(2,1)S(1)}, bf16[1024,256]{1,0:T(8,128)(2,1)S(1)}, bf16[1024,256]{1,0:T(8,128)(2,1)S(1)}) custom-call(s32[32]{0:T(128)S(1)} %pad_add_fusion.mine, s32[32]{0:T(128)S(1)} %collective-permute-done.other, bf16[512,256]{1,0:T(8,128)(2,1)S(1)} %bitcast.8, ...), custom_call_target="tpu_custom_call" | custom-call | tf_op jit(solution)/shard_map/first_forward/pallas_call | solution.py:340
  10.0 0.3 collective-permute-start.3
  10.3 0.4 copy-done.8
  10.7 0.2 collective-permute-start.1
  10.9 0.9 %collective-permute-done.1.rot_other = s32[4,128]{1,0:T(4,128)S(1)} collective-permute-done((s32[4,128]{1,0:T(4,128)S(1)}, s32[4,128]{1,0:T(4,128)S(1)}, u32[]{:S(2)}, u32[]{:S(2)}) %collective-permute-start.1) | collective-permute-done | bytes 2080 | tf_op jit(solution)/shard_map/ppermute | solution.py:375
  11.9 10.2 %second_layer.1 = (bf16[1024,256]{1,0:T(8,128)(2,1)S(1)}, bf16[1024,128]{1,0:T(8,128)(2,1)S(1)}, bf16[1024,256]{1,0:T(8,128)(2,1)S(1)}, bf16[4,256,128]{2,1,0:T(8,128)(2,1)S(1)}) custom-call(s32[32]{0:T(128)S(1)} %pad_add_fusion.mine, s32[32]{0:T(128)S(1)} %collective-permute-done.other, s32[4,128]{1,0:T(4,128)S(1)} %bitcast.15, ...), custom_call_target="tpu_custom_call" | custom-call | tf_op jit(solution)/shard_map/second_layer/pallas_call | solution.py:340
  22.1 0.3 collective-permute-start.5
  22.4 1.7 %collective-permute-done.5.part_other = bf16[1024,256]{1,0:T(8,128)(2,1)S(1)} collective-permute-done((bf16[1024,256]{1,0:T(8,128)(2,1)S(1)}, bf16[1024,256]{1,0:T(8,128)(2,1)S(1)}, u32[]{:S(2)}, u32[]{:S(2)}) %collective-permute-start.5) | collective-permute-done | bytes 524320 | tf_op jit(solution)/shard_map/ppermute | solution.py:375
  24.1 10.5 %first_backward.1 = (bf16[2,2,256,128]{3,2,1,0:T(8,128)(2,1)S(1)}, bf16[2,2,256,128]{3,2,1,0:T(8,128)(2,1)S(1)}, bf16[512,256]{1,0:T(8,128)(2,1)S(1)}, bf16[512,256]{1,0:T(8,128)(2,1)}, bf16[512,256]{1,0:T(8,128)(2,1)S(1)}) custom-call(s32[32]{0:T(128)S(1)} %pad_add_fusion.mine, s32[32]{0:T(128)S(1)} %collective-permute-done.other, s32[4,128]{1,0:T(4,128)S(1)} %bitcast.16, ...), custom_call_target="tpu_custom_call" | custom-call | tf_op jit(solution)/shard_map/first_backward/pallas_call | solution.py:340
  34.5 2.7 %collective-permute-start.8 = (bf16[2,2,256,128]{3,2,1,0:T(8,128)(2,1)S(1)}, bf16[2,2,256,128]{3,2,1,0:T(8,128)(2,1)S(1)}, u32[]{:S(2)}, u32[]{:S(2)}) collective-permute-start(bf16[2,2,256,128]{3,2,1,0:T(8,128)(2,1)S(1)} %get-tuple-element.43), channel_id=1, source_target_pairs={{0,2},{1,3},{2,0},{3,1},{4,6},{5,7},{6,4},{7,5},{8,10},{9,11},{10,... | collective-permute-start | bytes 786440 | tf_op jit(solution)/shard_map/ppermute | solution.py:378
  37.3 6.8 %collective-permute-done.8 = bf16[2,2,256,128]{3,2,1,0:T(8,128)(2,1)S(1)} collective-permute-done((bf16[2,2,256,128]{3,2,1,0:T(8,128)(2,1)S(1)}, bf16[2,2,256,128]{3,2,1,0:T(8,128)(2,1)S(1)}, u32[]{:S(2)}, u32[]{:S(2)}) %collective-permute-start.8) | collective-permute-done | bytes 262176 | tf_op jit(solution)/shard_map/ppermute | solution.py:378
  44.2 1.8 %collective-permute-start.9 = (bf16[1,2,256,128]{3,2,1,0:T(8,128)(2,1)S(1)}, bf16[1,2,256,128]{3,2,1,0:T(8,128)(2,1)S(1)}, u32[]{:S(2)}, u32[]{:S(2)}) collective-permute-start(bf16[1,2,256,128]{3,2,1,0:T(8,128)(2,1)S(1)} %slice.9), channel_id=1, source_target_pairs={{0,1},{1,0},{2,3},{3,2},{4,5},{5,4},{6,7},{7,6},{8,9},{9,8},{10,11... | collective-permute-start | bytes 393224 | tf_op jit(solution)/shard_map/ppermute | solution.py:378
  46.0 3.5 %collective-permute-done.9 = bf16[1,2,256,128]{3,2,1,0:T(8,128)(2,1)S(1)} collective-permute-done((bf16[1,2,256,128]{3,2,1,0:T(8,128)(2,1)S(1)}, bf16[1,2,256,128]{3,2,1,0:T(8,128)(2,1)S(1)}, u32[]{:S(2)}, u32[]{:S(2)}) %collective-permute-start.9) | collective-permute-done | bytes 131104 | tf_op jit(solution)/shard_map/ppermute | solution.py:378
  49.5 1.7 %collective-permute-start.10 = (bf16[1,2,256,128]{3,2,1,0:T(8,128)(2,1)S(1)}, bf16[1,2,256,128]{3,2,1,0:T(8,128)(2,1)S(1)}, u32[]{:S(2)}, u32[]{:S(2)}) collective-permute-start(bf16[1,2,256,128]{3,2,1,0:T(8,128)(2,1)S(1)} %add_convert_fusion.3), channel_id=1, source_target_pairs={{0,4},{1,5},{2,6},{3,7},{4,0},{5,1},{6,2},{7,3},{8,12},{9,13},{10,... | collective-permute-start | bytes 393224 | tf_op jit(solution)/shard_map/ppermute | solution.py:378
  51.1 3.4 %collective-permute-done.10 = bf16[1,2,256,128]{3,2,1,0:T(8,128)(2,1)S(1)} collective-permute-done((bf16[1,2,256,128]{3,2,1,0:T(8,128)(2,1)S(1)}, bf16[1,2,256,128]{3,2,1,0:T(8,128)(2,1)S(1)}, u32[]{:S(2)}, u32[]{:S(2)}) %collective-permute-start.10) | collective-permute-done | bytes 131104 | tf_op jit(solution)/shard_map/ppermute | solution.py:378
  54.5 2.8 %collective-permute-start.11 = (bf16[1,2,256,128]{3,2,1,0:T(8,128)(2,1)S(1)}, bf16[1,2,256,128]{3,2,1,0:T(8,128)(2,1)S(1)}, u32[]{:S(2)}, u32[]{:S(2)}) collective-permute-start(bf16[1,2,256,128]{3,2,1,0:T(8,128)(2,1)S(1)} %add_convert_fusion.2), channel_id=1, source_target_pairs={{0,8},{1,9},{2,10},{3,11},{4,12},{5,13},{6,14},{7,15},{8,0},{9,1},... | collective-permute-start | bytes 393224 | tf_op jit(solution)/shard_map/ppermute | solution.py:378
  57.4 4.5 %collective-permute-done.11 = bf16[1,2,256,128]{3,2,1,0:T(8,128)(2,1)S(1)} collective-permute-done((bf16[1,2,256,128]{3,2,1,0:T(8,128)(2,1)S(1)}, bf16[1,2,256,128]{3,2,1,0:T(8,128)(2,1)S(1)}, u32[]{:S(2)}, u32[]{:S(2)}) %collective-permute-start.11) | collective-permute-done | bytes 131104 | tf_op jit(solution)/shard_map/ppermute | solution.py:378
  61.9 1.6 %collective-permute-start.12 = (bf16[1,2,256,128]{3,2,1,0:T(8,128)(2,1)S(1)}, bf16[1,2,256,128]{3,2,1,0:T(8,128)(2,1)S(1)}, u32[]{:S(2)}, u32[]{:S(2)}) collective-permute-start(bf16[1,2,256,128]{3,2,1,0:T(8,128)(2,1)S(1)} %add_convert_fusion.1), channel_id=1, source_target_pairs={{0,1},{1,0},{2,3},{3,2},{4,5},{5,4},{6,7},{7,6},{8,9},{9,8},{10,11... | collective-permute-start | bytes 393224 | tf_op jit(solution)/shard_map/ppermute | solution.py:378
  63.5 3.5 %collective-permute-done.12 = bf16[1,2,256,128]{3,2,1,0:T(8,128)(2,1)S(1)} collective-permute-done((bf16[1,2,256,128]{3,2,1,0:T(8,128)(2,1)S(1)}, bf16[1,2,256,128]{3,2,1,0:T(8,128)(2,1)S(1)}, u32[]{:S(2)}, u32[]{:S(2)}) %collective-permute-start.12) | collective-permute-done | bytes 131104 | tf_op jit(solution)/shard_map/ppermute | solution.py:378
  67.0 1.6 %collective-permute-start.13 = (bf16[2,2,256,128]{3,2,1,0:T(8,128)(2,1)S(1)}, bf16[2,2,256,128]{3,2,1,0:T(8,128)(2,1)S(1)}, u32[]{:S(2)}, u32[]{:S(2)}) collective-permute-start(bf16[2,2,256,128]{3,2,1,0:T(8,128)(2,1)S(1)} %pad_maximum_fusion.near_mine), channel_id=1, source_target_pairs={{0,2},{1,3},{2,0},{3,1},{4,6},{5,7},{6,4},{7,5},{8,10},{9,11},{10,... | collective-permute-start | bytes 786440 | tf_op jit(solution)/shard_map/ppermute | solution.py:378
  68.6 0.5 collective-permute-start.14
  69.1 4.3 %collective-permute-done.13.far_mine = bf16[2,2,256,128]{3,2,1,0:T(8,128)(2,1)S(1)} collective-permute-done((bf16[2,2,256,128]{3,2,1,0:T(8,128)(2,1)S(1)}, bf16[2,2,256,128]{3,2,1,0:T(8,128)(2,1)S(1)}, u32[]{:S(2)}, u32[]{:S(2)}) %collective-permute-start.13) | collective-permute-done | bytes 262176 | tf_op jit(solution)/shard_map/ppermute | solution.py:378
  73.5 0.6 collective-permute-start.7
  74.0 1.1 %collective-permute-done.7.mixed_other = bf16[512,128]{1,0:T(8,128)(2,1)S(1)} collective-permute-done((bf16[512,128]{1,0:T(8,128)(2,1)S(1)}, bf16[512,128]{1,0:T(8,128)(2,1)S(1)}, u32[]{:S(2)}, u32[]{:S(2)}) %collective-permute-start.7) | collective-permute-done | bytes 131104 | tf_op jit(solution)/shard_map/ppermute | solution.py:375
  75.2 2.2 %finish_rows.1 = (bf16[512,256]{1,0:T(8,128)(2,1)}, bf16[512,256]{1,0:T(8,128)(2,1)}) custom-call(bf16[512,256]{1,0:T(8,128)(2,1)S(1)} %get-tuple-element.36.part_mine, bf16[512,256]{1,0:T(8,128)(2,1)} %collective-permute-done.6.part_other, bf16[512,256]{1,0:T(8,128)(2,1)S(1)} %bitcast.10, bf16[1,256]{1,0:T(2,128)(2,1)S(1)} %reshape.40.gain.gain_one, ...), custom_call_target="tpu_custom_call" | custom-call | tf_op jit(solution)/shard_map/finish_rows/pallas_call | solution.py:340
  77.4 1.6 %finish_weights.1 = (f32[1,256]{1,0:T(1,128)}, f32[256,768]{1,0:T(8,128)}, f32[256,256]{1,0:T(8,128)}, f32[1,256]{1,0:T(1,128)}, f32[256,768]{1,0:T(8,128)}, /*index=5*/f32[256,256]{1,0:T(8,128)}) custom-call(bf16[2,2,256,128]{3,2,1,0:T(8,128)(2,1)S(1)} %pad_maximum_fusion.near_mine, bf16[2,2,256,128]{3,2,1,0:T(8,128)(2,1)S(1)} %collective-permute-done.13.far_mine, ...), custom_call_target="tpu_custom_call" | custom-call | tf_op jit(solution)/shard_map/finish_weights/pallas_call | solution.py:340
  (41 shorter events, 0.7 us)
Async XLA Ops:
  0.6 1.3 %copy-start.9 = (s32[1,4,4]{2,1,0:T(4,128)S(1)}, s32[1,4,4]{2,1,0:T(4,128)}, u32[]{:S(2)}) copy-start(s32[1,4,4]{2,1,0:T(4,128)} %param.14) | copy-start | bytes 196
  0.6 2.6 %collective-permute-start.2 = (bf16[512,256]{1,0:T(8,128)(2,1)}, bf16[512,256]{1,0:T(8,128)(2,1)S(1)}, u32[]{:S(2)}, u32[]{:S(2)}) collective-permute-start(bf16[512,256]{1,0:T(8,128)(2,1)} %bitcast.7), channel_id=1, source_target_pairs={{0,16},{16,0},{1,17},{17,1},{2,18},{18,2},{3,19},{19,3},{4,20},{20... | collective-permute-start | bytes 786440 | tf_op jit(solution)/shard_map/ppermute | solution.py:375
  2.1 0.7 copy-start.10
  2.1 1.1 %collective-permute-start = (s32[32]{0:T(128)S(1)}, s32[32]{0:T(128)S(1)}, u32[]{:S(2)}, u32[]{:S(2)}) collective-permute-start(s32[32]{0:T(128)S(1)} %pad_add_fusion.mine), channel_id=1, source_target_pairs={{0,16},{16,0},{1,17},{17,1},{2,18},{18,2},{3,19},{19,3},{4,20},{20... | collective-permute-start | bytes 392 | tf_op jit(solution)/shard_map/ppermute | solution.py:375
  2.2 9.7 %collective-permute-start.4 = (bf16[512,256]{1,0:T(8,128)(2,1)}, bf16[512,256]{1,0:T(8,128)(2,1)S(1)}, u32[]{:S(2)}, u32[]{:S(2)}) collective-permute-start(bf16[512,256]{1,0:T(8,128)(2,1)} %bitcast.11), channel_id=1, source_target_pairs={{0,16},{16,0},{1,17},{17,1},{2,18},{18,2},{3,19},{19,3},{4,20},{20... | collective-permute-start | bytes 786440 | tf_op jit(solution)/shard_map/ppermute | solution.py:375
  3.2 1.0 %copy-start = (bf16[256,768]{1,0:T(8,128)(2,1)S(1)}, bf16[256,768]{1,0:T(8,128)(2,1)}, u32[]{:S(2)}) copy-start(bf16[256,768]{1,0:T(8,128)(2,1)} %weight_one.1) | copy-start | bytes 1179652
  4.2 0.9 %copy-start.2 = (bf16[1,512,256]{2,1,0:T(8,128)(2,1)S(1)}, bf16[1,512,256]{2,1,0:T(8,128)(2,1)}, u32[]{:S(2)}) copy-start(bf16[1,512,256]{2,1,0:T(8,128)(2,1)} %param.11) | copy-start | bytes 786436
  5.2 6.7 %copy-start.4 = (bf16[256,768]{1,0:T(8,128)(2,1)S(1)}, bf16[256,768]{1,0:T(8,128)(2,1)}, u32[]{:S(2)}) copy-start(bf16[256,768]{1,0:T(8,128)(2,1)} %weight_two.1) | copy-start | bytes 1179652
  5.2 6.7 %copy-start.5 = (bf16[1,512,256]{2,1,0:T(8,128)(2,1)S(1)}, bf16[1,512,256]{2,1,0:T(8,128)(2,1)}, u32[]{:S(2)}) copy-start(bf16[1,512,256]{2,1,0:T(8,128)(2,1)} %param.12) | copy-start | bytes 786436
  5.2 6.7 %copy-start.6 = (bf16[256,256]{1,0:T(8,128)(2,1)S(1)}, bf16[256,256]{1,0:T(8,128)(2,1)}, u32[]{:S(2)}) copy-start(bf16[256,256]{1,0:T(8,128)(2,1)} %out_one.3) | copy-start | bytes 393220
  5.2 6.7 %copy-start.7 = (bf16[256,256]{1,0:T(8,128)(2,1)S(1)}, bf16[256,256]{1,0:T(8,128)(2,1)}, u32[]{:S(2)}) copy-start(bf16[256,256]{1,0:T(8,128)(2,1)} %out_two.3) | copy-start | bytes 393220
  10.0 0.7 copy-start.8
  10.0 0.9 %copy-start.11 = (bf16[256]{0:T(256)(128)(2,1)S(1)}, bf16[256]{0:T(256)(128)(2,1)}, u32[]{:S(2)}) copy-start(bf16[256]{0:T(256)(128)(2,1)} %param.19) | copy-start | bytes 1540
  10.0 1.8 %collective-permute-start.3 = (bf16[1024,128]{1,0:T(8,128)(2,1)S(1)}, bf16[1024,128]{1,0:T(8,128)(2,1)S(1)}, u32[]{:S(2)}, u32[]{:S(2)}) collective-permute-start(bf16[1024,128]{1,0:T(8,128)(2,1)S(1)} %get-tuple-element.29.mixed_mine.mixed_ref), channel_id=1, source_target_pairs={{0,16},{16,0},{1,17},{17,1},{2,18},{18,2},{3,19},{19,3},{4,20},{20... | collective-permute-start | bytes 786440 | tf_op jit(solution)/shard_map/ppermute | solution.py:375
  10.7 1.2 %collective-permute-start.1 = (s32[4,128]{1,0:T(4,128)S(1)}, s32[4,128]{1,0:T(4,128)S(1)}, u32[]{:S(2)}, u32[]{:S(2)}) collective-permute-start(s32[4,128]{1,0:T(4,128)S(1)} %bitcast.14), channel_id=1, source_target_pairs={{0,16},{16,0},{1,17},{17,1},{2,18},{18,2},{3,19},{19,3},{4,20},{20... | collective-permute-start | bytes 6152 | tf_op jit(solution)/shard_map/ppermute | solution.py:375
  10.9 13.2 %copy-start.1 = (bf16[256,768]{1,0:T(8,128)(2,1)S(1)}, bf16[256,768]{1,0:T(8,128)(2,1)}, u32[]{:S(2)}) copy-start(bf16[256,768]{1,0:T(8,128)(2,1)} %weight_one.1) | copy-start | bytes 1179652
  22.1 2.0 %collective-permute-start.5 = (bf16[1024,256]{1,0:T(8,128)(2,1)S(1)}, bf16[1024,256]{1,0:T(8,128)(2,1)S(1)}, u32[]{:S(2)}, u32[]{:S(2)}) collective-permute-start(bf16[1024,256]{1,0:T(8,128)(2,1)S(1)} %get-tuple-element.30.part_mine), channel_id=1, source_target_pairs={{0,16},{16,0},{1,17},{17,1},{2,18},{18,2},{3,19},{19,3},{4,20},{20... | collective-permute-start | bytes 1572872 | tf_op jit(solution)/shard_map/ppermute | solution.py:375
  34.5 9.6 %collective-permute-start.8 = (bf16[2,2,256,128]{3,2,1,0:T(8,128)(2,1)S(1)}, bf16[2,2,256,128]{3,2,1,0:T(8,128)(2,1)S(1)}, u32[]{:S(2)}, u32[]{:S(2)}) collective-permute-start(bf16[2,2,256,128]{3,2,1,0:T(8,128)(2,1)S(1)} %get-tuple-element.43), channel_id=1, source_target_pairs={{0,2},{1,3},{2,0},{3,1},{4,6},{5,7},{6,4},{7,5},{8,10},{9,11},{10,... | collective-permute-start | bytes 786440 | tf_op jit(solution)/shard_map/ppermute | solution.py:378
  44.2 5.2 %collective-permute-start.9 = (bf16[1,2,256,128]{3,2,1,0:T(8,128)(2,1)S(1)}, bf16[1,2,256,128]{3,2,1,0:T(8,128)(2,1)S(1)}, u32[]{:S(2)}, u32[]{:S(2)}) collective-permute-start(bf16[1,2,256,128]{3,2,1,0:T(8,128)(2,1)S(1)} %slice.9), channel_id=1, source_target_pairs={{0,1},{1,0},{2,3},{3,2},{4,5},{5,4},{6,7},{7,6},{8,9},{9,8},{10,11... | collective-permute-start | bytes 393224 | tf_op jit(solution)/shard_map/ppermute | solution.py:378
  49.5 5.0 %collective-permute-start.10 = (bf16[1,2,256,128]{3,2,1,0:T(8,128)(2,1)S(1)}, bf16[1,2,256,128]{3,2,1,0:T(8,128)(2,1)S(1)}, u32[]{:S(2)}, u32[]{:S(2)}) collective-permute-start(bf16[1,2,256,128]{3,2,1,0:T(8,128)(2,1)S(1)} %add_convert_fusion.3), channel_id=1, source_target_pairs={{0,4},{1,5},{2,6},{3,7},{4,0},{5,1},{6,2},{7,3},{8,12},{9,13},{10,... | collective-permute-start | bytes 393224 | tf_op jit(solution)/shard_map/ppermute | solution.py:378
  54.5 7.3 %collective-permute-start.11 = (bf16[1,2,256,128]{3,2,1,0:T(8,128)(2,1)S(1)}, bf16[1,2,256,128]{3,2,1,0:T(8,128)(2,1)S(1)}, u32[]{:S(2)}, u32[]{:S(2)}) collective-permute-start(bf16[1,2,256,128]{3,2,1,0:T(8,128)(2,1)S(1)} %add_convert_fusion.2), channel_id=1, source_target_pairs={{0,8},{1,9},{2,10},{3,11},{4,12},{5,13},{6,14},{7,15},{8,0},{9,1},... | collective-permute-start | bytes 393224 | tf_op jit(solution)/shard_map/ppermute | solution.py:378
  61.9 5.0 %collective-permute-start.12 = (bf16[1,2,256,128]{3,2,1,0:T(8,128)(2,1)S(1)}, bf16[1,2,256,128]{3,2,1,0:T(8,128)(2,1)S(1)}, u32[]{:S(2)}, u32[]{:S(2)}) collective-permute-start(bf16[1,2,256,128]{3,2,1,0:T(8,128)(2,1)S(1)} %add_convert_fusion.1), channel_id=1, source_target_pairs={{0,1},{1,0},{2,3},{3,2},{4,5},{5,4},{6,7},{7,6},{8,9},{9,8},{10,11... | collective-permute-start | bytes 393224 | tf_op jit(solution)/shard_map/ppermute | solution.py:378
  67.0 8.2 %copy-start.3 = (bf16[1,512,256]{2,1,0:T(8,128)(2,1)S(1)}, bf16[1,512,256]{2,1,0:T(8,128)(2,1)}, u32[]{:S(2)}) copy-start(bf16[1,512,256]{2,1,0:T(8,128)(2,1)} %param.11) | copy-start | bytes 786436
  67.0 6.4 %collective-permute-start.13 = (bf16[2,2,256,128]{3,2,1,0:T(8,128)(2,1)S(1)}, bf16[2,2,256,128]{3,2,1,0:T(8,128)(2,1)S(1)}, u32[]{:S(2)}, u32[]{:S(2)}) collective-permute-start(bf16[2,2,256,128]{3,2,1,0:T(8,128)(2,1)S(1)} %pad_maximum_fusion.near_mine), channel_id=1, source_target_pairs={{0,2},{1,3},{2,0},{3,1},{4,6},{5,7},{6,4},{7,5},{8,10},{9,11},{10,... | collective-permute-start | bytes 786440 | tf_op jit(solution)/shard_map/ppermute | solution.py:378
  68.6 6.6 %collective-permute-start.6 = (bf16[512,256]{1,0:T(8,128)(2,1)}, bf16[512,256]{1,0:T(8,128)(2,1)}, u32[]{:S(2)}, u32[]{:S(2)}) collective-permute-start(bf16[512,256]{1,0:T(8,128)(2,1)} %get-tuple-element.37), channel_id=1, source_target_pairs={{0,16},{16,0},{1,17},{17,1},{2,18},{18,2},{3,19},{19,3},{4,20},{20... | collective-permute-start | bytes 786440 | tf_op jit(solution)/shard_map/ppermute | solution.py:375
  68.6 8.8 %collective-permute-start.14 = (bf16[2,2,256,128]{3,2,1,0:T(8,128)(2,1)S(1)}, bf16[2,2,256,128]{3,2,1,0:T(8,128)(2,1)S(1)}, u32[]{:S(2)}, u32[]{:S(2)}) collective-permute-start(bf16[2,2,256,128]{3,2,1,0:T(8,128)(2,1)S(1)} %pad_maximum_fusion.near_mine), channel_id=1, source_target_pairs={{0,16},{16,0},{1,17},{17,1},{2,18},{18,2},{3,19},{19,3},{4,20},{20... | collective-permute-start | bytes 786440 | tf_op jit(solution)/shard_map/ppermute | solution.py:375
  73.4 3.9 %collective-permute-start.15 = (bf16[2,2,256,128]{3,2,1,0:T(8,128)(2,1)S(1)}, bf16[2,2,256,128]{3,2,1,0:T(8,128)(2,1)S(1)}, u32[]{:S(2)}, u32[]{:S(2)}) collective-permute-start(bf16[2,2,256,128]{3,2,1,0:T(8,128)(2,1)S(1)} %collective-permute-done.13.far_mine), channel_id=1, source_target_pairs={{0,16},{16,0},{1,17},{17,1},{2,18},{18,2},{3,19},{19,3},{4,20},{20... | collective-permute-start | bytes 786440 | tf_op jit(solution)/shard_map/ppermute | solution.py:375
  73.5 1.7 %collective-permute-start.7 = (bf16[512,128]{1,0:T(8,128)(2,1)S(1)}, bf16[512,128]{1,0:T(8,128)(2,1)S(1)}, u32[]{:S(2)}, u32[]{:S(2)}) collective-permute-start(bf16[512,128]{1,0:T(8,128)(2,1)S(1)} %constant_dynamic-slice_fusion), channel_id=1, source_target_pairs={{0,16},{16,0},{1,17},{17,1},{2,18},{18,2},{3,19},{19,3},{4,20},{20... | collective-permute-start | bytes 393224 | tf_op jit(solution)/shard_map/ppermute | solution.py:375

commit v2 on v1

--- a/solution.py
+++ b/solution.py
@@ -103,9 +103,12 @@
     return jnp.concatenate(parts, axis=1)
 
 
-def store_pieces(ref, pieces, slot_bits):
+def store_pieces(ref, keep_ref, send_ref, pieces, core):
+    mask = slot_mask(core)
     for p, piece in enumerate(pieces):
-        ref[p ^ slot_bits] = piece.astype(BF)
+        ref[p ^ mask] = piece.astype(BF)
+    keep_ref[...] = ref[: PIECES // 2]
+    send_ref[...] = ref[PIECES // 2 :]
 
 
 def weight_pieces(normed, grads, mixed, grad_out):
@@ -123,8 +126,9 @@
     return (grad_out.astype(F32) + factor * scaled - x * (factor * factor * factor) * inner).astype(BF)
 
 
-def slot_bits():
-    return lax.rem(lax.axis_index("geo"), PIECES)
+def slot_mask(core):
+    low = lax.rem(lax.axis_index("geo"), PIECES)
+    return jnp.where(core == 0, low, (low & 1) * 2 + low // 2)
 
 
 def first_forward(mine, other, x_mine, x_other, gain, weight, mixed_ref, q_ref, kv_ref, normed_ref):
@@ -154,8 +158,8 @@
 def second_layer(
     mine, other, rot_mine, rot_other, x_mine, x_other, mixed_mine, mixed_other, grad_mine, grad_other,
     out_one, gain, weight, out_two,
-    moved_ref, mixed_ref, part_ref, pieces_ref,
-    both_ref, hidden_ref, grad_ref, normed_ref, q_ref, kv_ref, mg_ref, dq_ref, dk_ref, dv_ref,
+    moved_ref, mixed_ref, part_ref, keep_ref, send_ref,
+    both_ref, hidden_ref, grad_ref, normed_ref, q_ref, kv_ref, mg_ref, dq_ref, dk_ref, dv_ref, pieces_ref,
 ):
     core = lax.axis_index("pts")
     local, width = x_mine.shape
@@ -211,12 +215,13 @@
     lax.fori_loop(0, total // BALL, one_ball, 0)
     grads = qkv_grads(dq_ref[...], dk_ref, dv_ref)
     part_ref[...] = dot(grads, jnp.concatenate(columns, axis=1), ((1,), (1,))).astype(BF)
-    store_pieces(pieces_ref, weight_pieces(normed_ref[...], grads, mixed_ref[...], grad_ref[...]), slot_bits())
+    pieces = weight_pieces(normed_ref[...], grads, mixed_ref[...], grad_ref[...])
+    store_pieces(pieces_ref, keep_ref, send_ref, pieces, core)
 
 
 def first_backward(
     mine, other, rot_mine, rot_other, part_mine, part_other, moved_ref, grad_mine, grad_other, gain_two,
-    mixed_ref, normed_ref, q_ref, kv_ref, weight, out_one, pieces_two,
+    mixed_ref, normed_ref, q_ref, kv_ref, weight, out_one,
     keep_ref, send_ref, part_keep, part_send, hidden_grad_mine,
     rows_grad_ref, hg_ref, mg_ref, dq_ref, dk_ref, dv_ref, pieces_ref,
 ):
@@ -268,12 +273,8 @@
     lax.fori_loop(0, total // BALL, one_ball, 0)
     grads = qkv_grads(dq_ref[...], dk_ref, dv_ref)
     columns = jnp.concatenate(own_columns(weight, core, half), axis=1)
-    store_pieces(pieces_ref, weight_pieces(normed_ref[...], grads, mixed_ref[...], hidden_grad), slot_bits())
-    for slot in range(PIECES // 2):
-        keep_ref[slot, 0] = pieces_ref[slot]
-        keep_ref[slot, 1] = pieces_two[slot]
-        send_ref[slot, 0] = pieces_ref[slot + PIECES // 2]
-        send_ref[slot, 1] = pieces_two[slot + PIECES // 2]
+    pieces = weight_pieces(normed_ref[...], grads, mixed_ref[...], hidden_grad)
+    store_pieces(pieces_ref, keep_ref, send_ref, pieces, core)
     part = dot(grads, columns, ((1,), (1,)))
     hg_ref[...] = part.astype(BF)
     part_keep[...] = hg_ref[rows(core), :]
@@ -299,36 +300,27 @@
 
 
 def finish_weights(
-    near_mine, far_mine, near_other, far_other, gain_one, gain_two, weight_one, weight_two,
-    gain_one_grad, qkv_one_grad, out_one_grad, gain_two_grad, qkv_two_grad, out_two_grad,
-    slots_ref,
+    near_mine, far_mine, near_other, far_other, gain, weight, gain_grad, qkv_grad, out_grad, slots_ref
 ):
     core = lax.axis_index("pts")
     half = near_mine.shape[-1]
     width = 2 * half
-    mask = slot_bits()
     groups = ((core, near_mine, far_mine), (1 - core, near_other, far_other))
-    for side, (_, near, far) in enumerate(groups):
-        for slot in range(PIECES // 2):
-            slots_ref[side, slot] = near[slot]
-            slots_ref[side, slot + PIECES // 2] = far[slot]
-    layers = (
-        (gain_one, weight_one, gain_one_grad, qkv_one_grad, out_one_grad),
-        (gain_two, weight_two, gain_two_grad, qkv_two_grad, out_two_grad),
-    )
-    for layer, (gain, weight, gain_grad, qkv_grad, out_grad) in enumerate(layers):
-        folded = jnp.zeros((width, half), F32)
-        for side, (place, _, _) in enumerate(groups):
-            for p in range(3):
-                piece = slots_ref[side, p ^ mask, layer].astype(F32)
-                at = pl.ds(pl.multiple_of(p * width + place * half, half), half)
-                qkv_grad[:, at] = piece
-                folded = folded + piece * weight[:, at].astype(F32)
-            piece = slots_ref[side, 3 ^ mask, layer].astype(F32)
-            at = pl.ds(pl.multiple_of(place * half, half), half)
-            out_grad[at, :half] = piece[:half]
-            out_grad[at, half:] = piece[half:]
-        gain_grad[...] = jnp.sum(folded.T, axis=0, keepdims=True) / gain[...].astype(F32)
+    folded = jnp.zeros((width, half), F32)
+    for side, (place, near, far) in enumerate(groups):
+        slots_ref[side, : PIECES // 2] = near[...]
+        slots_ref[side, PIECES // 2 :] = far[...]
+        mask = slot_mask(place)
+        for p in range(3):
+            piece = slots_ref[side, p ^ mask].astype(F32)
+            at = pl.ds(pl.multiple_of(p * width + place * half, half), half)
+            qkv_grad[:, at] = piece
+            folded = folded + piece * weight[:, at].astype(F32)
+        piece = slots_ref[side, 3 ^ mask].astype(F32)
+        at = pl.ds(pl.multiple_of(place * half, half), half)
+        out_grad[at, :half] = piece[:half]
+        out_grad[at, half:] = piece[half:]
+    gain_grad[...] = jnp.sum(folded.T, axis=0, keepdims=True) / gain[...].astype(F32)
 
 
 def shape(dims, dtype=BF):
@@ -374,8 +366,9 @@
     def swap(array):
         return lax.ppermute(array, "pts", SWAP)
 
-    def across(array, bit):
-        return lax.ppermute(array, "geo", [(i, i ^ bit) for i in range(geo)])
+    def across(array, bits):
+        pairs = [(core * geo + i, core * geo + (i ^ bit)) for core, bit in enumerate(bits) for i in range(geo)]
+        return lax.ppermute(array, ("pts", "geo"), pairs)
 
     x = points[0]
     grad = result_grad[0]
@@ -396,7 +389,7 @@
     )
     mixed_other = swap(mixed)
     blocks = ((balls, half, BALL), F32)
-    moved, mixed_two, part_two, pieces_two = call(
+    moved, mixed_two, part_two, keep_two, send_two = call(
         second_layer,
         "second_layer",
         [("s", lists), ("s", lists_other)]
@@ -406,7 +399,7 @@
                 rot, rot_other, x, x_other, mixed, mixed_other, grad, grad_other, out_one, gain_two, qkv_two, out_two
             )
         ],
-        [shape((total, width)), shape((total, half)), shape((total, width)), shape((PIECES, width, half))],
+        [shape((total, width)), shape((total, half)), shape((total, width))] + [shape((PIECES // 2, width, half))] * 2,
         [
             ((total, width), BF),
             ((total, width), BF),
@@ -418,6 +411,7 @@
             ((total, half), BF),
             blocks,
             blocks,
+            ((PIECES, width, half), BF),
         ],
     )
     part_two_other = swap(part_two)
@@ -431,10 +425,10 @@
             ("v", a)
             for a in (
                 rot, rot_other, part_two, part_two_other, moved, grad, grad_other, gain_two,
-                mixed, normed, q, kv, qkv_one, out_one, pieces_two,
+                mixed, normed, q, kv, qkv_one, out_one,
             )
         ],
-        [shape((PIECES // 2, 2, width, half))] * 2 + [shape((rows, width))] * 3,
+        [shape((PIECES // 2, width, half))] * 2 + [shape((rows, width))] * 3,
         [
             ((total, width), BF),
             ((total, width), BF),
@@ -446,16 +440,20 @@
         ],
     )
     part_other = swap(part_send)
-    summed = add(keep, across(send, 2))
-    summed = add(summed[:1], across(summed[1:], 1))
-    bit = PIECES
-    while bit < geo:
-        summed = add(summed, across(summed, bit))
-        bit *= 2
-    near = jnp.concatenate([summed, across(summed, 1)], axis=0)
-    far = across(near, 2)
-    near_other = swap(near)
-    far_other = swap(far)
+    ups = [1 << i for i in range(2, geo.bit_length() - 1)]
+    highs = list(zip(ups, ups[1:] + ups[:1]))
+
+    def reduce(keep, send):
+        summed = add(keep, across(send, (2, 1)))
+        summed = add(summed[:1], across(summed[1:], (1, 2)))
+        for bits in highs:
+            summed = add(summed, across(summed, bits))
+        near = jnp.concatenate([summed, across(summed, (1, 2))], axis=0)
+        far = across(near, (2, 1))
+        return near, far, swap(near), swap(far)
+
+    pieces_two = reduce(keep_two, send_two)
+    pieces_one = reduce(keep, send)
     points_grad, result = call(
         finish_rows,
         "finish_rows",
@@ -467,23 +465,17 @@
         [((rows, width), BF)],
     )
     vector, matrix, square = (shape(dims, F32) for dims in ((1, width), (width, 3 * width), (width, width)))
-    grads = call(
-        finish_weights,
-        "finish_weights",
-        [("v", a) for a in (near, far, near_other, far_other, gain_one, gain_two, qkv_one, qkv_two)],
-        [vector, matrix, square] * 2,
-        [((2, PIECES, 2, width, half), BF)],
-    )
-    return (
-        result[None],
-        points_grad[None],
-        grads[0].reshape(width),
-        grads[1],
-        grads[2],
-        grads[3].reshape(width),
-        grads[4],
-        grads[5],
-    )
+    grads = []
+    for pieces, gain, weight in ((pieces_one, gain_one, qkv_one), (pieces_two, gain_two, qkv_two)):
+        found = call(
+            finish_weights,
+            "finish_weights",
+            [("v", a) for a in pieces + (gain, weight)],
+            [vector, matrix, square],
+            [((2, PIECES, width, half), BF)],
+        )
+        grads += [found[0].reshape(width), found[1], found[2]]
+    return (result[None], points_grad[None], *grads)
 
 
 def solution(mesh):

time: 79.3 us -> 68.2 us (0.86)
  waiting for transfers between devices: 30.2 us -> 9.5 us
  starting transfers between devices: 15.1 us -> 25.6 us
  Pallas kernels: 29.3 us -> 28.3 us
    ppermute x6 -> x12, waiting for transfers between devices: 26 us -> 8.07 us  [across(): return lax.ppermute(array, ('pts', 'geo'), pairs)]
    ppermute x6 -> x12, starting transfers between devices: 12.1 us -> 22.6 us  [across(): return lax.ppermute(array, ('pts', 'geo'), pairs)]
    ppermute x10 -> x12, waiting for transfers between devices: 4.22 us -> 1.43 us  [swap(): return lax.ppermute(array, 'pts', SWAP)]
    pallas_call x5 -> x6, Pallas kernels: 29.3 us -> 28.3 us  [call(): pl.pallas_call(body, name=name, out_shape=outs, in_specs=specs, out_specs...]
    ppermute x10 -> x12, starting transfers between devices: 2.91 us -> 3 us  [swap(): return lax.ppermute(array, 'pts', SWAP)]
  transfers between devices with their start and end apart: 16 -> 24, of which waited for: 10 -> 8; matrix products, arithmetic and copies ran while one was open for 1% -> 2% of each run, Pallas kernels for 9% -> 25%
where the time goes in v2:
time: 68.2 us; the launch traced here: 67.9 us
  Pallas kernels  28.3 us (41%)
  starting transfers between devices  25.6 us (38%)
  waiting for transfers between devices  9.5 us (14%)
  local copies, waits for them, and re-layouts  3.39 us (5%)
  between operations  0.82 us (1%)
    pallas_call x6, Pallas kernels, call(): pl.pallas_call(body, name=name, out_shape=outs, in_specs=specs, out_specs...  28.3 us
    ppermute x12, starting transfers between devices, across(): return lax.ppermute(array, ('pts', 'geo'), pairs)  22.6 us
    ppermute x12, waiting for transfers between devices, across(): return lax.ppermute(array, ('pts', 'geo'), pairs)  8.07 us
    ppermute x12, starting transfers between devices, swap(): return lax.ppermute(array, 'pts', SWAP)  3 us
    unnamed x24, local copies, waits for them, and re-layouts  2.51 us
    ppermute x12, waiting for transfers between devices, swap(): return lax.ppermute(array, 'pts', SWAP)  1.43 us
  transfers between devices with their start and end apart: 24, of which 8 were waited for; matrix products, arithmetic and copies ran while one was open for 2% of the time, Pallas kernels for 25%

profile of v2, /device:TPU:0, one launch (start us, length us, event | category | flops | bytes accessed | tf_op | source)
XLA Modules:
  0.0 67.9 jit_solution(10315684424977266135)
XLA Ops:
  0.6 0.5 collective-permute-start.2
  1.2 0.8 %reshape.38 = s32[16]{0:T(128)S(1)} reshape(s32[1,4,4]{2,1,0:T(4,128)} %param.14) | data formatting | bytes 128 | tf_op jit(solution)/shard_map/reshape | solution.py:375
  2.8 0.5 collective-permute-done.other
  3.2 1.0 %copy-done = bf16[256,768]{1,0:T(8,128)(2,1)S(1)} copy-done((bf16[256,768]{1,0:T(8,128)(2,1)S(1)}, bf16[256,768]{1,0:T(8,128)(2,1)}, u32[]{:S(2)}) %copy-start) | copy-done | bytes 393240
  4.2 0.9 %copy-done.2 = bf16[1,512,256]{2,1,0:T(8,128)(2,1)S(1)} copy-done((bf16[1,512,256]{2,1,0:T(8,128)(2,1)S(1)}, bf16[1,512,256]{2,1,0:T(8,128)(2,1)}, u32[]{:S(2)}) %copy-start.2) | copy-done | bytes 262168
  5.2 4.8 %first_forward.1 = (bf16[1024,128]{1,0:T(8,128)(2,1)S(1)}, bf16[1024,128]{1,0:T(8,128)(2,1)S(1)}, bf16[1024,256]{1,0:T(8,128)(2,1)S(1)}, bf16[1024,256]{1,0:T(8,128)(2,1)S(1)}) custom-call(s32[32]{0:T(128)S(1)} %pad_add_fusion.mine, s32[32]{0:T(128)S(1)} %collective-permute-done.other, bf16[512,256]{1,0:T(8,128)(2,1)S(1)} %bitcast.8, ...), custom_call_target="tpu_custom_call" | custom-call | tf_op jit(solution)/shard_map/first_forward/pallas_call | solution.py:332
  10.9 0.9 %collective-permute-done.1.rot_other = s32[4,128]{1,0:T(4,128)S(1)} collective-permute-done((s32[4,128]{1,0:T(4,128)S(1)}, s32[4,128]{1,0:T(4,128)S(1)}, u32[]{:S(2)}, u32[]{:S(2)}) %collective-permute-start.1) | collective-permute-done | bytes 2080 | tf_op jit(solution)/shard_map/ppermute | solution.py:367
  11.9 10.2 %second_layer.1 = (bf16[1024,256]{1,0:T(8,128)(2,1)S(1)}, bf16[1024,128]{1,0:T(8,128)(2,1)S(1)}, bf16[1024,256]{1,0:T(8,128)(2,1)S(1)}, bf16[2,256,128]{2,1,0:T(8,128)(2,1)S(1)}, bf16[2,256,128]{2,1,0:T(8,128)(2,1)S(1)}) custom-call(s32[32]{0:T(128)S(1)} %pad_add_fusion.mine, s32[32]{0:T(128)S(1)} %collective-permute-done.other, s32[4,128]{1,0:T(4,128)S(1)} %bitcast.15, ...), custom_call_target="tpu_custom_call" | custom-call | tf_op jit(solution)/shard_map/second_layer/pallas_call | solution.py:332
  22.4 2.8 %collective-permute-start.16 = (bf16[2,256,128]{2,1,0:T(8,128)(2,1)S(1)}, bf16[2,256,128]{2,1,0:T(8,128)(2,1)S(1)}, u32[]{:S(2)}, u32[]{:S(2)}) collective-permute-start(bf16[2,256,128]{2,1,0:T(8,128)(2,1)S(1)} %get-tuple-element.48), channel_id=1, source_target_pairs={{0,2},{1,3},{2,0},{3,1},{4,6},{5,7},{6,4},{7,5},{8,10},{9,11},{10,... | collective-permute-start | bytes 393224 | tf_op jit(solution)/shard_map/ppermute | solution.py:371
  25.3 9.7 %first_backward.1 = (bf16[2,256,128]{2,1,0:T(8,128)(2,1)S(1)}, bf16[2,256,128]{2,1,0:T(8,128)(2,1)S(1)}, bf16[512,256]{1,0:T(8,128)(2,1)S(1)}, bf16[512,256]{1,0:T(8,128)(2,1)S(1)}, bf16[512,256]{1,0:T(8,128)(2,1)S(1)}) custom-call(s32[32]{0:T(128)S(1)} %pad_add_fusion.mine, s32[32]{0:T(128)S(1)} %collective-permute-done.other, s32[4,128]{1,0:T(4,128)S(1)} %bitcast.16, ...), custom_call_target="tpu_custom_call" | custom-call | tf_op jit(solution)/shard_map/first_backward/pallas_call | solution.py:332
  34.9 1.7 %collective-permute-start.8 = (bf16[2,256,128]{2,1,0:T(8,128)(2,1)S(1)}, bf16[2,256,128]{2,1,0:T(8,128)(2,1)S(1)}, u32[]{:S(2)}, u32[]{:S(2)}) collective-permute-start(bf16[2,256,128]{2,1,0:T(8,128)(2,1)S(1)} %get-tuple-element.43), channel_id=1, source_target_pairs={{0,2},{1,3},{2,0},{3,1},{4,6},{5,7},{6,4},{7,5},{8,10},{9,11},{10,... | collective-permute-start | bytes 393224 | tf_op jit(solution)/shard_map/ppermute | solution.py:371
  36.7 1.5 %collective-permute-start.17 = (bf16[1,256,128]{2,1,0:T(8,128)(2,1)S(1)}, bf16[1,256,128]{2,1,0:T(8,128)(2,1)S(1)}, u32[]{:S(2)}, u32[]{:S(2)}) collective-permute-start(bf16[1,256,128]{2,1,0:T(8,128)(2,1)S(1)} %slice.19), channel_id=1, source_target_pairs={{0,1},{1,0},{2,3},{3,2},{4,5},{5,4},{6,7},{7,6},{8,9},{9,8},{10,11... | collective-permute-start | bytes 196616 | tf_op jit(solution)/shard_map/ppermute | solution.py:371
  38.2 2.4 %collective-permute-done.8 = bf16[2,256,128]{2,1,0:T(8,128)(2,1)S(1)} collective-permute-done((bf16[2,256,128]{2,1,0:T(8,128)(2,1)S(1)}, bf16[2,256,128]{2,1,0:T(8,128)(2,1)S(1)}, u32[]{:S(2)}, u32[]{:S(2)}) %collective-permute-start.8) | collective-permute-done | bytes 131104 | tf_op jit(solution)/shard_map/ppermute | solution.py:371
  40.7 1.2 %collective-permute-start.9 = (bf16[1,256,128]{2,1,0:T(8,128)(2,1)S(1)}, bf16[1,256,128]{2,1,0:T(8,128)(2,1)S(1)}, u32[]{:S(2)}, u32[]{:S(2)}) collective-permute-start(bf16[1,256,128]{2,1,0:T(8,128)(2,1)S(1)} %slice.17), channel_id=1, source_target_pairs={{0,1},{1,0},{2,3},{3,2},{4,5},{5,4},{6,7},{7,6},{8,9},{9,8},{10,11... | collective-permute-start | bytes 196616 | tf_op jit(solution)/shard_map/ppermute | solution.py:371
  41.9 1.9 %collective-permute-start.18 = (bf16[1,256,128]{2,1,0:T(8,128)(2,1)S(1)}, bf16[1,256,128]{2,1,0:T(8,128)(2,1)S(1)}, u32[]{:S(2)}, u32[]{:S(2)}) collective-permute-start(bf16[1,256,128]{2,1,0:T(8,128)(2,1)S(1)} %add_convert_fusion.4), channel_id=1, source_target_pairs={{0,4},{1,5},{2,6},{3,7},{4,0},{5,1},{6,2},{7,3},{8,12},{9,13},{10,... | collective-permute-start | bytes 196616 | tf_op jit(solution)/shard_map/ppermute | solution.py:371
  43.8 1.2 %collective-permute-done.9 = bf16[1,256,128]{2,1,0:T(8,128)(2,1)S(1)} collective-permute-done((bf16[1,256,128]{2,1,0:T(8,128)(2,1)S(1)}, bf16[1,256,128]{2,1,0:T(8,128)(2,1)S(1)}, u32[]{:S(2)}, u32[]{:S(2)}) %collective-permute-start.9) | collective-permute-done | bytes 65568 | tf_op jit(solution)/shard_map/ppermute | solution.py:371
  45.0 1.8 %collective-permute-start.10 = (bf16[1,256,128]{2,1,0:T(8,128)(2,1)S(1)}, bf16[1,256,128]{2,1,0:T(8,128)(2,1)S(1)}, u32[]{:S(2)}, u32[]{:S(2)}) collective-permute-start(bf16[1,256,128]{2,1,0:T(8,128)(2,1)S(1)} %add_convert_fusion.7), channel_id=1, source_target_pairs={{0,4},{1,5},{2,6},{3,7},{4,0},{5,1},{6,2},{7,3},{8,12},{9,13},{10,... | collective-permute-start | bytes 196616 | tf_op jit(solution)/shard_map/ppermute | solution.py:371
  46.8 2.8 %collective-permute-start.19 = (bf16[1,256,128]{2,1,0:T(8,128)(2,1)S(1)}, bf16[1,256,128]{2,1,0:T(8,128)(2,1)S(1)}, u32[]{:S(2)}, u32[]{:S(2)}) collective-permute-start(bf16[1,256,128]{2,1,0:T(8,128)(2,1)S(1)} %add_convert_fusion.3), channel_id=1, source_target_pairs={{0,8},{1,9},{2,10},{3,11},{4,12},{5,13},{6,14},{7,15},{8,0},{9,1},... | collective-permute-start | bytes 196616 | tf_op jit(solution)/shard_map/ppermute | solution.py:371
  49.6 2.7 %collective-permute-start.11 = (bf16[1,256,128]{2,1,0:T(8,128)(2,1)S(1)}, bf16[1,256,128]{2,1,0:T(8,128)(2,1)S(1)}, u32[]{:S(2)}, u32[]{:S(2)}) collective-permute-start(bf16[1,256,128]{2,1,0:T(8,128)(2,1)S(1)} %add_convert_fusion.6), channel_id=1, source_target_pairs={{0,8},{1,9},{2,10},{3,11},{4,12},{5,13},{6,14},{7,15},{8,0},{9,1},... | collective-permute-start | bytes 196616 | tf_op jit(solution)/shard_map/ppermute | solution.py:371
  52.4 1.7 %collective-permute-start.20 = (bf16[1,256,128]{2,1,0:T(8,128)(2,1)S(1)}, bf16[1,256,128]{2,1,0:T(8,128)(2,1)S(1)}, u32[]{:S(2)}, u32[]{:S(2)}) collective-permute-start(bf16[1,256,128]{2,1,0:T(8,128)(2,1)S(1)} %add_convert_fusion.2), channel_id=1, source_target_pairs={{0,1},{1,0},{2,3},{3,2},{4,5},{5,4},{6,7},{7,6},{8,9},{9,8},{10,11... | collective-permute-start | bytes 196616 | tf_op jit(solution)/shard_map/ppermute | solution.py:371
  54.1 0.8 %collective-permute-done.11 = bf16[1,256,128]{2,1,0:T(8,128)(2,1)S(1)} collective-permute-done((bf16[1,256,128]{2,1,0:T(8,128)(2,1)S(1)}, bf16[1,256,128]{2,1,0:T(8,128)(2,1)S(1)}, u32[]{:S(2)}, u32[]{:S(2)}) %collective-permute-start.11) | collective-permute-done | bytes 65568 | tf_op jit(solution)/shard_map/ppermute | solution.py:371
  54.9 1.4 %collective-permute-start.12 = (bf16[1,256,128]{2,1,0:T(8,128)(2,1)S(1)}, bf16[1,256,128]{2,1,0:T(8,128)(2,1)S(1)}, u32[]{:S(2)}, u32[]{:S(2)}) collective-permute-start(bf16[1,256,128]{2,1,0:T(8,128)(2,1)S(1)} %add_convert_fusion.5), channel_id=1, source_target_pairs={{0,1},{1,0},{2,3},{3,2},{4,5},{5,4},{6,7},{7,6},{8,9},{9,8},{10,11... | collective-permute-start | bytes 196616 | tf_op jit(solution)/shard_map/ppermute | solution.py:371
  56.3 1.1 %collective-permute-done.20 = bf16[1,256,128]{2,1,0:T(8,128)(2,1)S(1)} collective-permute-done((bf16[1,256,128]{2,1,0:T(8,128)(2,1)S(1)}, bf16[1,256,128]{2,1,0:T(8,128)(2,1)S(1)}, u32[]{:S(2)}, u32[]{:S(2)}) %collective-permute-start.20) | collective-permute-done | bytes 65568 | tf_op jit(solution)/shard_map/ppermute | solution.py:371
  57.4 1.3 %collective-permute-start.21 = (bf16[2,256,128]{2,1,0:T(8,128)(2,1)S(1)}, bf16[2,256,128]{2,1,0:T(8,128)(2,1)S(1)}, u32[]{:S(2)}, u32[]{:S(2)}) collective-permute-start(bf16[2,256,128]{2,1,0:T(8,128)(2,1)S(1)} %pad_maximum_fusion.1.near_mine), channel_id=1, source_target_pairs={{0,2},{1,3},{2,0},{3,1},{4,6},{5,7},{6,4},{7,5},{8,10},{9,11},{10,... | collective-permute-start | bytes 393224 | tf_op jit(solution)/shard_map/ppermute | solution.py:371
  58.7 0.5 collective-permute-start.6
  59.3 1.8 %collective-permute-start.13 = (bf16[2,256,128]{2,1,0:T(8,128)(2,1)S(1)}, bf16[2,256,128]{2,1,0:T(8,128)(2,1)S(1)}, u32[]{:S(2)}, u32[]{:S(2)}) collective-permute-start(bf16[2,256,128]{2,1,0:T(8,128)(2,1)S(1)} %pad_maximum_fusion.near_mine), channel_id=1, source_target_pairs={{0,2},{1,3},{2,0},{3,1},{4,6},{5,7},{6,4},{7,5},{8,10},{9,11},{10,... | collective-permute-start | bytes 393224 | tf_op jit(solution)/shard_map/ppermute | solution.py:371
  61.1 1.4 %collective-permute-done.21.far_mine = bf16[2,256,128]{2,1,0:T(8,128)(2,1)S(1)} collective-permute-done((bf16[2,256,128]{2,1,0:T(8,128)(2,1)S(1)}, bf16[2,256,128]{2,1,0:T(8,128)(2,1)S(1)}, u32[]{:S(2)}, u32[]{:S(2)}) %collective-permute-start.21) | collective-permute-done | bytes 131104 | tf_op jit(solution)/shard_map/ppermute | solution.py:371
  62.5 0.6 collective-permute-start.7
  63.1 1.2 %collective-permute-done.13.far_mine = bf16[2,256,128]{2,1,0:T(8,128)(2,1)S(1)} collective-permute-done((bf16[2,256,128]{2,1,0:T(8,128)(2,1)S(1)}, bf16[2,256,128]{2,1,0:T(8,128)(2,1)S(1)}, u32[]{:S(2)}, u32[]{:S(2)}) %collective-permute-start.13) | collective-permute-done | bytes 131104 | tf_op jit(solution)/shard_map/ppermute | solution.py:371
  64.3 1.2 %finish_weights.3 = (f32[1,256]{1,0:T(1,128)}, f32[256,768]{1,0:T(8,128)}, f32[256,256]{1,0:T(8,128)}) custom-call(bf16[2,256,128]{2,1,0:T(8,128)(2,1)S(1)} %pad_maximum_fusion.1.near_mine, bf16[2,256,128]{2,1,0:T(8,128)(2,1)S(1)} %collective-permute-done.21.far_mine, bf16[2,256,128]{2,1,0:T(8,128)(2,1)S(1)} %collective-permute-done.22.near_other, ...), custom_call_target="tpu_custom_call" | custom-call | tf_op jit(solution)/shard_map/finish_weights/pallas_call | solution.py:332
  65.5 1.3 %finish_rows.1 = (bf16[512,256]{1,0:T(8,128)(2,1)}, bf16[512,256]{1,0:T(8,128)(2,1)}) custom-call(bf16[512,256]{1,0:T(8,128)(2,1)S(1)} %get-tuple-element.36.part_mine, bf16[512,256]{1,0:T(8,128)(2,1)S(1)} %collective-permute-done.6.part_other, bf16[512,256]{1,0:T(8,128)(2,1)S(1)} %bitcast.10, bf16[1,256]{1,0:T(2,128)(2,1)S(1)} %reshape.40.gain, ...), custom_call_target="tpu_custom_call" | custom-call | tf_op jit(solution)/shard_map/finish_rows/pallas_call | solution.py:332
  66.8 1.2 %finish_weights.2 = (f32[1,256]{1,0:T(1,128)}, f32[256,768]{1,0:T(8,128)}, f32[256,256]{1,0:T(8,128)}) custom-call(bf16[2,256,128]{2,1,0:T(8,128)(2,1)S(1)} %pad_maximum_fusion.near_mine, bf16[2,256,128]{2,1,0:T(8,128)(2,1)S(1)} %collective-permute-done.13.far_mine, bf16[2,256,128]{2,1,0:T(8,128)(2,1)S(1)} %collective-permute-done.14.near_other, ...), custom_call_target="tpu_custom_call" | custom-call | tf_op jit(solution)/shard_map/finish_weights/pallas_call | solution.py:332
  (64 shorter events, 2.4 us)
Async XLA Ops:
  0.6 1.3 %copy-start.9 = (s32[1,4,4]{2,1,0:T(4,128)S(1)}, s32[1,4,4]{2,1,0:T(4,128)}, u32[]{:S(2)}) copy-start(s32[1,4,4]{2,1,0:T(4,128)} %param.13) | copy-start | bytes 196
  0.6 2.6 %collective-permute-start.2 = (bf16[512,256]{1,0:T(8,128)(2,1)}, bf16[512,256]{1,0:T(8,128)(2,1)S(1)}, u32[]{:S(2)}, u32[]{:S(2)}) collective-permute-start(bf16[512,256]{1,0:T(8,128)(2,1)} %bitcast.7), channel_id=1, source_target_pairs={{0,16},{16,0},{1,17},{17,1},{2,18},{18,2},{3,19},{19,3},{4,20},{20... | collective-permute-start | bytes 786440 | tf_op jit(solution)/shard_map/ppermute | solution.py:367
  2.1 1.1 %collective-permute-start = (s32[32]{0:T(128)S(1)}, s32[32]{0:T(128)S(1)}, u32[]{:S(2)}, u32[]{:S(2)}) collective-permute-start(s32[32]{0:T(128)S(1)} %pad_add_fusion.mine), channel_id=1, source_target_pairs={{0,16},{16,0},{1,17},{17,1},{2,18},{18,2},{3,19},{19,3},{4,20},{20... | collective-permute-start | bytes 392 | tf_op jit(solution)/shard_map/ppermute | solution.py:367
  2.2 9.7 %collective-permute-start.4 = (bf16[512,256]{1,0:T(8,128)(2,1)}, bf16[512,256]{1,0:T(8,128)(2,1)S(1)}, u32[]{:S(2)}, u32[]{:S(2)}) collective-permute-start(bf16[512,256]{1,0:T(8,128)(2,1)} %bitcast.11), channel_id=1, source_target_pairs={{0,16},{16,0},{1,17},{17,1},{2,18},{18,2},{3,19},{19,3},{4,20},{20... | collective-permute-start | bytes 786440 | tf_op jit(solution)/shard_map/ppermute | solution.py:367
  3.2 1.0 %copy-start = (bf16[256,768]{1,0:T(8,128)(2,1)S(1)}, bf16[256,768]{1,0:T(8,128)(2,1)}, u32[]{:S(2)}) copy-start(bf16[256,768]{1,0:T(8,128)(2,1)} %weight.8) | copy-start | bytes 1179652
  5.2 6.7 %copy-start.4 = (bf16[256,768]{1,0:T(8,128)(2,1)S(1)}, bf16[256,768]{1,0:T(8,128)(2,1)}, u32[]{:S(2)}) copy-start(bf16[256,768]{1,0:T(8,128)(2,1)} %weight.9) | copy-start | bytes 1179652
  5.2 6.7 %copy-start.5 = (bf16[1,512,256]{2,1,0:T(8,128)(2,1)S(1)}, bf16[1,512,256]{2,1,0:T(8,128)(2,1)}, u32[]{:S(2)}) copy-start(bf16[1,512,256]{2,1,0:T(8,128)(2,1)} %param.12) | copy-start | bytes 786436
  5.2 6.7 %copy-start.6 = (bf16[256,256]{1,0:T(8,128)(2,1)S(1)}, bf16[256,256]{1,0:T(8,128)(2,1)}, u32[]{:S(2)}) copy-start(bf16[256,256]{1,0:T(8,128)(2,1)} %out_one.3) | copy-start | bytes 393220
  5.2 6.7 %copy-start.7 = (bf16[256,256]{1,0:T(8,128)(2,1)S(1)}, bf16[256,256]{1,0:T(8,128)(2,1)}, u32[]{:S(2)}) copy-start(bf16[256,256]{1,0:T(8,128)(2,1)} %out_two.3) | copy-start | bytes 393220
  10.0 1.8 %collective-permute-start.3 = (bf16[1024,128]{1,0:T(8,128)(2,1)S(1)}, bf16[1024,128]{1,0:T(8,128)(2,1)S(1)}, u32[]{:S(2)}, u32[]{:S(2)}) collective-permute-start(bf16[1024,128]{1,0:T(8,128)(2,1)S(1)} %get-tuple-element.30.mixed_mine.mixed_ref), channel_id=1, source_target_pairs={{0,16},{16,0},{1,17},{17,1},{2,18},{18,2},{3,19},{19,3},{4,20},{20... | collective-permute-start | bytes 786440 | tf_op jit(solution)/shard_map/ppermute | solution.py:367
  10.7 1.2 %collective-permute-start.1 = (s32[4,128]{1,0:T(4,128)S(1)}, s32[4,128]{1,0:T(4,128)S(1)}, u32[]{:S(2)}, u32[]{:S(2)}) collective-permute-start(s32[4,128]{1,0:T(4,128)S(1)} %bitcast.14), channel_id=1, source_target_pairs={{0,16},{16,0},{1,17},{17,1},{2,18},{18,2},{3,19},{19,3},{4,20},{20... | collective-permute-start | bytes 6152 | tf_op jit(solution)/shard_map/ppermute | solution.py:367
  10.9 14.3 %copy-start.1 = (bf16[256,768]{1,0:T(8,128)(2,1)S(1)}, bf16[256,768]{1,0:T(8,128)(2,1)}, u32[]{:S(2)}) copy-start(bf16[256,768]{1,0:T(8,128)(2,1)} %weight.8) | copy-start | bytes 1179652
  22.1 3.1 %collective-permute-start.5 = (bf16[1024,256]{1,0:T(8,128)(2,1)S(1)}, bf16[1024,256]{1,0:T(8,128)(2,1)S(1)}, u32[]{:S(2)}, u32[]{:S(2)}) collective-permute-start(bf16[1024,256]{1,0:T(8,128)(2,1)S(1)} %get-tuple-element.31.part_mine), channel_id=1, source_target_pairs={{0,16},{16,0},{1,17},{17,1},{2,18},{18,2},{3,19},{19,3},{4,20},{20... | collective-permute-start | bytes 1572872 | tf_op jit(solution)/shard_map/ppermute | solution.py:367
  22.4 14.2 %collective-permute-start.16 = (bf16[2,256,128]{2,1,0:T(8,128)(2,1)S(1)}, bf16[2,256,128]{2,1,0:T(8,128)(2,1)S(1)}, u32[]{:S(2)}, u32[]{:S(2)}) collective-permute-start(bf16[2,256,128]{2,1,0:T(8,128)(2,1)S(1)} %get-tuple-element.48), channel_id=1, source_target_pairs={{0,2},{1,3},{2,0},{3,1},{4,6},{5,7},{6,4},{7,5},{8,10},{9,11},{10,... | collective-permute-start | bytes 393224 | tf_op jit(solution)/shard_map/ppermute | solution.py:371
  34.9 5.7 %collective-permute-start.8 = (bf16[2,256,128]{2,1,0:T(8,128)(2,1)S(1)}, bf16[2,256,128]{2,1,0:T(8,128)(2,1)S(1)}, u32[]{:S(2)}, u32[]{:S(2)}) collective-permute-start(bf16[2,256,128]{2,1,0:T(8,128)(2,1)S(1)} %get-tuple-element.43), channel_id=1, source_target_pairs={{0,2},{1,3},{2,0},{3,1},{4,6},{5,7},{6,4},{7,5},{8,10},{9,11},{10,... | collective-permute-start | bytes 393224 | tf_op jit(solution)/shard_map/ppermute | solution.py:371
  36.7 5.3 %collective-permute-start.17 = (bf16[1,256,128]{2,1,0:T(8,128)(2,1)S(1)}, bf16[1,256,128]{2,1,0:T(8,128)(2,1)S(1)}, u32[]{:S(2)}, u32[]{:S(2)}) collective-permute-start(bf16[1,256,128]{2,1,0:T(8,128)(2,1)S(1)} %slice.19), channel_id=1, source_target_pairs={{0,1},{1,0},{2,3},{3,2},{4,5},{5,4},{6,7},{7,6},{8,9},{9,8},{10,11... | collective-permute-start | bytes 196616 | tf_op jit(solution)/shard_map/ppermute | solution.py:371
  40.7 4.3 %collective-permute-start.9 = (bf16[1,256,128]{2,1,0:T(8,128)(2,1)S(1)}, bf16[1,256,128]{2,1,0:T(8,128)(2,1)S(1)}, u32[]{:S(2)}, u32[]{:S(2)}) collective-permute-start(bf16[1,256,128]{2,1,0:T(8,128)(2,1)S(1)} %slice.17), channel_id=1, source_target_pairs={{0,1},{1,0},{2,3},{3,2},{4,5},{5,4},{6,7},{7,6},{8,9},{9,8},{10,11... | collective-permute-start | bytes 196616 | tf_op jit(solution)/shard_map/ppermute | solution.py:371
  41.9 4.9 %collective-permute-start.18 = (bf16[1,256,128]{2,1,0:T(8,128)(2,1)S(1)}, bf16[1,256,128]{2,1,0:T(8,128)(2,1)S(1)}, u32[]{:S(2)}, u32[]{:S(2)}) collective-permute-start(bf16[1,256,128]{2,1,0:T(8,128)(2,1)S(1)} %add_convert_fusion.4), channel_id=1, source_target_pairs={{0,4},{1,5},{2,6},{3,7},{4,0},{5,1},{6,2},{7,3},{8,12},{9,13},{10,... | collective-permute-start | bytes 196616 | tf_op jit(solution)/shard_map/ppermute | solution.py:371
  45.0 4.6 %collective-permute-start.10 = (bf16[1,256,128]{2,1,0:T(8,128)(2,1)S(1)}, bf16[1,256,128]{2,1,0:T(8,128)(2,1)S(1)}, u32[]{:S(2)}, u32[]{:S(2)}) collective-permute-start(bf16[1,256,128]{2,1,0:T(8,128)(2,1)S(1)} %add_convert_fusion.7), channel_id=1, source_target_pairs={{0,4},{1,5},{2,6},{3,7},{4,0},{5,1},{6,2},{7,3},{8,12},{9,13},{10,... | collective-permute-start | bytes 196616 | tf_op jit(solution)/shard_map/ppermute | solution.py:371
  46.8 5.6 %collective-permute-start.19 = (bf16[1,256,128]{2,1,0:T(8,128)(2,1)S(1)}, bf16[1,256,128]{2,1,0:T(8,128)(2,1)S(1)}, u32[]{:S(2)}, u32[]{:S(2)}) collective-permute-start(bf16[1,256,128]{2,1,0:T(8,128)(2,1)S(1)} %add_convert_fusion.3), channel_id=1, source_target_pairs={{0,8},{1,9},{2,10},{3,11},{4,12},{5,13},{6,14},{7,15},{8,0},{9,1},... | collective-permute-start | bytes 196616 | tf_op jit(solution)/shard_map/ppermute | solution.py:371
  49.6 5.2 %collective-permute-start.11 = (bf16[1,256,128]{2,1,0:T(8,128)(2,1)S(1)}, bf16[1,256,128]{2,1,0:T(8,128)(2,1)S(1)}, u32[]{:S(2)}, u32[]{:S(2)}) collective-permute-start(bf16[1,256,128]{2,1,0:T(8,128)(2,1)S(1)} %add_convert_fusion.6), channel_id=1, source_target_pairs={{0,8},{1,9},{2,10},{3,11},{4,12},{5,13},{6,14},{7,15},{8,0},{9,1},... | collective-permute-start | bytes 196616 | tf_op jit(solution)/shard_map/ppermute | solution.py:371
  52.4 5.0 %collective-permute-start.20 = (bf16[1,256,128]{2,1,0:T(8,128)(2,1)S(1)}, bf16[1,256,128]{2,1,0:T(8,128)(2,1)S(1)}, u32[]{:S(2)}, u32[]{:S(2)}) collective-permute-start(bf16[1,256,128]{2,1,0:T(8,128)(2,1)S(1)} %add_convert_fusion.2), channel_id=1, source_target_pairs={{0,1},{1,0},{2,3},{3,2},{4,5},{5,4},{6,7},{7,6},{8,9},{9,8},{10,11... | collective-permute-start | bytes 196616 | tf_op jit(solution)/shard_map/ppermute | solution.py:371
  54.9 4.4 %collective-permute-start.12 = (bf16[1,256,128]{2,1,0:T(8,128)(2,1)S(1)}, bf16[1,256,128]{2,1,0:T(8,128)(2,1)S(1)}, u32[]{:S(2)}, u32[]{:S(2)}) collective-permute-start(bf16[1,256,128]{2,1,0:T(8,128)(2,1)S(1)} %add_convert_fusion.5), channel_id=1, source_target_pairs={{0,1},{1,0},{2,3},{3,2},{4,5},{5,4},{6,7},{7,6},{8,9},{9,8},{10,11... | collective-permute-start | bytes 196616 | tf_op jit(solution)/shard_map/ppermute | solution.py:371
  57.4 5.0 %collective-permute-start.21 = (bf16[2,256,128]{2,1,0:T(8,128)(2,1)S(1)}, bf16[2,256,128]{2,1,0:T(8,128)(2,1)S(1)}, u32[]{:S(2)}, u32[]{:S(2)}) collective-permute-start(bf16[2,256,128]{2,1,0:T(8,128)(2,1)S(1)} %pad_maximum_fusion.1.near_mine), channel_id=1, source_target_pairs={{0,2},{1,3},{2,0},{3,1},{4,6},{5,7},{6,4},{7,5},{8,10},{9,11},{10,... | collective-permute-start | bytes 393224 | tf_op jit(solution)/shard_map/ppermute | solution.py:371
  58.7 4.3 %collective-permute-start.22 = (bf16[2,256,128]{2,1,0:T(8,128)(2,1)S(1)}, bf16[2,256,128]{2,1,0:T(8,128)(2,1)S(1)}, u32[]{:S(2)}, u32[]{:S(2)}) collective-permute-start(bf16[2,256,128]{2,1,0:T(8,128)(2,1)S(1)} %pad_maximum_fusion.1.near_mine), channel_id=1, source_target_pairs={{0,16},{16,0},{1,17},{17,1},{2,18},{18,2},{3,19},{19,3},{4,20},{20... | collective-permute-start | bytes 393224 | tf_op jit(solution)/shard_map/ppermute | solution.py:367
  58.7 6.8 %collective-permute-start.6 = (bf16[512,256]{1,0:T(8,128)(2,1)S(1)}, bf16[512,256]{1,0:T(8,128)(2,1)S(1)}, u32[]{:S(2)}, u32[]{:S(2)}) collective-permute-start(bf16[512,256]{1,0:T(8,128)(2,1)S(1)} %get-tuple-element.37), channel_id=1, source_target_pairs={{0,16},{16,0},{1,17},{17,1},{2,18},{18,2},{3,19},{19,3},{4,20},{20... | collective-permute-start | bytes 786440 | tf_op jit(solution)/shard_map/ppermute | solution.py:367
  59.3 5.0 %collective-permute-start.13 = (bf16[2,256,128]{2,1,0:T(8,128)(2,1)S(1)}, bf16[2,256,128]{2,1,0:T(8,128)(2,1)S(1)}, u32[]{:S(2)}, u32[]{:S(2)}) collective-permute-start(bf16[2,256,128]{2,1,0:T(8,128)(2,1)S(1)} %pad_maximum_fusion.near_mine), channel_id=1, source_target_pairs={{0,2},{1,3},{2,0},{3,1},{4,6},{5,7},{6,4},{7,5},{8,10},{9,11},{10,... | collective-permute-start | bytes 393224 | tf_op jit(solution)/shard_map/ppermute | solution.py:371
  62.4 1.9 %collective-permute-start.23 = (bf16[2,256,128]{2,1,0:T(8,128)(2,1)S(1)}, bf16[2,256,128]{2,1,0:T(8,128)(2,1)S(1)}, u32[]{:S(2)}, u32[]{:S(2)}) collective-permute-start(bf16[2,256,128]{2,1,0:T(8,128)(2,1)S(1)} %collective-permute-done.21.far_mine), channel_id=1, source_target_pairs={{0,16},{16,0},{1,17},{17,1},{2,18},{18,2},{3,19},{19,3},{4,20},{20... | collective-permute-start | bytes 393224 | tf_op jit(solution)/shard_map/ppermute | solution.py:367
  62.5 3.0 %copy-start.3 = (bf16[1,512,256]{2,1,0:T(8,128)(2,1)S(1)}, bf16[1,512,256]{2,1,0:T(8,128)(2,1)}, u32[]{:S(2)}) copy-start(bf16[1,512,256]{2,1,0:T(8,128)(2,1)} %param.11) | copy-start | bytes 786436
  62.5 3.0 %collective-permute-start.7 = (bf16[512,128]{1,0:T(8,128)(2,1)S(1)}, bf16[512,128]{1,0:T(8,128)(2,1)S(1)}, u32[]{:S(2)}, u32[]{:S(2)}) collective-permute-start(bf16[512,128]{1,0:T(8,128)(2,1)S(1)} %constant_dynamic-slice_fusion), channel_id=1, source_target_pairs={{0,16},{16,0},{1,17},{17,1},{2,18},{18,2},{3,19},{19,3},{4,20},{20... | collective-permute-start | bytes 393224 | tf_op jit(solution)/shard_map/ppermute | solution.py:367
  63.0 3.7 %collective-permute-start.14 = (bf16[2,256,128]{2,1,0:T(8,128)(2,1)S(1)}, bf16[2,256,128]{2,1,0:T(8,128)(2,1)S(1)}, u32[]{:S(2)}, u32[]{:S(2)}) collective-permute-start(bf16[2,256,128]{2,1,0:T(8,128)(2,1)S(1)} %pad_maximum_fusion.near_mine), channel_id=1, source_target_pairs={{0,16},{16,0},{1,17},{17,1},{2,18},{18,2},{3,19},{19,3},{4,20},{20... | collective-permute-start | bytes 393224 | tf_op jit(solution)/shard_map/ppermute | solution.py:367
  64.3 2.5 %collective-permute-start.15 = (bf16[2,256,128]{2,1,0:T(8,128)(2,1)S(1)}, bf16[2,256,128]{2,1,0:T(8,128)(2,1)S(1)}, u32[]{:S(2)}, u32[]{:S(2)}) collective-permute-start(bf16[2,256,128]{2,1,0:T(8,128)(2,1)S(1)} %collective-permute-done.13.far_mine), channel_id=1, source_target_pairs={{0,16},{16,0},{1,17},{17,1},{2,18},{18,2},{3,19},{19,3},{4,20},{20... | collective-permute-start | bytes 393224 | tf_op jit(solution)/shard_map/ppermute | solution.py:367
  (4 other events, 3.2 us)

commit v3 on v2

v3 whole, which is shorter than its diff:
```python
import functools

import jax
import jax.numpy as jnp
from jax import lax
from jax.experimental import pallas as pl
from jax.experimental.pallas import tpu as pltpu
from jax.sharding import PartitionSpec as P

HEADS = 4
BALL = 128
LISTED = 4
EPSILON = 1e-06
BF = jnp.bfloat16
F32 = jnp.float32
SWAP = ((0, 1), (1, 0))

VMEM = pl.BlockSpec(memory_space=pltpu.VMEM)
SMEM = pl.BlockSpec(memory_space=pltpu.SMEM)
HBM = pl.BlockSpec(memory_space=pltpu.HBM)
PARAMS = pltpu.CompilerParams(vmem_limit_bytes=40 * 1024 * 1024)


def dot(a, b, dims=((1,), (0,))):
    return lax.dot_general(a, b, (dims, ((), ())), preferred_element_type=F32)


def norm_factor(x):
    return lax.rsqrt(jnp.mean(x * x, axis=-1, keepdims=True) + EPSILON)


def part_of(place, size):
    return pl.ds(pl.multiple_of(place * size, size), size)


def gain_row(gain):
    return gain[...].astype(F32).reshape(1, gain.shape[0])


def project(normed, columns):
    qkv = dot(normed, columns)
    half = columns.shape[1] // 3
    scale = (2 * half // HEADS) ** (-0.5)
    return qkv[:, :half].astype(BF) * BF(scale), qkv[:, half:].astype(BF)


def stack_heads(rows):
    lane = lax.broadcasted_iota(jnp.int32, rows.shape, 1)
    first = lane < rows.shape[1] // 2
    zero = jnp.zeros_like(rows)
    return jnp.concatenate([jnp.where(first, rows, zero), jnp.where(first, zero, rows)], axis=0)


def unstack_heads(stacked):
    rows = stacked.shape[0] // 2
    lane = lax.broadcasted_iota(jnp.int32, (rows, stacked.shape[1]), 1)
    return jnp.where(lane < stacked.shape[1] // 2, stacked[:rows], stacked[rows:])


def listed_balls(ball, mine, other, core):
    local_balls = mine.shape[1]
    lists, row = (mine, ball) if ball < local_balls else (other, ball - local_balls)
    return [lax.rem(lists[0, row, j] + core * local_balls, 2 * local_balls) for j in range(LISTED)]


def pick(ref, listed, first, half):
    return jnp.concatenate([ref[part_of(i, BALL), first : first + half] for i in listed], axis=0)


def softmax_parts(stacked, keys):
    scores = dot(stacked, keys, ((1,), (1,)))
    exponent = jnp.exp(scores - jnp.max(scores, axis=-1, keepdims=True))
    return exponent, 1.0 / jnp.sum(exponent, axis=-1, keepdims=True)


def mix(exponent, inverse, values):
    return unstack_heads(dot(exponent.astype(BF), values) * inverse)


def ball_backward(stacked, keys, values, exponent, inverse, mixed, mixed_grad):
    grad = stack_heads(mixed_grad.astype(F32)) * inverse
    inner = jnp.sum(grad * jnp.concatenate([mixed, mixed], axis=0), axis=-1, keepdims=True)
    grad = grad.astype(BF)
    scores_grad = (exponent * (dot(grad, values, ((1,), (1,))) - inner)).astype(BF)
    scale = (stacked.shape[1] // 2) ** (-0.5)
    queries_grad = unstack_heads(dot(scores_grad, keys)) * scale
    keys_grad = dot(stacked, scores_grad, ((0,), (0,)))
    values_grad = dot(grad, exponent.astype(BF), ((0,), (0,)))
    return queries_grad.astype(BF), keys_grad, values_grad


def add_listed(ref, listed, part):
    for j, i in enumerate(listed):
        ref[i] += part[:, j * BALL : (j + 1) * BALL]


def key_value_grads(dk_ref, dv_ref):
    balls = dk_ref.shape[0]
    parts = [jnp.concatenate([ref[i].T for i in range(balls)], axis=0).astype(BF) for ref in (dk_ref, dv_ref)]
    return jnp.concatenate(parts, axis=1)


def slot_bit(core):
    geo = lax.axis_index("geo")
    return jnp.where(core == 0, lax.rem(geo // 2, 2), lax.rem(geo, 2))


def weight_part(part, normed_ref, grads, mixed, grad_out_ref):
    half = mixed.shape[1]
    weight = dot(normed_ref[:, part_of(part, half)], grads, ((0,), (0,)))
    out = dot(mixed, grad_out_ref[:, part_of(part, half)], ((0,), (0,)))
    blocks = [weight[:, i * half : (i + 1) * half] for i in range(3)] + [out]
    return jnp.concatenate(blocks, axis=0).astype(BF)


def norm_backward(normed_grad, x, gain, grad_out):
    factor = norm_factor(x)
    scaled = normed_grad.astype(BF).astype(F32) * gain
    inner = jnp.mean(scaled * x, axis=-1, keepdims=True)
    return (grad_out.astype(F32) + factor * scaled - x * (factor * factor * factor) * inner).astype(BF)


def norm_project(x, gain, columns):
    normed = (x * norm_factor(x) * gain).astype(BF)
    return (normed, *project(normed, columns))


def project_mine(
    x_hbm, grad_hbm, rot_hbm, gain_one_hbm, gain_two_hbm, qkv_one_hbm, qkv_two_hbm, out_one_hbm, out_two_hbm,
    x, grad, rot, gain_one, gain_two, qkv_one, qkv_two, out_one, out_two, normed_ref, q_ref, kv_ref,
    sems,
):
    core = lax.axis_index("pts")
    half = x.shape[1] // 2
    copies = []

    def start(source, target):
        copies.append(pltpu.make_async_copy(source, target, sems.at[len(copies)]))
        copies[-1].start()

    def start_columns(source, target):
        for i in range(3):
            start(source.at[:, part_of(2 * i + core, half)], target.at[:, i * half : (i + 1) * half])

    start(x_hbm, x)
    start(gain_one_hbm, gain_one)
    start_columns(qkv_one_hbm, qkv_one)
    first = len(copies)
    start(grad_hbm, grad)
    start(rot_hbm, rot)
    start(gain_two_hbm, gain_two)
    start_columns(qkv_two_hbm, qkv_two)
    for source, target in ((out_one_hbm, out_one), (out_two_hbm, out_two)):
        start(source.at[part_of(core, half)], target.at[:half])
        start(source.at[part_of(1 - core, half)], target.at[half:])
    for copy in copies[:first]:
        copy.wait()
    normed_ref[...], q_ref[...], kv_ref[...] = norm_project(x[...].astype(F32), gain_row(gain_one), qkv_one[...])
    for copy in copies[first:]:
        copy.wait()


def first_forward(
    mine, other, x_other, gain, columns, normed_mine, q_mine, kv_mine, mixed_ref, q_ref, kv_ref, normed_ref
):
    core = lax.axis_index("pts")
    local, width = x_other.shape
    half = width // 2
    normed_ref[:local], q_ref[:local], kv_ref[:local] = normed_mine[...], q_mine[...], kv_mine[...]
    found = norm_project(x_other[...].astype(F32), gain_row(gain), columns[...])
    normed_ref[local:], q_ref[local:], kv_ref[local:] = found
    for ball in range(2 * local // BALL):
        listed = listed_balls(ball, mine, other, core)
        at = slice(ball * BALL, (ball + 1) * BALL)
        stacked = stack_heads(q_ref[at, :])
        exponent, inverse = softmax_parts(stacked, pick(kv_ref, listed, 0, half))
        mixed_ref[at, :] = mix(exponent, inverse, pick(kv_ref, listed, half, half)).astype(BF)


def before_second(
    rot_mine, rot_other, x_mine, x_other, mixed, grad_mine, grad_other, out_one, out_two,
    base_ref, chosen_ref, grad_ref, mg_ref,
):
    core = lax.axis_index("pts")
    local, width = x_mine.shape
    half = width // 2
    total = 2 * local
    own = out_one[:half]
    base_ref[:local] = x_mine[...].astype(F32) + dot(mixed[:local], own)
    base_ref[local:] = x_other[...].astype(F32) + dot(mixed[local:], own)
    grad_ref[:local] = grad_mine[...]
    grad_ref[local:] = grad_other[...]
    mg_ref[...] = dot(grad_ref[...], out_two[:half], ((1,), (1,))).astype(BF)
    lane = lax.broadcasted_iota(jnp.int32, (BALL, total), 1)
    lane = lax.rem(lane + core * local, total).astype(F32)
    for side, ref in enumerate((rot_mine, rot_other)):
        for j in range(local // BALL):
            row = ref[j : j + 1, :].astype(F32)
            column = jnp.broadcast_to(row, (BALL, BALL)).T[:, :1]
            first = side * local + j * BALL
            chosen_ref[first : first + BALL, :] = (lane == column).astype(BF)


def second_layer(
    mine, other, base, mixed_other, chosen, mg_ref, out_one, gain, columns,
    moved_ref, normed_ref, mixed_ref, mixed_send, grads_ref, part_ref,
    hidden_ref, q_ref, kv_ref, dk_ref, dv_ref,
):
    core = lax.axis_index("pts")
    total, width = base.shape
    local = total // 2
    half = width // 2
    far = out_one[half:]
    hidden_ref[:local] = (base[:local] + dot(mixed_other[local:], far)).astype(BF)
    hidden_ref[local:] = (base[local:] + dot(mixed_other[:local], far)).astype(BF)
    moved = dot(chosen[...], hidden_ref[...])
    moved_ref[...] = moved.astype(BF)
    normed_ref[...], q_ref[...], kv_ref[...] = norm_project(moved, gain_row(gain), columns[...])
    dk_ref[...] = jnp.zeros_like(dk_ref)
    dv_ref[...] = jnp.zeros_like(dv_ref)
    for ball in range(total // BALL):
        listed = listed_balls(ball, mine, other, core)
        at = slice(ball * BALL, (ball + 1) * BALL)
        stacked = stack_heads(q_ref[at, :])
        keys = pick(kv_ref, listed, 0, half)
        values = pick(kv_ref, listed, half, half)
        exponent, inverse = softmax_parts(stacked, keys)
        mixed = mix(exponent, inverse, values)
        mixed_ref[at, :] = mixed.astype(BF)
        dq, dk, dv = ball_backward(stacked, keys, values, exponent, inverse, mixed, mg_ref[at, :])
        grads_ref[at, :half] = dq
        add_listed(dk_ref, listed, dk)
        add_listed(dv_ref, listed, dv)
    grads_ref[:, half:] = key_value_grads(dk_ref, dv_ref)
    part_ref[...] = dot(grads_ref[...], columns[...], ((1,), (1,))).astype(BF)
    mixed_send[...] = mixed_ref[local:]


def second_weights(normed, grads, mixed, grad, keep_ref, send_ref):
    bit = slot_bit(lax.axis_index("pts"))
    send_ref[...] = weight_part(1 - bit, normed, grads[...], mixed[...], grad)
    keep_ref[...] = weight_part(bit, normed, grads[...], mixed[...], grad)


def first_backward(
    mine, other, rot_mine, rot_other, part_mine, part_other, moved, grad, gain_two,
    mixed_ref, normed, q_ref, kv_ref, out_one,
    hg_ref, grads_ref, send_ref,
    rows_grad_ref, mg_ref, dk_ref, dv_ref,
):
    core = lax.axis_index("pts")
    total, width = grad.shape
    local = total // 2
    half = width // 2
    gain = gain_row(gain_two)
    for first, far in ((0, local), (local, 0)):
        at = slice(first, first + local)
        normed_grad = part_mine[at].astype(F32) + part_other[far : far + local].astype(F32)
        rows_grad_ref[at] = norm_backward(normed_grad, moved[at].astype(F32), gain, grad[at])
    row_of = [ref[j : j + 1, :] for ref in (rot_mine, rot_other) for j in range(local // BALL)]
    order = jnp.concatenate(row_of, axis=1).astype(F32)
    rows_grad = rows_grad_ref[...]
    place = lax.broadcasted_iota(jnp.int32, (BALL, total), 0)
    for j in range(total // BALL):
        first = lax.rem(j * BALL + core * local, total)
        chosen = ((place + first).astype(F32) == order).astype(BF)
        hg_ref[j * BALL : (j + 1) * BALL, :] = dot(chosen, rows_grad).astype(BF)
    mg_ref[...] = dot(hg_ref[...], out_one[:half], ((1,), (1,))).astype(BF)
    dk_ref[...] = jnp.zeros_like(dk_ref)
    dv_ref[...] = jnp.zeros_like(dv_ref)
    for ball in range(total // BALL):
        listed = listed_balls(ball, mine, other, core)
        at = slice(ball * BALL, (ball + 1) * BALL)
        stacked = stack_heads(q_ref[at, :])
        keys = pick(kv_ref, listed, 0, half)
        values = pick(kv_ref, listed, half, half)
        exponent, inverse = softmax_parts(stacked, keys)
        mixed = mixed_ref[at, :].astype(F32)
        dq, dk, dv = ball_backward(stacked, keys, values, exponent, inverse, mixed, mg_ref[at, :])
        grads_ref[at, :half] = dq
        add_listed(dk_ref, listed, dk)
        add_listed(dv_ref, listed, dv)
    grads_ref[:, half:] = key_value_grads(dk_ref, dv_ref)
    send_ref[...] = weight_part(1 - slot_bit(core), normed, grads_ref[...], mixed_ref[...], hg_ref)


def first_weights(normed, grads, mixed, hidden_grad, columns, keep_ref, part_keep, part_send):
    core = lax.axis_index("pts")
    local = part_keep.shape[0]
    part_send[...] = dot(grads[local:], columns[...], ((1,), (1,))).astype(BF)
    part_keep[...] = dot(grads[:local], columns[...], ((1,), (1,)))
    keep_ref[...] = weight_part(slot_bit(core), normed, grads[...], mixed[...], hidden_grad)


def finish_rows(
    part_mine, part_other, x_mine, gain, hidden_grad, moved, mixed, mixed_other, out_two, points_grad, result
):
    local = x_mine.shape[0]
    normed_grad = part_mine[...] + part_other[...].astype(F32)
    points_grad[...] = norm_backward(
        normed_grad, x_mine[...].astype(F32), gain_row(gain), hidden_grad[:local]
    )
    both = jnp.concatenate([mixed[:local], mixed_other[...]], axis=1)
    result[...] = (moved[:local].astype(F32) + dot(both, out_two[...])).astype(BF)


def finish_weights(
    near_mine, far_mine, near_other, far_other, gain, weight, gain_grad, qkv_grad, out_grad, folded_ref
):
    core = lax.axis_index("pts")
    half = near_mine.shape[-1]
    for side, near, far in ((core, near_mine, far_mine), (1 - core, near_other, far_other)):
        bit = slot_bit(side)
        for part, ref in ((bit, near), (1 - bit, far)):
            at = part_of(part, half)
            folded = jnp.zeros((half, half), F32)
            for p in range(3):
                piece = ref[p * half : (p + 1) * half].astype(F32)
                columns = part_of(2 * p + side, half)
                qkv_grad[at, columns] = piece
                folded = folded + piece * weight[at, columns].astype(F32)
            folded_ref[side, at] = folded
            out_grad[part_of(side, half), at] = ref[3 * half :].astype(F32)
    folded = folded_ref[0] + folded_ref[1]
    gain_grad[...] = jnp.sum(folded.T, axis=0, keepdims=True) / gain_row(gain)


def shape(*dims, dtype=BF):
    return jax.ShapeDtypeStruct(dims, dtype)


def call(body, ins, outs, scratch=(), lists=()):
    return pl.pallas_call(
        body,
        name=body.__name__,
        out_shape=outs,
        in_specs=[SMEM] * len(lists) + [VMEM] * len(ins),
        out_specs=[VMEM] * len(outs),
        scratch_shapes=[pltpu.VMEM(item.shape, item.dtype) for item in scratch],
        compiler_params=PARAMS,
    )(*lists, *ins)


def add(a, b):
    return (a.astype(F32) + b.astype(F32)).astype(BF)


def local(
    geo,
    points,
    result_grad,
    lists_one,
    lists_two,
    rotation,
    gain_one,
    qkv_one,
    out_one,
    gain_two,
    qkv_two,
    out_two,
):
    rows, width = points.shape[1:]
    half = width // 2
    total = 2 * rows
    balls = total // BALL
    thin, wide, triple = shape(total, half), shape(total, width), shape(total, 3 * half)
    blocks = shape(balls, half, BALL, dtype=F32)
    weights = shape(4 * half, half)

    def swap(array):
        return lax.ppermute(array, "pts", SWAP)

    def across(array, bits):
        pairs = [(core * geo + i, core * geo + (i ^ bit)) for core, bit in enumerate(bits) for i in range(geo)]
        return lax.ppermute(array, ("pts", "geo"), pairs)

    ups = [1 << i for i in range(2, geo.bit_length() - 1)]
    doublings = [(1, 2)] + list(zip(ups, ups[1:] + ups[:1]))

    def reduce(summed):
        for bits in doublings:
            summed = add(summed, across(summed, bits))
        far = across(summed, (2, 1))
        return [summed, far, swap(summed), swap(far)]

    x = points[0]
    grad = result_grad[0]
    rot = rotation.reshape(rows // BALL, BALL)
    x_other = swap(x)
    one = [lists_one, swap(lists_one)]
    grad_other = swap(grad)
    rot_other = swap(rot)
    two = [lists_two, swap(lists_two)]
    arguments = (x, grad, rot, gain_one, gain_two, qkv_one, qkv_two, out_one, out_two)
    own_rows = shape(rows, width)
    own_columns = shape(width, 3 * half)
    square = shape(width, width)
    x, grad, rot, near_gain, far_gain, columns_one, columns_two, out_one, out_two, *projected = pl.pallas_call(
        project_mine,
        name="project_mine",
        out_shape=[own_rows, own_rows, shape(*rot.shape, dtype=rot.dtype), gain_one, gain_two]
        + [own_columns, own_columns, square, square, own_rows, shape(rows, half), own_rows],
        in_specs=[HBM] * 9,
        out_specs=[VMEM] * 12,
        scratch_shapes=[pltpu.SemaphoreType.DMA((15,))],
        compiler_params=PARAMS,
    )(*[pltpu.with_memory_space_constraint(a, pltpu.HBM) for a in arguments])
    mixed, q, kv, normed = call(
        first_forward, [x_other, near_gain, columns_one, *projected], [thin, thin, wide, wide], lists=one
    )
    mixed_other = swap(mixed)
    base, chosen, grads_in, mg = call(
        before_second,
        [rot, rot_other, x, x_other, mixed, grad, grad_other, out_one, out_two],
        [shape(total, width, dtype=F32), shape(total, total), wide, thin],
    )
    moved, normed_two, mixed_two, mixed_send, grads_two, part_two = call(
        second_layer,
        [base, mixed_other, chosen, mg, out_one, far_gain, columns_two],
        [wide, wide, thin, shape(rows, half), triple, wide],
        [wide, thin, wide, blocks, blocks],
        two,
    )
    part_two_other = swap(part_two)
    mixed_two_other = swap(mixed_send)
    keep_two, send_two = call(second_weights, [normed_two, grads_two, mixed_two, grads_in], [weights, weights])
    summed_two = add(keep_two, across(send_two, (2, 1)))
    hidden_grad, grads_one, send = call(
        first_backward,
        [rot, rot_other, part_two, part_two_other, moved, grads_in, far_gain, mixed, normed, q, kv, out_one],
        [wide, triple, weights],
        [wide, thin, blocks, blocks],
        one,
    )
    received = across(send, (2, 1))
    keep, part_keep, part_send = call(
        first_weights,
        [normed, grads_one, mixed, hidden_grad, columns_one],
        [weights, shape(rows, width, dtype=F32), shape(rows, width)],
    )
    points_grad, result = call(
        finish_rows,
        [part_keep, swap(part_send), x, near_gain, hidden_grad, moved, mixed_two, mixed_two_other, out_two],
        [shape(rows, width)] * 2,
    )
    summed = add(keep, received)
    summed, points_grad, result = lax.optimization_barrier((summed, points_grad, result))
    pieces_two = reduce(summed_two)
    pieces_one = reduce(summed)
    grads = []
    for pieces, gain, weight in ((pieces_one, near_gain, qkv_one), (pieces_two, far_gain, qkv_two)):
        found = call(
            finish_weights,
            pieces + [gain, weight],
            [shape(*dims, dtype=F32) for dims in ((1, width), (width, 3 * width), (width, width))],
            [shape(2, width, half, dtype=F32)],
        )
        grads += [found[0].reshape(width), found[1], found[2]]
    return (result[None], points_grad[None], *grads)


def solution(mesh):
    rows = P("geo", "pts", None)
    placed = (rows,) * 4 + (P("geo", "pts"),) + (P(),) * 6
    return jax.shard_map(
        functools.partial(local, mesh.shape["geo"]),
        mesh=mesh,
        in_specs=placed,
        out_specs=(rows, rows) + (P(),) * 6,
        check_vma=False,
    )
```

time: 68.2 us -> 63.6 us (0.933); the launches traced: 67.9 us -> 62.4 us
  local copies, waits for them, and re-layouts: 3.39 us -> 0.7 us
  starting transfers between devices: 25.6 us -> 23.9 us
  Pallas kernels: 28.3 us -> 27.1 us
    unnamed x24 -> x10, local copies, waits for them, and re-layouts: 2.51 us -> 0.7 us
    ppermute x12 -> x10, starting transfers between devices: 22.6 us -> 21 us  [across(): return lax.ppermute(array, ('pts', 'geo'), pairs)]
    pallas_call x6 -> x10, Pallas kernels: 28.3 us -> 27.1 us  [the longest x9 25.6 us: call(): pl.pallas_call(body, name=body.__name__, out_shape=outs, in_specs=[SMEM]...]
    reshape x4 -> x0, local copies, waits for them, and re-layouts: 0.85 us -> none  [the longest x2 0.84 us: local(): lists = jnp.concatenate([lists_one.reshape(-1), lists_two.reshape(-1)])]
    ppermute x12 -> x10, waiting for transfers between devices: 8.07 us -> 8.55 us  [across(): return lax.ppermute(array, ('pts', 'geo'), pairs)]
    ppermute x12 -> x13, waiting for transfers between devices: 1.43 us -> 1.1 us  [swap(): return lax.ppermute(array, 'pts', SWAP)]
    ppermute x12 -> x13, starting transfers between devices: 3 us -> 2.85 us  [swap(): return lax.ppermute(array, 'pts', SWAP)]
  transfers between devices with their start and end apart: 24 -> 23, of which waited for: 8 -> 8; matrix products, arithmetic and copies ran while one was open for 2% -> 0% of each run, Pallas kernels for 25% -> 28%
where the time goes in v3:
time: 63.6 us; the launch traced here: 62.4 us
  Pallas kernels  27.1 us (43%)
  starting transfers between devices  23.9 us (38%)
  waiting for transfers between devices  9.65 us (15%)
  between operations  0.82 us (1%)
  local copies, waits for them, and re-layouts  0.7 us (1%)
    pallas_call x9, Pallas kernels, call(): pl.pallas_call(body, name=body.__name__, out_shape=outs, in_specs=[SMEM]...  25.6 us
    ppermute x10, starting transfers between devices, across(): return lax.ppermute(array, ('pts', 'geo'), pairs)  21 us
    ppermute x10, waiting for transfers between devices, across(): return lax.ppermute(array, ('pts', 'geo'), pairs)  8.55 us
    ppermute x13, starting transfers between devices, swap(): return lax.ppermute(array, 'pts', SWAP)  2.85 us
    pallas_call x1, Pallas kernels, local(): pl.pallas_call(project_mine, name='project_mine', out_shape=[own_rows, ow...  1.52 us
  transfers between devices with their start and end apart: 23, of which 8 were waited for; matrix products, arithmetic and copies ran while one was open for 0% of the time, Pallas kernels for 28%

profile of v3, /device:TPU:0, one launch (start us, length us, event | category | flops | bytes accessed | tf_op | source)
XLA Modules:
  0.0 62.4 jit_solution(11292152617633865890)
XLA Ops:
  0.7 0.5 collective-permute-start.1
  1.3 0.4 collective-permute-start.4
  1.7 1.5 %project_mine.1 = (bf16[512,256]{1,0:T(8,128)(2,1)S(1)}, bf16[512,256]{1,0:T(8,128)(2,1)S(1)}, s32[4,128]{1,0:T(4,128)S(1)}, bf16[256]{0:T(256)(128)(2,1)S(1)}, ...) custom-call(bf16[512,256]{1,0:T(8,128)(2,1)} %bitcast.8, ...), custom_call_target="tpu_custom_call" | custom-call | tf_op jit(solution)/shard_map/project_mine/pallas_call | solution.py:398
  3.2 0.7 %copy-done.2 = s32[1,4,4]{2,1,0:T(4,128)S(1)} copy-done((s32[1,4,4]{2,1,0:T(4,128)S(1)}, s32[1,4,4]{2,1,0:T(4,128)}, u32[]{:S(2)}) %copy-start.2) | copy-done | bytes 88
  3.9 3.6 %first_forward.1 = (bf16[1024,128]{1,0:T(8,128)(2,1)S(1)}, bf16[1024,128]{1,0:T(8,128)(2,1)S(1)}, bf16[1024,256]{1,0:T(8,128)(2,1)S(1)}, bf16[1024,256]{1,0:T(8,128)(2,1)S(1)}) custom-call(s32[1,4,4]{2,1,0:T(4,128)S(1)} %copy-done.2, s32[1,4,4]{2,1,0:T(4,128)S(1)} %collective-permute-done.other, bf16[512,256]{1,0:T(8,128)(2,1)S(1)} %collective-permute-done.1.x_other, ...), custom_call_target="tpu_custom_call" | custom-call | tf_op jit(solution)/shard_map/first_forward/pallas_call | solution.py:333
  7.7 0.4 collective-permute-start.2
  8.2 0.9 %collective-permute-done.2.rot_other = s32[4,128]{1,0:T(4,128)S(1)} collective-permute-done((s32[4,128]{1,0:T(4,128)S(1)}, s32[4,128]{1,0:T(4,128)S(1)}, u32[]{:S(2)}, u32[]{:S(2)}) %collective-permute-start.2) | collective-permute-done | bytes 2080 | tf_op jit(solution)/shard_map/ppermute | solution.py:371
  9.1 0.6 %before_second.1 = (f32[1024,256]{1,0:T(8,128)S(1)}, bf16[1024,1024]{1,0:T(8,128)(2,1)S(1)}, bf16[1024,256]{1,0:T(8,128)(2,1)S(1)}, bf16[1024,128]{1,0:T(8,128)(2,1)S(1)}) custom-call(s32[4,128]{1,0:T(4,128)S(1)} %get-tuple-element.59.rot_mine, s32[4,128]{1,0:T(4,128)S(1)} %collective-permute-done.2.rot_other, ...), custom_call_target="tpu_custom_call" | custom-call | tf_op jit(solution)/shard_map/before_second/pallas_call | solution.py:333
  9.8 8.6 %second_layer.1 = (bf16[1024,256]{1,0:T(8,128)(2,1)S(1)}, bf16[1024,256]{1,0:T(8,128)(2,1)S(1)}, bf16[1024,128]{1,0:T(8,128)(2,1)S(1)}, bf16[512,128]{1,0:T(8,12...) custom-call(s32[1,4,4]{2,1,0:T(4,128)S(1)} %copy-done.3, ...), custom_call_target="tpu_custom_call" | custom-call | tf_op jit(solution)/shard_map/second_layer/pallas_call | solution.py:333
  18.6 0.6 %second_weights.1 = (bf16[512,128]{1,0:T(8,128)(2,1)S(1)}, bf16[512,128]{1,0:T(8,128)(2,1)S(1)}) custom-call(bf16[1024,256]{1,0:T(8,128)(2,1)S(1)} %get-tuple-element.91.normed, bf16[1024,384]{1,0:T(8,128)(2,1)S(1)} %get-tuple-element.92.grads, bf16[1024,128]{1,0:T(8,128)(2,1)S(1)} %get-tuple-element.81.mixed, bf16[1024,256]{1,0:T(8,128)(2,1)S(1)} %get-tuple-element.72.grad), custom_call_target="tpu_custom_call" | custom-call | tf_op jit(solution)/shard_map/second_weights/pallas_call | solution.py:333
  19.2 3.0 %collective-permute-start.16 = (bf16[512,128]{1,0:T(8,128)(2,1)S(1)}, bf16[512,128]{1,0:T(8,128)(2,1)S(1)}, u32[]{:S(2)}, u32[]{:S(2)}) collective-permute-start(bf16[512,128]{1,0:T(8,128)(2,1)S(1)} %get-tuple-element.94), channel_id=1, source_target_pairs={{0,2},{1,3},{2,0},{3,1},{4,6},{5,7},{6,4},{7,5},{8,10},{9,11},{10,... | collective-permute-start | bytes 393224 | tf_op jit(solution)/shard_map/ppermute | solution.py:375
  22.2 7.9 %first_backward.1 = (bf16[1024,256]{1,0:T(8,128)(2,1)S(1)}, bf16[1024,384]{1,0:T(8,128)(2,1)S(1)}, bf16[512,128]{1,0:T(8,128)(2,1)S(1)}) custom-call(s32[1,4,4]{2,1,0:T(4,128)S(1)} %copy-done.2, s32[1,4,4]{2,1,0:T(4,128)S(1)} %collective-permute-done.other, s32[4,128]{1,0:T(4,128)S(1)} %get-tuple-element.59.rot_mine, ...), custom_call_target="tpu_custom_call" | custom-call | tf_op jit(solution)/shard_map/first_backward/pallas_call | solution.py:333
  30.1 1.4 %collective-permute-start.7 = (bf16[512,128]{1,0:T(8,128)(2,1)S(1)}, bf16[512,128]{1,0:T(8,128)(2,1)S(1)}, u32[]{:S(2)}, u32[]{:S(2)}) collective-permute-start(bf16[512,128]{1,0:T(8,128)(2,1)S(1)} %get-tuple-element.78), channel_id=1, source_target_pairs={{0,2},{1,3},{2,0},{3,1},{4,6},{5,7},{6,4},{7,5},{8,10},{9,11},{10,... | collective-permute-start | bytes 393224 | tf_op jit(solution)/shard_map/ppermute | solution.py:375
  31.5 0.7 %first_weights.1 = (bf16[512,128]{1,0:T(8,128)(2,1)S(1)}, f32[512,256]{1,0:T(8,128)S(1)}, bf16[512,256]{1,0:T(8,128)(2,1)S(1)}) custom-call(bf16[1024,256]{1,0:T(8,128)(2,1)S(1)} %get-tuple-element.58.normed, bf16[1024,384]{1,0:T(8,128)(2,1)S(1)} %get-tuple-element.75.grads, bf16[1024,128]{1,0:T(8,128)(2,1)S(1)} %get-tuple-element.61.mixed.mixed_ref, ...), custom_call_target="tpu_custom_call" | custom-call | tf_op jit(solution)/shard_map/first_weights/pallas_call | solution.py:333
  32.2 0.4 collective-permute-start.8
  32.7 0.7 %collective-permute-start.17 = (bf16[512,128]{1,0:T(8,128)(2,1)S(1)}, bf16[512,128]{1,0:T(8,128)(2,1)S(1)}, u32[]{:S(2)}, u32[]{:S(2)}) collective-permute-start(bf16[512,128]{1,0:T(8,128)(2,1)S(1)} %add_convert_fusion.3), channel_id=1, source_target_pairs={{0,1},{1,0},{2,3},{3,2},{4,5},{5,4},{6,7},{7,6},{8,9},{9,8},{10,11... | collective-permute-start | bytes 393224 | tf_op jit(solution)/shard_map/ppermute | solution.py:375
  33.4 1.8 %collective-permute-done.7 = bf16[512,128]{1,0:T(8,128)(2,1)S(1)} collective-permute-done((bf16[512,128]{1,0:T(8,128)(2,1)S(1)}, bf16[512,128]{1,0:T(8,128)(2,1)S(1)}, u32[]{:S(2)}, u32[]{:S(2)}) %collective-permute-start.7) | collective-permute-done | bytes 131104 | tf_op jit(solution)/shard_map/ppermute | solution.py:375
  35.2 1.2 %finish_rows.1 = (bf16[512,256]{1,0:T(8,128)(2,1)}, bf16[512,256]{1,0:T(8,128)(2,1)}) custom-call(f32[512,256]{1,0:T(8,128)S(1)} %get-tuple-element.79.part_mine, bf16[512,256]{1,0:T(8,128)(2,1)S(1)} %collective-permute-done.8.part_other, bf16[512,256]{1,0:T(8,128)(2,1)S(1)} %get-tuple-element.60.x_mine, bf16[256]{0:T(256)(128)(2,1)S(1)} %get-tuple-element.53.gain, ...), custom_call_target="tpu_custom_call" | custom-call | tf_op jit(solution)/shard_map/finish_rows/pallas_call | solution.py:333
  36.4 1.6 %collective-permute-start.10 = (bf16[512,128]{1,0:T(8,128)(2,1)S(1)}, bf16[512,128]{1,0:T(8,128)(2,1)S(1)}, u32[]{:S(2)}, u32[]{:S(2)}) collective-permute-start(bf16[512,128]{1,0:T(8,128)(2,1)S(1)} %add_convert_fusion.7), channel_id=1, source_target_pairs={{0,1},{1,0},{2,3},{3,2},{4,5},{5,4},{6,7},{7,6},{8,9},{9,8},{10,11... | collective-permute-start | bytes 393224 | tf_op jit(solution)/shard_map/ppermute | solution.py:375
  38.1 1.6 %collective-permute-start.18 = (bf16[512,128]{1,0:T(8,128)(2,1)S(1)}, bf16[512,128]{1,0:T(8,128)(2,1)S(1)}, u32[]{:S(2)}, u32[]{:S(2)}) collective-permute-start(bf16[512,128]{1,0:T(8,128)(2,1)S(1)} %add_convert_fusion.2), channel_id=1, source_target_pairs={{0,4},{1,5},{2,6},{3,7},{4,0},{5,1},{6,2},{7,3},{8,12},{9,13},{10,... | collective-permute-start | bytes 393224 | tf_op jit(solution)/shard_map/ppermute | solution.py:375
  39.7 1.6 %collective-permute-done.10 = bf16[512,128]{1,0:T(8,128)(2,1)S(1)} collective-permute-done((bf16[512,128]{1,0:T(8,128)(2,1)S(1)}, bf16[512,128]{1,0:T(8,128)(2,1)S(1)}, u32[]{:S(2)}, u32[]{:S(2)}) %collective-permute-start.10) | collective-permute-done | bytes 131104 | tf_op jit(solution)/shard_map/ppermute | solution.py:375
  41.4 1.6 %collective-permute-start.11 = (bf16[512,128]{1,0:T(8,128)(2,1)S(1)}, bf16[512,128]{1,0:T(8,128)(2,1)S(1)}, u32[]{:S(2)}, u32[]{:S(2)}) collective-permute-start(bf16[512,128]{1,0:T(8,128)(2,1)S(1)} %add_convert_fusion.6), channel_id=1, source_target_pairs={{0,4},{1,5},{2,6},{3,7},{4,0},{5,1},{6,2},{7,3},{8,12},{9,13},{10,... | collective-permute-start | bytes 393224 | tf_op jit(solution)/shard_map/ppermute | solution.py:375
  43.2 3.1 %collective-permute-start.19 = (bf16[512,128]{1,0:T(8,128)(2,1)S(1)}, bf16[512,128]{1,0:T(8,128)(2,1)S(1)}, u32[]{:S(2)}, u32[]{:S(2)}) collective-permute-start(bf16[512,128]{1,0:T(8,128)(2,1)S(1)} %add_convert_fusion.1), channel_id=1, source_target_pairs={{0,8},{1,9},{2,10},{3,11},{4,12},{5,13},{6,14},{7,15},{8,0},{9,1},... | collective-permute-start | bytes 393224 | tf_op jit(solution)/shard_map/ppermute | solution.py:375
  46.3 1.2 %collective-permute-done.11 = bf16[512,128]{1,0:T(8,128)(2,1)S(1)} collective-permute-done((bf16[512,128]{1,0:T(8,128)(2,1)S(1)}, bf16[512,128]{1,0:T(8,128)(2,1)S(1)}, u32[]{:S(2)}, u32[]{:S(2)}) %collective-permute-start.11) | collective-permute-done | bytes 131104 | tf_op jit(solution)/shard_map/ppermute | solution.py:375
  47.5 3.2 %collective-permute-start.12 = (bf16[512,128]{1,0:T(8,128)(2,1)S(1)}, bf16[512,128]{1,0:T(8,128)(2,1)S(1)}, u32[]{:S(2)}, u32[]{:S(2)}) collective-permute-start(bf16[512,128]{1,0:T(8,128)(2,1)S(1)} %add_convert_fusion.5), channel_id=1, source_target_pairs={{0,8},{1,9},{2,10},{3,11},{4,12},{5,13},{6,14},{7,15},{8,0},{9,1},... | collective-permute-start | bytes 393224 | tf_op jit(solution)/shard_map/ppermute | solution.py:375
  50.8 1.5 %collective-permute-start.20 = (bf16[512,128]{1,0:T(8,128)(2,1)S(1)}, bf16[512,128]{1,0:T(8,128)(2,1)S(1)}, u32[]{:S(2)}, u32[]{:S(2)}) collective-permute-start(bf16[512,128]{1,0:T(8,128)(2,1)S(1)} %add_convert_fusion.near_mine), channel_id=1, source_target_pairs={{0,2},{1,3},{2,0},{3,1},{4,6},{5,7},{6,4},{7,5},{8,10},{9,11},{10,... | collective-permute-start | bytes 393224 | tf_op jit(solution)/shard_map/ppermute | solution.py:375
  52.2 1.4 %collective-permute-done.12 = bf16[512,128]{1,0:T(8,128)(2,1)S(1)} collective-permute-done((bf16[512,128]{1,0:T(8,128)(2,1)S(1)}, bf16[512,128]{1,0:T(8,128)(2,1)S(1)}, u32[]{:S(2)}, u32[]{:S(2)}) %collective-permute-start.12) | collective-permute-done | bytes 131104 | tf_op jit(solution)/shard_map/ppermute | solution.py:375
  53.7 3.3 %collective-permute-start.13 = (bf16[512,128]{1,0:T(8,128)(2,1)S(1)}, bf16[512,128]{1,0:T(8,128)(2,1)S(1)}, u32[]{:S(2)}, u32[]{:S(2)}) collective-permute-start(bf16[512,128]{1,0:T(8,128)(2,1)S(1)} %add_convert_fusion.4.near_mine), channel_id=1, source_target_pairs={{0,2},{1,3},{2,0},{3,1},{4,6},{5,7},{6,4},{7,5},{8,10},{9,11},{10,... | collective-permute-start | bytes 393224 | tf_op jit(solution)/shard_map/ppermute | solution.py:375
  57.0 0.5 collective-permute-start.22
  57.5 2.4 %collective-permute-done.13.far_mine = bf16[512,128]{1,0:T(8,128)(2,1)S(1)} collective-permute-done((bf16[512,128]{1,0:T(8,128)(2,1)S(1)}, bf16[512,128]{1,0:T(8,128)(2,1)S(1)}, u32[]{:S(2)}, u32[]{:S(2)}) %collective-permute-start.13) | collective-permute-done | bytes 131104 | tf_op jit(solution)/shard_map/ppermute | solution.py:375
  59.9 1.2 %finish_weights.3 = (f32[1,256]{1,0:T(1,128)}, f32[256,768]{1,0:T(8,128)}, f32[256,256]{1,0:T(8,128)}) custom-call(bf16[512,128]{1,0:T(8,128)(2,1)S(1)} %add_convert_fusion.near_mine, bf16[512,128]{1,0:T(8,128)(2,1)S(1)} %collective-permute-done.20.far_mine, bf16[512,128]{1,0:T(8,128)(2,1)S(1)} %collective-permute-done.21.near_other, ...), custom_call_target="tpu_custom_call" | custom-call | tf_op jit(solution)/shard_map/finish_weights/pallas_call | solution.py:333
  61.3 1.2 %finish_weights.2 = (f32[1,256]{1,0:T(1,128)}, f32[256,768]{1,0:T(8,128)}, f32[256,256]{1,0:T(8,128)}) custom-call(bf16[512,128]{1,0:T(8,128)(2,1)S(1)} %add_convert_fusion.4.near_mine, bf16[512,128]{1,0:T(8,128)(2,1)S(1)} %collective-permute-done.13.far_mine, bf16[512,128]{1,0:T(8,128)(2,1)S(1)} %collective-permute-done.14.near_other, ...), custom_call_target="tpu_custom_call" | custom-call | tf_op jit(solution)/shard_map/finish_weights/pallas_call | solution.py:333
  (42 shorter events, 1.1 us)
Async XLA Ops:
  0.6 7.0 %copy-start.4 = (s32[1,512]{1,0:T(1,128)S(1)}, s32[1,512]{1,0:T(1,128)}, u32[]{:S(2)}) copy-start(s32[1,512]{1,0:T(1,128)} %param.15) | copy-start | bytes 6148
  0.6 7.5 %copy-start.3 = (s32[1,4,4]{2,1,0:T(4,128)S(1)}, s32[1,4,4]{2,1,0:T(4,128)}, u32[]{:S(2)}) copy-start(s32[1,4,4]{2,1,0:T(4,128)} %mine.4) | copy-start | bytes 196
  0.7 2.6 %collective-permute-start.1 = (bf16[512,256]{1,0:T(8,128)(2,1)}, bf16[512,256]{1,0:T(8,128)(2,1)S(1)}, u32[]{:S(2)}, u32[]{:S(2)}) collective-permute-start(bf16[512,256]{1,0:T(8,128)(2,1)} %bitcast.7), channel_id=1, source_target_pairs={{0,16},{16,0},{1,17},{17,1},{2,18},{18,2},{3,19},{19,3},{4,20},{20... | collective-permute-start | bytes 786440 | tf_op jit(solution)/shard_map/ppermute | solution.py:371
  1.2 2.0 %collective-permute-start = (s32[1,4,4]{2,1,0:T(4,128)}, s32[1,4,4]{2,1,0:T(4,128)S(1)}, u32[]{:S(2)}, u32[]{:S(2)}) collective-permute-start(s32[1,4,4]{2,1,0:T(4,128)} %mine.5), channel_id=1, source_target_pairs={{0,16},{16,0},{1,17},{17,1},{2,18},{18,2},{3,19},{19,3},{4,20},{20... | collective-permute-start | bytes 200 | tf_op jit(solution)/shard_map/ppermute | solution.py:371
  1.3 7.9 %collective-permute-start.4 = (bf16[512,256]{1,0:T(8,128)(2,1)}, bf16[512,256]{1,0:T(8,128)(2,1)S(1)}, u32[]{:S(2)}, u32[]{:S(2)}) collective-permute-start(bf16[512,256]{1,0:T(8,128)(2,1)} %bitcast.9), channel_id=1, source_target_pairs={{0,16},{16,0},{1,17},{17,1},{2,18},{18,2},{3,19},{19,3},{4,20},{20... | collective-permute-start | bytes 786440 | tf_op jit(solution)/shard_map/ppermute | solution.py:371
  3.2 0.7 %copy-start.2 = (s32[1,4,4]{2,1,0:T(4,128)S(1)}, s32[1,4,4]{2,1,0:T(4,128)}, u32[]{:S(2)}) copy-start(s32[1,4,4]{2,1,0:T(4,128)} %mine.5) | copy-start | bytes 196
  7.5 2.3 %collective-permute-start.5 = (bf16[1024,128]{1,0:T(8,128)(2,1)S(1)}, bf16[1024,128]{1,0:T(8,128)(2,1)S(1)}, u32[]{:S(2)}, u32[]{:S(2)}) collective-permute-start(bf16[1024,128]{1,0:T(8,128)(2,1)S(1)} %get-tuple-element.61.mixed.mixed_ref), channel_id=1, source_target_pairs={{0,16},{16,0},{1,17},{17,1},{2,18},{18,2},{3,19},{19,3},{4,20},{20... | collective-permute-start | bytes 786440 | tf_op jit(solution)/shard_map/ppermute | solution.py:371
  7.7 1.4 %collective-permute-start.2 = (s32[4,128]{1,0:T(4,128)S(1)}, s32[4,128]{1,0:T(4,128)S(1)}, u32[]{:S(2)}, u32[]{:S(2)}) collective-permute-start(s32[4,128]{1,0:T(4,128)S(1)} %bitcast.12), channel_id=1, source_target_pairs={{0,16},{16,0},{1,17},{17,1},{2,18},{18,2},{3,19},{19,3},{4,20},{20... | collective-permute-start | bytes 6152 | tf_op jit(solution)/shard_map/ppermute | solution.py:371
  8.1 1.7 %collective-permute-start.3 = (s32[1,4,4]{2,1,0:T(4,128)S(1)}, s32[1,4,4]{2,1,0:T(4,128)S(1)}, u32[]{:S(2)}, u32[]{:S(2)}) collective-permute-start(s32[1,4,4]{2,1,0:T(4,128)S(1)} %copy-done.3), channel_id=1, source_target_pairs={{0,16},{16,0},{1,17},{17,1},{2,18},{18,2},{3,19},{19,3},{4,20},{20... | collective-permute-start | bytes 200 | tf_op jit(solution)/shard_map/ppermute | solution.py:371
  18.4 3.8 %collective-permute-start.6 = (bf16[1024,256]{1,0:T(8,128)(2,1)S(1)}, bf16[1024,256]{1,0:T(8,128)(2,1)S(1)}, u32[]{:S(2)}, u32[]{:S(2)}) collective-permute-start(bf16[1024,256]{1,0:T(8,128)(2,1)S(1)} %get-tuple-element.70.part_mine), channel_id=1, source_target_pairs={{0,16},{16,0},{1,17},{17,1},{2,18},{18,2},{3,19},{19,3},{4,20},{20... | collective-permute-start | bytes 1572872 | tf_op jit(solution)/shard_map/ppermute | solution.py:371
  19.2 13.4 %collective-permute-start.16 = (bf16[512,128]{1,0:T(8,128)(2,1)S(1)}, bf16[512,128]{1,0:T(8,128)(2,1)S(1)}, u32[]{:S(2)}, u32[]{:S(2)}) collective-permute-start(bf16[512,128]{1,0:T(8,128)(2,1)S(1)} %get-tuple-element.94), channel_id=1, source_target_pairs={{0,2},{1,3},{2,0},{3,1},{4,6},{5,7},{6,4},{7,5},{8,10},{9,11},{10,... | collective-permute-start | bytes 393224 | tf_op jit(solution)/shard_map/ppermute | solution.py:375
  22.2 13.0 %collective-permute-start.9 = (bf16[512,128]{1,0:T(8,128)(2,1)S(1)}, bf16[512,128]{1,0:T(8,128)(2,1)S(1)}, u32[]{:S(2)}, u32[]{:S(2)}) collective-permute-start(bf16[512,128]{1,0:T(8,128)(2,1)S(1)} %get-tuple-element.82), channel_id=1, source_target_pairs={{0,16},{16,0},{1,17},{17,1},{2,18},{18,2},{3,19},{19,3},{4,20},{20... | collective-permute-start | bytes 393224 | tf_op jit(solution)/shard_map/ppermute | solution.py:371
  30.1 5.0 %collective-permute-start.7 = (bf16[512,128]{1,0:T(8,128)(2,1)S(1)}, bf16[512,128]{1,0:T(8,128)(2,1)S(1)}, u32[]{:S(2)}, u32[]{:S(2)}) collective-permute-start(bf16[512,128]{1,0:T(8,128)(2,1)S(1)} %get-tuple-element.78), channel_id=1, source_target_pairs={{0,2},{1,3},{2,0},{3,1},{4,6},{5,7},{6,4},{7,5},{8,10},{9,11},{10,... | collective-permute-start | bytes 393224 | tf_op jit(solution)/shard_map/ppermute | solution.py:375
  32.2 3.0 %collective-permute-start.8 = (bf16[512,256]{1,0:T(8,128)(2,1)S(1)}, bf16[512,256]{1,0:T(8,128)(2,1)S(1)}, u32[]{:S(2)}, u32[]{:S(2)}) collective-permute-start(bf16[512,256]{1,0:T(8,128)(2,1)S(1)} %get-tuple-element.80), channel_id=1, source_target_pairs={{0,16},{16,0},{1,17},{17,1},{2,18},{18,2},{3,19},{19,3},{4,20},{20... | collective-permute-start | bytes 786440 | tf_op jit(solution)/shard_map/ppermute | solution.py:371
  32.7 5.4 %collective-permute-start.17 = (bf16[512,128]{1,0:T(8,128)(2,1)S(1)}, bf16[512,128]{1,0:T(8,128)(2,1)S(1)}, u32[]{:S(2)}, u32[]{:S(2)}) collective-permute-start(bf16[512,128]{1,0:T(8,128)(2,1)S(1)} %add_convert_fusion.3), channel_id=1, source_target_pairs={{0,1},{1,0},{2,3},{3,2},{4,5},{5,4},{6,7},{7,6},{8,9},{9,8},{10,11... | collective-permute-start | bytes 393224 | tf_op jit(solution)/shard_map/ppermute | solution.py:375
  35.2 24.7 %copy-start = (bf16[256,768]{1,0:T(8,128)(2,1)S(1)}, bf16[256,768]{1,0:T(8,128)(2,1)}, u32[]{:S(2)}) copy-start(bf16[256,768]{1,0:T(8,128)(2,1)} %weight.3) | copy-start | bytes 1179652
  36.4 24.9 %copy-start.1 = (bf16[256,768]{1,0:T(8,128)(2,1)S(1)}, bf16[256,768]{1,0:T(8,128)(2,1)}, u32[]{:S(2)}) copy-start(bf16[256,768]{1,0:T(8,128)(2,1)} %weight.2) | copy-start | bytes 1179652
  36.4 5.0 %collective-permute-start.10 = (bf16[512,128]{1,0:T(8,128)(2,1)S(1)}, bf16[512,128]{1,0:T(8,128)(2,1)S(1)}, u32[]{:S(2)}, u32[]{:S(2)}) collective-permute-start(bf16[512,128]{1,0:T(8,128)(2,1)S(1)} %add_convert_fusion.7), channel_id=1, source_target_pairs={{0,1},{1,0},{2,3},{3,2},{4,5},{5,4},{6,7},{7,6},{8,9},{9,8},{10,11... | collective-permute-start | bytes 393224 | tf_op jit(solution)/shard_map/ppermute | solution.py:375
  38.1 5.0 %collective-permute-start.18 = (bf16[512,128]{1,0:T(8,128)(2,1)S(1)}, bf16[512,128]{1,0:T(8,128)(2,1)S(1)}, u32[]{:S(2)}, u32[]{:S(2)}) collective-permute-start(bf16[512,128]{1,0:T(8,128)(2,1)S(1)} %add_convert_fusion.2), channel_id=1, source_target_pairs={{0,4},{1,5},{2,6},{3,7},{4,0},{5,1},{6,2},{7,3},{8,12},{9,13},{10,... | collective-permute-start | bytes 393224 | tf_op jit(solution)/shard_map/ppermute | solution.py:375
  41.4 6.1 %collective-permute-start.11 = (bf16[512,128]{1,0:T(8,128)(2,1)S(1)}, bf16[512,128]{1,0:T(8,128)(2,1)S(1)}, u32[]{:S(2)}, u32[]{:S(2)}) collective-permute-start(bf16[512,128]{1,0:T(8,128)(2,1)S(1)} %add_convert_fusion.6), channel_id=1, source_target_pairs={{0,4},{1,5},{2,6},{3,7},{4,0},{5,1},{6,2},{7,3},{8,12},{9,13},{10,... | collective-permute-start | bytes 393224 | tf_op jit(solution)/shard_map/ppermute | solution.py:375
  43.2 7.5 %collective-permute-start.19 = (bf16[512,128]{1,0:T(8,128)(2,1)S(1)}, bf16[512,128]{1,0:T(8,128)(2,1)S(1)}, u32[]{:S(2)}, u32[]{:S(2)}) collective-permute-start(bf16[512,128]{1,0:T(8,128)(2,1)S(1)} %add_convert_fusion.1), channel_id=1, source_target_pairs={{0,8},{1,9},{2,10},{3,11},{4,12},{5,13},{6,14},{7,15},{8,0},{9,1},... | collective-permute-start | bytes 393224 | tf_op jit(solution)/shard_map/ppermute | solution.py:375
  47.5 6.1 %collective-permute-start.12 = (bf16[512,128]{1,0:T(8,128)(2,1)S(1)}, bf16[512,128]{1,0:T(8,128)(2,1)S(1)}, u32[]{:S(2)}, u32[]{:S(2)}) collective-permute-start(bf16[512,128]{1,0:T(8,128)(2,1)S(1)} %add_convert_fusion.5), channel_id=1, source_target_pairs={{0,8},{1,9},{2,10},{3,11},{4,12},{5,13},{6,14},{7,15},{8,0},{9,1},... | collective-permute-start | bytes 393224 | tf_op jit(solution)/shard_map/ppermute | solution.py:375
  50.8 6.2 %collective-permute-start.20 = (bf16[512,128]{1,0:T(8,128)(2,1)S(1)}, bf16[512,128]{1,0:T(8,128)(2,1)S(1)}, u32[]{:S(2)}, u32[]{:S(2)}) collective-permute-start(bf16[512,128]{1,0:T(8,128)(2,1)S(1)} %add_convert_fusion.near_mine), channel_id=1, source_target_pairs={{0,2},{1,3},{2,0},{3,1},{4,6},{5,7},{6,4},{7,5},{8,10},{9,11},{10,... | collective-permute-start | bytes 393224 | tf_op jit(solution)/shard_map/ppermute | solution.py:375
  53.7 6.2 %collective-permute-start.13 = (bf16[512,128]{1,0:T(8,128)(2,1)S(1)}, bf16[512,128]{1,0:T(8,128)(2,1)S(1)}, u32[]{:S(2)}, u32[]{:S(2)}) collective-permute-start(bf16[512,128]{1,0:T(8,128)(2,1)S(1)} %add_convert_fusion.4.near_mine), channel_id=1, source_target_pairs={{0,2},{1,3},{2,0},{3,1},{4,6},{5,7},{6,4},{7,5},{8,10},{9,11},{10,... | collective-permute-start | bytes 393224 | tf_op jit(solution)/shard_map/ppermute | solution.py:375
  57.0 3.0 %collective-permute-start.21 = (bf16[512,128]{1,0:T(8,128)(2,1)S(1)}, bf16[512,128]{1,0:T(8,128)(2,1)S(1)}, u32[]{:S(2)}, u32[]{:S(2)}) collective-permute-start(bf16[512,128]{1,0:T(8,128)(2,1)S(1)} %add_convert_fusion.near_mine), channel_id=1, source_target_pairs={{0,16},{16,0},{1,17},{17,1},{2,18},{18,2},{3,19},{19,3},{4,20},{20... | collective-permute-start | bytes 393224 | tf_op jit(solution)/shard_map/ppermute | solution.py:371
  57.0 3.0 %collective-permute-start.22 = (bf16[512,128]{1,0:T(8,128)(2,1)S(1)}, bf16[512,128]{1,0:T(8,128)(2,1)S(1)}, u32[]{:S(2)}, u32[]{:S(2)}) collective-permute-start(bf16[512,128]{1,0:T(8,128)(2,1)S(1)} %collective-permute-done.20.far_mine), channel_id=1, source_target_pairs={{0,16},{16,0},{1,17},{17,1},{2,18},{18,2},{3,19},{19,3},{4,20},{20... | collective-permute-start | bytes 393224 | tf_op jit(solution)/shard_map/ppermute | solution.py:371
  57.5 3.6 %collective-permute-start.14 = (bf16[512,128]{1,0:T(8,128)(2,1)S(1)}, bf16[512,128]{1,0:T(8,128)(2,1)S(1)}, u32[]{:S(2)}, u32[]{:S(2)}) collective-permute-start(bf16[512,128]{1,0:T(8,128)(2,1)S(1)} %add_convert_fusion.4.near_mine), channel_id=1, source_target_pairs={{0,16},{16,0},{1,17},{17,1},{2,18},{18,2},{3,19},{19,3},{4,20},{20... | collective-permute-start | bytes 393224 | tf_op jit(solution)/shard_map/ppermute | solution.py:371
  59.9 1.3 %collective-permute-start.15 = (bf16[512,128]{1,0:T(8,128)(2,1)S(1)}, bf16[512,128]{1,0:T(8,128)(2,1)S(1)}, u32[]{:S(2)}, u32[]{:S(2)}) collective-permute-start(bf16[512,128]{1,0:T(8,128)(2,1)S(1)} %collective-permute-done.13.far_mine), channel_id=1, source_target_pairs={{0,16},{16,0},{1,17},{17,1},{2,18},{18,2},{3,19},{19,3},{4,20},{20... | collective-permute-start | bytes 393224 | tf_op jit(solution)/shard_map/ppermute | solution.py:371

commit v4 on v3

v4 whole, which is shorter than its diff:
```python
import functools

import jax
import jax.numpy as jnp
from jax import lax
from jax.experimental import pallas as pl
from jax.experimental.pallas import tpu as pltpu
from jax.sharding import PartitionSpec as P

HEADS = 4
BALL = 128
LISTED = 4
CHUNK = 256
QUARTERED = (True, True)
EPSILON = 1e-06
BF = jnp.bfloat16
F32 = jnp.float32
SWAP = ((0, 1), (1, 0))

VMEM = pl.BlockSpec(memory_space=pltpu.VMEM)
SMEM = pl.BlockSpec(memory_space=pltpu.SMEM)
HBM = pl.BlockSpec(memory_space=pltpu.HBM)
PARAMS = pltpu.CompilerParams(vmem_limit_bytes=40 * 1024 * 1024)


def dot(a, b, dims=((1,), (0,))):
    return lax.dot_general(a, b, (dims, ((), ())), preferred_element_type=F32)


def norm_factor(x):
    return lax.rsqrt(jnp.mean(x * x, axis=-1, keepdims=True) + EPSILON)


def part_of(place, size):
    return pl.ds(pl.multiple_of(place * size, size), size)


def gain_row(gain):
    return gain[...].astype(F32).reshape(1, gain.shape[0])


def project(normed, columns):
    qkv = dot(normed, columns)
    half = columns.shape[1] // 3
    scale = (2 * half // HEADS) ** (-0.5)
    return qkv[:, :half].astype(BF) * BF(scale), qkv[:, half:].astype(BF)


def stack_heads(rows):
    lane = lax.broadcasted_iota(jnp.int32, rows.shape, 1)
    first = lane < rows.shape[1] // 2
    zero = jnp.zeros_like(rows)
    return jnp.concatenate([jnp.where(first, rows, zero), jnp.where(first, zero, rows)], axis=0)


def unstack_heads(stacked):
    rows = stacked.shape[0] // 2
    lane = lax.broadcasted_iota(jnp.int32, (rows, stacked.shape[1]), 1)
    return jnp.where(lane < stacked.shape[1] // 2, stacked[:rows], stacked[rows:])


def listed_balls(ball, mine, other, core):
    local_balls = mine.shape[1]
    lists, row = (mine, ball) if ball < local_balls else (other, ball - local_balls)
    return [lax.rem(lists[0, row, j] + core * local_balls, 2 * local_balls) for j in range(LISTED)]


def pick(ref, listed, first, half):
    return jnp.concatenate([ref[part_of(i, BALL), first : first + half] for i in listed], axis=0)


def in_stages(count, *stages):
    held = {}
    for step in range(count + len(stages) - 1):
        for depth, stage in enumerate(stages):
            ball = step - depth
            if 0 <= ball < count:
                held[ball] = stage(ball, *held.pop(ball, ()))


def softmax_parts(scores):
    exponent = jnp.exp(scores - jnp.max(scores, axis=-1, keepdims=True))
    return exponent, 1.0 / jnp.sum(exponent, axis=-1, keepdims=True)


def backward_stages(lists, core, q_ref, kv_ref, mg_ref, mixed_ref, grads_ref, dk_ref, dv_ref, forward):
    half = q_ref.shape[1]
    scale = (half // 2) ** (-0.5)

    def products(ball):
        at = slice(ball * BALL, (ball + 1) * BALL)
        listed = listed_balls(ball, *lists, core)
        stacked, grad = stack_heads(q_ref[at, :]), stack_heads(mg_ref[at, :])
        scores = dot(stacked, pick(kv_ref, listed, 0, half), ((1,), (1,)))
        weights_grad = dot(grad, pick(kv_ref, listed, half, half), ((1,), (1,)))
        return listed, stacked, grad, scores, weights_grad

    def elements(ball, listed, stacked, grad, scores, weights_grad):
        exponent, inverse = softmax_parts(scores)
        attention = exponent * inverse
        if forward:
            inner = jnp.sum(attention * weights_grad, axis=-1, keepdims=True)
        else:
            mixed = mixed_ref[ball * BALL : (ball + 1) * BALL, :].astype(F32)
            inner = jnp.sum(grad.astype(F32) * jnp.concatenate([mixed, mixed], axis=0), axis=-1, keepdims=True)
        scores_grad = attention * (weights_grad - inner)
        return listed, stacked, grad, attention.astype(BF), scores_grad.astype(BF)

    def gradients(ball, listed, stacked, grad, attention, scores_grad):
        at = slice(ball * BALL, (ball + 1) * BALL)
        if forward:
            mixed_ref[at, :] = unstack_heads(dot(attention, pick(kv_ref, listed, half, half))).astype(BF)
        queries_grad = unstack_heads(dot(scores_grad, pick(kv_ref, listed, 0, half))) * scale
        grads_ref[at, :half] = queries_grad.astype(BF)
        add_listed(dk_ref, listed, dot(stacked, scores_grad, ((0,), (0,))))
        add_listed(dv_ref, listed, dot(grad, attention, ((0,), (0,))))
        return ()

    dk_ref[...] = jnp.zeros_like(dk_ref)
    dv_ref[...] = jnp.zeros_like(dv_ref)
    in_stages(q_ref.shape[0] // BALL, products, elements, gradients)


def add_listed(ref, listed, part):
    for j, i in enumerate(listed):
        ref[i] += part[:, j * BALL : (j + 1) * BALL]


def normed_grads(grads_ref, dk_ref, dv_ref, columns, store):
    half = dk_ref.shape[1]

    def turn(ball):
        at = slice(ball * BALL, (ball + 1) * BALL)
        grads_ref[at, half : 2 * half] = dk_ref[ball].T.astype(BF)
        grads_ref[at, 2 * half :] = dv_ref[ball].T.astype(BF)
        return ()

    def multiply(ball):
        at = slice(ball * BALL, (ball + 1) * BALL)
        store(at, dot(grads_ref[at, :], columns, ((1,), (1,))))
        return ()

    in_stages(dk_ref.shape[0], turn, multiply)


def geo_bit(bit):
    return lax.rem(lax.axis_index("geo") // bit, 2)


def kept(core, quartered):
    half = geo_bit(jnp.where(core == 0, 2, 1))
    return half, geo_bit(jnp.where(core == 0, 1, 2)) if quartered else 0


def store_quarters(ref, blocks, slot):
    size = ref.shape[1]
    ref[slot] = blocks[:size]
    ref[1 - slot] = blocks[size:]


def weight_part(part, normed_ref, grads, mixed, grad_out_ref):
    half = mixed.shape[1]
    weight = dot(normed_ref[:, part_of(part, half)], grads, ((0,), (0,)))
    out = dot(mixed, grad_out_ref[:, part_of(part, half)], ((0,), (0,)))
    blocks = [weight[:, i * half : (i + 1) * half] for i in range(3)] + [out]
    return jnp.concatenate(blocks, axis=0).astype(BF)


def norm_backward(normed_grad, x, gain, grad_out):
    factor = norm_factor(x)
    scaled = normed_grad.astype(BF).astype(F32) * gain
    inner = jnp.mean(scaled * x, axis=-1, keepdims=True)
    return (grad_out.astype(F32) + factor * scaled - x * (factor * factor * factor) * inner).astype(BF)


def norm_project(rows_count, rows_of, gain, columns, normed_ref, q_ref, kv_ref, first=0):
    def norm(chunk, x):
        return ((x * norm_factor(x) * gain).astype(BF),)

    def store(chunk, normed):
        at = slice(first + chunk * CHUNK, first + (chunk + 1) * CHUNK)
        normed_ref[at], (q_ref[at], kv_ref[at]) = normed, project(normed, columns)
        return ()

    in_stages(rows_count // CHUNK, lambda chunk: (rows_of(slice(chunk * CHUNK, (chunk + 1) * CHUNK)),), norm, store)


def project_mine(
    x_hbm, grad_hbm, rot_hbm, lists_one_hbm, lists_two_hbm, gain_one_hbm, gain_two_hbm, qkv_one_hbm, qkv_two_hbm, out_one_hbm, out_two_hbm,
    x, grad, rot, lists_one, lists_two, gain_one, gain_two, qkv_one, qkv_two, out_one, out_two,
    normed_ref, q_ref, kv_ref, sems,
):
    core = lax.axis_index("pts")
    half = x.shape[1] // 2
    copies = []

    def start(source, target):
        copies.append(pltpu.make_async_copy(source, target, sems.at[len(copies)]))
        copies[-1].start()

    def start_columns(source, target):
        for i in range(3):
            start(source.at[:, part_of(2 * i + core, half)], target.at[:, i * half : (i + 1) * half])

    start(x_hbm, x)
    start(gain_one_hbm, gain_one)
    start_columns(qkv_one_hbm, qkv_one)
    first = len(copies)
    start(grad_hbm, grad)
    start(rot_hbm, rot)
    start(lists_one_hbm, lists_one)
    start(lists_two_hbm, lists_two)
    start(gain_two_hbm, gain_two)
    start_columns(qkv_two_hbm, qkv_two)
    for source, target in ((out_one_hbm, out_one), (out_two_hbm, out_two)):
        start(source.at[part_of(core, half)], target.at[:half])
        start(source.at[part_of(1 - core, half)], target.at[half:])
    for copy in copies[:first]:
        copy.wait()
    norm_project(
        x.shape[0], lambda at: x[at].astype(F32), gain_row(gain_one), qkv_one[...], normed_ref, q_ref, kv_ref
    )
    for copy in copies[first:]:
        copy.wait()


def first_forward(
    mine, other, x_other, gain, columns, normed_mine, q_mine, kv_mine, mixed_ref, q_ref, kv_ref, normed_ref
):
    core = lax.axis_index("pts")
    local, width = x_other.shape
    half = width // 2
    normed_ref[:local], q_ref[:local], kv_ref[:local] = normed_mine[...], q_mine[...], kv_mine[...]
    norm_project(
        local, lambda at: x_other[at].astype(F32), gain_row(gain), columns[...], normed_ref, q_ref, kv_ref, local
    )

    def products(ball):
        listed = listed_balls(ball, mine, other, core)
        stacked = stack_heads(q_ref[ball * BALL : (ball + 1) * BALL, :])
        return listed, dot(stacked, pick(kv_ref, listed, 0, half), ((1,), (1,)))

    def elements(ball, listed, scores):
        exponent, inverse = softmax_parts(scores)
        return listed, exponent.astype(BF), inverse

    def outputs(ball, listed, exponent, inverse):
        mixed = unstack_heads(dot(exponent, pick(kv_ref, listed, half, half)) * inverse)
        mixed_ref[ball * BALL : (ball + 1) * BALL, :] = mixed.astype(BF)
        return ()

    in_stages(2 * local // BALL, products, elements, outputs)


def before_second(
    rot_mine, rot_other, x_mine, x_other, mixed, grad_mine, grad_other, out_one, out_two,
    base_ref, chosen_ref, chosen_back, grad_ref, mg_ref,
):
    core = lax.axis_index("pts")
    local, width = x_mine.shape
    half = width // 2
    total = 2 * local
    own = out_one[:half]
    base_ref[:local] = x_mine[...].astype(F32) + dot(mixed[:local], own)
    base_ref[local:] = x_other[...].astype(F32) + dot(mixed[local:], own)
    grad_ref[:local] = grad_mine[...]
    grad_ref[local:] = grad_other[...]
    mg_ref[...] = dot(grad_ref[...], out_two[:half], ((1,), (1,))).astype(BF)
    lane = lax.broadcasted_iota(jnp.int32, (BALL, total), 1)
    lane = lax.rem(lane + core * local, total).astype(F32)
    for side, ref in enumerate((rot_mine, rot_other)):
        for j in range(local // BALL):
            row = ref[j : j + 1, :].astype(F32)
            column = jnp.broadcast_to(row, (BALL, BALL)).T[:, :1]
            first = side * local + j * BALL
            chosen_ref[first : first + BALL, :] = (lane == column).astype(BF)
    row_of = [ref[j : j + 1, :] for ref in (rot_mine, rot_other) for j in range(local // BALL)]
    order = lax.rem(jnp.concatenate(row_of, axis=1) + core * local, total)
    place = lax.broadcasted_iota(jnp.int32, (BALL, total), 0)
    for first in range(0, total, BALL):
        chosen_back[first : first + BALL, :] = (place == order - first).astype(BF)


def second_layer(
    mine, other, base, mixed_other, chosen, mg_ref, out_one, gain, columns,
    moved_ref, normed_ref, mixed_ref, mixed_send, grads_ref, part_ref,
    hidden_ref, q_ref, kv_ref, dk_ref, dv_ref,
):
    core = lax.axis_index("pts")
    total, width = base.shape
    local = total // 2
    half = width // 2
    far = out_one[half:]
    for first in range(0, total, CHUNK):
        other_first = (first + local) % total
        added = dot(mixed_other[other_first : other_first + CHUNK], far)
        hidden_ref[first : first + CHUNK] = (base[first : first + CHUNK] + added).astype(BF)

    def rotate(at):
        moved = dot(chosen[at], hidden_ref[...])
        moved_ref[at] = moved.astype(BF)
        return moved

    norm_project(total, rotate, gain_row(gain), columns[...], normed_ref, q_ref, kv_ref)
    backward_stages((mine, other), core, q_ref, kv_ref, mg_ref, mixed_ref, grads_ref, dk_ref, dv_ref, True)

    def store(at, part):
        part_ref[at] = part.astype(BF)

    normed_grads(grads_ref, dk_ref, dv_ref, columns[...], store)
    mixed_send[...] = mixed_ref[local:]


def second_weights(normed, grads, mixed, grad, keep_ref, send_ref):
    part, slot = kept(lax.axis_index("pts"), QUARTERED[1])
    store_quarters(send_ref, weight_part(1 - part, normed, grads[...], mixed[...], grad), slot)
    store_quarters(keep_ref, weight_part(part, normed, grads[...], mixed[...], grad), slot)


def first_backward(
    mine, other, chosen_back, part_mine, part_other, moved, grad, gain_two,
    mixed_ref, normed, q_ref, kv_ref, out_one, columns,
    hg_ref, grads_ref, send_ref, part_keep, part_send,
    rows_grad_ref, mg_ref, dk_ref, dv_ref,
):
    core = lax.axis_index("pts")
    total, width = grad.shape
    local = total // 2
    half = width // 2
    gain = gain_row(gain_two)
    for first, far in ((0, local), (local, 0)):
        at = slice(first, first + local)
        normed_grad = part_mine[at].astype(F32) + part_other[far : far + local].astype(F32)
        rows_grad_ref[at] = norm_backward(normed_grad, moved[at].astype(F32), gain, grad[at])

    def rotate(chunk):
        return (dot(chosen_back[chunk * CHUNK : (chunk + 1) * CHUNK], rows_grad_ref[...]).astype(BF),)

    def project_back(chunk, hidden_grad):
        at = slice(chunk * CHUNK, (chunk + 1) * CHUNK)
        hg_ref[at] = hidden_grad
        mg_ref[at] = dot(hidden_grad, out_one[:half], ((1,), (1,))).astype(BF)
        return ()

    in_stages(total // CHUNK, rotate, project_back)
    backward_stages((mine, other), core, q_ref, kv_ref, mg_ref, mixed_ref, grads_ref, dk_ref, dv_ref, False)

    def store(at, part):
        if at.start < local:
            part_keep[at] = part
        else:
            part_send[at.start - local : at.stop - local] = part.astype(BF)

    normed_grads(grads_ref, dk_ref, dv_ref, columns[...], store)
    part, slot = kept(core, QUARTERED[0])
    store_quarters(send_ref, weight_part(1 - part, normed, grads_ref[...], mixed_ref[...], hg_ref), slot)


def finish_rows(
    normed, grads, mixed, hidden_grad, part_mine, part_other, x_mine, gain, moved, mixed_two, mixed_two_other, out_two,
    keep_ref, points_grad, result,
):
    local = x_mine.shape[0]
    part, slot = kept(lax.axis_index("pts"), QUARTERED[0])
    store_quarters(keep_ref, weight_part(part, normed, grads[...], mixed[...], hidden_grad), slot)
    normed_grad = part_mine[...] + part_other[...].astype(F32)
    points_grad[...] = norm_backward(
        normed_grad, x_mine[...].astype(F32), gain_row(gain), hidden_grad[:local]
    )
    both = jnp.concatenate([mixed_two[:local], mixed_two_other[...]], axis=1)
    result[...] = (moved[:local].astype(F32) + dot(both, out_two[...])).astype(BF)


def finish_weights(
    quartered, near_mine, far_mine, near_other, far_other, gain, weight, gain_grad, qkv_grad, out_grad, folded_ref
):
    core = lax.axis_index("pts")
    size, half = near_mine.shape[1:]
    for side, near, far in ((core, near_mine, far_mine), (1 - core, near_other, far_other)):
        bit, slot = kept(side, quartered)
        for part, ref in ((bit, near), (1 - bit, far)):

            def block(p):
                first = p * half
                quarter = slot if first < size else 1 - slot
                return ref[quarter, first % size : first % size + half].astype(F32)

            at = part_of(part, half)
            folded = jnp.zeros((half, half), F32)
            for p in range(3):
                columns = part_of(2 * p + side, half)
                qkv_grad[at, columns] = block(p)
                folded = folded + block(p) * weight[at, columns].astype(F32)
            folded_ref[side, at] = folded
            out_grad[part_of(side, half), at] = block(3)
    folded = folded_ref[0] + folded_ref[1]
    gain_grad[...] = jnp.sum(folded.T, axis=0, keepdims=True) / gain_row(gain)


def shape(*dims, dtype=BF):
    return jax.ShapeDtypeStruct(dims, dtype)


def call(body, ins, outs, scratch=(), lists=()):
    return pl.pallas_call(
        body,
        name=getattr(body, "func", body).__name__,
        out_shape=outs,
        in_specs=[SMEM] * len(lists) + [VMEM] * len(ins),
        out_specs=[VMEM] * len(outs),
        scratch_shapes=[pltpu.VMEM(item.shape, item.dtype) for item in scratch],
        compiler_params=PARAMS,
    )(*lists, *ins)


def add(a, b):
    return (a.astype(F32) + b.astype(F32)).astype(BF)


def local(
    geo,
    points,
    result_grad,
    lists_one,
    lists_two,
    rotation,
    gain_one,
    qkv_one,
    out_one,
    gain_two,
    qkv_two,
    out_two,
):
    rows, width = points.shape[1:]
    half = width // 2
    total = 2 * rows
    balls = total // BALL
    thin, wide, triple = shape(total, half), shape(total, width), shape(total, 3 * half)
    blocks = shape(balls, half, BALL, dtype=F32)
    weights = shape(2, width, half)

    def swap(array):
        return lax.ppermute(array, "pts", SWAP)

    def across(array, bits):
        pairs = [(core * geo + i, core * geo + (i ^ bit)) for core, bit in enumerate(bits) for i in range(geo)]
        return lax.ppermute(array, ("pts", "geo"), pairs)

    ups = [1 << i for i in range(2, geo.bit_length() - 1)]
    doublings = [(1, 2)] + list(zip(ups, ups[1:] + ups[:1]))

    x = points[0]
    grad = result_grad[0]
    rot = rotation.reshape(rows // BALL, BALL)
    others = [swap(a) for a in (x, lists_one, lists_two, rot, grad)]
    arguments = (x, grad, rot, lists_one, lists_two, gain_one, gain_two, qkv_one, qkv_two, out_one, out_two)
    own_rows = shape(rows, width)
    own_columns = shape(width, 3 * half)
    square = shape(width, width)
    x, grad, rot, *mine, near_gain, far_gain, columns_one, columns_two, out_one, out_two, normed, q, kv = pl.pallas_call(
        project_mine,
        name="project_mine",
        out_shape=[shape(*a.shape, dtype=a.dtype) for a in arguments[:7]]
        + [own_columns, own_columns, square, square, own_rows, shape(rows, half), own_rows],
        in_specs=[HBM] * len(arguments),
        out_specs=[VMEM] * 14,
        scratch_shapes=[pltpu.SemaphoreType.DMA((17,))],
        compiler_params=PARAMS,
    )(*[pltpu.with_memory_space_constraint(a, pltpu.HBM) for a in arguments])
    x_other, one_other, two_other, rot_other, grad_other = lax.optimization_barrier(others)
    one = [mine[0], one_other]
    two = [mine[1], two_other]
    mixed, q, kv, normed = call(
        first_forward, [x_other, near_gain, columns_one, normed, q, kv], [thin, thin, wide, wide], lists=one
    )
    mixed_other = swap(mixed)
    base, chosen, chosen_back, grads_in, mg = call(
        before_second,
        [rot, rot_other, x, x_other, mixed, grad, grad_other, out_one, out_two],
        [shape(total, width, dtype=F32), shape(total, total), shape(total, total), wide, thin],
    )
    moved, normed_two, mixed_two, mixed_send, grads_two, part_two = call(
        second_layer,
        [base, mixed_other, chosen, mg, out_one, far_gain, columns_two],
        [wide, wide, thin, shape(rows, half), triple, wide],
        [wide, thin, wide, blocks, blocks],
        two,
    )
    part_two_other = swap(part_two)
    mixed_two_other = swap(mixed_send)
    keep_two, send_two = call(second_weights, [normed_two, grads_two, mixed_two, grads_in], [weights, weights])
    summed_two = add(keep_two, across(send_two, (2, 1)))
    hidden_grad, grads_one, send, part_keep, part_send = call(
        first_backward,
        [chosen_back, part_two, part_two_other, moved, grads_in, far_gain, mixed, normed, q, kv, out_one, columns_one],
        [wide, triple, weights, shape(rows, width, dtype=F32), own_rows],
        [wide, thin, blocks, blocks],
        one,
    )
    part_other = swap(part_send)
    received = across(send, (2, 1))
    keep, points_grad, result = call(
        finish_rows,
        [normed, grads_one, mixed, hidden_grad, part_keep, part_other, x, near_gain]
        + [moved, mixed_two, mixed_two_other, out_two],
        [weights, own_rows, own_rows],
    )
    summed = add(keep, received)

    first, rest = doublings[0], doublings[1:]

    def second_step(array, quartered):
        return add(array[:1], across(array[1:], first)) if quartered else add(array, across(array, first))

    summed_two = second_step(summed_two, QUARTERED[1])
    summed = second_step(summed, QUARTERED[0])
    for bits in rest:
        summed_two = add(summed_two, across(summed_two, bits))
        summed = add(summed, across(summed, bits))

    def widen(array, quartered):
        return jnp.concatenate([array, across(array, first)], axis=0) if quartered else array

    summed_two = widen(summed_two, QUARTERED[1])
    summed = widen(summed, QUARTERED[0])
    far_two = across(summed_two, (2, 1))
    far = across(summed, (2, 1))
    tied_two, tied_far_two, _ = lax.optimization_barrier((summed_two, far_two, summed))
    pieces_two = [summed_two, far_two, swap(tied_two), swap(tied_far_two)]
    pieces_one = [summed, far, swap(summed), swap(far)]
    grads = []
    for quartered, pieces, gain, weight in (
        (QUARTERED[0], pieces_one, near_gain, qkv_one),
        (QUARTERED[1], pieces_two, far_gain, qkv_two),
    ):
        found = call(
            functools.partial(finish_weights, quartered),
            pieces + [gain, weight],
            [shape(*dims, dtype=F32) for dims in ((1, width), (width, 3 * width), (width, width))],
            [shape(2, width, half, dtype=F32)],
        )
        grads += [found[0].reshape(width), found[1], found[2]]
    return (result[None], points_grad[None], *grads)


def solution(mesh):
    rows = P("geo", "pts", None)
    placed = (rows,) * 4 + (P("geo", "pts"),) + (P(),) * 6
    return jax.shard_map(
        functools.partial(local, mesh.shape["geo"]),
        mesh=mesh,
        in_specs=placed,
        out_specs=(rows, rows) + (P(),) * 6,
        check_vma=False,
    )
```

time: 63.6 us -> 57.4 us (0.903); the launches traced: 62.4 us -> 57.3 us
  Pallas kernels: 27.1 us -> 23 us
  starting transfers between devices: 23.9 us -> 22.6 us
  waiting for transfers between devices: 9.65 us -> 10.7 us
  local copies, waits for them, and re-layouts: 0.7 us -> 0.02 us
    pallas_call x10 -> x9, Pallas kernels: 27.1 us -> 23 us  [the longest x8 21.4 us: call(): pl.pallas_call(body, name=getattr(body, 'func', body).__name__, out_shape...]
    ppermute x10 -> x12, waiting for transfers between devices: 8.55 us -> 10.4 us  [across(): return lax.ppermute(array, ('pts', 'geo'), pairs)]
    ppermute x10 -> x12, starting transfers between devices: 21 us -> 19.4 us  [across(): return lax.ppermute(array, ('pts', 'geo'), pairs)]
    ppermute x13, waiting for transfers between devices: 1.1 us -> 0.24 us  [swap(): return lax.ppermute(array, 'pts', SWAP)]
    unnamed x10 -> x4, local copies, waits for them, and re-layouts: 0.7 us -> 0.01 us
  transfers between devices with their start and end apart: 23 -> 25, of which waited for: 8 -> 10; matrix products, arithmetic and copies ran while one was open for 0% -> 0% of each run, Pallas kernels for 28% -> 22%
where the time goes in v4:
time: 57.4 us; the launch traced here: 57.3 us
  Pallas kernels  23 us (40%)
  starting transfers between devices  22.6 us (39%)
  waiting for transfers between devices  10.7 us (19%)
  between operations  0.81 us (1%)
    pallas_call x8, Pallas kernels, call(): pl.pallas_call(body, name=getattr(body, 'func', body).__name__, out_shape...  21.4 us
    ppermute x12, starting transfers between devices, across(): return lax.ppermute(array, ('pts', 'geo'), pairs)  19.4 us
    ppermute x12, waiting for transfers between devices, across(): return lax.ppermute(array, ('pts', 'geo'), pairs)  10.4 us
    ppermute x13, starting transfers between devices, swap(): return lax.ppermute(array, 'pts', SWAP)  3.2 us
    pallas_call x1, Pallas kernels, local(): pl.pallas_call(project_mine, name='project_mine', out_shape=[shape(*a.sha...  1.56 us
  transfers between devices with their start and end apart: 25, of which 10 were waited for; matrix products, arithmetic and copies ran while one was open for 0% of the time, Pallas kernels for 22%

profile of v4, /device:TPU:0, one launch (start us, length us, event | category | flops | bytes accessed | tf_op | source)
XLA Modules:
  0.0 57.3 jit_solution(12350593289134591135)
XLA Ops:
  0.6 0.5 collective-permute-start
  1.2 0.4 collective-permute-start.3
  2.2 1.6 %project_mine.1 = (bf16[512,256]{1,0:T(8,128)(2,1)S(1)}, bf16[512,256]{1,0:T(8,128)(2,1)S(1)}, s32[4,128]{1,0:T(4,128)S(1)}, s32[1,4,4]{2,1,0:T(4,128)S(1)}, s32...) custom-call(bf16[512,256]{1,0:T(8,128)(2,1)} %bitcast.8, ...), custom_call_target="tpu_custom_call" | custom-call | tf_op jit(solution)/shard_map/project_mine/pallas_call | solution.py:460
  3.8 2.5 %first_forward.1 = (bf16[1024,128]{1,0:T(8,128)(2,1)S(1)}, bf16[1024,128]{1,0:T(8,128)(2,1)S(1)}, bf16[1024,256]{1,0:T(8,128)(2,1)S(1)}, bf16[1024,256]{1,0:T(8,128)(2,1)S(1)}) custom-call(s32[1,4,4]{2,1,0:T(4,128)S(1)} %get-tuple-element.60.mine, s32[1,4,4]{2,1,0:T(4,128)S(1)} %collective-permute-done.1.other, ...), custom_call_target="tpu_custom_call" | custom-call | tf_op jit(solution)/shard_map/first_forward/pallas_call | solution.py:405
  6.4 1.4 %before_second.1 = (f32[1024,256]{1,0:T(8,128)S(1)}, bf16[1024,1024]{1,0:T(8,128)(2,1)S(1)}, bf16[1024,1024]{1,0:T(8,128)(2,1)S(1)}, bf16[1024,256]{1,0:T(8,128)(2,1)S(1)}, bf16[1024,128]{1,0:T(8,128)(2,1)S(1)}) custom-call(s32[4,128]{1,0:T(4,128)S(1)} %get-tuple-element.69.rot_mine, s32[4,128]{1,0:T(4,128)S(1)} %collective-permute-done.3.rot_other, ...), custom_call_target="tpu_custom_call" | custom-call | tf_op jit(solution)/shard_map/before_second/pallas_call | solution.py:405
  7.9 6.8 %second_layer.1 = (bf16[1024,256]{1,0:T(8,128)(2,1)S(1)}, bf16[1024,256]{1,0:T(8,128)(2,1)S(1)}, bf16[1024,128]{1,0:T(8,128)(2,1)S(1)}, bf16[512,128]{1,0:T(8,12...) custom-call(s32[1,4,4]{2,1,0:T(4,128)S(1)} %get-tuple-element.78.mine, ...), custom_call_target="tpu_custom_call" | custom-call | tf_op jit(solution)/shard_map/second_layer/pallas_call | solution.py:405
  15.1 0.7 %second_weights.1 = (bf16[2,256,128]{2,1,0:T(8,128)(2,1)S(1)}, bf16[2,256,128]{2,1,0:T(8,128)(2,1)S(1)}) custom-call(bf16[1024,256]{1,0:T(8,128)(2,1)S(1)} %get-tuple-element.103.normed, bf16[1024,384]{1,0:T(8,128)(2,1)S(1)} %get-tuple-element.104.grads, bf16[1024,128]{1,0:T(8,128)(2,1)S(1)} %get-tuple-element.94.mixed_two.mixed, ...), custom_call_target="tpu_custom_call" | custom-call | tf_op jit(solution)/shard_map/second_weights/pallas_call | solution.py:405
  15.8 2.7 %collective-permute-start.17 = (bf16[2,256,128]{2,1,0:T(8,128)(2,1)S(1)}, bf16[2,256,128]{2,1,0:T(8,128)(2,1)S(1)}, u32[]{:S(2)}, u32[]{:S(2)}) collective-permute-start(bf16[2,256,128]{2,1,0:T(8,128)(2,1)S(1)} %get-tuple-element.106), channel_id=1, source_target_pairs={{0,2},{1,3},{2,0},{3,1},{4,6},{5,7},{6,4},{7,5},{8,10},{9,11},{10,... | collective-permute-start | bytes 393224 | tf_op jit(solution)/shard_map/ppermute | solution.py:447
  18.5 6.3 %first_backward.1 = (bf16[1024,256]{1,0:T(8,128)(2,1)S(1)}, bf16[1024,384]{1,0:T(8,128)(2,1)S(1)}, bf16[2,256,128]{2,1,0:T(8,128)(2,1)S(1)}, f32[512,256]{1,0:T(8,128)S(1)}, bf16[512,256]{1,0:T(8,128)(2,1)S(1)}) custom-call(s32[1,4,4]{2,1,0:T(4,128)S(1)} %get-tuple-element.60.mine, s32[1,4,4]{2,1,0:T(4,128)S(1)} %collective-permute-done.1.other, ...), custom_call_target="tpu_custom_call" | custom-call | tf_op jit(solution)/shard_map/first_backward/pallas_call | solution.py:405
  25.0 0.5 collective-permute-start.8
  25.5 1.1 %collective-permute-start.9 = (bf16[2,256,128]{2,1,0:T(8,128)(2,1)S(1)}, bf16[2,256,128]{2,1,0:T(8,128)(2,1)S(1)}, u32[]{:S(2)}, u32[]{:S(2)}) collective-permute-start(bf16[2,256,128]{2,1,0:T(8,128)(2,1)S(1)} %get-tuple-element.99), channel_id=1, source_target_pairs={{0,2},{1,3},{2,0},{3,1},{4,6},{5,7},{6,4},{7,5},{8,10},{9,11},{10,... | collective-permute-start | bytes 393224 | tf_op jit(solution)/shard_map/ppermute | solution.py:447
  26.6 1.5 %collective-permute-start.18 = (bf16[1,256,128]{2,1,0:T(8,128)(2,1)S(1)}, bf16[1,256,128]{2,1,0:T(8,128)(2,1)S(1)}, u32[]{:S(2)}, u32[]{:S(2)}) collective-permute-start(bf16[1,256,128]{2,1,0:T(8,128)(2,1)S(1)} %slice.19), channel_id=1, source_target_pairs={{0,1},{1,0},{2,3},{3,2},{4,5},{5,4},{6,7},{7,6},{8,9},{9,8},{10,11... | collective-permute-start | bytes 196616 | tf_op jit(solution)/shard_map/ppermute | solution.py:447
  28.1 1.4 %finish_rows.1 = (bf16[2,256,128]{2,1,0:T(8,128)(2,1)S(1)}, bf16[512,256]{1,0:T(8,128)(2,1)}, bf16[512,256]{1,0:T(8,128)(2,1)}) custom-call(bf16[1024,256]{1,0:T(8,128)(2,1)S(1)} %get-tuple-element.68.normed, bf16[1024,384]{1,0:T(8,128)(2,1)S(1)} %get-tuple-element.90.grads, bf16[1024,128]{1,0:T(8,128)(2,1)S(1)} %get-tuple-element.72.mixed.mixed_ref, ...), custom_call_target="tpu_custom_call" | custom-call | tf_op jit(solution)/shard_map/finish_rows/pallas_call | solution.py:405
  29.5 1.6 %collective-permute-done.9 = bf16[2,256,128]{2,1,0:T(8,128)(2,1)S(1)} collective-permute-done((bf16[2,256,128]{2,1,0:T(8,128)(2,1)S(1)}, bf16[2,256,128]{2,1,0:T(8,128)(2,1)S(1)}, u32[]{:S(2)}, u32[]{:S(2)}) %collective-permute-start.9) | collective-permute-done | bytes 131104 | tf_op jit(solution)/shard_map/ppermute | solution.py:447
  31.2 1.0 %collective-permute-start.10 = (bf16[1,256,128]{2,1,0:T(8,128)(2,1)S(1)}, bf16[1,256,128]{2,1,0:T(8,128)(2,1)S(1)}, u32[]{:S(2)}, u32[]{:S(2)}) collective-permute-start(bf16[1,256,128]{2,1,0:T(8,128)(2,1)S(1)} %slice.17), channel_id=1, source_target_pairs={{0,1},{1,0},{2,3},{3,2},{4,5},{5,4},{6,7},{7,6},{8,9},{9,8},{10,11... | collective-permute-start | bytes 196616 | tf_op jit(solution)/shard_map/ppermute | solution.py:447
  32.3 1.6 %collective-permute-start.19 = (bf16[1,256,128]{2,1,0:T(8,128)(2,1)S(1)}, bf16[1,256,128]{2,1,0:T(8,128)(2,1)S(1)}, u32[]{:S(2)}, u32[]{:S(2)}) collective-permute-start(bf16[1,256,128]{2,1,0:T(8,128)(2,1)S(1)} %add_convert_fusion.4), channel_id=1, source_target_pairs={{0,4},{1,5},{2,6},{3,7},{4,0},{5,1},{6,2},{7,3},{8,12},{9,13},{10,... | collective-permute-start | bytes 196616 | tf_op jit(solution)/shard_map/ppermute | solution.py:447
  33.9 1.6 %collective-permute-done.10 = bf16[1,256,128]{2,1,0:T(8,128)(2,1)S(1)} collective-permute-done((bf16[1,256,128]{2,1,0:T(8,128)(2,1)S(1)}, bf16[1,256,128]{2,1,0:T(8,128)(2,1)S(1)}, u32[]{:S(2)}, u32[]{:S(2)}) %collective-permute-start.10) | collective-permute-done | bytes 65568 | tf_op jit(solution)/shard_map/ppermute | solution.py:447
  35.5 1.6 %collective-permute-start.11 = (bf16[1,256,128]{2,1,0:T(8,128)(2,1)S(1)}, bf16[1,256,128]{2,1,0:T(8,128)(2,1)S(1)}, u32[]{:S(2)}, u32[]{:S(2)}) collective-permute-start(bf16[1,256,128]{2,1,0:T(8,128)(2,1)S(1)} %add_convert_fusion.7), channel_id=1, source_target_pairs={{0,4},{1,5},{2,6},{3,7},{4,0},{5,1},{6,2},{7,3},{8,12},{9,13},{10,... | collective-permute-start | bytes 196616 | tf_op jit(solution)/shard_map/ppermute | solution.py:447
  37.2 2.7 %collective-permute-start.20 = (bf16[1,256,128]{2,1,0:T(8,128)(2,1)S(1)}, bf16[1,256,128]{2,1,0:T(8,128)(2,1)S(1)}, u32[]{:S(2)}, u32[]{:S(2)}) collective-permute-start(bf16[1,256,128]{2,1,0:T(8,128)(2,1)S(1)} %add_convert_fusion.3), channel_id=1, source_target_pairs={{0,8},{1,9},{2,10},{3,11},{4,12},{5,13},{6,14},{7,15},{8,0},{9,1},... | collective-permute-start | bytes 196616 | tf_op jit(solution)/shard_map/ppermute | solution.py:447
  39.9 2.6 %collective-permute-start.12 = (bf16[1,256,128]{2,1,0:T(8,128)(2,1)S(1)}, bf16[1,256,128]{2,1,0:T(8,128)(2,1)S(1)}, u32[]{:S(2)}, u32[]{:S(2)}) collective-permute-start(bf16[1,256,128]{2,1,0:T(8,128)(2,1)S(1)} %add_convert_fusion.6), channel_id=1, source_target_pairs={{0,8},{1,9},{2,10},{3,11},{4,12},{5,13},{6,14},{7,15},{8,0},{9,1},... | collective-permute-start | bytes 196616 | tf_op jit(solution)/shard_map/ppermute | solution.py:447
  42.7 1.3 %collective-permute-start.21 = (bf16[1,256,128]{2,1,0:T(8,128)(2,1)S(1)}, bf16[1,256,128]{2,1,0:T(8,128)(2,1)S(1)}, u32[]{:S(2)}, u32[]{:S(2)}) collective-permute-start(bf16[1,256,128]{2,1,0:T(8,128)(2,1)S(1)} %add_convert_fusion.2), channel_id=1, source_target_pairs={{0,1},{1,0},{2,3},{3,2},{4,5},{5,4},{6,7},{7,6},{8,9},{9,8},{10,11... | collective-permute-start | bytes 196616 | tf_op jit(solution)/shard_map/ppermute | solution.py:447
  44.1 1.1 %collective-permute-done.12 = bf16[1,256,128]{2,1,0:T(8,128)(2,1)S(1)} collective-permute-done((bf16[1,256,128]{2,1,0:T(8,128)(2,1)S(1)}, bf16[1,256,128]{2,1,0:T(8,128)(2,1)S(1)}, u32[]{:S(2)}, u32[]{:S(2)}) %collective-permute-start.12) | collective-permute-done | bytes 65568 | tf_op jit(solution)/shard_map/ppermute | solution.py:447
  45.2 1.0 %collective-permute-start.13 = (bf16[1,256,128]{2,1,0:T(8,128)(2,1)S(1)}, bf16[1,256,128]{2,1,0:T(8,128)(2,1)S(1)}, u32[]{:S(2)}, u32[]{:S(2)}) collective-permute-start(bf16[1,256,128]{2,1,0:T(8,128)(2,1)S(1)} %add_convert_fusion.5), channel_id=1, source_target_pairs={{0,1},{1,0},{2,3},{3,2},{4,5},{5,4},{6,7},{7,6},{8,9},{9,8},{10,11... | collective-permute-start | bytes 196616 | tf_op jit(solution)/shard_map/ppermute | solution.py:447
  46.2 1.5 %collective-permute-done.21 = bf16[1,256,128]{2,1,0:T(8,128)(2,1)S(1)} collective-permute-done((bf16[1,256,128]{2,1,0:T(8,128)(2,1)S(1)}, bf16[1,256,128]{2,1,0:T(8,128)(2,1)S(1)}, u32[]{:S(2)}, u32[]{:S(2)}) %collective-permute-start.21) | collective-permute-done | bytes 65568 | tf_op jit(solution)/shard_map/ppermute | solution.py:447
  47.8 1.1 %collective-permute-start.22 = (bf16[2,256,128]{2,1,0:T(8,128)(2,1)S(1)}, bf16[2,256,128]{2,1,0:T(8,128)(2,1)S(1)}, u32[]{:S(2)}, u32[]{:S(2)}) collective-permute-start(bf16[2,256,128]{2,1,0:T(8,128)(2,1)S(1)} %pad_maximum_fusion.1.near_mine), channel_id=1, source_target_pairs={{0,2},{1,3},{2,0},{3,1},{4,6},{5,7},{6,4},{7,5},{8,10},{9,11},{10,... | collective-permute-start | bytes 393224 | tf_op jit(solution)/shard_map/ppermute | solution.py:447
  48.8 0.9 %collective-permute-done.13 = bf16[1,256,128]{2,1,0:T(8,128)(2,1)S(1)} collective-permute-done((bf16[1,256,128]{2,1,0:T(8,128)(2,1)S(1)}, bf16[1,256,128]{2,1,0:T(8,128)(2,1)S(1)}, u32[]{:S(2)}, u32[]{:S(2)}) %collective-permute-start.13) | collective-permute-done | bytes 65568 | tf_op jit(solution)/shard_map/ppermute | solution.py:447
  49.7 1.0 %collective-permute-start.14 = (bf16[2,256,128]{2,1,0:T(8,128)(2,1)S(1)}, bf16[2,256,128]{2,1,0:T(8,128)(2,1)S(1)}, u32[]{:S(2)}, u32[]{:S(2)}) collective-permute-start(bf16[2,256,128]{2,1,0:T(8,128)(2,1)S(1)} %pad_maximum_fusion.near_mine), channel_id=1, source_target_pairs={{0,2},{1,3},{2,0},{3,1},{4,6},{5,7},{6,4},{7,5},{8,10},{9,11},{10,... | collective-permute-start | bytes 393224 | tf_op jit(solution)/shard_map/ppermute | solution.py:447
  50.7 2.0 %collective-permute-done.22.far_mine = bf16[2,256,128]{2,1,0:T(8,128)(2,1)S(1)} collective-permute-done((bf16[2,256,128]{2,1,0:T(8,128)(2,1)S(1)}, bf16[2,256,128]{2,1,0:T(8,128)(2,1)S(1)}, u32[]{:S(2)}, u32[]{:S(2)}) %collective-permute-start.22) | collective-permute-done | bytes 131104 | tf_op jit(solution)/shard_map/ppermute | solution.py:447
  52.8 0.5 collective-permute-start.24
  53.3 1.5 %collective-permute-done.14.far_mine = bf16[2,256,128]{2,1,0:T(8,128)(2,1)S(1)} collective-permute-done((bf16[2,256,128]{2,1,0:T(8,128)(2,1)S(1)}, bf16[2,256,128]{2,1,0:T(8,128)(2,1)S(1)}, u32[]{:S(2)}, u32[]{:S(2)}) %collective-permute-start.14) | collective-permute-done | bytes 131104 | tf_op jit(solution)/shard_map/ppermute | solution.py:447
  54.8 1.2 %finish_weights.3 = (f32[1,256]{1,0:T(1,128)}, f32[256,768]{1,0:T(8,128)}, f32[256,256]{1,0:T(8,128)}) custom-call(bf16[2,256,128]{2,1,0:T(8,128)(2,1)S(1)} %pad_maximum_fusion.1.near_mine, bf16[2,256,128]{2,1,0:T(8,128)(2,1)S(1)} %collective-permute-done.22.far_mine, bf16[2,256,128]{2,1,0:T(8,128)(2,1)S(1)} %collective-permute-done.23.near_other, ...), custom_call_target="tpu_custom_call" | custom-call | tf_op jit(solution)/shard_map/finish_weights/pallas_call | solution.py:405
  56.1 1.2 %finish_weights.2 = (f32[1,256]{1,0:T(1,128)}, f32[256,768]{1,0:T(8,128)}, f32[256,256]{1,0:T(8,128)}) custom-call(bf16[2,256,128]{2,1,0:T(8,128)(2,1)S(1)} %pad_maximum_fusion.near_mine, bf16[2,256,128]{2,1,0:T(8,128)(2,1)S(1)} %collective-permute-done.14.far_mine, bf16[2,256,128]{2,1,0:T(8,128)(2,1)S(1)} %collective-permute-done.15.near_other, ...), custom_call_target="tpu_custom_call" | custom-call | tf_op jit(solution)/shard_map/finish_weights/pallas_call | solution.py:405
  (43 shorter events, 1.9 us)
Async XLA Ops:
  0.6 3.1 %collective-permute-start = (bf16[512,256]{1,0:T(8,128)(2,1)}, bf16[512,256]{1,0:T(8,128)(2,1)S(1)}, u32[]{:S(2)}, u32[]{:S(2)}) collective-permute-start(bf16[512,256]{1,0:T(8,128)(2,1)} %bitcast.7), channel_id=1, source_target_pairs={{0,16},{16,0},{1,17},{17,1},{2,18},{18,2},{3,19},{19,3},{4,20},{20... | collective-permute-start | bytes 786440 | tf_op jit(solution)/shard_map/ppermute | solution.py:443
  1.2 2.6 %collective-permute-start.4 = (bf16[512,256]{1,0:T(8,128)(2,1)}, bf16[512,256]{1,0:T(8,128)(2,1)S(1)}, u32[]{:S(2)}, u32[]{:S(2)}) collective-permute-start(bf16[512,256]{1,0:T(8,128)(2,1)} %bitcast.9), channel_id=1, source_target_pairs={{0,16},{16,0},{1,17},{17,1},{2,18},{18,2},{3,19},{19,3},{4,20},{20... | collective-permute-start | bytes 786440 | tf_op jit(solution)/shard_map/ppermute | solution.py:443
  1.2 2.5 %collective-permute-start.3 = (s32[4,128]{1,0:T(4,128)}, s32[4,128]{1,0:T(4,128)S(1)}, u32[]{:S(2)}, u32[]{:S(2)}) collective-permute-start(s32[4,128]{1,0:T(4,128)} %bitcast.11), channel_id=1, source_target_pairs={{0,16},{16,0},{1,17},{17,1},{2,18},{18,2},{3,19},{19,3},{4,20},{20... | collective-permute-start | bytes 6152 | tf_op jit(solution)/shard_map/ppermute | solution.py:443
  1.7 2.1 %collective-permute-start.1 = (s32[1,4,4]{2,1,0:T(4,128)}, s32[1,4,4]{2,1,0:T(4,128)S(1)}, u32[]{:S(2)}, u32[]{:S(2)}) collective-permute-start(s32[1,4,4]{2,1,0:T(4,128)} %lists_one_hbm.1), channel_id=1, source_target_pairs={{0,16},{16,0},{1,17},{17,1},{2,18},{18,2},{3,19},{19,3},{4,20},{20... | collective-permute-start | bytes 200 | tf_op jit(solution)/shard_map/ppermute | solution.py:443
  1.7 2.0 %collective-permute-start.2 = (s32[1,4,4]{2,1,0:T(4,128)}, s32[1,4,4]{2,1,0:T(4,128)S(1)}, u32[]{:S(2)}, u32[]{:S(2)}) collective-permute-start(s32[1,4,4]{2,1,0:T(4,128)} %lists_two_hbm.1), channel_id=1, source_target_pairs={{0,16},{16,0},{1,17},{17,1},{2,18},{18,2},{3,19},{19,3},{4,20},{20... | collective-permute-start | bytes 200 | tf_op jit(solution)/shard_map/ppermute | solution.py:443
  6.3 1.6 %collective-permute-start.5 = (bf16[1024,128]{1,0:T(8,128)(2,1)S(1)}, bf16[1024,128]{1,0:T(8,128)(2,1)S(1)}, u32[]{:S(2)}, u32[]{:S(2)}) collective-permute-start(bf16[1024,128]{1,0:T(8,128)(2,1)S(1)} %get-tuple-element.72.mixed.mixed_ref), channel_id=1, source_target_pairs={{0,16},{16,0},{1,17},{17,1},{2,18},{18,2},{3,19},{19,3},{4,20},{20... | collective-permute-start | bytes 786440 | tf_op jit(solution)/shard_map/ppermute | solution.py:443
  14.7 3.8 %collective-permute-start.6 = (bf16[1024,256]{1,0:T(8,128)(2,1)S(1)}, bf16[1024,256]{1,0:T(8,128)(2,1)S(1)}, u32[]{:S(2)}, u32[]{:S(2)}) collective-permute-start(bf16[1024,256]{1,0:T(8,128)(2,1)S(1)} %get-tuple-element.85.part_mine), channel_id=1, source_target_pairs={{0,16},{16,0},{1,17},{17,1},{2,18},{18,2},{3,19},{19,3},{4,20},{20... | collective-permute-start | bytes 1572872 | tf_op jit(solution)/shard_map/ppermute | solution.py:443
  15.8 10.8 %collective-permute-start.17 = (bf16[2,256,128]{2,1,0:T(8,128)(2,1)S(1)}, bf16[2,256,128]{2,1,0:T(8,128)(2,1)S(1)}, u32[]{:S(2)}, u32[]{:S(2)}) collective-permute-start(bf16[2,256,128]{2,1,0:T(8,128)(2,1)S(1)} %get-tuple-element.106), channel_id=1, source_target_pairs={{0,2},{1,3},{2,0},{3,1},{4,6},{5,7},{6,4},{7,5},{8,10},{9,11},{10,... | collective-permute-start | bytes 393224 | tf_op jit(solution)/shard_map/ppermute | solution.py:447
  24.9 3.2 %collective-permute-start.7 = (bf16[512,256]{1,0:T(8,128)(2,1)S(1)}, bf16[512,256]{1,0:T(8,128)(2,1)S(1)}, u32[]{:S(2)}, u32[]{:S(2)}) collective-permute-start(bf16[512,256]{1,0:T(8,128)(2,1)S(1)} %get-tuple-element.93), channel_id=1, source_target_pairs={{0,16},{16,0},{1,17},{17,1},{2,18},{18,2},{3,19},{19,3},{4,20},{20... | collective-permute-start | bytes 786440 | tf_op jit(solution)/shard_map/ppermute | solution.py:443
  25.0 3.1 %collective-permute-start.8 = (bf16[512,128]{1,0:T(8,128)(2,1)S(1)}, bf16[512,128]{1,0:T(8,128)(2,1)S(1)}, u32[]{:S(2)}, u32[]{:S(2)}) collective-permute-start(bf16[512,128]{1,0:T(8,128)(2,1)S(1)} %get-tuple-element.95), channel_id=1, source_target_pairs={{0,16},{16,0},{1,17},{17,1},{2,18},{18,2},{3,19},{19,3},{4,20},{20... | collective-permute-start | bytes 393224 | tf_op jit(solution)/shard_map/ppermute | solution.py:443
  25.5 5.7 %collective-permute-start.9 = (bf16[2,256,128]{2,1,0:T(8,128)(2,1)S(1)}, bf16[2,256,128]{2,1,0:T(8,128)(2,1)S(1)}, u32[]{:S(2)}, u32[]{:S(2)}) collective-permute-start(bf16[2,256,128]{2,1,0:T(8,128)(2,1)S(1)} %get-tuple-element.99), channel_id=1, source_target_pairs={{0,2},{1,3},{2,0},{3,1},{4,6},{5,7},{6,4},{7,5},{8,10},{9,11},{10,... | collective-permute-start | bytes 393224 | tf_op jit(solution)/shard_map/ppermute | solution.py:447
  26.6 5.6 %collective-permute-start.18 = (bf16[1,256,128]{2,1,0:T(8,128)(2,1)S(1)}, bf16[1,256,128]{2,1,0:T(8,128)(2,1)S(1)}, u32[]{:S(2)}, u32[]{:S(2)}) collective-permute-start(bf16[1,256,128]{2,1,0:T(8,128)(2,1)S(1)} %slice.19), channel_id=1, source_target_pairs={{0,1},{1,0},{2,3},{3,2},{4,5},{5,4},{6,7},{7,6},{8,9},{9,8},{10,11... | collective-permute-start | bytes 196616 | tf_op jit(solution)/shard_map/ppermute | solution.py:447
  29.5 25.3 %copy-start = (bf16[256,768]{1,0:T(8,128)(2,1)S(1)}, bf16[256,768]{1,0:T(8,128)(2,1)}, u32[]{:S(2)}) copy-start(bf16[256,768]{1,0:T(8,128)(2,1)} %weight.3) | copy-start | bytes 1179652
  29.5 26.6 %copy-start.1 = (bf16[256,768]{1,0:T(8,128)(2,1)S(1)}, bf16[256,768]{1,0:T(8,128)(2,1)}, u32[]{:S(2)}) copy-start(bf16[256,768]{1,0:T(8,128)(2,1)} %weight.2) | copy-start | bytes 1179652
  31.2 4.3 %collective-permute-start.10 = (bf16[1,256,128]{2,1,0:T(8,128)(2,1)S(1)}, bf16[1,256,128]{2,1,0:T(8,128)(2,1)S(1)}, u32[]{:S(2)}, u32[]{:S(2)}) collective-permute-start(bf16[1,256,128]{2,1,0:T(8,128)(2,1)S(1)} %slice.17), channel_id=1, source_target_pairs={{0,1},{1,0},{2,3},{3,2},{4,5},{5,4},{6,7},{7,6},{8,9},{9,8},{10,11... | collective-permute-start | bytes 196616 | tf_op jit(solution)/shard_map/ppermute | solution.py:447
  32.3 4.9 %collective-permute-start.19 = (bf16[1,256,128]{2,1,0:T(8,128)(2,1)S(1)}, bf16[1,256,128]{2,1,0:T(8,128)(2,1)S(1)}, u32[]{:S(2)}, u32[]{:S(2)}) collective-permute-start(bf16[1,256,128]{2,1,0:T(8,128)(2,1)S(1)} %add_convert_fusion.4), channel_id=1, source_target_pairs={{0,4},{1,5},{2,6},{3,7},{4,0},{5,1},{6,2},{7,3},{8,12},{9,13},{10,... | collective-permute-start | bytes 196616 | tf_op jit(solution)/shard_map/ppermute | solution.py:447
  35.5 4.4 %collective-permute-start.11 = (bf16[1,256,128]{2,1,0:T(8,128)(2,1)S(1)}, bf16[1,256,128]{2,1,0:T(8,128)(2,1)S(1)}, u32[]{:S(2)}, u32[]{:S(2)}) collective-permute-start(bf16[1,256,128]{2,1,0:T(8,128)(2,1)S(1)} %add_convert_fusion.7), channel_id=1, source_target_pairs={{0,4},{1,5},{2,6},{3,7},{4,0},{5,1},{6,2},{7,3},{8,12},{9,13},{10,... | collective-permute-start | bytes 196616 | tf_op jit(solution)/shard_map/ppermute | solution.py:447
  37.2 5.5 %collective-permute-start.20 = (bf16[1,256,128]{2,1,0:T(8,128)(2,1)S(1)}, bf16[1,256,128]{2,1,0:T(8,128)(2,1)S(1)}, u32[]{:S(2)}, u32[]{:S(2)}) collective-permute-start(bf16[1,256,128]{2,1,0:T(8,128)(2,1)S(1)} %add_convert_fusion.3), channel_id=1, source_target_pairs={{0,8},{1,9},{2,10},{3,11},{4,12},{5,13},{6,14},{7,15},{8,0},{9,1},... | collective-permute-start | bytes 196616 | tf_op jit(solution)/shard_map/ppermute | solution.py:447
  39.9 5.2 %collective-permute-start.12 = (bf16[1,256,128]{2,1,0:T(8,128)(2,1)S(1)}, bf16[1,256,128]{2,1,0:T(8,128)(2,1)S(1)}, u32[]{:S(2)}, u32[]{:S(2)}) collective-permute-start(bf16[1,256,128]{2,1,0:T(8,128)(2,1)S(1)} %add_convert_fusion.6), channel_id=1, source_target_pairs={{0,8},{1,9},{2,10},{3,11},{4,12},{5,13},{6,14},{7,15},{8,0},{9,1},... | collective-permute-start | bytes 196616 | tf_op jit(solution)/shard_map/ppermute | solution.py:447
  42.7 5.0 %collective-permute-start.21 = (bf16[1,256,128]{2,1,0:T(8,128)(2,1)S(1)}, bf16[1,256,128]{2,1,0:T(8,128)(2,1)S(1)}, u32[]{:S(2)}, u32[]{:S(2)}) collective-permute-start(bf16[1,256,128]{2,1,0:T(8,128)(2,1)S(1)} %add_convert_fusion.2), channel_id=1, source_target_pairs={{0,1},{1,0},{2,3},{3,2},{4,5},{5,4},{6,7},{7,6},{8,9},{9,8},{10,11... | collective-permute-start | bytes 196616 | tf_op jit(solution)/shard_map/ppermute | solution.py:447
  45.2 4.5 %collective-permute-start.13 = (bf16[1,256,128]{2,1,0:T(8,128)(2,1)S(1)}, bf16[1,256,128]{2,1,0:T(8,128)(2,1)S(1)}, u32[]{:S(2)}, u32[]{:S(2)}) collective-permute-start(bf16[1,256,128]{2,1,0:T(8,128)(2,1)S(1)} %add_convert_fusion.5), channel_id=1, source_target_pairs={{0,1},{1,0},{2,3},{3,2},{4,5},{5,4},{6,7},{7,6},{8,9},{9,8},{10,11... | collective-permute-start | bytes 196616 | tf_op jit(solution)/shard_map/ppermute | solution.py:447
  47.8 5.0 %collective-permute-start.22 = (bf16[2,256,128]{2,1,0:T(8,128)(2,1)S(1)}, bf16[2,256,128]{2,1,0:T(8,128)(2,1)S(1)}, u32[]{:S(2)}, u32[]{:S(2)}) collective-permute-start(bf16[2,256,128]{2,1,0:T(8,128)(2,1)S(1)} %pad_maximum_fusion.1.near_mine), channel_id=1, source_target_pairs={{0,2},{1,3},{2,0},{3,1},{4,6},{5,7},{6,4},{7,5},{8,10},{9,11},{10,... | collective-permute-start | bytes 393224 | tf_op jit(solution)/shard_map/ppermute | solution.py:447
  49.7 5.0 %collective-permute-start.14 = (bf16[2,256,128]{2,1,0:T(8,128)(2,1)S(1)}, bf16[2,256,128]{2,1,0:T(8,128)(2,1)S(1)}, u32[]{:S(2)}, u32[]{:S(2)}) collective-permute-start(bf16[2,256,128]{2,1,0:T(8,128)(2,1)S(1)} %pad_maximum_fusion.near_mine), channel_id=1, source_target_pairs={{0,2},{1,3},{2,0},{3,1},{4,6},{5,7},{6,4},{7,5},{8,10},{9,11},{10,... | collective-permute-start | bytes 393224 | tf_op jit(solution)/shard_map/ppermute | solution.py:447
  52.8 2.0 %collective-permute-start.23 = (bf16[2,256,128]{2,1,0:T(8,128)(2,1)S(1)}, bf16[2,256,128]{2,1,0:T(8,128)(2,1)S(1)}, u32[]{:S(2)}, u32[]{:S(2)}) collective-permute-start(bf16[2,256,128]{2,1,0:T(8,128)(2,1)S(1)} %pad_maximum_fusion.1.near_mine), channel_id=1, source_target_pairs={{0,16},{16,0},{1,17},{17,1},{2,18},{18,2},{3,19},{19,3},{4,20},{20... | collective-permute-start | bytes 393224 | tf_op jit(solution)/shard_map/ppermute | solution.py:443
  52.8 2.0 %collective-permute-start.24 = (bf16[2,256,128]{2,1,0:T(8,128)(2,1)S(1)}, bf16[2,256,128]{2,1,0:T(8,128)(2,1)S(1)}, u32[]{:S(2)}, u32[]{:S(2)}) collective-permute-start(bf16[2,256,128]{2,1,0:T(8,128)(2,1)S(1)} %collective-permute-done.22.far_mine), channel_id=1, source_target_pairs={{0,16},{16,0},{1,17},{17,1},{2,18},{18,2},{3,19},{19,3},{4,20},{20... | collective-permute-start | bytes 393224 | tf_op jit(solution)/shard_map/ppermute | solution.py:443
  53.3 2.7 %collective-permute-start.15 = (bf16[2,256,128]{2,1,0:T(8,128)(2,1)S(1)}, bf16[2,256,128]{2,1,0:T(8,128)(2,1)S(1)}, u32[]{:S(2)}, u32[]{:S(2)}) collective-permute-start(bf16[2,256,128]{2,1,0:T(8,128)(2,1)S(1)} %pad_maximum_fusion.near_mine), channel_id=1, source_target_pairs={{0,16},{16,0},{1,17},{17,1},{2,18},{18,2},{3,19},{19,3},{4,20},{20... | collective-permute-start | bytes 393224 | tf_op jit(solution)/shard_map/ppermute | solution.py:443
  54.8 1.3 %collective-permute-start.16 = (bf16[2,256,128]{2,1,0:T(8,128)(2,1)S(1)}, bf16[2,256,128]{2,1,0:T(8,128)(2,1)S(1)}, u32[]{:S(2)}, u32[]{:S(2)}) collective-permute-start(bf16[2,256,128]{2,1,0:T(8,128)(2,1)S(1)} %collective-permute-done.14.far_mine), channel_id=1, source_target_pairs={{0,16},{16,0},{1,17},{17,1},{2,18},{18,2},{3,19},{19,3},{4,20},{20... | collective-permute-start | bytes 393224 | tf_op jit(solution)/shard_map/ppermute | solution.py:443

commit v5 on v4

--- a/solution.py
+++ b/solution.py
@@ -10,7 +10,7 @@
 HEADS = 4
 BALL = 128
 LISTED = 4
-CHUNK = 256
+CHUNK = 512
 QUARTERED = (True, True)
 EPSILON = 1e-06
 BF = jnp.bfloat16
@@ -31,6 +31,16 @@
     return lax.rsqrt(jnp.mean(x * x, axis=-1, keepdims=True) + EPSILON)
 
 
+def parity(index):
+    for shift in (8, 4, 2, 1):
+        index = index ^ (index >> shift)
+    return index & 1
+
+
+def own_side():
+    return lax.axis_index("pts") ^ parity(lax.axis_index("geo"))
+
+
 def part_of(place, size):
     return pl.ds(pl.multiple_of(place * size, size), size)
 
@@ -67,6 +77,21 @@
 
 def pick(ref, listed, first, half):
     return jnp.concatenate([ref[part_of(i, BALL), first : first + half] for i in listed], axis=0)
+
+
+def turn_balls(turned_ref, kv_ref):
+    for ball in range(turned_ref.shape[0]):
+        turned_ref[ball] = kv_ref[ball * BALL : (ball + 1) * BALL, :].T
+
+
+def pick_turned(ref, listed, first, half):
+    return jnp.concatenate([ref[i, first : first + half, :] for i in listed], axis=1)
+
+
+def combine(turned, weights):
+    both = dot(turned, weights, ((1,), (1,)))
+    rows, features = both.shape[1] // 2, both.shape[0] // 2
+    return jnp.concatenate([both[:features, :rows], both[features:, rows:]], axis=0).T
 
 
 def in_stages(count, *stages):
@@ -83,7 +108,7 @@
     return exponent, 1.0 / jnp.sum(exponent, axis=-1, keepdims=True)
 
 
-def backward_stages(lists, core, q_ref, kv_ref, mg_ref, mixed_ref, grads_ref, dk_ref, dv_ref, forward):
+def backward_stages(lists, core, q_ref, kv_ref, turned_ref, mg_ref, mixed_ref, grads_ref, dk_ref, dv_ref, forward):
     half = q_ref.shape[1]
     scale = (half // 2) ** (-0.5)
 
@@ -109,13 +134,14 @@
     def gradients(ball, listed, stacked, grad, attention, scores_grad):
         at = slice(ball * BALL, (ball + 1) * BALL)
         if forward:
-            mixed_ref[at, :] = unstack_heads(dot(attention, pick(kv_ref, listed, half, half))).astype(BF)
-        queries_grad = unstack_heads(dot(scores_grad, pick(kv_ref, listed, 0, half))) * scale
+            mixed_ref[at, :] = combine(pick_turned(turned_ref, listed, half, half), attention).astype(BF)
+        queries_grad = combine(pick_turned(turned_ref, listed, 0, half), scores_grad) * scale
         grads_ref[at, :half] = queries_grad.astype(BF)
         add_listed(dk_ref, listed, dot(stacked, scores_grad, ((0,), (0,))))
         add_listed(dv_ref, listed, dot(grad, attention, ((0,), (0,))))
         return ()
 
+    turn_balls(turned_ref, kv_ref)
     dk_ref[...] = jnp.zeros_like(dk_ref)
     dv_ref[...] = jnp.zeros_like(dv_ref)
     in_stages(q_ref.shape[0] // BALL, products, elements, gradients)
@@ -129,27 +155,28 @@
 def normed_grads(grads_ref, dk_ref, dv_ref, columns, store):
     half = dk_ref.shape[1]
 
-    def turn(ball):
-        at = slice(ball * BALL, (ball + 1) * BALL)
-        grads_ref[at, half : 2 * half] = dk_ref[ball].T.astype(BF)
-        grads_ref[at, 2 * half :] = dv_ref[ball].T.astype(BF)
+    def turn(chunk):
+        for ball in range(chunk * CHUNK // BALL, (chunk + 1) * CHUNK // BALL):
+            at = slice(ball * BALL, (ball + 1) * BALL)
+            grads_ref[at, half : 2 * half] = dk_ref[ball].T.astype(BF)
+            grads_ref[at, 2 * half :] = dv_ref[ball].T.astype(BF)
         return ()
 
-    def multiply(ball):
-        at = slice(ball * BALL, (ball + 1) * BALL)
+    def multiply(chunk):
+        at = slice(chunk * CHUNK, (chunk + 1) * CHUNK)
         store(at, dot(grads_ref[at, :], columns, ((1,), (1,))))
         return ()
 
-    in_stages(dk_ref.shape[0], turn, multiply)
+    in_stages(grads_ref.shape[0] // CHUNK, turn, multiply)
 
 
 def geo_bit(bit):
     return lax.rem(lax.axis_index("geo") // bit, 2)
 
 
-def kept(core, quartered):
-    half = geo_bit(jnp.where(core == 0, 2, 1))
-    return half, geo_bit(jnp.where(core == 0, 1, 2)) if quartered else 0
+def kept(side, quartered):
+    half = geo_bit(jnp.where(side == 0, 2, 1))
+    return half, geo_bit(jnp.where(side == 0, 1, 2)) if quartered else 0
 
 
 def store_quarters(ref, blocks, slot):
@@ -190,7 +217,7 @@
     x, grad, rot, lists_one, lists_two, gain_one, gain_two, qkv_one, qkv_two, out_one, out_two,
     normed_ref, q_ref, kv_ref, sems,
 ):
-    core = lax.axis_index("pts")
+    side = own_side()
     half = x.shape[1] // 2
     copies = []
 
@@ -200,7 +227,7 @@
 
     def start_columns(source, target):
         for i in range(3):
-            start(source.at[:, part_of(2 * i + core, half)], target.at[:, i * half : (i + 1) * half])
+            start(source.at[:, part_of(2 * i + side, half)], target.at[:, i * half : (i + 1) * half])
 
     start(x_hbm, x)
     start(gain_one_hbm, gain_one)
@@ -213,8 +240,8 @@
     start(gain_two_hbm, gain_two)
     start_columns(qkv_two_hbm, qkv_two)
     for source, target in ((out_one_hbm, out_one), (out_two_hbm, out_two)):
-        start(source.at[part_of(core, half)], target.at[:half])
-        start(source.at[part_of(1 - core, half)], target.at[half:])
+        start(source.at[part_of(side, half)], target.at[:half])
+        start(source.at[part_of(1 - side, half)], target.at[half:])
     for copy in copies[:first]:
         copy.wait()
     norm_project(
@@ -284,7 +311,7 @@
 def second_layer(
     mine, other, base, mixed_other, chosen, mg_ref, out_one, gain, columns,
     moved_ref, normed_ref, mixed_ref, mixed_send, grads_ref, part_ref,
-    hidden_ref, q_ref, kv_ref, dk_ref, dv_ref,
+    hidden_ref, q_ref, kv_ref, turned_ref, dk_ref, dv_ref,
 ):
     core = lax.axis_index("pts")
     total, width = base.shape
@@ -302,7 +329,7 @@
         return moved
 
     norm_project(total, rotate, gain_row(gain), columns[...], normed_ref, q_ref, kv_ref)
-    backward_stages((mine, other), core, q_ref, kv_ref, mg_ref, mixed_ref, grads_ref, dk_ref, dv_ref, True)
+    backward_stages((mine, other), core, q_ref, kv_ref, turned_ref, mg_ref, mixed_ref, grads_ref, dk_ref, dv_ref, True)
 
     def store(at, part):
         part_ref[at] = part.astype(BF)
@@ -312,7 +339,7 @@
 
 
 def second_weights(normed, grads, mixed, grad, keep_ref, send_ref):
-    part, slot = kept(lax.axis_index("pts"), QUARTERED[1])
+    part, slot = kept(own_side(), QUARTERED[1])
     store_quarters(send_ref, weight_part(1 - part, normed, grads[...], mixed[...], grad), slot)
     store_quarters(keep_ref, weight_part(part, normed, grads[...], mixed[...], grad), slot)
 
@@ -321,7 +348,7 @@
     mine, other, chosen_back, part_mine, part_other, moved, grad, gain_two,
     mixed_ref, normed, q_ref, kv_ref, out_one, columns,
     hg_ref, grads_ref, send_ref, part_keep, part_send,
-    rows_grad_ref, mg_ref, dk_ref, dv_ref,
+    rows_grad_ref, mg_ref, turned_ref, dk_ref, dv_ref,
 ):
     core = lax.axis_index("pts")
     total, width = grad.shape
@@ -343,7 +370,7 @@
         return ()
 
     in_stages(total // CHUNK, rotate, project_back)
-    backward_stages((mine, other), core, q_ref, kv_ref, mg_ref, mixed_ref, grads_ref, dk_ref, dv_ref, False)
+    backward_stages((mine, other), core, q_ref, kv_ref, turned_ref, mg_ref, mixed_ref, grads_ref, dk_ref, dv_ref, False)
 
     def store(at, part):
         if at.start < local:
@@ -352,7 +379,7 @@
             part_send[at.start - local : at.stop - local] = part.astype(BF)
 
     normed_grads(grads_ref, dk_ref, dv_ref, columns[...], store)
-    part, slot = kept(core, QUARTERED[0])
+    part, slot = kept(own_side(), QUARTERED[0])
     store_quarters(send_ref, weight_part(1 - part, normed, grads_ref[...], mixed_ref[...], hg_ref), slot)
 
 
@@ -361,7 +388,7 @@
     keep_ref, points_grad, result,
 ):
     local = x_mine.shape[0]
-    part, slot = kept(lax.axis_index("pts"), QUARTERED[0])
+    part, slot = kept(own_side(), QUARTERED[0])
     store_quarters(keep_ref, weight_part(part, normed, grads[...], mixed[...], hidden_grad), slot)
     normed_grad = part_mine[...] + part_other[...].astype(F32)
     points_grad[...] = norm_backward(
@@ -374,9 +401,9 @@
 def finish_weights(
     quartered, near_mine, far_mine, near_other, far_other, gain, weight, gain_grad, qkv_grad, out_grad, folded_ref
 ):
-    core = lax.axis_index("pts")
+    own = own_side()
     size, half = near_mine.shape[1:]
-    for side, near, far in ((core, near_mine, far_mine), (1 - core, near_other, far_other)):
+    for side, near, far in ((own, near_mine, far_mine), (1 - own, near_other, far_other)):
         bit, slot = kept(side, quartered)
         for part, ref in ((bit, near), (1 - bit, far)):
 
@@ -436,6 +463,7 @@
     total = 2 * rows
     balls = total // BALL
     thin, wide, triple = shape(total, half), shape(total, width), shape(total, 3 * half)
+    turned = shape(balls, width, BALL)
     blocks = shape(balls, half, BALL, dtype=F32)
     weights = shape(2, width, half)
 
@@ -443,7 +471,10 @@
         return lax.ppermute(array, "pts", SWAP)
 
     def across(array, bits):
-        pairs = [(core * geo + i, core * geo + (i ^ bit)) for core, bit in enumerate(bits) for i in range(geo)]
+        def place(side, index):
+            return (side ^ parity(index)) * geo + index
+
+        pairs = [(place(side, i), place(side, i ^ bit)) for side, bit in enumerate(bits) for i in range(geo)]
         return lax.ppermute(array, ("pts", "geo"), pairs)
 
     ups = [1 << i for i in range(2, geo.bit_length() - 1)]
@@ -483,20 +514,22 @@
         second_layer,
         [base, mixed_other, chosen, mg, out_one, far_gain, columns_two],
         [wide, wide, thin, shape(rows, half), triple, wide],
-        [wide, thin, wide, blocks, blocks],
+        [wide, thin, wide, turned, blocks, blocks],
         two,
     )
     part_two_other = swap(part_two)
     mixed_two_other = swap(mixed_send)
     keep_two, send_two = call(second_weights, [normed_two, grads_two, mixed_two, grads_in], [weights, weights])
-    summed_two = add(keep_two, across(send_two, (2, 1)))
+    received_two = across(send_two, (2, 1))
     hidden_grad, grads_one, send, part_keep, part_send = call(
         first_backward,
         [chosen_back, part_two, part_two_other, moved, grads_in, far_gain, mixed, normed, q, kv, out_one, columns_one],
         [wide, triple, weights, shape(rows, width, dtype=F32), own_rows],
-        [wide, thin, blocks, blocks],
+        [wide, thin, turned, blocks, blocks],
         one,
     )
+    received_two, send = lax.optimization_barrier((received_two, send))
+    summed_two = add(keep_two, received_two)
     part_other = swap(part_send)
     received = across(send, (2, 1))
     keep, points_grad, result = call(

time: 57.4 us -> 54.9 us (0.956)
  waiting for transfers between devices: 10.7 us -> 3.94 us
  starting transfers between devices: 22.6 us -> 27.9 us
  Pallas kernels: 23 us -> 21.9 us
    ppermute x12, waiting for transfers between devices: 10.4 us -> 3.82 us  [across(): return lax.ppermute(array, ('pts', 'geo'), pairs)]
    ppermute x12, starting transfers between devices: 19.4 us -> 24 us  [across(): return lax.ppermute(array, ('pts', 'geo'), pairs)]
    pallas_call x8, Pallas kernels: 21.4 us -> 20.3 us  [call(): pl.pallas_call(body, name=getattr(body, 'func', body).__name__, out_shape...]
    ppermute x13, starting transfers between devices: 3.2 us -> 3.9 us  [swap(): return lax.ppermute(array, 'pts', SWAP)]
  transfers between devices with their start and end apart: 25 -> 25, of which waited for: 10 -> 6; matrix products, arithmetic and copies ran while one was open for 0% -> 0% of each run, Pallas kernels for 22% -> 22%
where the time goes in v5:
time: 54.9 us; the launch traced here: 54.8 us
  starting transfers between devices  27.9 us (51%)
  Pallas kernels  21.9 us (40%)
  waiting for transfers between devices  3.94 us (7%)
  between operations  0.8 us (1%)
    ppermute x12, starting transfers between devices, across(): return lax.ppermute(array, ('pts', 'geo'), pairs)  24 us
    pallas_call x8, Pallas kernels, call(): pl.pallas_call(body, name=getattr(body, 'func', body).__name__, out_shape...  20.3 us
    ppermute x13, starting transfers between devices, swap(): return lax.ppermute(array, 'pts', SWAP)  3.9 us
    ppermute x12, waiting for transfers between devices, across(): return lax.ppermute(array, ('pts', 'geo'), pairs)  3.82 us
    pallas_call x1, Pallas kernels, local(): pl.pallas_call(project_mine, name='project_mine', out_shape=[shape(*a.sha...  1.54 us
  transfers between devices with their start and end apart: 25, of which 6 were waited for; matrix products, arithmetic and copies ran while one was open for 0% of the time, Pallas kernels for 22%

profile of v5, /device:TPU:0, one launch (start us, length us, event | category | flops | bytes accessed | tf_op | source)
XLA Modules:
  0.0 54.8 jit_solution(9248735929583332167)
XLA Ops:
  0.6 0.5 collective-permute-start
  1.2 0.4 collective-permute-start.3
  1.7 0.4 collective-permute-start.2
  2.2 1.5 %project_mine.1 = (bf16[512,256]{1,0:T(8,128)(2,1)S(1)}, bf16[512,256]{1,0:T(8,128)(2,1)S(1)}, s32[4,128]{1,0:T(4,128)S(1)}, s32[1,4,4]{2,1,0:T(4,128)S(1)}, s32...) custom-call(bf16[512,256]{1,0:T(8,128)(2,1)} %bitcast.8, ...), custom_call_target="tpu_custom_call" | custom-call | tf_op jit(solution)/shard_map/project_mine/pallas_call | solution.py:491
  3.8 2.5 %first_forward.1 = (bf16[1024,128]{1,0:T(8,128)(2,1)S(1)}, bf16[1024,128]{1,0:T(8,128)(2,1)S(1)}, bf16[1024,256]{1,0:T(8,128)(2,1)S(1)}, bf16[1024,256]{1,0:T(8,128)(2,1)S(1)}) custom-call(s32[1,4,4]{2,1,0:T(4,128)S(1)} %get-tuple-element.62.mine, s32[1,4,4]{2,1,0:T(4,128)S(1)} %collective-permute-done.1.other, ...), custom_call_target="tpu_custom_call" | custom-call | tf_op jit(solution)/shard_map/first_forward/pallas_call | solution.py:432
  6.4 1.4 %before_second.1 = (f32[1024,256]{1,0:T(8,128)S(1)}, bf16[1024,1024]{1,0:T(8,128)(2,1)S(1)}, bf16[1024,1024]{1,0:T(8,128)(2,1)S(1)}, bf16[1024,256]{1,0:T(8,128)(2,1)S(1)}, bf16[1024,128]{1,0:T(8,128)(2,1)S(1)}) custom-call(s32[4,128]{1,0:T(4,128)S(1)} %get-tuple-element.71.rot_mine, s32[4,128]{1,0:T(4,128)S(1)} %collective-permute-done.3.rot_other, ...), custom_call_target="tpu_custom_call" | custom-call | tf_op jit(solution)/shard_map/before_second/pallas_call | solution.py:432
  7.8 6.4 %second_layer.1 = (bf16[1024,256]{1,0:T(8,128)(2,1)S(1)}, bf16[1024,256]{1,0:T(8,128)(2,1)S(1)}, bf16[1024,128]{1,0:T(8,128)(2,1)S(1)}, bf16[512,128]{1,0:T(8,12...) custom-call(s32[1,4,4]{2,1,0:T(4,128)S(1)} %get-tuple-element.80.mine, ...), custom_call_target="tpu_custom_call" | custom-call | tf_op jit(solution)/shard_map/second_layer/pallas_call | solution.py:432
  14.3 0.4 collective-permute-start.6
  14.7 0.7 %second_weights.1 = (bf16[2,256,128]{2,1,0:T(8,128)(2,1)S(1)}, bf16[2,256,128]{2,1,0:T(8,128)(2,1)S(1)}) custom-call(bf16[1024,256]{1,0:T(8,128)(2,1)S(1)} %get-tuple-element.101.normed, bf16[1024,384]{1,0:T(8,128)(2,1)S(1)} %get-tuple-element.102.grads, bf16[1024,128]{1,0:T(8,128)(2,1)S(1)} %get-tuple-element.96.mixed_two.mixed, ...), custom_call_target="tpu_custom_call" | custom-call | tf_op jit(solution)/shard_map/second_weights/pallas_call | solution.py:432
  15.3 2.7 %collective-permute-start.9 = (bf16[2,256,128]{2,1,0:T(8,128)(2,1)S(1)}, bf16[2,256,128]{2,1,0:T(8,128)(2,1)S(1)}, u32[]{:S(2)}, u32[]{:S(2)}) collective-permute-start(bf16[2,256,128]{2,1,0:T(8,128)(2,1)S(1)} %get-tuple-element.103), channel_id=1, source_target_pairs={{0,18},{17,3},{18,0},{3,17},{20,6},{5,23},{6,20},{23,5},{24,10},{9... | collective-permute-start | bytes 393224 | tf_op jit(solution)/shard_map/ppermute | solution.py:478
  18.0 5.8 %first_backward.1 = (bf16[1024,256]{1,0:T(8,128)(2,1)S(1)}, bf16[1024,384]{1,0:T(8,128)(2,1)S(1)}, bf16[2,256,128]{2,1,0:T(8,128)(2,1)S(1)}, f32[512,256]{1,0:T(8,128)S(1)}, bf16[512,256]{1,0:T(8,128)(2,1)S(1)}) custom-call(s32[1,4,4]{2,1,0:T(4,128)S(1)} %get-tuple-element.62.mine, s32[1,4,4]{2,1,0:T(4,128)S(1)} %collective-permute-done.1.other, ...), custom_call_target="tpu_custom_call" | custom-call | tf_op jit(solution)/shard_map/first_backward/pallas_call | solution.py:432
  24.1 0.4 collective-permute-start.8
  24.5 1.2 %collective-permute-start.10 = (bf16[2,256,128]{2,1,0:T(8,128)(2,1)S(1)}, bf16[2,256,128]{2,1,0:T(8,128)(2,1)S(1)}, u32[]{:S(2)}, u32[]{:S(2)}) collective-permute-start(bf16[2,256,128]{2,1,0:T(8,128)(2,1)S(1)} %get-tuple-element.105), channel_id=1, source_target_pairs={{0,18},{17,3},{18,0},{3,17},{20,6},{5,23},{6,20},{23,5},{24,10},{9... | collective-permute-start | bytes 393224 | tf_op jit(solution)/shard_map/ppermute | solution.py:478
  25.7 1.2 %collective-permute-start.18 = (bf16[1,256,128]{2,1,0:T(8,128)(2,1)S(1)}, bf16[1,256,128]{2,1,0:T(8,128)(2,1)S(1)}, u32[]{:S(2)}, u32[]{:S(2)}) collective-permute-start(bf16[1,256,128]{2,1,0:T(8,128)(2,1)S(1)} %slice.19), channel_id=1, source_target_pairs={{0,17},{17,0},{18,3},{3,18},{20,5},{5,20},{6,23},{23,6},{24,9},{9,... | collective-permute-start | bytes 196616 | tf_op jit(solution)/shard_map/ppermute | solution.py:478
  26.9 1.4 %finish_rows.1 = (bf16[2,256,128]{2,1,0:T(8,128)(2,1)S(1)}, bf16[512,256]{1,0:T(8,128)(2,1)}, bf16[512,256]{1,0:T(8,128)(2,1)}) custom-call(bf16[1024,256]{1,0:T(8,128)(2,1)S(1)} %get-tuple-element.70.normed, bf16[1024,384]{1,0:T(8,128)(2,1)S(1)} %get-tuple-element.92.grads, bf16[1024,128]{1,0:T(8,128)(2,1)S(1)} %get-tuple-element.74.mixed.mixed_ref, ...), custom_call_target="tpu_custom_call" | custom-call | tf_op jit(solution)/shard_map/finish_rows/pallas_call | solution.py:432
  28.3 0.6 %collective-permute-done.10 = bf16[2,256,128]{2,1,0:T(8,128)(2,1)S(1)} collective-permute-done((bf16[2,256,128]{2,1,0:T(8,128)(2,1)S(1)}, bf16[2,256,128]{2,1,0:T(8,128)(2,1)S(1)}, u32[]{:S(2)}, u32[]{:S(2)}) %collective-permute-start.10) | collective-permute-done | bytes 131104 | tf_op jit(solution)/shard_map/ppermute | solution.py:478
  28.9 2.0 %collective-permute-start.11 = (bf16[1,256,128]{2,1,0:T(8,128)(2,1)S(1)}, bf16[1,256,128]{2,1,0:T(8,128)(2,1)S(1)}, u32[]{:S(2)}, u32[]{:S(2)}) collective-permute-start(bf16[1,256,128]{2,1,0:T(8,128)(2,1)S(1)} %slice.17), channel_id=1, source_target_pairs={{0,17},{17,0},{18,3},{3,18},{20,5},{5,20},{6,23},{23,6},{24,9},{9,... | collective-permute-start | bytes 196616 | tf_op jit(solution)/shard_map/ppermute | solution.py:478
  30.9 1.4 %collective-permute-start.19 = (bf16[1,256,128]{2,1,0:T(8,128)(2,1)S(1)}, bf16[1,256,128]{2,1,0:T(8,128)(2,1)S(1)}, u32[]{:S(2)}, u32[]{:S(2)}) collective-permute-start(bf16[1,256,128]{2,1,0:T(8,128)(2,1)S(1)} %add_convert_fusion.4), channel_id=1, source_target_pairs={{0,20},{17,5},{18,6},{3,23},{20,0},{5,17},{6,18},{23,3},{24,12},{9... | collective-permute-start | bytes 196616 | tf_op jit(solution)/shard_map/ppermute | solution.py:478
  32.3 0.5 collective-permute-done.11
  32.9 1.9 %collective-permute-start.12 = (bf16[1,256,128]{2,1,0:T(8,128)(2,1)S(1)}, bf16[1,256,128]{2,1,0:T(8,128)(2,1)S(1)}, u32[]{:S(2)}, u32[]{:S(2)}) collective-permute-start(bf16[1,256,128]{2,1,0:T(8,128)(2,1)S(1)} %add_convert_fusion.7), channel_id=1, source_target_pairs={{0,20},{17,5},{18,6},{3,23},{20,0},{5,17},{6,18},{23,3},{24,12},{9... | collective-permute-start | bytes 196616 | tf_op jit(solution)/shard_map/ppermute | solution.py:478
  34.9 2.8 %collective-permute-start.20 = (bf16[1,256,128]{2,1,0:T(8,128)(2,1)S(1)}, bf16[1,256,128]{2,1,0:T(8,128)(2,1)S(1)}, u32[]{:S(2)}, u32[]{:S(2)}) collective-permute-start(bf16[1,256,128]{2,1,0:T(8,128)(2,1)S(1)} %add_convert_fusion.3), channel_id=1, source_target_pairs={{0,24},{17,9},{18,10},{3,27},{20,12},{5,29},{6,30},{23,15},{24,0},... | collective-permute-start | bytes 196616 | tf_op jit(solution)/shard_map/ppermute | solution.py:478
  37.7 2.4 %collective-permute-start.13 = (bf16[1,256,128]{2,1,0:T(8,128)(2,1)S(1)}, bf16[1,256,128]{2,1,0:T(8,128)(2,1)S(1)}, u32[]{:S(2)}, u32[]{:S(2)}) collective-permute-start(bf16[1,256,128]{2,1,0:T(8,128)(2,1)S(1)} %add_convert_fusion.6), channel_id=1, source_target_pairs={{0,24},{17,9},{18,10},{3,27},{20,12},{5,29},{6,30},{23,15},{24,0},... | collective-permute-start | bytes 196616 | tf_op jit(solution)/shard_map/ppermute | solution.py:478
  40.1 2.0 %collective-permute-start.21 = (bf16[1,256,128]{2,1,0:T(8,128)(2,1)S(1)}, bf16[1,256,128]{2,1,0:T(8,128)(2,1)S(1)}, u32[]{:S(2)}, u32[]{:S(2)}) collective-permute-start(bf16[1,256,128]{2,1,0:T(8,128)(2,1)S(1)} %add_convert_fusion.2), channel_id=1, source_target_pairs={{0,17},{17,0},{18,3},{3,18},{20,5},{5,20},{6,23},{23,6},{24,9},{9,... | collective-permute-start | bytes 196616 | tf_op jit(solution)/shard_map/ppermute | solution.py:478
  42.4 1.8 %collective-permute-start.14 = (bf16[1,256,128]{2,1,0:T(8,128)(2,1)S(1)}, bf16[1,256,128]{2,1,0:T(8,128)(2,1)S(1)}, u32[]{:S(2)}, u32[]{:S(2)}) collective-permute-start(bf16[1,256,128]{2,1,0:T(8,128)(2,1)S(1)} %add_convert_fusion.5), channel_id=1, source_target_pairs={{0,17},{17,0},{18,3},{3,18},{20,5},{5,20},{6,23},{23,6},{24,9},{9,... | collective-permute-start | bytes 196616 | tf_op jit(solution)/shard_map/ppermute | solution.py:478
  44.2 1.7 %collective-permute-start.22 = (bf16[2,256,128]{2,1,0:T(8,128)(2,1)S(1)}, bf16[2,256,128]{2,1,0:T(8,128)(2,1)S(1)}, u32[]{:S(2)}, u32[]{:S(2)}) collective-permute-start(bf16[2,256,128]{2,1,0:T(8,128)(2,1)S(1)} %pad_maximum_fusion.1.near_mine), channel_id=1, source_target_pairs={{0,18},{17,3},{18,0},{3,17},{20,6},{5,23},{6,20},{23,5},{24,10},{9... | collective-permute-start | bytes 393224 | tf_op jit(solution)/shard_map/ppermute | solution.py:478
  45.9 0.3 collective-permute-done.14
  46.2 3.0 %collective-permute-start.15 = (bf16[2,256,128]{2,1,0:T(8,128)(2,1)S(1)}, bf16[2,256,128]{2,1,0:T(8,128)(2,1)S(1)}, u32[]{:S(2)}, u32[]{:S(2)}) collective-permute-start(bf16[2,256,128]{2,1,0:T(8,128)(2,1)S(1)} %pad_maximum_fusion.near_mine), channel_id=1, source_target_pairs={{0,18},{17,3},{18,0},{3,17},{20,6},{5,23},{6,20},{23,5},{24,10},{9... | collective-permute-start | bytes 393224 | tf_op jit(solution)/shard_map/ppermute | solution.py:478
  49.2 0.5 collective-permute-start.24
  49.7 2.1 %collective-permute-done.15.far_mine = bf16[2,256,128]{2,1,0:T(8,128)(2,1)S(1)} collective-permute-done((bf16[2,256,128]{2,1,0:T(8,128)(2,1)S(1)}, bf16[2,256,128]{2,1,0:T(8,128)(2,1)S(1)}, u32[]{:S(2)}, u32[]{:S(2)}) %collective-permute-start.15) | collective-permute-done | bytes 131104 | tf_op jit(solution)/shard_map/ppermute | solution.py:478
  51.8 0.7 %collective-permute-start.17 = (bf16[2,256,128]{2,1,0:T(8,128)(2,1)S(1)}, bf16[2,256,128]{2,1,0:T(8,128)(2,1)S(1)}, u32[]{:S(2)}, u32[]{:S(2)}) collective-permute-start(bf16[2,256,128]{2,1,0:T(8,128)(2,1)S(1)} %collective-permute-done.15.far_mine), channel_id=1, source_target_pairs={{0,16},{16,0},{1,17},{17,1},{2,18},{18,2},{3,19},{19,3},{4,20},{20... | collective-permute-start | bytes 393224 | tf_op jit(solution)/shard_map/ppermute | solution.py:471
  52.6 1.1 %finish_weights.3 = (f32[1,256]{1,0:T(1,128)}, f32[256,768]{1,0:T(8,128)}, f32[256,256]{1,0:T(8,128)}) custom-call(bf16[2,256,128]{2,1,0:T(8,128)(2,1)S(1)} %pad_maximum_fusion.1.near_mine, bf16[2,256,128]{2,1,0:T(8,128)(2,1)S(1)} %collective-permute-done.22.far_mine, bf16[2,256,128]{2,1,0:T(8,128)(2,1)S(1)} %collective-permute-done.23.near_other, ...), custom_call_target="tpu_custom_call" | custom-call | tf_op jit(solution)/shard_map/finish_weights/pallas_call | solution.py:432
  53.7 1.1 %finish_weights.2 = (f32[1,256]{1,0:T(1,128)}, f32[256,768]{1,0:T(8,128)}, f32[256,256]{1,0:T(8,128)}) custom-call(bf16[2,256,128]{2,1,0:T(8,128)(2,1)S(1)} %pad_maximum_fusion.near_mine, bf16[2,256,128]{2,1,0:T(8,128)(2,1)S(1)} %collective-permute-done.15.far_mine, bf16[2,256,128]{2,1,0:T(8,128)(2,1)S(1)} %collective-permute-done.16.near_other, ...), custom_call_target="tpu_custom_call" | custom-call | tf_op jit(solution)/shard_map/finish_weights/pallas_call | solution.py:432
  (43 shorter events, 1.2 us)
Async XLA Ops:
  0.6 3.1 %collective-permute-start = (bf16[512,256]{1,0:T(8,128)(2,1)}, bf16[512,256]{1,0:T(8,128)(2,1)S(1)}, u32[]{:S(2)}, u32[]{:S(2)}) collective-permute-start(bf16[512,256]{1,0:T(8,128)(2,1)} %bitcast.7), channel_id=1, source_target_pairs={{0,16},{16,0},{1,17},{17,1},{2,18},{18,2},{3,19},{19,3},{4,20},{20... | collective-permute-start | bytes 786440 | tf_op jit(solution)/shard_map/ppermute | solution.py:471
  1.2 2.6 %collective-permute-start.4 = (bf16[512,256]{1,0:T(8,128)(2,1)}, bf16[512,256]{1,0:T(8,128)(2,1)S(1)}, u32[]{:S(2)}, u32[]{:S(2)}) collective-permute-start(bf16[512,256]{1,0:T(8,128)(2,1)} %bitcast.9), channel_id=1, source_target_pairs={{0,16},{16,0},{1,17},{17,1},{2,18},{18,2},{3,19},{19,3},{4,20},{20... | collective-permute-start | bytes 786440 | tf_op jit(solution)/shard_map/ppermute | solution.py:471
  1.2 2.5 %collective-permute-start.3 = (s32[4,128]{1,0:T(4,128)}, s32[4,128]{1,0:T(4,128)S(1)}, u32[]{:S(2)}, u32[]{:S(2)}) collective-permute-start(s32[4,128]{1,0:T(4,128)} %bitcast.11), channel_id=1, source_target_pairs={{0,16},{16,0},{1,17},{17,1},{2,18},{18,2},{3,19},{19,3},{4,20},{20... | collective-permute-start | bytes 6152 | tf_op jit(solution)/shard_map/ppermute | solution.py:471
  1.7 2.1 %collective-permute-start.1 = (s32[1,4,4]{2,1,0:T(4,128)}, s32[1,4,4]{2,1,0:T(4,128)S(1)}, u32[]{:S(2)}, u32[]{:S(2)}) collective-permute-start(s32[1,4,4]{2,1,0:T(4,128)} %lists_one_hbm.1), channel_id=1, source_target_pairs={{0,16},{16,0},{1,17},{17,1},{2,18},{18,2},{3,19},{19,3},{4,20},{20... | collective-permute-start | bytes 200 | tf_op jit(solution)/shard_map/ppermute | solution.py:471
  1.7 2.0 %collective-permute-start.2 = (s32[1,4,4]{2,1,0:T(4,128)}, s32[1,4,4]{2,1,0:T(4,128)S(1)}, u32[]{:S(2)}, u32[]{:S(2)}) collective-permute-start(s32[1,4,4]{2,1,0:T(4,128)} %lists_two_hbm.1), channel_id=1, source_target_pairs={{0,16},{16,0},{1,17},{17,1},{2,18},{18,2},{3,19},{19,3},{4,20},{20... | collective-permute-start | bytes 200 | tf_op jit(solution)/shard_map/ppermute | solution.py:471
  6.2 1.6 %collective-permute-start.5 = (bf16[1024,128]{1,0:T(8,128)(2,1)S(1)}, bf16[1024,128]{1,0:T(8,128)(2,1)S(1)}, u32[]{:S(2)}, u32[]{:S(2)}) collective-permute-start(bf16[1024,128]{1,0:T(8,128)(2,1)S(1)} %get-tuple-element.74.mixed.mixed_ref), channel_id=1, source_target_pairs={{0,16},{16,0},{1,17},{17,1},{2,18},{18,2},{3,19},{19,3},{4,20},{20... | collective-permute-start | bytes 786440 | tf_op jit(solution)/shard_map/ppermute | solution.py:471
  14.3 3.8 %collective-permute-start.6 = (bf16[1024,256]{1,0:T(8,128)(2,1)S(1)}, bf16[1024,256]{1,0:T(8,128)(2,1)S(1)}, u32[]{:S(2)}, u32[]{:S(2)}) collective-permute-start(bf16[1024,256]{1,0:T(8,128)(2,1)S(1)} %get-tuple-element.87.part_mine), channel_id=1, source_target_pairs={{0,16},{16,0},{1,17},{17,1},{2,18},{18,2},{3,19},{19,3},{4,20},{20... | collective-permute-start | bytes 1572872 | tf_op jit(solution)/shard_map/ppermute | solution.py:471
  15.3 9.1 %collective-permute-start.9 = (bf16[2,256,128]{2,1,0:T(8,128)(2,1)S(1)}, bf16[2,256,128]{2,1,0:T(8,128)(2,1)S(1)}, u32[]{:S(2)}, u32[]{:S(2)}) collective-permute-start(bf16[2,256,128]{2,1,0:T(8,128)(2,1)S(1)} %get-tuple-element.103), channel_id=1, source_target_pairs={{0,18},{17,3},{18,0},{3,17},{20,6},{5,23},{6,20},{23,5},{24,10},{9... | collective-permute-start | bytes 393224 | tf_op jit(solution)/shard_map/ppermute | solution.py:478
  23.9 3.0 %collective-permute-start.7 = (bf16[512,256]{1,0:T(8,128)(2,1)S(1)}, bf16[512,256]{1,0:T(8,128)(2,1)S(1)}, u32[]{:S(2)}, u32[]{:S(2)}) collective-permute-start(bf16[512,256]{1,0:T(8,128)(2,1)S(1)} %get-tuple-element.95), channel_id=1, source_target_pairs={{0,16},{16,0},{1,17},{17,1},{2,18},{18,2},{3,19},{19,3},{4,20},{20... | collective-permute-start | bytes 786440 | tf_op jit(solution)/shard_map/ppermute | solution.py:471
  24.1 2.8 %collective-permute-start.8 = (bf16[512,128]{1,0:T(8,128)(2,1)S(1)}, bf16[512,128]{1,0:T(8,128)(2,1)S(1)}, u32[]{:S(2)}, u32[]{:S(2)}) collective-permute-start(bf16[512,128]{1,0:T(8,128)(2,1)S(1)} %get-tuple-element.97), channel_id=1, source_target_pairs={{0,16},{16,0},{1,17},{17,1},{2,18},{18,2},{3,19},{19,3},{4,20},{20... | collective-permute-start | bytes 393224 | tf_op jit(solution)/shard_map/ppermute | solution.py:471
  24.5 4.4 %collective-permute-start.10 = (bf16[2,256,128]{2,1,0:T(8,128)(2,1)S(1)}, bf16[2,256,128]{2,1,0:T(8,128)(2,1)S(1)}, u32[]{:S(2)}, u32[]{:S(2)}) collective-permute-start(bf16[2,256,128]{2,1,0:T(8,128)(2,1)S(1)} %get-tuple-element.105), channel_id=1, source_target_pairs={{0,18},{17,3},{18,0},{3,17},{20,6},{5,23},{6,20},{23,5},{24,10},{9... | collective-permute-start | bytes 393224 | tf_op jit(solution)/shard_map/ppermute | solution.py:478
  25.7 5.2 %collective-permute-start.18 = (bf16[1,256,128]{2,1,0:T(8,128)(2,1)S(1)}, bf16[1,256,128]{2,1,0:T(8,128)(2,1)S(1)}, u32[]{:S(2)}, u32[]{:S(2)}) collective-permute-start(bf16[1,256,128]{2,1,0:T(8,128)(2,1)S(1)} %slice.19), channel_id=1, source_target_pairs={{0,17},{17,0},{18,3},{3,18},{20,5},{5,20},{6,23},{23,6},{24,9},{9,... | collective-permute-start | bytes 196616 | tf_op jit(solution)/shard_map/ppermute | solution.py:478
  28.3 24.3 %copy-start = (bf16[256,768]{1,0:T(8,128)(2,1)S(1)}, bf16[256,768]{1,0:T(8,128)(2,1)}, u32[]{:S(2)}) copy-start(bf16[256,768]{1,0:T(8,128)(2,1)} %weight.3) | copy-start | bytes 1179652
  28.3 25.4 %copy-start.1 = (bf16[256,768]{1,0:T(8,128)(2,1)S(1)}, bf16[256,768]{1,0:T(8,128)(2,1)}, u32[]{:S(2)}) copy-start(bf16[256,768]{1,0:T(8,128)(2,1)} %weight.2) | copy-start | bytes 1179652
  28.9 4.0 %collective-permute-start.11 = (bf16[1,256,128]{2,1,0:T(8,128)(2,1)S(1)}, bf16[1,256,128]{2,1,0:T(8,128)(2,1)S(1)}, u32[]{:S(2)}, u32[]{:S(2)}) collective-permute-start(bf16[1,256,128]{2,1,0:T(8,128)(2,1)S(1)} %slice.17), channel_id=1, source_target_pairs={{0,17},{17,0},{18,3},{3,18},{20,5},{5,20},{6,23},{23,6},{24,9},{9,... | collective-permute-start | bytes 196616 | tf_op jit(solution)/shard_map/ppermute | solution.py:478
  30.9 3.9 %collective-permute-start.19 = (bf16[1,256,128]{2,1,0:T(8,128)(2,1)S(1)}, bf16[1,256,128]{2,1,0:T(8,128)(2,1)S(1)}, u32[]{:S(2)}, u32[]{:S(2)}) collective-permute-start(bf16[1,256,128]{2,1,0:T(8,128)(2,1)S(1)} %add_convert_fusion.4), channel_id=1, source_target_pairs={{0,20},{17,5},{18,6},{3,23},{20,0},{5,17},{6,18},{23,3},{24,12},{9... | collective-permute-start | bytes 196616 | tf_op jit(solution)/shard_map/ppermute | solution.py:478
  32.9 4.8 %collective-permute-start.12 = (bf16[1,256,128]{2,1,0:T(8,128)(2,1)S(1)}, bf16[1,256,128]{2,1,0:T(8,128)(2,1)S(1)}, u32[]{:S(2)}, u32[]{:S(2)}) collective-permute-start(bf16[1,256,128]{2,1,0:T(8,128)(2,1)S(1)} %add_convert_fusion.7), channel_id=1, source_target_pairs={{0,20},{17,5},{18,6},{3,23},{20,0},{5,17},{6,18},{23,3},{24,12},{9... | collective-permute-start | bytes 196616 | tf_op jit(solution)/shard_map/ppermute | solution.py:478
  34.9 5.2 %collective-permute-start.20 = (bf16[1,256,128]{2,1,0:T(8,128)(2,1)S(1)}, bf16[1,256,128]{2,1,0:T(8,128)(2,1)S(1)}, u32[]{:S(2)}, u32[]{:S(2)}) collective-permute-start(bf16[1,256,128]{2,1,0:T(8,128)(2,1)S(1)} %add_convert_fusion.3), channel_id=1, source_target_pairs={{0,24},{17,9},{18,10},{3,27},{20,12},{5,29},{6,30},{23,15},{24,0},... | collective-permute-start | bytes 196616 | tf_op jit(solution)/shard_map/ppermute | solution.py:478
  37.7 4.7 %collective-permute-start.13 = (bf16[1,256,128]{2,1,0:T(8,128)(2,1)S(1)}, bf16[1,256,128]{2,1,0:T(8,128)(2,1)S(1)}, u32[]{:S(2)}, u32[]{:S(2)}) collective-permute-start(bf16[1,256,128]{2,1,0:T(8,128)(2,1)S(1)} %add_convert_fusion.6), channel_id=1, source_target_pairs={{0,24},{17,9},{18,10},{3,27},{20,12},{5,29},{6,30},{23,15},{24,0},... | collective-permute-start | bytes 196616 | tf_op jit(solution)/shard_map/ppermute | solution.py:478
  40.1 4.1 %collective-permute-start.21 = (bf16[1,256,128]{2,1,0:T(8,128)(2,1)S(1)}, bf16[1,256,128]{2,1,0:T(8,128)(2,1)S(1)}, u32[]{:S(2)}, u32[]{:S(2)}) collective-permute-start(bf16[1,256,128]{2,1,0:T(8,128)(2,1)S(1)} %add_convert_fusion.2), channel_id=1, source_target_pairs={{0,17},{17,0},{18,3},{3,18},{20,5},{5,20},{6,23},{23,6},{24,9},{9,... | collective-permute-start | bytes 196616 | tf_op jit(solution)/shard_map/ppermute | solution.py:478
  42.4 3.8 %collective-permute-start.14 = (bf16[1,256,128]{2,1,0:T(8,128)(2,1)S(1)}, bf16[1,256,128]{2,1,0:T(8,128)(2,1)S(1)}, u32[]{:S(2)}, u32[]{:S(2)}) collective-permute-start(bf16[1,256,128]{2,1,0:T(8,128)(2,1)S(1)} %add_convert_fusion.5), channel_id=1, source_target_pairs={{0,17},{17,0},{18,3},{3,18},{20,5},{5,20},{6,23},{23,6},{24,9},{9,... | collective-permute-start | bytes 196616 | tf_op jit(solution)/shard_map/ppermute | solution.py:478
  44.2 5.0 %collective-permute-start.22 = (bf16[2,256,128]{2,1,0:T(8,128)(2,1)S(1)}, bf16[2,256,128]{2,1,0:T(8,128)(2,1)S(1)}, u32[]{:S(2)}, u32[]{:S(2)}) collective-permute-start(bf16[2,256,128]{2,1,0:T(8,128)(2,1)S(1)} %pad_maximum_fusion.1.near_mine), channel_id=1, source_target_pairs={{0,18},{17,3},{18,0},{3,17},{20,6},{5,23},{6,20},{23,5},{24,10},{9... | collective-permute-start | bytes 393224 | tf_op jit(solution)/shard_map/ppermute | solution.py:478
  46.2 5.7 %collective-permute-start.15 = (bf16[2,256,128]{2,1,0:T(8,128)(2,1)S(1)}, bf16[2,256,128]{2,1,0:T(8,128)(2,1)S(1)}, u32[]{:S(2)}, u32[]{:S(2)}) collective-permute-start(bf16[2,256,128]{2,1,0:T(8,128)(2,1)S(1)} %pad_maximum_fusion.near_mine), channel_id=1, source_target_pairs={{0,18},{17,3},{18,0},{3,17},{20,6},{5,23},{6,20},{23,5},{24,10},{9... | collective-permute-start | bytes 393224 | tf_op jit(solution)/shard_map/ppermute | solution.py:478
  49.2 3.4 %collective-permute-start.23 = (bf16[2,256,128]{2,1,0:T(8,128)(2,1)S(1)}, bf16[2,256,128]{2,1,0:T(8,128)(2,1)S(1)}, u32[]{:S(2)}, u32[]{:S(2)}) collective-permute-start(bf16[2,256,128]{2,1,0:T(8,128)(2,1)S(1)} %pad_maximum_fusion.1.near_mine), channel_id=1, source_target_pairs={{0,16},{16,0},{1,17},{17,1},{2,18},{18,2},{3,19},{19,3},{4,20},{20... | collective-permute-start | bytes 393224 | tf_op jit(solution)/shard_map/ppermute | solution.py:471
  49.2 3.4 %collective-permute-start.24 = (bf16[2,256,128]{2,1,0:T(8,128)(2,1)S(1)}, bf16[2,256,128]{2,1,0:T(8,128)(2,1)S(1)}, u32[]{:S(2)}, u32[]{:S(2)}) collective-permute-start(bf16[2,256,128]{2,1,0:T(8,128)(2,1)S(1)} %collective-permute-done.22.far_mine), channel_id=1, source_target_pairs={{0,16},{16,0},{1,17},{17,1},{2,18},{18,2},{3,19},{19,3},{4,20},{20... | collective-permute-start | bytes 393224 | tf_op jit(solution)/shard_map/ppermute | solution.py:471
  49.7 4.0 %collective-permute-start.16 = (bf16[2,256,128]{2,1,0:T(8,128)(2,1)S(1)}, bf16[2,256,128]{2,1,0:T(8,128)(2,1)S(1)}, u32[]{:S(2)}, u32[]{:S(2)}) collective-permute-start(bf16[2,256,128]{2,1,0:T(8,128)(2,1)S(1)} %pad_maximum_fusion.near_mine), channel_id=1, source_target_pairs={{0,16},{16,0},{1,17},{17,1},{2,18},{18,2},{3,19},{19,3},{4,20},{20... | collective-permute-start | bytes 393224 | tf_op jit(solution)/shard_map/ppermute | solution.py:471
  51.8 1.8 %collective-permute-start.17 = (bf16[2,256,128]{2,1,0:T(8,128)(2,1)S(1)}, bf16[2,256,128]{2,1,0:T(8,128)(2,1)S(1)}, u32[]{:S(2)}, u32[]{:S(2)}) collective-permute-start(bf16[2,256,128]{2,1,0:T(8,128)(2,1)S(1)} %collective-permute-done.15.far_mine), channel_id=1, source_target_pairs={{0,16},{16,0},{1,17},{17,1},{2,18},{18,2},{3,19},{19,3},{4,20},{20... | collective-permute-start | bytes 393224 | tf_op jit(solution)/shard_map/ppermute | solution.py:471

commit v6 on v5

--- a/solution.py
+++ b/solution.py
@@ -108,7 +108,10 @@
     return exponent, 1.0 / jnp.sum(exponent, axis=-1, keepdims=True)
 
 
-def backward_stages(lists, core, q_ref, kv_ref, turned_ref, mg_ref, mixed_ref, grads_ref, dk_ref, dv_ref, forward):
+def backward_stages(
+    lists, core, q_ref, kv_ref, turned_ref, mg_ref, mixed_ref, grads_ref, dk_ref, dv_ref, attention_ref=None
+):
+    forward = attention_ref is None
     half = q_ref.shape[1]
     scale = (half // 2) ** (-0.5)
 
@@ -116,16 +119,17 @@
         at = slice(ball * BALL, (ball + 1) * BALL)
         listed = listed_balls(ball, *lists, core)
         stacked, grad = stack_heads(q_ref[at, :]), stack_heads(mg_ref[at, :])
-        scores = dot(stacked, pick(kv_ref, listed, 0, half), ((1,), (1,)))
+        scores = dot(stacked, pick(kv_ref, listed, 0, half), ((1,), (1,))) if forward else None
         weights_grad = dot(grad, pick(kv_ref, listed, half, half), ((1,), (1,)))
         return listed, stacked, grad, scores, weights_grad
 
     def elements(ball, listed, stacked, grad, scores, weights_grad):
-        exponent, inverse = softmax_parts(scores)
-        attention = exponent * inverse
         if forward:
+            exponent, inverse = softmax_parts(scores)
+            attention = exponent * inverse
             inner = jnp.sum(attention * weights_grad, axis=-1, keepdims=True)
         else:
+            attention = attention_ref[ball].astype(F32)
             mixed = mixed_ref[ball * BALL : (ball + 1) * BALL, :].astype(F32)
             inner = jnp.sum(grad.astype(F32) * jnp.concatenate([mixed, mixed], axis=0), axis=-1, keepdims=True)
         scores_grad = attention * (weights_grad - inner)
@@ -252,7 +256,8 @@
 
 
 def first_forward(
-    mine, other, x_other, gain, columns, normed_mine, q_mine, kv_mine, mixed_ref, q_ref, kv_ref, normed_ref
+    mine, other, x_other, gain, columns, normed_mine, q_mine, kv_mine, mixed_ref, q_ref, kv_ref, normed_ref,
+    attention_ref,
 ):
     core = lax.axis_index("pts")
     local, width = x_other.shape
@@ -269,10 +274,12 @@
 
     def elements(ball, listed, scores):
         exponent, inverse = softmax_parts(scores)
-        return listed, exponent.astype(BF), inverse
-
-    def outputs(ball, listed, exponent, inverse):
-        mixed = unstack_heads(dot(exponent, pick(kv_ref, listed, half, half)) * inverse)
+        attention = (exponent * inverse).astype(BF)
+        attention_ref[ball] = attention
+        return listed, attention
+
+    def outputs(ball, listed, attention):
+        mixed = unstack_heads(dot(attention, pick(kv_ref, listed, half, half)))
         mixed_ref[ball * BALL : (ball + 1) * BALL, :] = mixed.astype(BF)
         return ()
 
@@ -329,7 +336,7 @@
         return moved
 
     norm_project(total, rotate, gain_row(gain), columns[...], normed_ref, q_ref, kv_ref)
-    backward_stages((mine, other), core, q_ref, kv_ref, turned_ref, mg_ref, mixed_ref, grads_ref, dk_ref, dv_ref, True)
+    backward_stages((mine, other), core, q_ref, kv_ref, turned_ref, mg_ref, mixed_ref, grads_ref, dk_ref, dv_ref)
 
     def store(at, part):
         part_ref[at] = part.astype(BF)
@@ -346,7 +353,7 @@
 
 def first_backward(
     mine, other, chosen_back, part_mine, part_other, moved, grad, gain_two,
-    mixed_ref, normed, q_ref, kv_ref, out_one, columns,
+    mixed_ref, normed, q_ref, kv_ref, attention_ref, out_one, columns,
     hg_ref, grads_ref, send_ref, part_keep, part_send,
     rows_grad_ref, mg_ref, turned_ref, dk_ref, dv_ref,
 ):
@@ -370,7 +377,9 @@
         return ()
 
     in_stages(total // CHUNK, rotate, project_back)
-    backward_stages((mine, other), core, q_ref, kv_ref, turned_ref, mg_ref, mixed_ref, grads_ref, dk_ref, dv_ref, False)
+    backward_stages(
+        (mine, other), core, q_ref, kv_ref, turned_ref, mg_ref, mixed_ref, grads_ref, dk_ref, dv_ref, attention_ref
+    )
 
     def store(at, part):
         if at.start < local:
@@ -501,8 +510,8 @@
     x_other, one_other, two_other, rot_other, grad_other = lax.optimization_barrier(others)
     one = [mine[0], one_other]
     two = [mine[1], two_other]
-    mixed, q, kv, normed = call(
-        first_forward, [x_other, near_gain, columns_one, normed, q, kv], [thin, thin, wide, wide], lists=one
+    mixed, q, kv, normed, attention = call(
+        first_forward, [x_other, near_gain, columns_one, normed, q, kv], [thin, thin, wide, wide, shape(balls, 2 * BALL, LISTED * BALL)], lists=one
     )
     mixed_other = swap(mixed)
     base, chosen, chosen_back, grads_in, mg = call(
@@ -523,7 +532,8 @@
     received_two = across(send_two, (2, 1))
     hidden_grad, grads_one, send, part_keep, part_send = call(
         first_backward,
-        [chosen_back, part_two, part_two_other, moved, grads_in, far_gain, mixed, normed, q, kv, out_one, columns_one],
+        [chosen_back, part_two, part_two_other, moved, grads_in, far_gain, mixed, normed, q, kv, attention]
+        + [out_one, columns_one],
         [wide, triple, weights, shape(rows, width, dtype=F32), own_rows],
         [wide, thin, turned, blocks, blocks],
         one,

time: 54.9 us -> 54.5 us (level)
  transfers between devices with their start and end apart: 25 -> 25, of which waited for: 6 -> 6; matrix products, arithmetic and copies ran while one was open for 0% -> 0% of each run, Pallas kernels for 22% -> 20%
where the time goes in v6:
time: 54.5 us; the launch traced here: 54.4 us
  starting transfers between devices  27.9 us (51%)
  Pallas kernels  21.5 us (39%)
  waiting for transfers between devices  3.94 us (7%)
  between operations  0.8 us (1%)
    ppermute x12, starting transfers between devices, across(): return lax.ppermute(array, ('pts', 'geo'), pairs)  24 us
    pallas_call x8, Pallas kernels, call(): pl.pallas_call(body, name=getattr(body, 'func', body).__name__, out_shape...  19.9 us
    ppermute x13, starting transfers between devices, swap(): return lax.ppermute(array, 'pts', SWAP)  3.89 us
    ppermute x12, waiting for transfers between devices, across(): return lax.ppermute(array, ('pts', 'geo'), pairs)  3.82 us
    pallas_call x1, Pallas kernels, local(): pl.pallas_call(project_mine, name='project_mine', out_shape=[shape(*a.sha...  1.54 us
  transfers between devices with their start and end apart: 25, of which 6 were waited for; matrix products, arithmetic and copies ran while one was open for 0% of the time, Pallas kernels for 20%

profile of v6, /device:TPU:0, one launch (start us, length us, event | category | flops | bytes accessed | tf_op | source)
XLA Modules:
  0.0 54.4 jit_solution(9546892517105287874)
XLA Ops:
  0.6 0.5 collective-permute-start
  1.2 0.4 collective-permute-start.3
  1.7 0.4 collective-permute-start.2
  2.2 1.5 %project_mine.1 = (bf16[512,256]{1,0:T(8,128)(2,1)S(1)}, bf16[512,256]{1,0:T(8,128)(2,1)S(1)}, s32[4,128]{1,0:T(4,128)S(1)}, s32[1,4,4]{2,1,0:T(4,128)S(1)}, s32...) custom-call(bf16[512,256]{1,0:T(8,128)(2,1)} %bitcast.8, ...), custom_call_target="tpu_custom_call" | custom-call | tf_op jit(solution)/shard_map/project_mine/pallas_call | solution.py:500
  3.8 3.1 %first_forward.1 = (bf16[1024,128]{1,0:T(8,128)(2,1)S(1)}, bf16[1024,128]{1,0:T(8,128)(2,1)S(1)}, bf16[1024,256]{1,0:T(8,128)(2,1)S(1)}, bf16[1024,256]{1,0:T(8,128)(2,1)S(1)}, bf16[8,256,512]{2,1,0:T(8,128)(2,1)S(1)}) custom-call(s32[1,4,4]{2,1,0:T(4,128)S(1)} %get-tuple-element.63.mine, s32[1,4,4]{2,1,0:T(4,128)S(1)} %collective-permute-done.1.other, ...), custom_call_target="tpu_custom_call" | custom-call | tf_op jit(solution)/shard_map/first_forward/pallas_call | solution.py:441
  7.0 1.4 %before_second.1 = (f32[1024,256]{1,0:T(8,128)S(1)}, bf16[1024,1024]{1,0:T(8,128)(2,1)S(1)}, bf16[1024,1024]{1,0:T(8,128)(2,1)S(1)}, bf16[1024,256]{1,0:T(8,128)(2,1)S(1)}, bf16[1024,128]{1,0:T(8,128)(2,1)S(1)}) custom-call(s32[4,128]{1,0:T(4,128)S(1)} %get-tuple-element.72.rot_mine, s32[4,128]{1,0:T(4,128)S(1)} %collective-permute-done.3.rot_other, ...), custom_call_target="tpu_custom_call" | custom-call | tf_op jit(solution)/shard_map/before_second/pallas_call | solution.py:441
  8.4 6.4 %second_layer.1 = (bf16[1024,256]{1,0:T(8,128)(2,1)S(1)}, bf16[1024,256]{1,0:T(8,128)(2,1)S(1)}, bf16[1024,128]{1,0:T(8,128)(2,1)S(1)}, bf16[512,128]{1,0:T(8,12...) custom-call(s32[1,4,4]{2,1,0:T(4,128)S(1)} %get-tuple-element.81.mine, ...), custom_call_target="tpu_custom_call" | custom-call | tf_op jit(solution)/shard_map/second_layer/pallas_call | solution.py:441
  14.9 0.4 collective-permute-start.6
  15.3 0.6 %second_weights.1 = (bf16[2,256,128]{2,1,0:T(8,128)(2,1)S(1)}, bf16[2,256,128]{2,1,0:T(8,128)(2,1)S(1)}) custom-call(bf16[1024,256]{1,0:T(8,128)(2,1)S(1)} %get-tuple-element.103.normed, bf16[1024,384]{1,0:T(8,128)(2,1)S(1)} %get-tuple-element.104.grads, bf16[1024,128]{1,0:T(8,128)(2,1)S(1)} %get-tuple-element.98.mixed_two.mixed, ...), custom_call_target="tpu_custom_call" | custom-call | tf_op jit(solution)/shard_map/second_weights/pallas_call | solution.py:441
  15.9 2.7 %collective-permute-start.9 = (bf16[2,256,128]{2,1,0:T(8,128)(2,1)S(1)}, bf16[2,256,128]{2,1,0:T(8,128)(2,1)S(1)}, u32[]{:S(2)}, u32[]{:S(2)}) collective-permute-start(bf16[2,256,128]{2,1,0:T(8,128)(2,1)S(1)} %get-tuple-element.105), channel_id=1, source_target_pairs={{0,18},{17,3},{18,0},{3,17},{20,6},{5,23},{6,20},{23,5},{24,10},{9... | collective-permute-start | bytes 393224 | tf_op jit(solution)/shard_map/ppermute | solution.py:487
  18.6 4.9 %first_backward.1 = (bf16[1024,256]{1,0:T(8,128)(2,1)S(1)}, bf16[1024,384]{1,0:T(8,128)(2,1)S(1)}, bf16[2,256,128]{2,1,0:T(8,128)(2,1)S(1)}, f32[512,256]{1,0:T(8,128)S(1)}, bf16[512,256]{1,0:T(8,128)(2,1)S(1)}) custom-call(s32[1,4,4]{2,1,0:T(4,128)S(1)} %get-tuple-element.63.mine, s32[1,4,4]{2,1,0:T(4,128)S(1)} %collective-permute-done.1.other, ...), custom_call_target="tpu_custom_call" | custom-call | tf_op jit(solution)/shard_map/first_backward/pallas_call | solution.py:441
  23.7 0.4 collective-permute-start.8
  24.1 1.2 %collective-permute-start.10 = (bf16[2,256,128]{2,1,0:T(8,128)(2,1)S(1)}, bf16[2,256,128]{2,1,0:T(8,128)(2,1)S(1)}, u32[]{:S(2)}, u32[]{:S(2)}) collective-permute-start(bf16[2,256,128]{2,1,0:T(8,128)(2,1)S(1)} %get-tuple-element.107), channel_id=1, source_target_pairs={{0,18},{17,3},{18,0},{3,17},{20,6},{5,23},{6,20},{23,5},{24,10},{9... | collective-permute-start | bytes 393224 | tf_op jit(solution)/shard_map/ppermute | solution.py:487
  25.3 1.2 %collective-permute-start.18 = (bf16[1,256,128]{2,1,0:T(8,128)(2,1)S(1)}, bf16[1,256,128]{2,1,0:T(8,128)(2,1)S(1)}, u32[]{:S(2)}, u32[]{:S(2)}) collective-permute-start(bf16[1,256,128]{2,1,0:T(8,128)(2,1)S(1)} %slice.19), channel_id=1, source_target_pairs={{0,17},{17,0},{18,3},{3,18},{20,5},{5,20},{6,23},{23,6},{24,9},{9,... | collective-permute-start | bytes 196616 | tf_op jit(solution)/shard_map/ppermute | solution.py:487
  26.5 1.4 %finish_rows.1 = (bf16[2,256,128]{2,1,0:T(8,128)(2,1)S(1)}, bf16[512,256]{1,0:T(8,128)(2,1)}, bf16[512,256]{1,0:T(8,128)(2,1)}) custom-call(bf16[1024,256]{1,0:T(8,128)(2,1)S(1)} %get-tuple-element.71.normed, bf16[1024,384]{1,0:T(8,128)(2,1)S(1)} %get-tuple-element.94.grads, bf16[1024,128]{1,0:T(8,128)(2,1)S(1)} %get-tuple-element.75.mixed.mixed_ref, ...), custom_call_target="tpu_custom_call" | custom-call | tf_op jit(solution)/shard_map/finish_rows/pallas_call | solution.py:441
  27.9 0.6 %collective-permute-done.10 = bf16[2,256,128]{2,1,0:T(8,128)(2,1)S(1)} collective-permute-done((bf16[2,256,128]{2,1,0:T(8,128)(2,1)S(1)}, bf16[2,256,128]{2,1,0:T(8,128)(2,1)S(1)}, u32[]{:S(2)}, u32[]{:S(2)}) %collective-permute-start.10) | collective-permute-done | bytes 131104 | tf_op jit(solution)/shard_map/ppermute | solution.py:487
  28.5 2.0 %collective-permute-start.11 = (bf16[1,256,128]{2,1,0:T(8,128)(2,1)S(1)}, bf16[1,256,128]{2,1,0:T(8,128)(2,1)S(1)}, u32[]{:S(2)}, u32[]{:S(2)}) collective-permute-start(bf16[1,256,128]{2,1,0:T(8,128)(2,1)S(1)} %slice.17), channel_id=1, source_target_pairs={{0,17},{17,0},{18,3},{3,18},{20,5},{5,20},{6,23},{23,6},{24,9},{9,... | collective-permute-start | bytes 196616 | tf_op jit(solution)/shard_map/ppermute | solution.py:487
  30.6 1.4 %collective-permute-start.19 = (bf16[1,256,128]{2,1,0:T(8,128)(2,1)S(1)}, bf16[1,256,128]{2,1,0:T(8,128)(2,1)S(1)}, u32[]{:S(2)}, u32[]{:S(2)}) collective-permute-start(bf16[1,256,128]{2,1,0:T(8,128)(2,1)S(1)} %add_convert_fusion.4), channel_id=1, source_target_pairs={{0,20},{17,5},{18,6},{3,23},{20,0},{5,17},{6,18},{23,3},{24,12},{9... | collective-permute-start | bytes 196616 | tf_op jit(solution)/shard_map/ppermute | solution.py:487
  32.0 0.5 collective-permute-done.11
  32.5 1.9 %collective-permute-start.12 = (bf16[1,256,128]{2,1,0:T(8,128)(2,1)S(1)}, bf16[1,256,128]{2,1,0:T(8,128)(2,1)S(1)}, u32[]{:S(2)}, u32[]{:S(2)}) collective-permute-start(bf16[1,256,128]{2,1,0:T(8,128)(2,1)S(1)} %add_convert_fusion.7), channel_id=1, source_target_pairs={{0,20},{17,5},{18,6},{3,23},{20,0},{5,17},{6,18},{23,3},{24,12},{9... | collective-permute-start | bytes 196616 | tf_op jit(solution)/shard_map/ppermute | solution.py:487
  34.5 2.9 %collective-permute-start.20 = (bf16[1,256,128]{2,1,0:T(8,128)(2,1)S(1)}, bf16[1,256,128]{2,1,0:T(8,128)(2,1)S(1)}, u32[]{:S(2)}, u32[]{:S(2)}) collective-permute-start(bf16[1,256,128]{2,1,0:T(8,128)(2,1)S(1)} %add_convert_fusion.3), channel_id=1, source_target_pairs={{0,24},{17,9},{18,10},{3,27},{20,12},{5,29},{6,30},{23,15},{24,0},... | collective-permute-start | bytes 196616 | tf_op jit(solution)/shard_map/ppermute | solution.py:487
  37.3 2.4 %collective-permute-start.13 = (bf16[1,256,128]{2,1,0:T(8,128)(2,1)S(1)}, bf16[1,256,128]{2,1,0:T(8,128)(2,1)S(1)}, u32[]{:S(2)}, u32[]{:S(2)}) collective-permute-start(bf16[1,256,128]{2,1,0:T(8,128)(2,1)S(1)} %add_convert_fusion.6), channel_id=1, source_target_pairs={{0,24},{17,9},{18,10},{3,27},{20,12},{5,29},{6,30},{23,15},{24,0},... | collective-permute-start | bytes 196616 | tf_op jit(solution)/shard_map/ppermute | solution.py:487
  39.8 2.0 %collective-permute-start.21 = (bf16[1,256,128]{2,1,0:T(8,128)(2,1)S(1)}, bf16[1,256,128]{2,1,0:T(8,128)(2,1)S(1)}, u32[]{:S(2)}, u32[]{:S(2)}) collective-permute-start(bf16[1,256,128]{2,1,0:T(8,128)(2,1)S(1)} %add_convert_fusion.2), channel_id=1, source_target_pairs={{0,17},{17,0},{18,3},{3,18},{20,5},{5,20},{6,23},{23,6},{24,9},{9,... | collective-permute-start | bytes 196616 | tf_op jit(solution)/shard_map/ppermute | solution.py:487
  42.0 1.8 %collective-permute-start.14 = (bf16[1,256,128]{2,1,0:T(8,128)(2,1)S(1)}, bf16[1,256,128]{2,1,0:T(8,128)(2,1)S(1)}, u32[]{:S(2)}, u32[]{:S(2)}) collective-permute-start(bf16[1,256,128]{2,1,0:T(8,128)(2,1)S(1)} %add_convert_fusion.5), channel_id=1, source_target_pairs={{0,17},{17,0},{18,3},{3,18},{20,5},{5,20},{6,23},{23,6},{24,9},{9,... | collective-permute-start | bytes 196616 | tf_op jit(solution)/shard_map/ppermute | solution.py:487
  43.8 1.7 %collective-permute-start.22 = (bf16[2,256,128]{2,1,0:T(8,128)(2,1)S(1)}, bf16[2,256,128]{2,1,0:T(8,128)(2,1)S(1)}, u32[]{:S(2)}, u32[]{:S(2)}) collective-permute-start(bf16[2,256,128]{2,1,0:T(8,128)(2,1)S(1)} %pad_maximum_fusion.1.near_mine), channel_id=1, source_target_pairs={{0,18},{17,3},{18,0},{3,17},{20,6},{5,23},{6,20},{23,5},{24,10},{9... | collective-permute-start | bytes 393224 | tf_op jit(solution)/shard_map/ppermute | solution.py:487
  45.5 0.3 collective-permute-done.14
  45.8 3.0 %collective-permute-start.15 = (bf16[2,256,128]{2,1,0:T(8,128)(2,1)S(1)}, bf16[2,256,128]{2,1,0:T(8,128)(2,1)S(1)}, u32[]{:S(2)}, u32[]{:S(2)}) collective-permute-start(bf16[2,256,128]{2,1,0:T(8,128)(2,1)S(1)} %pad_maximum_fusion.near_mine), channel_id=1, source_target_pairs={{0,18},{17,3},{18,0},{3,17},{20,6},{5,23},{6,20},{23,5},{24,10},{9... | collective-permute-start | bytes 393224 | tf_op jit(solution)/shard_map/ppermute | solution.py:487
  48.8 0.5 collective-permute-start.24
  49.3 2.1 %collective-permute-done.15.far_mine = bf16[2,256,128]{2,1,0:T(8,128)(2,1)S(1)} collective-permute-done((bf16[2,256,128]{2,1,0:T(8,128)(2,1)S(1)}, bf16[2,256,128]{2,1,0:T(8,128)(2,1)S(1)}, u32[]{:S(2)}, u32[]{:S(2)}) %collective-permute-start.15) | collective-permute-done | bytes 131104 | tf_op jit(solution)/shard_map/ppermute | solution.py:487
  51.5 0.7 %collective-permute-start.17 = (bf16[2,256,128]{2,1,0:T(8,128)(2,1)S(1)}, bf16[2,256,128]{2,1,0:T(8,128)(2,1)S(1)}, u32[]{:S(2)}, u32[]{:S(2)}) collective-permute-start(bf16[2,256,128]{2,1,0:T(8,128)(2,1)S(1)} %collective-permute-done.15.far_mine), channel_id=1, source_target_pairs={{0,16},{16,0},{1,17},{17,1},{2,18},{18,2},{3,19},{19,3},{4,20},{20... | collective-permute-start | bytes 393224 | tf_op jit(solution)/shard_map/ppermute | solution.py:480
  52.2 1.1 %finish_weights.3 = (f32[1,256]{1,0:T(1,128)}, f32[256,768]{1,0:T(8,128)}, f32[256,256]{1,0:T(8,128)}) custom-call(bf16[2,256,128]{2,1,0:T(8,128)(2,1)S(1)} %pad_maximum_fusion.1.near_mine, bf16[2,256,128]{2,1,0:T(8,128)(2,1)S(1)} %collective-permute-done.22.far_mine, bf16[2,256,128]{2,1,0:T(8,128)(2,1)S(1)} %collective-permute-done.23.near_other, ...), custom_call_target="tpu_custom_call" | custom-call | tf_op jit(solution)/shard_map/finish_weights/pallas_call | solution.py:441
  53.3 1.1 %finish_weights.2 = (f32[1,256]{1,0:T(1,128)}, f32[256,768]{1,0:T(8,128)}, f32[256,256]{1,0:T(8,128)}) custom-call(bf16[2,256,128]{2,1,0:T(8,128)(2,1)S(1)} %pad_maximum_fusion.near_mine, bf16[2,256,128]{2,1,0:T(8,128)(2,1)S(1)} %collective-permute-done.15.far_mine, bf16[2,256,128]{2,1,0:T(8,128)(2,1)S(1)} %collective-permute-done.16.near_other, ...), custom_call_target="tpu_custom_call" | custom-call | tf_op jit(solution)/shard_map/finish_weights/pallas_call | solution.py:441
  (43 shorter events, 1.2 us)
Async XLA Ops:
  0.6 3.1 %collective-permute-start = (bf16[512,256]{1,0:T(8,128)(2,1)}, bf16[512,256]{1,0:T(8,128)(2,1)S(1)}, u32[]{:S(2)}, u32[]{:S(2)}) collective-permute-start(bf16[512,256]{1,0:T(8,128)(2,1)} %bitcast.7), channel_id=1, source_target_pairs={{0,16},{16,0},{1,17},{17,1},{2,18},{18,2},{3,19},{19,3},{4,20},{20... | collective-permute-start | bytes 786440 | tf_op jit(solution)/shard_map/ppermute | solution.py:480
  1.2 2.6 %collective-permute-start.4 = (bf16[512,256]{1,0:T(8,128)(2,1)}, bf16[512,256]{1,0:T(8,128)(2,1)S(1)}, u32[]{:S(2)}, u32[]{:S(2)}) collective-permute-start(bf16[512,256]{1,0:T(8,128)(2,1)} %bitcast.9), channel_id=1, source_target_pairs={{0,16},{16,0},{1,17},{17,1},{2,18},{18,2},{3,19},{19,3},{4,20},{20... | collective-permute-start | bytes 786440 | tf_op jit(solution)/shard_map/ppermute | solution.py:480
  1.2 2.5 %collective-permute-start.3 = (s32[4,128]{1,0:T(4,128)}, s32[4,128]{1,0:T(4,128)S(1)}, u32[]{:S(2)}, u32[]{:S(2)}) collective-permute-start(s32[4,128]{1,0:T(4,128)} %bitcast.11), channel_id=1, source_target_pairs={{0,16},{16,0},{1,17},{17,1},{2,18},{18,2},{3,19},{19,3},{4,20},{20... | collective-permute-start | bytes 6152 | tf_op jit(solution)/shard_map/ppermute | solution.py:480
  1.7 2.1 %collective-permute-start.1 = (s32[1,4,4]{2,1,0:T(4,128)}, s32[1,4,4]{2,1,0:T(4,128)S(1)}, u32[]{:S(2)}, u32[]{:S(2)}) collective-permute-start(s32[1,4,4]{2,1,0:T(4,128)} %lists_one_hbm.1), channel_id=1, source_target_pairs={{0,16},{16,0},{1,17},{17,1},{2,18},{18,2},{3,19},{19,3},{4,20},{20... | collective-permute-start | bytes 200 | tf_op jit(solution)/shard_map/ppermute | solution.py:480
  1.7 2.0 %collective-permute-start.2 = (s32[1,4,4]{2,1,0:T(4,128)}, s32[1,4,4]{2,1,0:T(4,128)S(1)}, u32[]{:S(2)}, u32[]{:S(2)}) collective-permute-start(s32[1,4,4]{2,1,0:T(4,128)} %lists_two_hbm.1), channel_id=1, source_target_pairs={{0,16},{16,0},{1,17},{17,1},{2,18},{18,2},{3,19},{19,3},{4,20},{20... | collective-permute-start | bytes 200 | tf_op jit(solution)/shard_map/ppermute | solution.py:480
  6.8 1.6 %collective-permute-start.5 = (bf16[1024,128]{1,0:T(8,128)(2,1)S(1)}, bf16[1024,128]{1,0:T(8,128)(2,1)S(1)}, u32[]{:S(2)}, u32[]{:S(2)}) collective-permute-start(bf16[1024,128]{1,0:T(8,128)(2,1)S(1)} %get-tuple-element.75.mixed.mixed_ref), channel_id=1, source_target_pairs={{0,16},{16,0},{1,17},{17,1},{2,18},{18,2},{3,19},{19,3},{4,20},{20... | collective-permute-start | bytes 786440 | tf_op jit(solution)/shard_map/ppermute | solution.py:480
  14.9 3.8 %collective-permute-start.6 = (bf16[1024,256]{1,0:T(8,128)(2,1)S(1)}, bf16[1024,256]{1,0:T(8,128)(2,1)S(1)}, u32[]{:S(2)}, u32[]{:S(2)}) collective-permute-start(bf16[1024,256]{1,0:T(8,128)(2,1)S(1)} %get-tuple-element.88.part_mine), channel_id=1, source_target_pairs={{0,16},{16,0},{1,17},{17,1},{2,18},{18,2},{3,19},{19,3},{4,20},{20... | collective-permute-start | bytes 1572872 | tf_op jit(solution)/shard_map/ppermute | solution.py:480
  15.9 8.2 %collective-permute-start.9 = (bf16[2,256,128]{2,1,0:T(8,128)(2,1)S(1)}, bf16[2,256,128]{2,1,0:T(8,128)(2,1)S(1)}, u32[]{:S(2)}, u32[]{:S(2)}) collective-permute-start(bf16[2,256,128]{2,1,0:T(8,128)(2,1)S(1)} %get-tuple-element.105), channel_id=1, source_target_pairs={{0,18},{17,3},{18,0},{3,17},{20,6},{5,23},{6,20},{23,5},{24,10},{9... | collective-permute-start | bytes 393224 | tf_op jit(solution)/shard_map/ppermute | solution.py:487
  23.5 3.0 %collective-permute-start.7 = (bf16[512,256]{1,0:T(8,128)(2,1)S(1)}, bf16[512,256]{1,0:T(8,128)(2,1)S(1)}, u32[]{:S(2)}, u32[]{:S(2)}) collective-permute-start(bf16[512,256]{1,0:T(8,128)(2,1)S(1)} %get-tuple-element.97), channel_id=1, source_target_pairs={{0,16},{16,0},{1,17},{17,1},{2,18},{18,2},{3,19},{19,3},{4,20},{20... | collective-permute-start | bytes 786440 | tf_op jit(solution)/shard_map/ppermute | solution.py:480
  23.7 2.8 %collective-permute-start.8 = (bf16[512,128]{1,0:T(8,128)(2,1)S(1)}, bf16[512,128]{1,0:T(8,128)(2,1)S(1)}, u32[]{:S(2)}, u32[]{:S(2)}) collective-permute-start(bf16[512,128]{1,0:T(8,128)(2,1)S(1)} %get-tuple-element.99), channel_id=1, source_target_pairs={{0,16},{16,0},{1,17},{17,1},{2,18},{18,2},{3,19},{19,3},{4,20},{20... | collective-permute-start | bytes 393224 | tf_op jit(solution)/shard_map/ppermute | solution.py:480
  24.1 4.4 %collective-permute-start.10 = (bf16[2,256,128]{2,1,0:T(8,128)(2,1)S(1)}, bf16[2,256,128]{2,1,0:T(8,128)(2,1)S(1)}, u32[]{:S(2)}, u32[]{:S(2)}) collective-permute-start(bf16[2,256,128]{2,1,0:T(8,128)(2,1)S(1)} %get-tuple-element.107), channel_id=1, source_target_pairs={{0,18},{17,3},{18,0},{3,17},{20,6},{5,23},{6,20},{23,5},{24,10},{9... | collective-permute-start | bytes 393224 | tf_op jit(solution)/shard_map/ppermute | solution.py:487
  25.3 5.2 %collective-permute-start.18 = (bf16[1,256,128]{2,1,0:T(8,128)(2,1)S(1)}, bf16[1,256,128]{2,1,0:T(8,128)(2,1)S(1)}, u32[]{:S(2)}, u32[]{:S(2)}) collective-permute-start(bf16[1,256,128]{2,1,0:T(8,128)(2,1)S(1)} %slice.19), channel_id=1, source_target_pairs={{0,17},{17,0},{18,3},{3,18},{20,5},{5,20},{6,23},{23,6},{24,9},{9,... | collective-permute-start | bytes 196616 | tf_op jit(solution)/shard_map/ppermute | solution.py:487
  27.9 24.3 %copy-start = (bf16[256,768]{1,0:T(8,128)(2,1)S(1)}, bf16[256,768]{1,0:T(8,128)(2,1)}, u32[]{:S(2)}) copy-start(bf16[256,768]{1,0:T(8,128)(2,1)} %weight.3) | copy-start | bytes 1179652
  27.9 25.4 %copy-start.1 = (bf16[256,768]{1,0:T(8,128)(2,1)S(1)}, bf16[256,768]{1,0:T(8,128)(2,1)}, u32[]{:S(2)}) copy-start(bf16[256,768]{1,0:T(8,128)(2,1)} %weight.2) | copy-start | bytes 1179652
  28.5 4.0 %collective-permute-start.11 = (bf16[1,256,128]{2,1,0:T(8,128)(2,1)S(1)}, bf16[1,256,128]{2,1,0:T(8,128)(2,1)S(1)}, u32[]{:S(2)}, u32[]{:S(2)}) collective-permute-start(bf16[1,256,128]{2,1,0:T(8,128)(2,1)S(1)} %slice.17), channel_id=1, source_target_pairs={{0,17},{17,0},{18,3},{3,18},{20,5},{5,20},{6,23},{23,6},{24,9},{9,... | collective-permute-start | bytes 196616 | tf_op jit(solution)/shard_map/ppermute | solution.py:487
  30.6 3.9 %collective-permute-start.19 = (bf16[1,256,128]{2,1,0:T(8,128)(2,1)S(1)}, bf16[1,256,128]{2,1,0:T(8,128)(2,1)S(1)}, u32[]{:S(2)}, u32[]{:S(2)}) collective-permute-start(bf16[1,256,128]{2,1,0:T(8,128)(2,1)S(1)} %add_convert_fusion.4), channel_id=1, source_target_pairs={{0,20},{17,5},{18,6},{3,23},{20,0},{5,17},{6,18},{23,3},{24,12},{9... | collective-permute-start | bytes 196616 | tf_op jit(solution)/shard_map/ppermute | solution.py:487
  32.5 4.8 %collective-permute-start.12 = (bf16[1,256,128]{2,1,0:T(8,128)(2,1)S(1)}, bf16[1,256,128]{2,1,0:T(8,128)(2,1)S(1)}, u32[]{:S(2)}, u32[]{:S(2)}) collective-permute-start(bf16[1,256,128]{2,1,0:T(8,128)(2,1)S(1)} %add_convert_fusion.7), channel_id=1, source_target_pairs={{0,20},{17,5},{18,6},{3,23},{20,0},{5,17},{6,18},{23,3},{24,12},{9... | collective-permute-start | bytes 196616 | tf_op jit(solution)/shard_map/ppermute | solution.py:487
  34.5 5.3 %collective-permute-start.20 = (bf16[1,256,128]{2,1,0:T(8,128)(2,1)S(1)}, bf16[1,256,128]{2,1,0:T(8,128)(2,1)S(1)}, u32[]{:S(2)}, u32[]{:S(2)}) collective-permute-start(bf16[1,256,128]{2,1,0:T(8,128)(2,1)S(1)} %add_convert_fusion.3), channel_id=1, source_target_pairs={{0,24},{17,9},{18,10},{3,27},{20,12},{5,29},{6,30},{23,15},{24,0},... | collective-permute-start | bytes 196616 | tf_op jit(solution)/shard_map/ppermute | solution.py:487
  37.3 4.7 %collective-permute-start.13 = (bf16[1,256,128]{2,1,0:T(8,128)(2,1)S(1)}, bf16[1,256,128]{2,1,0:T(8,128)(2,1)S(1)}, u32[]{:S(2)}, u32[]{:S(2)}) collective-permute-start(bf16[1,256,128]{2,1,0:T(8,128)(2,1)S(1)} %add_convert_fusion.6), channel_id=1, source_target_pairs={{0,24},{17,9},{18,10},{3,27},{20,12},{5,29},{6,30},{23,15},{24,0},... | collective-permute-start | bytes 196616 | tf_op jit(solution)/shard_map/ppermute | solution.py:487
  39.8 4.0 %collective-permute-start.21 = (bf16[1,256,128]{2,1,0:T(8,128)(2,1)S(1)}, bf16[1,256,128]{2,1,0:T(8,128)(2,1)S(1)}, u32[]{:S(2)}, u32[]{:S(2)}) collective-permute-start(bf16[1,256,128]{2,1,0:T(8,128)(2,1)S(1)} %add_convert_fusion.2), channel_id=1, source_target_pairs={{0,17},{17,0},{18,3},{3,18},{20,5},{5,20},{6,23},{23,6},{24,9},{9,... | collective-permute-start | bytes 196616 | tf_op jit(solution)/shard_map/ppermute | solution.py:487
  42.0 3.8 %collective-permute-start.14 = (bf16[1,256,128]{2,1,0:T(8,128)(2,1)S(1)}, bf16[1,256,128]{2,1,0:T(8,128)(2,1)S(1)}, u32[]{:S(2)}, u32[]{:S(2)}) collective-permute-start(bf16[1,256,128]{2,1,0:T(8,128)(2,1)S(1)} %add_convert_fusion.5), channel_id=1, source_target_pairs={{0,17},{17,0},{18,3},{3,18},{20,5},{5,20},{6,23},{23,6},{24,9},{9,... | collective-permute-start | bytes 196616 | tf_op jit(solution)/shard_map/ppermute | solution.py:487
  43.8 5.0 %collective-permute-start.22 = (bf16[2,256,128]{2,1,0:T(8,128)(2,1)S(1)}, bf16[2,256,128]{2,1,0:T(8,128)(2,1)S(1)}, u32[]{:S(2)}, u32[]{:S(2)}) collective-permute-start(bf16[2,256,128]{2,1,0:T(8,128)(2,1)S(1)} %pad_maximum_fusion.1.near_mine), channel_id=1, source_target_pairs={{0,18},{17,3},{18,0},{3,17},{20,6},{5,23},{6,20},{23,5},{24,10},{9... | collective-permute-start | bytes 393224 | tf_op jit(solution)/shard_map/ppermute | solution.py:487
  45.8 5.7 %collective-permute-start.15 = (bf16[2,256,128]{2,1,0:T(8,128)(2,1)S(1)}, bf16[2,256,128]{2,1,0:T(8,128)(2,1)S(1)}, u32[]{:S(2)}, u32[]{:S(2)}) collective-permute-start(bf16[2,256,128]{2,1,0:T(8,128)(2,1)S(1)} %pad_maximum_fusion.near_mine), channel_id=1, source_target_pairs={{0,18},{17,3},{18,0},{3,17},{20,6},{5,23},{6,20},{23,5},{24,10},{9... | collective-permute-start | bytes 393224 | tf_op jit(solution)/shard_map/ppermute | solution.py:487
  48.8 3.4 %collective-permute-start.23 = (bf16[2,256,128]{2,1,0:T(8,128)(2,1)S(1)}, bf16[2,256,128]{2,1,0:T(8,128)(2,1)S(1)}, u32[]{:S(2)}, u32[]{:S(2)}) collective-permute-start(bf16[2,256,128]{2,1,0:T(8,128)(2,1)S(1)} %pad_maximum_fusion.1.near_mine), channel_id=1, source_target_pairs={{0,16},{16,0},{1,17},{17,1},{2,18},{18,2},{3,19},{19,3},{4,20},{20... | collective-permute-start | bytes 393224 | tf_op jit(solution)/shard_map/ppermute | solution.py:480
  48.8 3.4 %collective-permute-start.24 = (bf16[2,256,128]{2,1,0:T(8,128)(2,1)S(1)}, bf16[2,256,128]{2,1,0:T(8,128)(2,1)S(1)}, u32[]{:S(2)}, u32[]{:S(2)}) collective-permute-start(bf16[2,256,128]{2,1,0:T(8,128)(2,1)S(1)} %collective-permute-done.22.far_mine), channel_id=1, source_target_pairs={{0,16},{16,0},{1,17},{17,1},{2,18},{18,2},{3,19},{19,3},{4,20},{20... | collective-permute-start | bytes 393224 | tf_op jit(solution)/shard_map/ppermute | solution.py:480
  49.3 4.0 %collective-permute-start.16 = (bf16[2,256,128]{2,1,0:T(8,128)(2,1)S(1)}, bf16[2,256,128]{2,1,0:T(8,128)(2,1)S(1)}, u32[]{:S(2)}, u32[]{:S(2)}) collective-permute-start(bf16[2,256,128]{2,1,0:T(8,128)(2,1)S(1)} %pad_maximum_fusion.near_mine), channel_id=1, source_target_pairs={{0,16},{16,0},{1,17},{17,1},{2,18},{18,2},{3,19},{19,3},{4,20},{20... | collective-permute-start | bytes 393224 | tf_op jit(solution)/shard_map/ppermute | solution.py:480
  51.5 1.8 %collective-permute-start.17 = (bf16[2,256,128]{2,1,0:T(8,128)(2,1)S(1)}, bf16[2,256,128]{2,1,0:T(8,128)(2,1)S(1)}, u32[]{:S(2)}, u32[]{:S(2)}) collective-permute-start(bf16[2,256,128]{2,1,0:T(8,128)(2,1)S(1)} %collective-permute-done.15.far_mine), channel_id=1, source_target_pairs={{0,16},{16,0},{1,17},{17,1},{2,18},{18,2},{3,19},{19,3},{4,20},{20... | collective-permute-start | bytes 393224 | tf_op jit(solution)/shard_map/ppermute | solution.py:480

commit v7 on v6

--- a/solution.py
+++ b/solution.py
@@ -108,47 +108,57 @@
     return exponent, 1.0 / jnp.sum(exponent, axis=-1, keepdims=True)
 
 
+def forward_stages(lists, core, q_ref, kv_ref, attention_ref, mixed_ref):
+    half = q_ref.shape[1]
+
+    def products(ball):
+        listed = listed_balls(ball, *lists, core)
+        stacked = stack_heads(q_ref[ball * BALL : (ball + 1) * BALL, :])
+        return listed, dot(stacked, pick(kv_ref, listed, 0, half), ((1,), (1,)))
+
+    def elements(ball, listed, scores):
+        exponent, inverse = softmax_parts(scores)
+        attention = (exponent * inverse).astype(BF)
+        attention_ref[ball] = attention
+        return listed, attention
+
+    def outputs(ball, listed, attention):
+        mixed = unstack_heads(dot(attention, pick(kv_ref, listed, half, half)))
+        mixed_ref[ball * BALL : (ball + 1) * BALL, :] = mixed.astype(BF)
+        return ()
+
+    return products, elements, outputs
+
+
 def backward_stages(
-    lists, core, q_ref, kv_ref, turned_ref, mg_ref, mixed_ref, grads_ref, dk_ref, dv_ref, attention_ref=None
-):
-    forward = attention_ref is None
+    lists, core, q_ref, kv_ref, turned_ref, mg_ref, mixed_ref, grads_ref, dk_ref, dv_ref, attention_ref
+):
     half = q_ref.shape[1]
     scale = (half // 2) ** (-0.5)
 
     def products(ball):
+        listed = listed_balls(ball, *lists, core)
+        grad = stack_heads(mg_ref[ball * BALL : (ball + 1) * BALL, :])
+        return listed, grad, dot(grad, pick(kv_ref, listed, half, half), ((1,), (1,)))
+
+    def elements(ball, listed, grad, weights_grad):
+        mixed = mixed_ref[ball * BALL : (ball + 1) * BALL, :].astype(F32)
+        inner = jnp.sum(grad.astype(F32) * jnp.concatenate([mixed, mixed], axis=0), axis=-1, keepdims=True)
+        attention = attention_ref[ball]
+        return listed, grad, attention, (attention.astype(F32) * (weights_grad - inner)).astype(BF)
+
+    def gradients(ball, listed, grad, attention, scores_grad):
         at = slice(ball * BALL, (ball + 1) * BALL)
-        listed = listed_balls(ball, *lists, core)
-        stacked, grad = stack_heads(q_ref[at, :]), stack_heads(mg_ref[at, :])
-        scores = dot(stacked, pick(kv_ref, listed, 0, half), ((1,), (1,))) if forward else None
-        weights_grad = dot(grad, pick(kv_ref, listed, half, half), ((1,), (1,)))
-        return listed, stacked, grad, scores, weights_grad
-
-    def elements(ball, listed, stacked, grad, scores, weights_grad):
-        if forward:
-            exponent, inverse = softmax_parts(scores)
-            attention = exponent * inverse
-            inner = jnp.sum(attention * weights_grad, axis=-1, keepdims=True)
-        else:
-            attention = attention_ref[ball].astype(F32)
-            mixed = mixed_ref[ball * BALL : (ball + 1) * BALL, :].astype(F32)
-            inner = jnp.sum(grad.astype(F32) * jnp.concatenate([mixed, mixed], axis=0), axis=-1, keepdims=True)
-        scores_grad = attention * (weights_grad - inner)
-        return listed, stacked, grad, attention.astype(BF), scores_grad.astype(BF)
-
-    def gradients(ball, listed, stacked, grad, attention, scores_grad):
-        at = slice(ball * BALL, (ball + 1) * BALL)
-        if forward:
-            mixed_ref[at, :] = combine(pick_turned(turned_ref, listed, half, half), attention).astype(BF)
         queries_grad = combine(pick_turned(turned_ref, listed, 0, half), scores_grad) * scale
         grads_ref[at, :half] = queries_grad.astype(BF)
-        add_listed(dk_ref, listed, dot(stacked, scores_grad, ((0,), (0,))))
+        add_listed(dk_ref, listed, dot(stack_heads(q_ref[at, :]), scores_grad, ((0,), (0,))))
         add_listed(dv_ref, listed, dot(grad, attention, ((0,), (0,))))
         return ()
 
     turn_balls(turned_ref, kv_ref)
     dk_ref[...] = jnp.zeros_like(dk_ref)
     dv_ref[...] = jnp.zeros_like(dv_ref)
-    in_stages(q_ref.shape[0] // BALL, products, elements, gradients)
+    return products, elements, gradients
 
 
 def add_listed(ref, listed, part):
@@ -266,24 +276,8 @@
     norm_project(
         local, lambda at: x_other[at].astype(F32), gain_row(gain), columns[...], normed_ref, q_ref, kv_ref, local
     )
-
-    def products(ball):
-        listed = listed_balls(ball, mine, other, core)
-        stacked = stack_heads(q_ref[ball * BALL : (ball + 1) * BALL, :])
-        return listed, dot(stacked, pick(kv_ref, listed, 0, half), ((1,), (1,)))
-
-    def elements(ball, listed, scores):
-        exponent, inverse = softmax_parts(scores)
-        attention = (exponent * inverse).astype(BF)
-        attention_ref[ball] = attention
-        return listed, attention
-
-    def outputs(ball, listed, attention):
-        mixed = unstack_heads(dot(attention, pick(kv_ref, listed, half, half)))
-        mixed_ref[ball * BALL : (ball + 1) * BALL, :] = mixed.astype(BF)
-        return ()
-
-    in_stages(2 * local // BALL, products, elements, outputs)
+    stages = forward_stages((mine, other), core, q_ref, kv_ref, attention_ref, mixed_ref)
+    in_stages(2 * local // BALL, *stages)
 
 
 def before_second(
@@ -318,7 +312,7 @@
 def second_layer(
     mine, other, base, mixed_other, chosen, mg_ref, out_one, gain, columns,
     moved_ref, normed_ref, mixed_ref, mixed_send, grads_ref, part_ref,
-    hidden_ref, q_ref, kv_ref, turned_ref, dk_ref, dv_ref,
+    hidden_ref, q_ref, kv_ref, turned_ref, attention_ref, dk_ref, dv_ref,
 ):
     core = lax.axis_index("pts")
     total, width = base.shape
@@ -336,7 +330,12 @@
         return moved
 
     norm_project(total, rotate, gain_row(gain), columns[...], normed_ref, q_ref, kv_ref)
-    backward_stages((mine, other), core, q_ref, kv_ref, turned_ref, mg_ref, mixed_ref, grads_ref, dk_ref, dv_ref)
+    lists = (mine, other)
+    forward = forward_stages(lists, core, q_ref, kv_ref, attention_ref, mixed_ref)
+    backward = backward_stages(
+        lists, core, q_ref, kv_ref, turned_ref, mg_ref, mixed_ref, grads_ref, dk_ref, dv_ref, attention_ref
+    )
+    in_stages(total // BALL, *forward, *backward)
 
     def store(at, part):
         part_ref[at] = part.astype(BF)
@@ -377,9 +376,10 @@
         return ()
 
     in_stages(total // CHUNK, rotate, project_back)
-    backward_stages(
+    stages = backward_stages(
         (mine, other), core, q_ref, kv_ref, turned_ref, mg_ref, mixed_ref, grads_ref, dk_ref, dv_ref, attention_ref
     )
+    in_stages(total // BALL, *stages)
 
     def store(at, part):
         if at.start < local:
@@ -473,6 +473,7 @@
     balls = total // BALL
     thin, wide, triple = shape(total, half), shape(total, width), shape(total, 3 * half)
     turned = shape(balls, width, BALL)
+    kept_attention = shape(balls, 2 * BALL, LISTED * BALL)
     blocks = shape(balls, half, BALL, dtype=F32)
     weights = shape(2, width, half)
 
@@ -511,7 +512,7 @@
     one = [mine[0], one_other]
     two = [mine[1], two_other]
     mixed, q, kv, normed, attention = call(
-        first_forward, [x_other, near_gain, columns_one, normed, q, kv], [thin, thin, wide, wide, shape(balls, 2 * BALL, LISTED * BALL)], lists=one
+        first_forward, [x_other, near_gain, columns_one, normed, q, kv], [thin, thin, wide, wide, kept_attention], lists=one
     )
     mixed_other = swap(mixed)
     base, chosen, chosen_back, grads_in, mg = call(
@@ -523,7 +524,7 @@
         second_layer,
         [base, mixed_other, chosen, mg, out_one, far_gain, columns_two],
         [wide, wide, thin, shape(rows, half), triple, wide],
-        [wide, thin, wide, turned, blocks, blocks],
+        [wide, thin, wide, turned, kept_attention, blocks, blocks],
         two,
     )
     part_two_other = swap(part_two)

time: 54.5 us -> 54.5 us (level)
  no operation moved by 1% of the time
where the time goes in v7:
time: 54.5 us; the launch traced here: 54.3 us
  starting transfers between devices  27.9 us (51%)
  Pallas kernels  21.4 us (39%)
  waiting for transfers between devices  3.95 us (7%)
  between operations  0.8 us (1%)
    ppermute x12, starting transfers between devices, across(): return lax.ppermute(array, ('pts', 'geo'), pairs)  24 us
    pallas_call x8, Pallas kernels, call(): pl.pallas_call(body, name=getattr(body, 'func', body).__name__, out_shape...  19.9 us
    ppermute x13, starting transfers between devices, swap(): return lax.ppermute(array, 'pts', SWAP)  3.92 us
    ppermute x12, waiting for transfers between devices, across(): return lax.ppermute(array, ('pts', 'geo'), pairs)  3.82 us
    pallas_call x1, Pallas kernels, local(): pl.pallas_call(project_mine, name='project_mine', out_shape=[shape(*a.sha...  1.54 us
  transfers between devices with their start and end apart: 25, of which 6 were waited for; matrix products, arithmetic and copies ran while one was open for 0% of the time, Pallas kernels for 20%

profile of v7, /device:TPU:0, one launch (start us, length us, event | category | flops | bytes accessed | tf_op | source)
XLA Modules:
  0.0 54.3 jit_solution(4763913008473236003)
XLA Ops:
  0.6 0.5 collective-permute-start
  1.2 0.4 collective-permute-start.3
  1.7 0.4 collective-permute-start.2
  2.2 1.5 %project_mine.1 = (bf16[512,256]{1,0:T(8,128)(2,1)S(1)}, bf16[512,256]{1,0:T(8,128)(2,1)S(1)}, s32[4,128]{1,0:T(4,128)S(1)}, s32[1,4,4]{2,1,0:T(4,128)S(1)}, s32...) custom-call(bf16[512,256]{1,0:T(8,128)(2,1)} %bitcast.8, ...), custom_call_target="tpu_custom_call" | custom-call | tf_op jit(solution)/shard_map/project_mine/pallas_call | solution.py:501
  3.8 3.1 %first_forward.1 = (bf16[1024,128]{1,0:T(8,128)(2,1)S(1)}, bf16[1024,128]{1,0:T(8,128)(2,1)S(1)}, bf16[1024,256]{1,0:T(8,128)(2,1)S(1)}, bf16[1024,256]{1,0:T(8,128)(2,1)S(1)}, bf16[8,256,512]{2,1,0:T(8,128)(2,1)S(1)}) custom-call(s32[1,4,4]{2,1,0:T(4,128)S(1)} %get-tuple-element.63.mine, s32[1,4,4]{2,1,0:T(4,128)S(1)} %collective-permute-done.1.other, ...), custom_call_target="tpu_custom_call" | custom-call | tf_op jit(solution)/shard_map/first_forward/pallas_call | solution.py:441
  7.0 1.4 %before_second.1 = (f32[1024,256]{1,0:T(8,128)S(1)}, bf16[1024,1024]{1,0:T(8,128)(2,1)S(1)}, bf16[1024,1024]{1,0:T(8,128)(2,1)S(1)}, bf16[1024,256]{1,0:T(8,128)(2,1)S(1)}, bf16[1024,128]{1,0:T(8,128)(2,1)S(1)}) custom-call(s32[4,128]{1,0:T(4,128)S(1)} %get-tuple-element.72.rot_mine, s32[4,128]{1,0:T(4,128)S(1)} %collective-permute-done.3.rot_other, ...), custom_call_target="tpu_custom_call" | custom-call | tf_op jit(solution)/shard_map/before_second/pallas_call | solution.py:441
  8.4 6.3 %second_layer.1 = (bf16[1024,256]{1,0:T(8,128)(2,1)S(1)}, bf16[1024,256]{1,0:T(8,128)(2,1)S(1)}, bf16[1024,128]{1,0:T(8,128)(2,1)S(1)}, bf16[512,128]{1,0:T(8,12...) custom-call(s32[1,4,4]{2,1,0:T(4,128)S(1)} %get-tuple-element.81.mine, ...), custom_call_target="tpu_custom_call" | custom-call | tf_op jit(solution)/shard_map/second_layer/pallas_call | solution.py:441
  14.8 0.4 collective-permute-start.6
  15.2 0.7 %second_weights.1 = (bf16[2,256,128]{2,1,0:T(8,128)(2,1)S(1)}, bf16[2,256,128]{2,1,0:T(8,128)(2,1)S(1)}) custom-call(bf16[1024,256]{1,0:T(8,128)(2,1)S(1)} %get-tuple-element.103.normed, bf16[1024,384]{1,0:T(8,128)(2,1)S(1)} %get-tuple-element.104.grads, bf16[1024,128]{1,0:T(8,128)(2,1)S(1)} %get-tuple-element.98.mixed_two.mixed, ...), custom_call_target="tpu_custom_call" | custom-call | tf_op jit(solution)/shard_map/second_weights/pallas_call | solution.py:441
  15.9 2.7 %collective-permute-start.9 = (bf16[2,256,128]{2,1,0:T(8,128)(2,1)S(1)}, bf16[2,256,128]{2,1,0:T(8,128)(2,1)S(1)}, u32[]{:S(2)}, u32[]{:S(2)}) collective-permute-start(bf16[2,256,128]{2,1,0:T(8,128)(2,1)S(1)} %get-tuple-element.105), channel_id=1, source_target_pairs={{0,18},{17,3},{18,0},{3,17},{20,6},{5,23},{6,20},{23,5},{24,10},{9... | collective-permute-start | bytes 393224 | tf_op jit(solution)/shard_map/ppermute | solution.py:488
  18.6 4.9 %first_backward.1 = (bf16[1024,256]{1,0:T(8,128)(2,1)S(1)}, bf16[1024,384]{1,0:T(8,128)(2,1)S(1)}, bf16[2,256,128]{2,1,0:T(8,128)(2,1)S(1)}, f32[512,256]{1,0:T(8,128)S(1)}, bf16[512,256]{1,0:T(8,128)(2,1)S(1)}) custom-call(s32[1,4,4]{2,1,0:T(4,128)S(1)} %get-tuple-element.63.mine, s32[1,4,4]{2,1,0:T(4,128)S(1)} %collective-permute-done.1.other, ...), custom_call_target="tpu_custom_call" | custom-call | tf_op jit(solution)/shard_map/first_backward/pallas_call | solution.py:441
  23.6 0.4 collective-permute-start.8
  24.0 1.2 %collective-permute-start.10 = (bf16[2,256,128]{2,1,0:T(8,128)(2,1)S(1)}, bf16[2,256,128]{2,1,0:T(8,128)(2,1)S(1)}, u32[]{:S(2)}, u32[]{:S(2)}) collective-permute-start(bf16[2,256,128]{2,1,0:T(8,128)(2,1)S(1)} %get-tuple-element.107), channel_id=1, source_target_pairs={{0,18},{17,3},{18,0},{3,17},{20,6},{5,23},{6,20},{23,5},{24,10},{9... | collective-permute-start | bytes 393224 | tf_op jit(solution)/shard_map/ppermute | solution.py:488
  25.2 1.2 %collective-permute-start.18 = (bf16[1,256,128]{2,1,0:T(8,128)(2,1)S(1)}, bf16[1,256,128]{2,1,0:T(8,128)(2,1)S(1)}, u32[]{:S(2)}, u32[]{:S(2)}) collective-permute-start(bf16[1,256,128]{2,1,0:T(8,128)(2,1)S(1)} %slice.19), channel_id=1, source_target_pairs={{0,17},{17,0},{18,3},{3,18},{20,5},{5,20},{6,23},{23,6},{24,9},{9,... | collective-permute-start | bytes 196616 | tf_op jit(solution)/shard_map/ppermute | solution.py:488
  26.4 1.4 %finish_rows.1 = (bf16[2,256,128]{2,1,0:T(8,128)(2,1)S(1)}, bf16[512,256]{1,0:T(8,128)(2,1)}, bf16[512,256]{1,0:T(8,128)(2,1)}) custom-call(bf16[1024,256]{1,0:T(8,128)(2,1)S(1)} %get-tuple-element.71.normed, bf16[1024,384]{1,0:T(8,128)(2,1)S(1)} %get-tuple-element.94.grads, bf16[1024,128]{1,0:T(8,128)(2,1)S(1)} %get-tuple-element.75.mixed.mixed_ref, ...), custom_call_target="tpu_custom_call" | custom-call | tf_op jit(solution)/shard_map/finish_rows/pallas_call | solution.py:441
  27.8 0.6 %collective-permute-done.10 = bf16[2,256,128]{2,1,0:T(8,128)(2,1)S(1)} collective-permute-done((bf16[2,256,128]{2,1,0:T(8,128)(2,1)S(1)}, bf16[2,256,128]{2,1,0:T(8,128)(2,1)S(1)}, u32[]{:S(2)}, u32[]{:S(2)}) %collective-permute-start.10) | collective-permute-done | bytes 131104 | tf_op jit(solution)/shard_map/ppermute | solution.py:488
  28.5 2.0 %collective-permute-start.11 = (bf16[1,256,128]{2,1,0:T(8,128)(2,1)S(1)}, bf16[1,256,128]{2,1,0:T(8,128)(2,1)S(1)}, u32[]{:S(2)}, u32[]{:S(2)}) collective-permute-start(bf16[1,256,128]{2,1,0:T(8,128)(2,1)S(1)} %slice.17), channel_id=1, source_target_pairs={{0,17},{17,0},{18,3},{3,18},{20,5},{5,20},{6,23},{23,6},{24,9},{9,... | collective-permute-start | bytes 196616 | tf_op jit(solution)/shard_map/ppermute | solution.py:488
  30.5 1.4 %collective-permute-start.19 = (bf16[1,256,128]{2,1,0:T(8,128)(2,1)S(1)}, bf16[1,256,128]{2,1,0:T(8,128)(2,1)S(1)}, u32[]{:S(2)}, u32[]{:S(2)}) collective-permute-start(bf16[1,256,128]{2,1,0:T(8,128)(2,1)S(1)} %add_convert_fusion.4), channel_id=1, source_target_pairs={{0,20},{17,5},{18,6},{3,23},{20,0},{5,17},{6,18},{23,3},{24,12},{9... | collective-permute-start | bytes 196616 | tf_op jit(solution)/shard_map/ppermute | solution.py:488
  31.9 0.5 collective-permute-done.11
  32.4 1.9 %collective-permute-start.12 = (bf16[1,256,128]{2,1,0:T(8,128)(2,1)S(1)}, bf16[1,256,128]{2,1,0:T(8,128)(2,1)S(1)}, u32[]{:S(2)}, u32[]{:S(2)}) collective-permute-start(bf16[1,256,128]{2,1,0:T(8,128)(2,1)S(1)} %add_convert_fusion.7), channel_id=1, source_target_pairs={{0,20},{17,5},{18,6},{3,23},{20,0},{5,17},{6,18},{23,3},{24,12},{9... | collective-permute-start | bytes 196616 | tf_op jit(solution)/shard_map/ppermute | solution.py:488
  34.4 2.9 %collective-permute-start.20 = (bf16[1,256,128]{2,1,0:T(8,128)(2,1)S(1)}, bf16[1,256,128]{2,1,0:T(8,128)(2,1)S(1)}, u32[]{:S(2)}, u32[]{:S(2)}) collective-permute-start(bf16[1,256,128]{2,1,0:T(8,128)(2,1)S(1)} %add_convert_fusion.3), channel_id=1, source_target_pairs={{0,24},{17,9},{18,10},{3,27},{20,12},{5,29},{6,30},{23,15},{24,0},... | collective-permute-start | bytes 196616 | tf_op jit(solution)/shard_map/ppermute | solution.py:488
  37.3 2.4 %collective-permute-start.13 = (bf16[1,256,128]{2,1,0:T(8,128)(2,1)S(1)}, bf16[1,256,128]{2,1,0:T(8,128)(2,1)S(1)}, u32[]{:S(2)}, u32[]{:S(2)}) collective-permute-start(bf16[1,256,128]{2,1,0:T(8,128)(2,1)S(1)} %add_convert_fusion.6), channel_id=1, source_target_pairs={{0,24},{17,9},{18,10},{3,27},{20,12},{5,29},{6,30},{23,15},{24,0},... | collective-permute-start | bytes 196616 | tf_op jit(solution)/shard_map/ppermute | solution.py:488
  39.7 2.0 %collective-permute-start.21 = (bf16[1,256,128]{2,1,0:T(8,128)(2,1)S(1)}, bf16[1,256,128]{2,1,0:T(8,128)(2,1)S(1)}, u32[]{:S(2)}, u32[]{:S(2)}) collective-permute-start(bf16[1,256,128]{2,1,0:T(8,128)(2,1)S(1)} %add_convert_fusion.2), channel_id=1, source_target_pairs={{0,17},{17,0},{18,3},{3,18},{20,5},{5,20},{6,23},{23,6},{24,9},{9,... | collective-permute-start | bytes 196616 | tf_op jit(solution)/shard_map/ppermute | solution.py:488
  41.6 0.3 collective-permute-done.13
  41.9 1.7 %collective-permute-start.14 = (bf16[1,256,128]{2,1,0:T(8,128)(2,1)S(1)}, bf16[1,256,128]{2,1,0:T(8,128)(2,1)S(1)}, u32[]{:S(2)}, u32[]{:S(2)}) collective-permute-start(bf16[1,256,128]{2,1,0:T(8,128)(2,1)S(1)} %add_convert_fusion.5), channel_id=1, source_target_pairs={{0,17},{17,0},{18,3},{3,18},{20,5},{5,20},{6,23},{23,6},{24,9},{9,... | collective-permute-start | bytes 196616 | tf_op jit(solution)/shard_map/ppermute | solution.py:488
  43.7 1.7 %collective-permute-start.22 = (bf16[2,256,128]{2,1,0:T(8,128)(2,1)S(1)}, bf16[2,256,128]{2,1,0:T(8,128)(2,1)S(1)}, u32[]{:S(2)}, u32[]{:S(2)}) collective-permute-start(bf16[2,256,128]{2,1,0:T(8,128)(2,1)S(1)} %pad_maximum_fusion.1.near_mine), channel_id=1, source_target_pairs={{0,18},{17,3},{18,0},{3,17},{20,6},{5,23},{6,20},{23,5},{24,10},{9... | collective-permute-start | bytes 393224 | tf_op jit(solution)/shard_map/ppermute | solution.py:488
  45.7 3.0 %collective-permute-start.15 = (bf16[2,256,128]{2,1,0:T(8,128)(2,1)S(1)}, bf16[2,256,128]{2,1,0:T(8,128)(2,1)S(1)}, u32[]{:S(2)}, u32[]{:S(2)}) collective-permute-start(bf16[2,256,128]{2,1,0:T(8,128)(2,1)S(1)} %pad_maximum_fusion.near_mine), channel_id=1, source_target_pairs={{0,18},{17,3},{18,0},{3,17},{20,6},{5,23},{6,20},{23,5},{24,10},{9... | collective-permute-start | bytes 393224 | tf_op jit(solution)/shard_map/ppermute | solution.py:488
  48.7 0.5 collective-permute-start.24
  49.3 2.1 %collective-permute-done.15.far_mine = bf16[2,256,128]{2,1,0:T(8,128)(2,1)S(1)} collective-permute-done((bf16[2,256,128]{2,1,0:T(8,128)(2,1)S(1)}, bf16[2,256,128]{2,1,0:T(8,128)(2,1)S(1)}, u32[]{:S(2)}, u32[]{:S(2)}) %collective-permute-start.15) | collective-permute-done | bytes 131104 | tf_op jit(solution)/shard_map/ppermute | solution.py:488
  51.4 0.7 %collective-permute-start.17 = (bf16[2,256,128]{2,1,0:T(8,128)(2,1)S(1)}, bf16[2,256,128]{2,1,0:T(8,128)(2,1)S(1)}, u32[]{:S(2)}, u32[]{:S(2)}) collective-permute-start(bf16[2,256,128]{2,1,0:T(8,128)(2,1)S(1)} %collective-permute-done.15.far_mine), channel_id=1, source_target_pairs={{0,16},{16,0},{1,17},{17,1},{2,18},{18,2},{3,19},{19,3},{4,20},{20... | collective-permute-start | bytes 393224 | tf_op jit(solution)/shard_map/ppermute | solution.py:481
  52.1 1.1 %finish_weights.3 = (f32[1,256]{1,0:T(1,128)}, f32[256,768]{1,0:T(8,128)}, f32[256,256]{1,0:T(8,128)}) custom-call(bf16[2,256,128]{2,1,0:T(8,128)(2,1)S(1)} %pad_maximum_fusion.1.near_mine, bf16[2,256,128]{2,1,0:T(8,128)(2,1)S(1)} %collective-permute-done.22.far_mine, bf16[2,256,128]{2,1,0:T(8,128)(2,1)S(1)} %collective-permute-done.23.near_other, ...), custom_call_target="tpu_custom_call" | custom-call | tf_op jit(solution)/shard_map/finish_weights/pallas_call | solution.py:441
  53.2 1.1 %finish_weights.2 = (f32[1,256]{1,0:T(1,128)}, f32[256,768]{1,0:T(8,128)}, f32[256,256]{1,0:T(8,128)}) custom-call(bf16[2,256,128]{2,1,0:T(8,128)(2,1)S(1)} %pad_maximum_fusion.near_mine, bf16[2,256,128]{2,1,0:T(8,128)(2,1)S(1)} %collective-permute-done.15.far_mine, bf16[2,256,128]{2,1,0:T(8,128)(2,1)S(1)} %collective-permute-done.16.near_other, ...), custom_call_target="tpu_custom_call" | custom-call | tf_op jit(solution)/shard_map/finish_weights/pallas_call | solution.py:441
  (43 shorter events, 1.2 us)
Async XLA Ops:
  0.6 3.1 %collective-permute-start = (bf16[512,256]{1,0:T(8,128)(2,1)}, bf16[512,256]{1,0:T(8,128)(2,1)S(1)}, u32[]{:S(2)}, u32[]{:S(2)}) collective-permute-start(bf16[512,256]{1,0:T(8,128)(2,1)} %bitcast.7), channel_id=1, source_target_pairs={{0,16},{16,0},{1,17},{17,1},{2,18},{18,2},{3,19},{19,3},{4,20},{20... | collective-permute-start | bytes 786440 | tf_op jit(solution)/shard_map/ppermute | solution.py:481
  1.2 2.6 %collective-permute-start.4 = (bf16[512,256]{1,0:T(8,128)(2,1)}, bf16[512,256]{1,0:T(8,128)(2,1)S(1)}, u32[]{:S(2)}, u32[]{:S(2)}) collective-permute-start(bf16[512,256]{1,0:T(8,128)(2,1)} %bitcast.9), channel_id=1, source_target_pairs={{0,16},{16,0},{1,17},{17,1},{2,18},{18,2},{3,19},{19,3},{4,20},{20... | collective-permute-start | bytes 786440 | tf_op jit(solution)/shard_map/ppermute | solution.py:481
  1.2 2.5 %collective-permute-start.3 = (s32[4,128]{1,0:T(4,128)}, s32[4,128]{1,0:T(4,128)S(1)}, u32[]{:S(2)}, u32[]{:S(2)}) collective-permute-start(s32[4,128]{1,0:T(4,128)} %bitcast.11), channel_id=1, source_target_pairs={{0,16},{16,0},{1,17},{17,1},{2,18},{18,2},{3,19},{19,3},{4,20},{20... | collective-permute-start | bytes 6152 | tf_op jit(solution)/shard_map/ppermute | solution.py:481
  1.7 2.1 %collective-permute-start.1 = (s32[1,4,4]{2,1,0:T(4,128)}, s32[1,4,4]{2,1,0:T(4,128)S(1)}, u32[]{:S(2)}, u32[]{:S(2)}) collective-permute-start(s32[1,4,4]{2,1,0:T(4,128)} %lists_one_hbm.1), channel_id=1, source_target_pairs={{0,16},{16,0},{1,17},{17,1},{2,18},{18,2},{3,19},{19,3},{4,20},{20... | collective-permute-start | bytes 200 | tf_op jit(solution)/shard_map/ppermute | solution.py:481
  1.7 2.0 %collective-permute-start.2 = (s32[1,4,4]{2,1,0:T(4,128)}, s32[1,4,4]{2,1,0:T(4,128)S(1)}, u32[]{:S(2)}, u32[]{:S(2)}) collective-permute-start(s32[1,4,4]{2,1,0:T(4,128)} %lists_two_hbm.1), channel_id=1, source_target_pairs={{0,16},{16,0},{1,17},{17,1},{2,18},{18,2},{3,19},{19,3},{4,20},{20... | collective-permute-start | bytes 200 | tf_op jit(solution)/shard_map/ppermute | solution.py:481
  6.8 1.6 %collective-permute-start.5 = (bf16[1024,128]{1,0:T(8,128)(2,1)S(1)}, bf16[1024,128]{1,0:T(8,128)(2,1)S(1)}, u32[]{:S(2)}, u32[]{:S(2)}) collective-permute-start(bf16[1024,128]{1,0:T(8,128)(2,1)S(1)} %get-tuple-element.75.mixed.mixed_ref), channel_id=1, source_target_pairs={{0,16},{16,0},{1,17},{17,1},{2,18},{18,2},{3,19},{19,3},{4,20},{20... | collective-permute-start | bytes 786440 | tf_op jit(solution)/shard_map/ppermute | solution.py:481
  14.8 3.8 %collective-permute-start.6 = (bf16[1024,256]{1,0:T(8,128)(2,1)S(1)}, bf16[1024,256]{1,0:T(8,128)(2,1)S(1)}, u32[]{:S(2)}, u32[]{:S(2)}) collective-permute-start(bf16[1024,256]{1,0:T(8,128)(2,1)S(1)} %get-tuple-element.88.part_mine), channel_id=1, source_target_pairs={{0,16},{16,0},{1,17},{17,1},{2,18},{18,2},{3,19},{19,3},{4,20},{20... | collective-permute-start | bytes 1572872 | tf_op jit(solution)/shard_map/ppermute | solution.py:481
  15.9 8.1 %collective-permute-start.9 = (bf16[2,256,128]{2,1,0:T(8,128)(2,1)S(1)}, bf16[2,256,128]{2,1,0:T(8,128)(2,1)S(1)}, u32[]{:S(2)}, u32[]{:S(2)}) collective-permute-start(bf16[2,256,128]{2,1,0:T(8,128)(2,1)S(1)} %get-tuple-element.105), channel_id=1, source_target_pairs={{0,18},{17,3},{18,0},{3,17},{20,6},{5,23},{6,20},{23,5},{24,10},{9... | collective-permute-start | bytes 393224 | tf_op jit(solution)/shard_map/ppermute | solution.py:488
  23.4 3.0 %collective-permute-start.7 = (bf16[512,256]{1,0:T(8,128)(2,1)S(1)}, bf16[512,256]{1,0:T(8,128)(2,1)S(1)}, u32[]{:S(2)}, u32[]{:S(2)}) collective-permute-start(bf16[512,256]{1,0:T(8,128)(2,1)S(1)} %get-tuple-element.97), channel_id=1, source_target_pairs={{0,16},{16,0},{1,17},{17,1},{2,18},{18,2},{3,19},{19,3},{4,20},{20... | collective-permute-start | bytes 786440 | tf_op jit(solution)/shard_map/ppermute | solution.py:481
  23.6 2.8 %collective-permute-start.8 = (bf16[512,128]{1,0:T(8,128)(2,1)S(1)}, bf16[512,128]{1,0:T(8,128)(2,1)S(1)}, u32[]{:S(2)}, u32[]{:S(2)}) collective-permute-start(bf16[512,128]{1,0:T(8,128)(2,1)S(1)} %get-tuple-element.99), channel_id=1, source_target_pairs={{0,16},{16,0},{1,17},{17,1},{2,18},{18,2},{3,19},{19,3},{4,20},{20... | collective-permute-start | bytes 393224 | tf_op jit(solution)/shard_map/ppermute | solution.py:481
  24.0 4.4 %collective-permute-start.10 = (bf16[2,256,128]{2,1,0:T(8,128)(2,1)S(1)}, bf16[2,256,128]{2,1,0:T(8,128)(2,1)S(1)}, u32[]{:S(2)}, u32[]{:S(2)}) collective-permute-start(bf16[2,256,128]{2,1,0:T(8,128)(2,1)S(1)} %get-tuple-element.107), channel_id=1, source_target_pairs={{0,18},{17,3},{18,0},{3,17},{20,6},{5,23},{6,20},{23,5},{24,10},{9... | collective-permute-start | bytes 393224 | tf_op jit(solution)/shard_map/ppermute | solution.py:488
  25.2 5.2 %collective-permute-start.18 = (bf16[1,256,128]{2,1,0:T(8,128)(2,1)S(1)}, bf16[1,256,128]{2,1,0:T(8,128)(2,1)S(1)}, u32[]{:S(2)}, u32[]{:S(2)}) collective-permute-start(bf16[1,256,128]{2,1,0:T(8,128)(2,1)S(1)} %slice.19), channel_id=1, source_target_pairs={{0,17},{17,0},{18,3},{3,18},{20,5},{5,20},{6,23},{23,6},{24,9},{9,... | collective-permute-start | bytes 196616 | tf_op jit(solution)/shard_map/ppermute | solution.py:488
  27.8 24.3 %copy-start = (bf16[256,768]{1,0:T(8,128)(2,1)S(1)}, bf16[256,768]{1,0:T(8,128)(2,1)}, u32[]{:S(2)}) copy-start(bf16[256,768]{1,0:T(8,128)(2,1)} %weight.3) | copy-start | bytes 1179652
  27.8 25.4 %copy-start.1 = (bf16[256,768]{1,0:T(8,128)(2,1)S(1)}, bf16[256,768]{1,0:T(8,128)(2,1)}, u32[]{:S(2)}) copy-start(bf16[256,768]{1,0:T(8,128)(2,1)} %weight.2) | copy-start | bytes 1179652
  28.5 4.0 %collective-permute-start.11 = (bf16[1,256,128]{2,1,0:T(8,128)(2,1)S(1)}, bf16[1,256,128]{2,1,0:T(8,128)(2,1)S(1)}, u32[]{:S(2)}, u32[]{:S(2)}) collective-permute-start(bf16[1,256,128]{2,1,0:T(8,128)(2,1)S(1)} %slice.17), channel_id=1, source_target_pairs={{0,17},{17,0},{18,3},{3,18},{20,5},{5,20},{6,23},{23,6},{24,9},{9,... | collective-permute-start | bytes 196616 | tf_op jit(solution)/shard_map/ppermute | solution.py:488
  30.5 3.9 %collective-permute-start.19 = (bf16[1,256,128]{2,1,0:T(8,128)(2,1)S(1)}, bf16[1,256,128]{2,1,0:T(8,128)(2,1)S(1)}, u32[]{:S(2)}, u32[]{:S(2)}) collective-permute-start(bf16[1,256,128]{2,1,0:T(8,128)(2,1)S(1)} %add_convert_fusion.4), channel_id=1, source_target_pairs={{0,20},{17,5},{18,6},{3,23},{20,0},{5,17},{6,18},{23,3},{24,12},{9... | collective-permute-start | bytes 196616 | tf_op jit(solution)/shard_map/ppermute | solution.py:488
  32.4 4.8 %collective-permute-start.12 = (bf16[1,256,128]{2,1,0:T(8,128)(2,1)S(1)}, bf16[1,256,128]{2,1,0:T(8,128)(2,1)S(1)}, u32[]{:S(2)}, u32[]{:S(2)}) collective-permute-start(bf16[1,256,128]{2,1,0:T(8,128)(2,1)S(1)} %add_convert_fusion.7), channel_id=1, source_target_pairs={{0,20},{17,5},{18,6},{3,23},{20,0},{5,17},{6,18},{23,3},{24,12},{9... | collective-permute-start | bytes 196616 | tf_op jit(solution)/shard_map/ppermute | solution.py:488
  34.4 5.3 %collective-permute-start.20 = (bf16[1,256,128]{2,1,0:T(8,128)(2,1)S(1)}, bf16[1,256,128]{2,1,0:T(8,128)(2,1)S(1)}, u32[]{:S(2)}, u32[]{:S(2)}) collective-permute-start(bf16[1,256,128]{2,1,0:T(8,128)(2,1)S(1)} %add_convert_fusion.3), channel_id=1, source_target_pairs={{0,24},{17,9},{18,10},{3,27},{20,12},{5,29},{6,30},{23,15},{24,0},... | collective-permute-start | bytes 196616 | tf_op jit(solution)/shard_map/ppermute | solution.py:488
  37.3 4.7 %collective-permute-start.13 = (bf16[1,256,128]{2,1,0:T(8,128)(2,1)S(1)}, bf16[1,256,128]{2,1,0:T(8,128)(2,1)S(1)}, u32[]{:S(2)}, u32[]{:S(2)}) collective-permute-start(bf16[1,256,128]{2,1,0:T(8,128)(2,1)S(1)} %add_convert_fusion.6), channel_id=1, source_target_pairs={{0,24},{17,9},{18,10},{3,27},{20,12},{5,29},{6,30},{23,15},{24,0},... | collective-permute-start | bytes 196616 | tf_op jit(solution)/shard_map/ppermute | solution.py:488
  39.7 4.0 %collective-permute-start.21 = (bf16[1,256,128]{2,1,0:T(8,128)(2,1)S(1)}, bf16[1,256,128]{2,1,0:T(8,128)(2,1)S(1)}, u32[]{:S(2)}, u32[]{:S(2)}) collective-permute-start(bf16[1,256,128]{2,1,0:T(8,128)(2,1)S(1)} %add_convert_fusion.2), channel_id=1, source_target_pairs={{0,17},{17,0},{18,3},{3,18},{20,5},{5,20},{6,23},{23,6},{24,9},{9,... | collective-permute-start | bytes 196616 | tf_op jit(solution)/shard_map/ppermute | solution.py:488
  41.9 3.8 %collective-permute-start.14 = (bf16[1,256,128]{2,1,0:T(8,128)(2,1)S(1)}, bf16[1,256,128]{2,1,0:T(8,128)(2,1)S(1)}, u32[]{:S(2)}, u32[]{:S(2)}) collective-permute-start(bf16[1,256,128]{2,1,0:T(8,128)(2,1)S(1)} %add_convert_fusion.5), channel_id=1, source_target_pairs={{0,17},{17,0},{18,3},{3,18},{20,5},{5,20},{6,23},{23,6},{24,9},{9,... | collective-permute-start | bytes 196616 | tf_op jit(solution)/shard_map/ppermute | solution.py:488
  43.7 5.0 %collective-permute-start.22 = (bf16[2,256,128]{2,1,0:T(8,128)(2,1)S(1)}, bf16[2,256,128]{2,1,0:T(8,128)(2,1)S(1)}, u32[]{:S(2)}, u32[]{:S(2)}) collective-permute-start(bf16[2,256,128]{2,1,0:T(8,128)(2,1)S(1)} %pad_maximum_fusion.1.near_mine), channel_id=1, source_target_pairs={{0,18},{17,3},{18,0},{3,17},{20,6},{5,23},{6,20},{23,5},{24,10},{9... | collective-permute-start | bytes 393224 | tf_op jit(solution)/shard_map/ppermute | solution.py:488
  45.7 5.7 %collective-permute-start.15 = (bf16[2,256,128]{2,1,0:T(8,128)(2,1)S(1)}, bf16[2,256,128]{2,1,0:T(8,128)(2,1)S(1)}, u32[]{:S(2)}, u32[]{:S(2)}) collective-permute-start(bf16[2,256,128]{2,1,0:T(8,128)(2,1)S(1)} %pad_maximum_fusion.near_mine), channel_id=1, source_target_pairs={{0,18},{17,3},{18,0},{3,17},{20,6},{5,23},{6,20},{23,5},{24,10},{9... | collective-permute-start | bytes 393224 | tf_op jit(solution)/shard_map/ppermute | solution.py:488
  48.7 3.4 %collective-permute-start.23 = (bf16[2,256,128]{2,1,0:T(8,128)(2,1)S(1)}, bf16[2,256,128]{2,1,0:T(8,128)(2,1)S(1)}, u32[]{:S(2)}, u32[]{:S(2)}) collective-permute-start(bf16[2,256,128]{2,1,0:T(8,128)(2,1)S(1)} %pad_maximum_fusion.1.near_mine), channel_id=1, source_target_pairs={{0,16},{16,0},{1,17},{17,1},{2,18},{18,2},{3,19},{19,3},{4,20},{20... | collective-permute-start | bytes 393224 | tf_op jit(solution)/shard_map/ppermute | solution.py:481
  48.7 3.4 %collective-permute-start.24 = (bf16[2,256,128]{2,1,0:T(8,128)(2,1)S(1)}, bf16[2,256,128]{2,1,0:T(8,128)(2,1)S(1)}, u32[]{:S(2)}, u32[]{:S(2)}) collective-permute-start(bf16[2,256,128]{2,1,0:T(8,128)(2,1)S(1)} %collective-permute-done.22.far_mine), channel_id=1, source_target_pairs={{0,16},{16,0},{1,17},{17,1},{2,18},{18,2},{3,19},{19,3},{4,20},{20... | collective-permute-start | bytes 393224 | tf_op jit(solution)/shard_map/ppermute | solution.py:481
  49.3 4.0 %collective-permute-start.16 = (bf16[2,256,128]{2,1,0:T(8,128)(2,1)S(1)}, bf16[2,256,128]{2,1,0:T(8,128)(2,1)S(1)}, u32[]{:S(2)}, u32[]{:S(2)}) collective-permute-start(bf16[2,256,128]{2,1,0:T(8,128)(2,1)S(1)} %pad_maximum_fusion.near_mine), channel_id=1, source_target_pairs={{0,16},{16,0},{1,17},{17,1},{2,18},{18,2},{3,19},{19,3},{4,20},{20... | collective-permute-start | bytes 393224 | tf_op jit(solution)/shard_map/ppermute | solution.py:481
  51.4 1.8 %collective-permute-start.17 = (bf16[2,256,128]{2,1,0:T(8,128)(2,1)S(1)}, bf16[2,256,128]{2,1,0:T(8,128)(2,1)S(1)}, u32[]{:S(2)}, u32[]{:S(2)}) collective-permute-start(bf16[2,256,128]{2,1,0:T(8,128)(2,1)S(1)} %collective-permute-done.15.far_mine), channel_id=1, source_target_pairs={{0,16},{16,0},{1,17},{17,1},{2,18},{18,2},{3,19},{19,3},{4,20},{20... | collective-permute-start | bytes 393224 | tf_op jit(solution)/shard_map/ppermute | solution.py:481

commit v8 on v7

--- a/solution.py
+++ b/solution.py
@@ -375,10 +375,10 @@
         mg_ref[at] = dot(hidden_grad, out_one[:half], ((1,), (1,))).astype(BF)
         return ()
 
-    in_stages(total // CHUNK, rotate, project_back)
     stages = backward_stages(
         (mine, other), core, q_ref, kv_ref, turned_ref, mg_ref, mixed_ref, grads_ref, dk_ref, dv_ref, attention_ref
     )
+    in_stages(total // CHUNK, rotate, project_back)
     in_stages(total // BALL, *stages)
 
     def store(at, part):

time: 54.5 us -> 54.5 us (level)
  no operation moved by 1% of the time
where the time goes in v8:
time: 54.5 us; the launch traced here: 54.3 us
  starting transfers between devices  27.9 us (51%)
  Pallas kernels  21.4 us (39%)
  waiting for transfers between devices  3.95 us (7%)
  between operations  0.8 us (1%)
    ppermute x12, starting transfers between devices, across(): return lax.ppermute(array, ('pts', 'geo'), pairs)  24 us
    pallas_call x8, Pallas kernels, call(): pl.pallas_call(body, name=getattr(body, 'func', body).__name__, out_shape...  19.9 us
    ppermute x13, starting transfers between devices, swap(): return lax.ppermute(array, 'pts', SWAP)  3.92 us
    ppermute x12, waiting for transfers between devices, across(): return lax.ppermute(array, ('pts', 'geo'), pairs)  3.82 us
    pallas_call x1, Pallas kernels, local(): pl.pallas_call(project_mine, name='project_mine', out_shape=[shape(*a.sha...  1.54 us
  transfers between devices with their start and end apart: 25, of which 6 were waited for; matrix products, arithmetic and copies ran while one was open for 0% of the time, Pallas kernels for 20%

profile of v8, /device:TPU:0, one launch (start us, length us, event | category | flops | bytes accessed | tf_op | source)
XLA Modules:
  0.0 54.3 jit_solution(4763913008473236003)
XLA Ops:
  0.6 0.5 collective-permute-start
  1.2 0.4 collective-permute-start.3
  1.7 0.4 collective-permute-start.2
  2.2 1.5 %project_mine.1 = (bf16[512,256]{1,0:T(8,128)(2,1)S(1)}, bf16[512,256]{1,0:T(8,128)(2,1)S(1)}, s32[4,128]{1,0:T(4,128)S(1)}, s32[1,4,4]{2,1,0:T(4,128)S(1)}, s32...) custom-call(bf16[512,256]{1,0:T(8,128)(2,1)} %bitcast.8, ...), custom_call_target="tpu_custom_call" | custom-call | tf_op jit(solution)/shard_map/project_mine/pallas_call | solution.py:501
  3.8 3.1 %first_forward.1 = (bf16[1024,128]{1,0:T(8,128)(2,1)S(1)}, bf16[1024,128]{1,0:T(8,128)(2,1)S(1)}, bf16[1024,256]{1,0:T(8,128)(2,1)S(1)}, bf16[1024,256]{1,0:T(8,128)(2,1)S(1)}, bf16[8,256,512]{2,1,0:T(8,128)(2,1)S(1)}) custom-call(s32[1,4,4]{2,1,0:T(4,128)S(1)} %get-tuple-element.63.mine, s32[1,4,4]{2,1,0:T(4,128)S(1)} %collective-permute-done.1.other, ...), custom_call_target="tpu_custom_call" | custom-call | tf_op jit(solution)/shard_map/first_forward/pallas_call | solution.py:441
  7.0 1.4 %before_second.1 = (f32[1024,256]{1,0:T(8,128)S(1)}, bf16[1024,1024]{1,0:T(8,128)(2,1)S(1)}, bf16[1024,1024]{1,0:T(8,128)(2,1)S(1)}, bf16[1024,256]{1,0:T(8,128)(2,1)S(1)}, bf16[1024,128]{1,0:T(8,128)(2,1)S(1)}) custom-call(s32[4,128]{1,0:T(4,128)S(1)} %get-tuple-element.72.rot_mine, s32[4,128]{1,0:T(4,128)S(1)} %collective-permute-done.3.rot_other, ...), custom_call_target="tpu_custom_call" | custom-call | tf_op jit(solution)/shard_map/before_second/pallas_call | solution.py:441
  8.4 6.3 %second_layer.1 = (bf16[1024,256]{1,0:T(8,128)(2,1)S(1)}, bf16[1024,256]{1,0:T(8,128)(2,1)S(1)}, bf16[1024,128]{1,0:T(8,128)(2,1)S(1)}, bf16[512,128]{1,0:T(8,12...) custom-call(s32[1,4,4]{2,1,0:T(4,128)S(1)} %get-tuple-element.81.mine, ...), custom_call_target="tpu_custom_call" | custom-call | tf_op jit(solution)/shard_map/second_layer/pallas_call | solution.py:441
  14.8 0.4 collective-permute-start.6
  15.2 0.7 %second_weights.1 = (bf16[2,256,128]{2,1,0:T(8,128)(2,1)S(1)}, bf16[2,256,128]{2,1,0:T(8,128)(2,1)S(1)}) custom-call(bf16[1024,256]{1,0:T(8,128)(2,1)S(1)} %get-tuple-element.103.normed, bf16[1024,384]{1,0:T(8,128)(2,1)S(1)} %get-tuple-element.104.grads, bf16[1024,128]{1,0:T(8,128)(2,1)S(1)} %get-tuple-element.98.mixed_two.mixed, ...), custom_call_target="tpu_custom_call" | custom-call | tf_op jit(solution)/shard_map/second_weights/pallas_call | solution.py:441
  15.9 2.7 %collective-permute-start.9 = (bf16[2,256,128]{2,1,0:T(8,128)(2,1)S(1)}, bf16[2,256,128]{2,1,0:T(8,128)(2,1)S(1)}, u32[]{:S(2)}, u32[]{:S(2)}) collective-permute-start(bf16[2,256,128]{2,1,0:T(8,128)(2,1)S(1)} %get-tuple-element.105), channel_id=1, source_target_pairs={{0,18},{17,3},{18,0},{3,17},{20,6},{5,23},{6,20},{23,5},{24,10},{9... | collective-permute-start | bytes 393224 | tf_op jit(solution)/shard_map/ppermute | solution.py:488
  18.6 4.9 %first_backward.1 = (bf16[1024,256]{1,0:T(8,128)(2,1)S(1)}, bf16[1024,384]{1,0:T(8,128)(2,1)S(1)}, bf16[2,256,128]{2,1,0:T(8,128)(2,1)S(1)}, f32[512,256]{1,0:T(8,128)S(1)}, bf16[512,256]{1,0:T(8,128)(2,1)S(1)}) custom-call(s32[1,4,4]{2,1,0:T(4,128)S(1)} %get-tuple-element.63.mine, s32[1,4,4]{2,1,0:T(4,128)S(1)} %collective-permute-done.1.other, ...), custom_call_target="tpu_custom_call" | custom-call | tf_op jit(solution)/shard_map/first_backward/pallas_call | solution.py:441
  23.6 0.4 collective-permute-start.8
  24.0 1.2 %collective-permute-start.10 = (bf16[2,256,128]{2,1,0:T(8,128)(2,1)S(1)}, bf16[2,256,128]{2,1,0:T(8,128)(2,1)S(1)}, u32[]{:S(2)}, u32[]{:S(2)}) collective-permute-start(bf16[2,256,128]{2,1,0:T(8,128)(2,1)S(1)} %get-tuple-element.107), channel_id=1, source_target_pairs={{0,18},{17,3},{18,0},{3,17},{20,6},{5,23},{6,20},{23,5},{24,10},{9... | collective-permute-start | bytes 393224 | tf_op jit(solution)/shard_map/ppermute | solution.py:488
  25.2 1.2 %collective-permute-start.18 = (bf16[1,256,128]{2,1,0:T(8,128)(2,1)S(1)}, bf16[1,256,128]{2,1,0:T(8,128)(2,1)S(1)}, u32[]{:S(2)}, u32[]{:S(2)}) collective-permute-start(bf16[1,256,128]{2,1,0:T(8,128)(2,1)S(1)} %slice.19), channel_id=1, source_target_pairs={{0,17},{17,0},{18,3},{3,18},{20,5},{5,20},{6,23},{23,6},{24,9},{9,... | collective-permute-start | bytes 196616 | tf_op jit(solution)/shard_map/ppermute | solution.py:488
  26.4 1.4 %finish_rows.1 = (bf16[2,256,128]{2,1,0:T(8,128)(2,1)S(1)}, bf16[512,256]{1,0:T(8,128)(2,1)}, bf16[512,256]{1,0:T(8,128)(2,1)}) custom-call(bf16[1024,256]{1,0:T(8,128)(2,1)S(1)} %get-tuple-element.71.normed, bf16[1024,384]{1,0:T(8,128)(2,1)S(1)} %get-tuple-element.94.grads, bf16[1024,128]{1,0:T(8,128)(2,1)S(1)} %get-tuple-element.75.mixed.mixed_ref, ...), custom_call_target="tpu_custom_call" | custom-call | tf_op jit(solution)/shard_map/finish_rows/pallas_call | solution.py:441
  27.8 0.6 %collective-permute-done.10 = bf16[2,256,128]{2,1,0:T(8,128)(2,1)S(1)} collective-permute-done((bf16[2,256,128]{2,1,0:T(8,128)(2,1)S(1)}, bf16[2,256,128]{2,1,0:T(8,128)(2,1)S(1)}, u32[]{:S(2)}, u32[]{:S(2)}) %collective-permute-start.10) | collective-permute-done | bytes 131104 | tf_op jit(solution)/shard_map/ppermute | solution.py:488
  28.5 2.0 %collective-permute-start.11 = (bf16[1,256,128]{2,1,0:T(8,128)(2,1)S(1)}, bf16[1,256,128]{2,1,0:T(8,128)(2,1)S(1)}, u32[]{:S(2)}, u32[]{:S(2)}) collective-permute-start(bf16[1,256,128]{2,1,0:T(8,128)(2,1)S(1)} %slice.17), channel_id=1, source_target_pairs={{0,17},{17,0},{18,3},{3,18},{20,5},{5,20},{6,23},{23,6},{24,9},{9,... | collective-permute-start | bytes 196616 | tf_op jit(solution)/shard_map/ppermute | solution.py:488
  30.5 1.4 %collective-permute-start.19 = (bf16[1,256,128]{2,1,0:T(8,128)(2,1)S(1)}, bf16[1,256,128]{2,1,0:T(8,128)(2,1)S(1)}, u32[]{:S(2)}, u32[]{:S(2)}) collective-permute-start(bf16[1,256,128]{2,1,0:T(8,128)(2,1)S(1)} %add_convert_fusion.4), channel_id=1, source_target_pairs={{0,20},{17,5},{18,6},{3,23},{20,0},{5,17},{6,18},{23,3},{24,12},{9... | collective-permute-start | bytes 196616 | tf_op jit(solution)/shard_map/ppermute | solution.py:488
  31.9 0.5 collective-permute-done.11
  32.4 1.9 %collective-permute-start.12 = (bf16[1,256,128]{2,1,0:T(8,128)(2,1)S(1)}, bf16[1,256,128]{2,1,0:T(8,128)(2,1)S(1)}, u32[]{:S(2)}, u32[]{:S(2)}) collective-permute-start(bf16[1,256,128]{2,1,0:T(8,128)(2,1)S(1)} %add_convert_fusion.7), channel_id=1, source_target_pairs={{0,20},{17,5},{18,6},{3,23},{20,0},{5,17},{6,18},{23,3},{24,12},{9... | collective-permute-start | bytes 196616 | tf_op jit(solution)/shard_map/ppermute | solution.py:488
  34.4 2.9 %collective-permute-start.20 = (bf16[1,256,128]{2,1,0:T(8,128)(2,1)S(1)}, bf16[1,256,128]{2,1,0:T(8,128)(2,1)S(1)}, u32[]{:S(2)}, u32[]{:S(2)}) collective-permute-start(bf16[1,256,128]{2,1,0:T(8,128)(2,1)S(1)} %add_convert_fusion.3), channel_id=1, source_target_pairs={{0,24},{17,9},{18,10},{3,27},{20,12},{5,29},{6,30},{23,15},{24,0},... | collective-permute-start | bytes 196616 | tf_op jit(solution)/shard_map/ppermute | solution.py:488
  37.3 2.4 %collective-permute-start.13 = (bf16[1,256,128]{2,1,0:T(8,128)(2,1)S(1)}, bf16[1,256,128]{2,1,0:T(8,128)(2,1)S(1)}, u32[]{:S(2)}, u32[]{:S(2)}) collective-permute-start(bf16[1,256,128]{2,1,0:T(8,128)(2,1)S(1)} %add_convert_fusion.6), channel_id=1, source_target_pairs={{0,24},{17,9},{18,10},{3,27},{20,12},{5,29},{6,30},{23,15},{24,0},... | collective-permute-start | bytes 196616 | tf_op jit(solution)/shard_map/ppermute | solution.py:488
  39.7 2.0 %collective-permute-start.21 = (bf16[1,256,128]{2,1,0:T(8,128)(2,1)S(1)}, bf16[1,256,128]{2,1,0:T(8,128)(2,1)S(1)}, u32[]{:S(2)}, u32[]{:S(2)}) collective-permute-start(bf16[1,256,128]{2,1,0:T(8,128)(2,1)S(1)} %add_convert_fusion.2), channel_id=1, source_target_pairs={{0,17},{17,0},{18,3},{3,18},{20,5},{5,20},{6,23},{23,6},{24,9},{9,... | collective-permute-start | bytes 196616 | tf_op jit(solution)/shard_map/ppermute | solution.py:488
  41.6 0.3 collective-permute-done.13
  41.9 1.7 %collective-permute-start.14 = (bf16[1,256,128]{2,1,0:T(8,128)(2,1)S(1)}, bf16[1,256,128]{2,1,0:T(8,128)(2,1)S(1)}, u32[]{:S(2)}, u32[]{:S(2)}) collective-permute-start(bf16[1,256,128]{2,1,0:T(8,128)(2,1)S(1)} %add_convert_fusion.5), channel_id=1, source_target_pairs={{0,17},{17,0},{18,3},{3,18},{20,5},{5,20},{6,23},{23,6},{24,9},{9,... | collective-permute-start | bytes 196616 | tf_op jit(solution)/shard_map/ppermute | solution.py:488
  43.7 1.7 %collective-permute-start.22 = (bf16[2,256,128]{2,1,0:T(8,128)(2,1)S(1)}, bf16[2,256,128]{2,1,0:T(8,128)(2,1)S(1)}, u32[]{:S(2)}, u32[]{:S(2)}) collective-permute-start(bf16[2,256,128]{2,1,0:T(8,128)(2,1)S(1)} %pad_maximum_fusion.1.near_mine), channel_id=1, source_target_pairs={{0,18},{17,3},{18,0},{3,17},{20,6},{5,23},{6,20},{23,5},{24,10},{9... | collective-permute-start | bytes 393224 | tf_op jit(solution)/shard_map/ppermute | solution.py:488
  45.7 3.0 %collective-permute-start.15 = (bf16[2,256,128]{2,1,0:T(8,128)(2,1)S(1)}, bf16[2,256,128]{2,1,0:T(8,128)(2,1)S(1)}, u32[]{:S(2)}, u32[]{:S(2)}) collective-permute-start(bf16[2,256,128]{2,1,0:T(8,128)(2,1)S(1)} %pad_maximum_fusion.near_mine), channel_id=1, source_target_pairs={{0,18},{17,3},{18,0},{3,17},{20,6},{5,23},{6,20},{23,5},{24,10},{9... | collective-permute-start | bytes 393224 | tf_op jit(solution)/shard_map/ppermute | solution.py:488
  48.7 0.5 collective-permute-start.24
  49.3 2.1 %collective-permute-done.15.far_mine = bf16[2,256,128]{2,1,0:T(8,128)(2,1)S(1)} collective-permute-done((bf16[2,256,128]{2,1,0:T(8,128)(2,1)S(1)}, bf16[2,256,128]{2,1,0:T(8,128)(2,1)S(1)}, u32[]{:S(2)}, u32[]{:S(2)}) %collective-permute-start.15) | collective-permute-done | bytes 131104 | tf_op jit(solution)/shard_map/ppermute | solution.py:488
  51.4 0.7 %collective-permute-start.17 = (bf16[2,256,128]{2,1,0:T(8,128)(2,1)S(1)}, bf16[2,256,128]{2,1,0:T(8,128)(2,1)S(1)}, u32[]{:S(2)}, u32[]{:S(2)}) collective-permute-start(bf16[2,256,128]{2,1,0:T(8,128)(2,1)S(1)} %collective-permute-done.15.far_mine), channel_id=1, source_target_pairs={{0,16},{16,0},{1,17},{17,1},{2,18},{18,2},{3,19},{19,3},{4,20},{20... | collective-permute-start | bytes 393224 | tf_op jit(solution)/shard_map/ppermute | solution.py:481
  52.1 1.1 %finish_weights.3 = (f32[1,256]{1,0:T(1,128)}, f32[256,768]{1,0:T(8,128)}, f32[256,256]{1,0:T(8,128)}) custom-call(bf16[2,256,128]{2,1,0:T(8,128)(2,1)S(1)} %pad_maximum_fusion.1.near_mine, bf16[2,256,128]{2,1,0:T(8,128)(2,1)S(1)} %collective-permute-done.22.far_mine, bf16[2,256,128]{2,1,0:T(8,128)(2,1)S(1)} %collective-permute-done.23.near_other, ...), custom_call_target="tpu_custom_call" | custom-call | tf_op jit(solution)/shard_map/finish_weights/pallas_call | solution.py:441
  53.2 1.1 %finish_weights.2 = (f32[1,256]{1,0:T(1,128)}, f32[256,768]{1,0:T(8,128)}, f32[256,256]{1,0:T(8,128)}) custom-call(bf16[2,256,128]{2,1,0:T(8,128)(2,1)S(1)} %pad_maximum_fusion.near_mine, bf16[2,256,128]{2,1,0:T(8,128)(2,1)S(1)} %collective-permute-done.15.far_mine, bf16[2,256,128]{2,1,0:T(8,128)(2,1)S(1)} %collective-permute-done.16.near_other, ...), custom_call_target="tpu_custom_call" | custom-call | tf_op jit(solution)/shard_map/finish_weights/pallas_call | solution.py:441
  (43 shorter events, 1.2 us)
Async XLA Ops:
  0.6 3.1 %collective-permute-start = (bf16[512,256]{1,0:T(8,128)(2,1)}, bf16[512,256]{1,0:T(8,128)(2,1)S(1)}, u32[]{:S(2)}, u32[]{:S(2)}) collective-permute-start(bf16[512,256]{1,0:T(8,128)(2,1)} %bitcast.7), channel_id=1, source_target_pairs={{0,16},{16,0},{1,17},{17,1},{2,18},{18,2},{3,19},{19,3},{4,20},{20... | collective-permute-start | bytes 786440 | tf_op jit(solution)/shard_map/ppermute | solution.py:481
  1.2 2.6 %collective-permute-start.4 = (bf16[512,256]{1,0:T(8,128)(2,1)}, bf16[512,256]{1,0:T(8,128)(2,1)S(1)}, u32[]{:S(2)}, u32[]{:S(2)}) collective-permute-start(bf16[512,256]{1,0:T(8,128)(2,1)} %bitcast.9), channel_id=1, source_target_pairs={{0,16},{16,0},{1,17},{17,1},{2,18},{18,2},{3,19},{19,3},{4,20},{20... | collective-permute-start | bytes 786440 | tf_op jit(solution)/shard_map/ppermute | solution.py:481
  1.2 2.5 %collective-permute-start.3 = (s32[4,128]{1,0:T(4,128)}, s32[4,128]{1,0:T(4,128)S(1)}, u32[]{:S(2)}, u32[]{:S(2)}) collective-permute-start(s32[4,128]{1,0:T(4,128)} %bitcast.11), channel_id=1, source_target_pairs={{0,16},{16,0},{1,17},{17,1},{2,18},{18,2},{3,19},{19,3},{4,20},{20... | collective-permute-start | bytes 6152 | tf_op jit(solution)/shard_map/ppermute | solution.py:481
  1.7 2.1 %collective-permute-start.1 = (s32[1,4,4]{2,1,0:T(4,128)}, s32[1,4,4]{2,1,0:T(4,128)S(1)}, u32[]{:S(2)}, u32[]{:S(2)}) collective-permute-start(s32[1,4,4]{2,1,0:T(4,128)} %lists_one_hbm.1), channel_id=1, source_target_pairs={{0,16},{16,0},{1,17},{17,1},{2,18},{18,2},{3,19},{19,3},{4,20},{20... | collective-permute-start | bytes 200 | tf_op jit(solution)/shard_map/ppermute | solution.py:481
  1.7 2.0 %collective-permute-start.2 = (s32[1,4,4]{2,1,0:T(4,128)}, s32[1,4,4]{2,1,0:T(4,128)S(1)}, u32[]{:S(2)}, u32[]{:S(2)}) collective-permute-start(s32[1,4,4]{2,1,0:T(4,128)} %lists_two_hbm.1), channel_id=1, source_target_pairs={{0,16},{16,0},{1,17},{17,1},{2,18},{18,2},{3,19},{19,3},{4,20},{20... | collective-permute-start | bytes 200 | tf_op jit(solution)/shard_map/ppermute | solution.py:481
  6.8 1.6 %collective-permute-start.5 = (bf16[1024,128]{1,0:T(8,128)(2,1)S(1)}, bf16[1024,128]{1,0:T(8,128)(2,1)S(1)}, u32[]{:S(2)}, u32[]{:S(2)}) collective-permute-start(bf16[1024,128]{1,0:T(8,128)(2,1)S(1)} %get-tuple-element.75.mixed.mixed_ref), channel_id=1, source_target_pairs={{0,16},{16,0},{1,17},{17,1},{2,18},{18,2},{3,19},{19,3},{4,20},{20... | collective-permute-start | bytes 786440 | tf_op jit(solution)/shard_map/ppermute | solution.py:481
  14.8 3.8 %collective-permute-start.6 = (bf16[1024,256]{1,0:T(8,128)(2,1)S(1)}, bf16[1024,256]{1,0:T(8,128)(2,1)S(1)}, u32[]{:S(2)}, u32[]{:S(2)}) collective-permute-start(bf16[1024,256]{1,0:T(8,128)(2,1)S(1)} %get-tuple-element.88.part_mine), channel_id=1, source_target_pairs={{0,16},{16,0},{1,17},{17,1},{2,18},{18,2},{3,19},{19,3},{4,20},{20... | collective-permute-start | bytes 1572872 | tf_op jit(solution)/shard_map/ppermute | solution.py:481
  15.9 8.1 %collective-permute-start.9 = (bf16[2,256,128]{2,1,0:T(8,128)(2,1)S(1)}, bf16[2,256,128]{2,1,0:T(8,128)(2,1)S(1)}, u32[]{:S(2)}, u32[]{:S(2)}) collective-permute-start(bf16[2,256,128]{2,1,0:T(8,128)(2,1)S(1)} %get-tuple-element.105), channel_id=1, source_target_pairs={{0,18},{17,3},{18,0},{3,17},{20,6},{5,23},{6,20},{23,5},{24,10},{9... | collective-permute-start | bytes 393224 | tf_op jit(solution)/shard_map/ppermute | solution.py:488
  23.4 3.0 %collective-permute-start.7 = (bf16[512,256]{1,0:T(8,128)(2,1)S(1)}, bf16[512,256]{1,0:T(8,128)(2,1)S(1)}, u32[]{:S(2)}, u32[]{:S(2)}) collective-permute-start(bf16[512,256]{1,0:T(8,128)(2,1)S(1)} %get-tuple-element.97), channel_id=1, source_target_pairs={{0,16},{16,0},{1,17},{17,1},{2,18},{18,2},{3,19},{19,3},{4,20},{20... | collective-permute-start | bytes 786440 | tf_op jit(solution)/shard_map/ppermute | solution.py:481
  23.6 2.8 %collective-permute-start.8 = (bf16[512,128]{1,0:T(8,128)(2,1)S(1)}, bf16[512,128]{1,0:T(8,128)(2,1)S(1)}, u32[]{:S(2)}, u32[]{:S(2)}) collective-permute-start(bf16[512,128]{1,0:T(8,128)(2,1)S(1)} %get-tuple-element.99), channel_id=1, source_target_pairs={{0,16},{16,0},{1,17},{17,1},{2,18},{18,2},{3,19},{19,3},{4,20},{20... | collective-permute-start | bytes 393224 | tf_op jit(solution)/shard_map/ppermute | solution.py:481
  24.0 4.4 %collective-permute-start.10 = (bf16[2,256,128]{2,1,0:T(8,128)(2,1)S(1)}, bf16[2,256,128]{2,1,0:T(8,128)(2,1)S(1)}, u32[]{:S(2)}, u32[]{:S(2)}) collective-permute-start(bf16[2,256,128]{2,1,0:T(8,128)(2,1)S(1)} %get-tuple-element.107), channel_id=1, source_target_pairs={{0,18},{17,3},{18,0},{3,17},{20,6},{5,23},{6,20},{23,5},{24,10},{9... | collective-permute-start | bytes 393224 | tf_op jit(solution)/shard_map/ppermute | solution.py:488
  25.2 5.2 %collective-permute-start.18 = (bf16[1,256,128]{2,1,0:T(8,128)(2,1)S(1)}, bf16[1,256,128]{2,1,0:T(8,128)(2,1)S(1)}, u32[]{:S(2)}, u32[]{:S(2)}) collective-permute-start(bf16[1,256,128]{2,1,0:T(8,128)(2,1)S(1)} %slice.19), channel_id=1, source_target_pairs={{0,17},{17,0},{18,3},{3,18},{20,5},{5,20},{6,23},{23,6},{24,9},{9,... | collective-permute-start | bytes 196616 | tf_op jit(solution)/shard_map/ppermute | solution.py:488
  27.8 24.3 %copy-start = (bf16[256,768]{1,0:T(8,128)(2,1)S(1)}, bf16[256,768]{1,0:T(8,128)(2,1)}, u32[]{:S(2)}) copy-start(bf16[256,768]{1,0:T(8,128)(2,1)} %weight.3) | copy-start | bytes 1179652
  27.8 25.4 %copy-start.1 = (bf16[256,768]{1,0:T(8,128)(2,1)S(1)}, bf16[256,768]{1,0:T(8,128)(2,1)}, u32[]{:S(2)}) copy-start(bf16[256,768]{1,0:T(8,128)(2,1)} %weight.2) | copy-start | bytes 1179652
  28.5 4.0 %collective-permute-start.11 = (bf16[1,256,128]{2,1,0:T(8,128)(2,1)S(1)}, bf16[1,256,128]{2,1,0:T(8,128)(2,1)S(1)}, u32[]{:S(2)}, u32[]{:S(2)}) collective-permute-start(bf16[1,256,128]{2,1,0:T(8,128)(2,1)S(1)} %slice.17), channel_id=1, source_target_pairs={{0,17},{17,0},{18,3},{3,18},{20,5},{5,20},{6,23},{23,6},{24,9},{9,... | collective-permute-start | bytes 196616 | tf_op jit(solution)/shard_map/ppermute | solution.py:488
  30.5 3.9 %collective-permute-start.19 = (bf16[1,256,128]{2,1,0:T(8,128)(2,1)S(1)}, bf16[1,256,128]{2,1,0:T(8,128)(2,1)S(1)}, u32[]{:S(2)}, u32[]{:S(2)}) collective-permute-start(bf16[1,256,128]{2,1,0:T(8,128)(2,1)S(1)} %add_convert_fusion.4), channel_id=1, source_target_pairs={{0,20},{17,5},{18,6},{3,23},{20,0},{5,17},{6,18},{23,3},{24,12},{9... | collective-permute-start | bytes 196616 | tf_op jit(solution)/shard_map/ppermute | solution.py:488
  32.4 4.8 %collective-permute-start.12 = (bf16[1,256,128]{2,1,0:T(8,128)(2,1)S(1)}, bf16[1,256,128]{2,1,0:T(8,128)(2,1)S(1)}, u32[]{:S(2)}, u32[]{:S(2)}) collective-permute-start(bf16[1,256,128]{2,1,0:T(8,128)(2,1)S(1)} %add_convert_fusion.7), channel_id=1, source_target_pairs={{0,20},{17,5},{18,6},{3,23},{20,0},{5,17},{6,18},{23,3},{24,12},{9... | collective-permute-start | bytes 196616 | tf_op jit(solution)/shard_map/ppermute | solution.py:488
  34.4 5.3 %collective-permute-start.20 = (bf16[1,256,128]{2,1,0:T(8,128)(2,1)S(1)}, bf16[1,256,128]{2,1,0:T(8,128)(2,1)S(1)}, u32[]{:S(2)}, u32[]{:S(2)}) collective-permute-start(bf16[1,256,128]{2,1,0:T(8,128)(2,1)S(1)} %add_convert_fusion.3), channel_id=1, source_target_pairs={{0,24},{17,9},{18,10},{3,27},{20,12},{5,29},{6,30},{23,15},{24,0},... | collective-permute-start | bytes 196616 | tf_op jit(solution)/shard_map/ppermute | solution.py:488
  37.3 4.7 %collective-permute-start.13 = (bf16[1,256,128]{2,1,0:T(8,128)(2,1)S(1)}, bf16[1,256,128]{2,1,0:T(8,128)(2,1)S(1)}, u32[]{:S(2)}, u32[]{:S(2)}) collective-permute-start(bf16[1,256,128]{2,1,0:T(8,128)(2,1)S(1)} %add_convert_fusion.6), channel_id=1, source_target_pairs={{0,24},{17,9},{18,10},{3,27},{20,12},{5,29},{6,30},{23,15},{24,0},... | collective-permute-start | bytes 196616 | tf_op jit(solution)/shard_map/ppermute | solution.py:488
  39.7 4.0 %collective-permute-start.21 = (bf16[1,256,128]{2,1,0:T(8,128)(2,1)S(1)}, bf16[1,256,128]{2,1,0:T(8,128)(2,1)S(1)}, u32[]{:S(2)}, u32[]{:S(2)}) collective-permute-start(bf16[1,256,128]{2,1,0:T(8,128)(2,1)S(1)} %add_convert_fusion.2), channel_id=1, source_target_pairs={{0,17},{17,0},{18,3},{3,18},{20,5},{5,20},{6,23},{23,6},{24,9},{9,... | collective-permute-start | bytes 196616 | tf_op jit(solution)/shard_map/ppermute | solution.py:488
  41.9 3.8 %collective-permute-start.14 = (bf16[1,256,128]{2,1,0:T(8,128)(2,1)S(1)}, bf16[1,256,128]{2,1,0:T(8,128)(2,1)S(1)}, u32[]{:S(2)}, u32[]{:S(2)}) collective-permute-start(bf16[1,256,128]{2,1,0:T(8,128)(2,1)S(1)} %add_convert_fusion.5), channel_id=1, source_target_pairs={{0,17},{17,0},{18,3},{3,18},{20,5},{5,20},{6,23},{23,6},{24,9},{9,... | collective-permute-start | bytes 196616 | tf_op jit(solution)/shard_map/ppermute | solution.py:488
  43.7 5.0 %collective-permute-start.22 = (bf16[2,256,128]{2,1,0:T(8,128)(2,1)S(1)}, bf16[2,256,128]{2,1,0:T(8,128)(2,1)S(1)}, u32[]{:S(2)}, u32[]{:S(2)}) collective-permute-start(bf16[2,256,128]{2,1,0:T(8,128)(2,1)S(1)} %pad_maximum_fusion.1.near_mine), channel_id=1, source_target_pairs={{0,18},{17,3},{18,0},{3,17},{20,6},{5,23},{6,20},{23,5},{24,10},{9... | collective-permute-start | bytes 393224 | tf_op jit(solution)/shard_map/ppermute | solution.py:488
  45.7 5.7 %collective-permute-start.15 = (bf16[2,256,128]{2,1,0:T(8,128)(2,1)S(1)}, bf16[2,256,128]{2,1,0:T(8,128)(2,1)S(1)}, u32[]{:S(2)}, u32[]{:S(2)}) collective-permute-start(bf16[2,256,128]{2,1,0:T(8,128)(2,1)S(1)} %pad_maximum_fusion.near_mine), channel_id=1, source_target_pairs={{0,18},{17,3},{18,0},{3,17},{20,6},{5,23},{6,20},{23,5},{24,10},{9... | collective-permute-start | bytes 393224 | tf_op jit(solution)/shard_map/ppermute | solution.py:488
  48.7 3.4 %collective-permute-start.23 = (bf16[2,256,128]{2,1,0:T(8,128)(2,1)S(1)}, bf16[2,256,128]{2,1,0:T(8,128)(2,1)S(1)}, u32[]{:S(2)}, u32[]{:S(2)}) collective-permute-start(bf16[2,256,128]{2,1,0:T(8,128)(2,1)S(1)} %pad_maximum_fusion.1.near_mine), channel_id=1, source_target_pairs={{0,16},{16,0},{1,17},{17,1},{2,18},{18,2},{3,19},{19,3},{4,20},{20... | collective-permute-start | bytes 393224 | tf_op jit(solution)/shard_map/ppermute | solution.py:481
  48.7 3.4 %collective-permute-start.24 = (bf16[2,256,128]{2,1,0:T(8,128)(2,1)S(1)}, bf16[2,256,128]{2,1,0:T(8,128)(2,1)S(1)}, u32[]{:S(2)}, u32[]{:S(2)}) collective-permute-start(bf16[2,256,128]{2,1,0:T(8,128)(2,1)S(1)} %collective-permute-done.22.far_mine), channel_id=1, source_target_pairs={{0,16},{16,0},{1,17},{17,1},{2,18},{18,2},{3,19},{19,3},{4,20},{20... | collective-permute-start | bytes 393224 | tf_op jit(solution)/shard_map/ppermute | solution.py:481
  49.3 4.0 %collective-permute-start.16 = (bf16[2,256,128]{2,1,0:T(8,128)(2,1)S(1)}, bf16[2,256,128]{2,1,0:T(8,128)(2,1)S(1)}, u32[]{:S(2)}, u32[]{:S(2)}) collective-permute-start(bf16[2,256,128]{2,1,0:T(8,128)(2,1)S(1)} %pad_maximum_fusion.near_mine), channel_id=1, source_target_pairs={{0,16},{16,0},{1,17},{17,1},{2,18},{18,2},{3,19},{19,3},{4,20},{20... | collective-permute-start | bytes 393224 | tf_op jit(solution)/shard_map/ppermute | solution.py:481
  51.4 1.8 %collective-permute-start.17 = (bf16[2,256,128]{2,1,0:T(8,128)(2,1)S(1)}, bf16[2,256,128]{2,1,0:T(8,128)(2,1)S(1)}, u32[]{:S(2)}, u32[]{:S(2)}) collective-permute-start(bf16[2,256,128]{2,1,0:T(8,128)(2,1)S(1)} %collective-permute-done.15.far_mine), channel_id=1, source_target_pairs={{0,16},{16,0},{1,17},{17,1},{2,18},{18,2},{3,19},{19,3},{4,20},{20... | collective-permute-start | bytes 393224 | tf_op jit(solution)/shard_map/ppermute | solution.py:481
